TPU v7x, 32 devices: a whole 2x2x4 slice. The times are simulated.
32 devices in a mesh: groups: 2 (over y), replica: 4 (over z), tensor: 4 (over x, core).
Axes of the slice: x: 2, y: 2, z: 4, core: 2. Of those that a mesh axis runs over, the one named last changes fastest.
Arguments:
- x_new: bfloat16 [2048, 8192], P(('groups', 'replica'), 'tensor'), parts along dimension 0, may hold values from -6 to 6
- z_new: bfloat16 [2048, 8192], P(('groups', 'replica'), 'tensor'), parts along dimension 0, may hold values from -6 to 6
- conv_weight: bfloat16 [4, 8192], P(None, 'tensor'), may hold values from -3 to 3
- conv_bias: float32 [8192], P('tensor'), may hold values from -0.5 to 0.5
- x_proj_weight: bfloat16 [8192, 288], P('tensor'), may hold values from -0.0625 to 0.0625
- dt_proj_weight: bfloat16 [256, 8192], P(None, 'tensor'), may hold values from -0.75 to 0.75
- dt_bias: float32 [8192], P('tensor'), may hold values from -6 to -2.5
- a_log: float32 [16, 8192], P(None, 'tensor'), may hold values from 0 to 2.8
- d_skip: float32 [8192], P('tensor'), may hold values from 0.5 to 1.5
- cache_ssm: bfloat16 [16, 16, 8192], P(('groups', 'replica'), None, 'tensor'), parts along dimension 0, may hold values from -6 to 6
- cache_conv: bfloat16 [16, 3, 8192], P(('groups', 'replica'), None, 'tensor'), parts along dimension 0, may hold values from -6 to 6
- holder: int32 [64], P('groups'), parts along dimension 0, may hold values from 0 to 3, as said below
- slot_id: int32 [64], P('groups'), parts along dimension 0, may hold values from 0 to 1, as said below
- prefix_len: int32 [64], P('groups'), parts along dimension 0, may hold values from 0 to 4096, as said below
Outputs:
- gated_out: bfloat16 [2048, 8192], P(('groups', 'replica'), 'tensor'), parts along dimension 0
- new_state: bfloat16 [64, 16, 8192], P(('groups', 'replica'), None, 'tensor'), parts along dimension 0
There are 2 independent parts, one for each index of `groups`. A program takes and returns all parts, laid end to end along the dimension named above; an argument that names none is the same for every part. Nothing has to cross between parts.
Inputs may be any that keep to these rules, and one draw needn't show every extreme that they name: `holder`: every replica holds some request's prefix. `slot_id`: slot among the holder's 2 slots. `prefix_len`: 0 means no cached prefix.
All inputs are finite; a program needn't handle non-finite values.
Results may differ from a plain program's by a relative error of at most 0.0077.
Values may be sent and summed in bfloat16 or wider, within the bound.
No kernel may reach another device: no remote copies, remote signals or barrier semaphores. Data moves between devices by JAX's collectives and lax.ppermute only.
A program may use at most 64 MiB of HBM per device.

v0:
```python
import jax
import jax.numpy as jnp
from jax import lax
from jax.sharding import PartitionSpec as P

NEW = 32


def conv_mix(history, tokens_in, conv_weight, conv_bias):
    tap_count = conv_weight.shape[0]
    length = tokens_in.shape[1]
    joined = jnp.concatenate([history, tokens_in], axis=1)
    summed = jnp.zeros(tokens_in.shape, jnp.float32) + conv_bias
    for offset in range(tap_count):
        summed = summed + joined[:, offset : offset + length].astype(jnp.float32) * conv_weight[
            offset
        ].astype(jnp.float32)
    return jax.nn.silu(summed).astype(jnp.bfloat16)


def time_blocks(values, per_dev, block_len):
    ordered = values.reshape(per_dev, NEW, -1).transpose(1, 0, 2)
    return ordered.reshape((NEW // block_len, block_len) + ordered.shape[1:])


def shards(
    x_new,
    z_new,
    conv_weight,
    conv_bias,
    x_proj_weight,
    dt_proj_weight,
    dt_bias,
    a_log,
    d_skip,
    cache_ssm,
    cache_conv,
    holder,
    slot_id,
    prefix_len,
):
    channels = x_new.shape[1]
    per_dev = x_new.shape[0] // NEW
    state_dim = a_log.shape[0]
    rank_width = dt_proj_weight.shape[0]
    tap_count = conv_weight.shape[0]
    slot_index = holder * cache_ssm.shape[0] + slot_id
    first_req = lax.axis_index("replica") * per_dev
    own_slots = lax.dynamic_slice_in_dim(slot_index, first_req, per_dev)
    own_len = lax.dynamic_slice_in_dim(prefix_len, first_req, per_dev)
    initial = (
        jnp.zeros((per_dev,) + cache_ssm.shape[1:], cache_ssm.dtype),
        jnp.zeros((per_dev,) + cache_conv.shape[1:], cache_conv.dtype),
    )
    pieces = (
        lax.all_gather(cache_ssm, "replica", axis=0, tiled=True),
        lax.all_gather(cache_conv, "replica", axis=0, tiled=True),
    )
    piece_rows = pieces[0].shape[0]
    present = (own_slots >= 0) & (own_slots < piece_rows)
    clipped = jnp.clip(own_slots, 0, piece_rows - 1)
    found_ssm = jnp.take(pieces[0], clipped, axis=0)
    found_conv = jnp.take(pieces[1], clipped, axis=0)
    keep_mask = present[:, None, None]
    fetched_ssm = jnp.where(keep_mask, found_ssm, initial[0])
    fetched_conv = jnp.where(keep_mask, found_conv, initial[1])
    has_cache = own_len > 0
    fetched_float = fetched_ssm.astype(jnp.float32)
    start_state = jnp.where(has_cache[:, None, None], fetched_float, jnp.zeros_like(fetched_float))
    row_age = tap_count - 1 - jnp.arange(tap_count - 1, dtype=jnp.int32)
    conv_live = row_age[None, :] <= own_len[:, None]
    history = jnp.where(conv_live[:, :, None], fetched_conv, jnp.zeros_like(fetched_conv))
    mixed = conv_mix(history, x_new.reshape(per_dev, NEW, channels), conv_weight, conv_bias)
    flat_rows = mixed.reshape(per_dev * NEW, channels)
    partial_sum = jnp.dot(flat_rows, x_proj_weight, preferred_element_type=jnp.float32)
    projected = lax.psum(partial_sum, "tensor")
    dt_low = projected[:, :rank_width].astype(jnp.bfloat16)
    b_rows = projected[:, rank_width : rank_width + state_dim]
    c_rows = projected[:, rank_width + state_dim :]
    step_size = jax.nn.softplus(
        jnp.dot(dt_low, dt_proj_weight, preferred_element_type=jnp.float32) + dt_bias
    )
    a_matrix = -jnp.exp(a_log)
    mixed_float = flat_rows.astype(jnp.float32)
    driven = step_size * mixed_float
    block_len = 8

    def advance_block(state_now, token_data):
        results = []
        for position in range(block_len):
            step_now, drive_now, mixed_now, b_values, c_values = [
                member[position] for member in token_data
            ]
            state_now = (
                jnp.exp(step_now[:, None, :] * a_matrix) * state_now
                + drive_now[:, None, :] * b_values[:, :, None]
            )
            results.append(jnp.sum(c_values[:, :, None] * state_now, axis=1) + d_skip * mixed_now)
        return (state_now, jnp.stack(results))

    token_data = tuple(
        (
            time_blocks(member, per_dev, block_len)
            for member in (step_size, driven, mixed_float, b_rows, c_rows)
        )
    )
    final_state, outputs = lax.scan(advance_block, start_state, token_data)
    ssm_out = (
        outputs.reshape(NEW, per_dev, channels).transpose(1, 0, 2).reshape(per_dev * NEW, channels)
    )
    gated_out = (ssm_out * jax.nn.silu(z_new.astype(jnp.float32))).astype(jnp.bfloat16)
    return (gated_out, final_state.astype(jnp.bfloat16))


def solution(mesh):
    placed = (
        P(("groups", "replica"), "tensor"),
        P(("groups", "replica"), "tensor"),
        P(None, "tensor"),
        P("tensor"),
        P("tensor", None),
        P(None, "tensor"),
        P("tensor"),
        P(None, "tensor"),
        P("tensor"),
        P(("groups", "replica"), None, "tensor"),
        P(("groups", "replica"), None, "tensor"),
        P("groups"),
        P("groups"),
        P("groups"),
    )
    return jax.shard_map(
        shards,
        mesh=mesh,
        in_specs=placed,
        out_specs=(P(("groups", "replica"), "tensor"), P(("groups", "replica"), None, "tensor")),
        check_vma=False,
    )
```

profile of v0, /device:TPU:0, one launch (start us, length us, event | category | flops | bytes accessed | tf_op | source)
XLA Modules:
  0.0 147.4 jit_solution(17552744590372009479)
XLA Ops:
  8.9 15.1 %all_gather.7 = bf16[8,3,2048]{2,1,0:T(4,128)(2,1)S(1)} all-gather(bf16[2,3,2048]{2,1,0:T(4,128)(2,1)S(1)} %copy.30), channel_id=1, replica_groups=mesh['groups'=2,'replica'=4,'tensor'=4] {'replica'}, dimensions={0}, use_global_device_ids=true | all-gather | bytes 122880 | tf_op jit(solution)/shard_map/all_gather | solution.py:57
  26.5 4.7 %convert_bitcast_fusion = (f32[32,8,2048]{2,0,1:T(8,128)}, bf16[8,32,2048]{2,1,0:T(8,128)(2,1)S(1)}) fusion(f32[2048]{0:T(1024)S(1)} %bitcast.234, bf16[8,32,2048]{2,1,0:T(8,128)(2,1)} %bitcast.227, f32[2048]{0:T(1024)S(1)} %bitcast.235, bf16[8,3,2048]{2,1,0:T(4,128)(2,1)S(1)} %select_select_fusion, f32[2048]{0:T(1024)S(1)} %bitcast.233, ...), kind=kLoop, calls=%fused_computation.107 | loop fusion | flops 14155776 | bytes 4333568 | tf_op jit(solution)/shard_map/reshape | solution.py:23
  32.4 16.1 %all_gather.6 = bf16[8,16,2048]{2,1,0:T(8,128)(2,1)S(1)} all-gather(bf16[2,16,2048]{2,1,0:T(8,128)(2,1)S(1)} %copy-done.3), channel_id=1, replica_groups=mesh['groups'=2,'replica'=4,'tensor'=4] {'replica'}, dimensions={0}, use_global_device_ids=true | all-gather | bytes 655360 | tf_op jit(solution)/shard_map/all_gather | solution.py:56
  48.5 1.4 gather_fusion
  51.2 4.2 %copy.35 = f32[32,8,2048]{2,1,0:T(8,128)} copy(f32[32,8,2048]{2,0,1:T(8,128)} %get-tuple-element.87) | data formatting | bytes 4194304 | tf_op jit(solution)/shard_map/reshape | solution.py:23
  55.3 10.7 %all-reduce.2.cloned.1.call-done = f32[256,288]{0,1:T(8,128)} async-done(((f32[256,288]{0,1:T(8,128)}), f32[256,288]{0,1:T(8,128)}) %all-reduce.2.cloned.1.call-update) | async-done | bytes 294928 | tf_op jit(solution)/shard_map/psum | solution.py:76
  66.0 2.8 %convert_multiply_fusion.1 = (f32[256,2048]{1,0:T(8,128)S(1)}, f32[256,2048]{1,0:T(8,128)S(1)}) fusion(bf16[8,32,2048]{2,1,0:T(8,128)(2,1)S(1)} %get-tuple-element.88, f32[2048]{0:T(1024)S(1)} %copy-done.5, bf16[256,2048]{1,0:T(8,128)(2,1)} %param.21, f32[256,288]{0,1:T(8,128)} %all-reduce.2.cloned.1.call-done), kind=kOutput, calls=%fused_computation.108 | convolution fusion | flops 273154048 | bytes 6430720 | tf_op jit(solution)/shard_map/dot_general | solution.py:81
  68.9 2.5 %copy.31 = f32[32,8,2048]{2,1,0:T(8,128)} copy(f32[32,8,2048]{2,0,1:T(8,128)S(1)} %bitcast.226) | data formatting | bytes 4194304 | tf_op jit(solution)/shard_map/transpose | solution.py:22
  71.4 2.5 %copy.32 = f32[32,8,2048]{2,1,0:T(8,128)} copy(f32[32,8,2048]{2,0,1:T(8,128)S(1)} %bitcast.225) | data formatting | bytes 4194304 | tf_op jit(solution)/shard_map/transpose | solution.py:22
  75.1 60.0 %while.12 = (s32[]{:T(128)}, f32[8,16,2048]{2,1,0:T(8,128)S(1)}, f32[4,8,8,2048]{3,2,1,0:T(8,128)}, f32[4,8,8,2048]{3,2,1,0:T(8,128)}, f32[16,2048]{1,0:T(8,128)...) while((s32[]{:T(128)}, f32[8,16,2048]{2,1,0:T(8,128)S(1)}, ...), condition=%wide.region_10.11_spmd, body=%wide.region_1.10_spmd.sunk | while | flops 19005448 | bytes 12808061 | solution.py:107
  76.7 1.5 %multiply_reduce_fusion.12 = (f32[8,2048]{1,0:T(8,128)S(1)}, f32[8,2048]{1,0:T(8,128)S(1)}, f32[8,2048]{1,0:T(8,128)S(1)}) fusion(f32[8,16]{1,0:T(8,128)S(1)} %get-tuple-element.279, f32[8,16]{1,0:T(8,128)S(1)} %get-tuple-element.268, f32[8,2048]{1,0:T(8,128)S(1)} %get-tuple-element.269, f32[8,2048]{1,0:T(8,128)S(1)} %get-tuple-element.276, ...), kind=kLoop, calls=%fused_computation.7.clone.1 | loop fusion | flops 4669440 | bytes 1772544 | tf_op jit(solution)/shard_map/while/body/eval_jaxpr/reduce_sum | solution.py:98
  78.2 2.5 %multiply_reduce_fusion.11 = (f32[8,2048]{1,0:T(8,128)S(1)}, f32[8,16,2048]{2,1,0:T(8,128)S(1)}, f32[8,16,2048]{2,1,0:T(8,128)S(1)}) fusion(f32[8,16]{1,0:T(8,128)S(1)} %get-tuple-element.253, f32[8,16]{1,0:T(8,128)S(1)} %get-tuple-element.254, f32[8,2048]{1,0:T(8,128)S(1)} %get-tuple-element.255, f32[8,16]{1,0:T(8,128)S(1)} %get-tuple-element.256, ...), kind=kLoop, calls=%fused_computation.2.clone.1 | loop fusion | flops 8896512 | bytes 4395520 | tf_op jit(solution)/shard_map/while/body/eval_jaxpr/reduce_sum | solution.py:98
  80.7 1.8 %multiply_reduce_fusion.13 = (f32[8,2048]{1,0:T(8,128)S(1)}, f32[8,2048]{1,0:T(8,128)S(1)}, f32[8,2048]{1,0:T(8,128)S(1)}, f32[8,2048]{1,0:T(8,128)S(1)}) fusion(f32[8,16]{1,0:T(8,128)S(1)} %get-tuple-element.285, f32[8,16]{1,0:T(8,128)S(1)} %get-tuple-element.256, f32[8,2048]{1,0:T(8,128)S(1)} %get-tuple-element.257, ...), kind=kLoop, calls=%fused_computation.3.clone.1 | loop fusion | flops 5177344 | bytes 1838592 | tf_op jit(solution)/shard_map/while/body/eval_jaxpr/reduce_sum | solution.py:98
  91.6 1.5 %multiply_reduce_fusion.12 = (f32[8,2048]{1,0:T(8,128)S(1)}, f32[8,2048]{1,0:T(8,128)S(1)}, f32[8,2048]{1,0:T(8,128)S(1)}) fusion(f32[8,16]{1,0:T(8,128)S(1)} %get-tuple-element.279, f32[8,16]{1,0:T(8,128)S(1)} %get-tuple-element.268, f32[8,2048]{1,0:T(8,128)S(1)} %get-tuple-element.269, f32[8,2048]{1,0:T(8,128)S(1)} %get-tuple-element.276, ...), kind=kLoop, calls=%fused_computation.7.clone.1 | loop fusion | flops 4669440 | bytes 1772544 | tf_op jit(solution)/shard_map/while/body/eval_jaxpr/reduce_sum | solution.py:98
  93.1 2.5 %multiply_reduce_fusion.11 = (f32[8,2048]{1,0:T(8,128)S(1)}, f32[8,16,2048]{2,1,0:T(8,128)S(1)}, f32[8,16,2048]{2,1,0:T(8,128)S(1)}) fusion(f32[8,16]{1,0:T(8,128)S(1)} %get-tuple-element.253, f32[8,16]{1,0:T(8,128)S(1)} %get-tuple-element.254, f32[8,2048]{1,0:T(8,128)S(1)} %get-tuple-element.255, f32[8,16]{1,0:T(8,128)S(1)} %get-tuple-element.256, ...), kind=kLoop, calls=%fused_computation.2.clone.1 | loop fusion | flops 8896512 | bytes 4395520 | tf_op jit(solution)/shard_map/while/body/eval_jaxpr/reduce_sum | solution.py:98
  95.7 1.8 %multiply_reduce_fusion.13 = (f32[8,2048]{1,0:T(8,128)S(1)}, f32[8,2048]{1,0:T(8,128)S(1)}, f32[8,2048]{1,0:T(8,128)S(1)}, f32[8,2048]{1,0:T(8,128)S(1)}) fusion(f32[8,16]{1,0:T(8,128)S(1)} %get-tuple-element.285, f32[8,16]{1,0:T(8,128)S(1)} %get-tuple-element.256, f32[8,2048]{1,0:T(8,128)S(1)} %get-tuple-element.257, ...), kind=kLoop, calls=%fused_computation.3.clone.1 | loop fusion | flops 5177344 | bytes 1838592 | tf_op jit(solution)/shard_map/while/body/eval_jaxpr/reduce_sum | solution.py:98
  106.6 1.5 %multiply_reduce_fusion.12 = (f32[8,2048]{1,0:T(8,128)S(1)}, f32[8,2048]{1,0:T(8,128)S(1)}, f32[8,2048]{1,0:T(8,128)S(1)}) fusion(f32[8,16]{1,0:T(8,128)S(1)} %get-tuple-element.279, f32[8,16]{1,0:T(8,128)S(1)} %get-tuple-element.268, f32[8,2048]{1,0:T(8,128)S(1)} %get-tuple-element.269, f32[8,2048]{1,0:T(8,128)S(1)} %get-tuple-element.276, ...), kind=kLoop, calls=%fused_computation.7.clone.1 | loop fusion | flops 4669440 | bytes 1772544 | tf_op jit(solution)/shard_map/while/body/eval_jaxpr/reduce_sum | solution.py:98
  108.1 2.5 %multiply_reduce_fusion.11 = (f32[8,2048]{1,0:T(8,128)S(1)}, f32[8,16,2048]{2,1,0:T(8,128)S(1)}, f32[8,16,2048]{2,1,0:T(8,128)S(1)}) fusion(f32[8,16]{1,0:T(8,128)S(1)} %get-tuple-element.253, f32[8,16]{1,0:T(8,128)S(1)} %get-tuple-element.254, f32[8,2048]{1,0:T(8,128)S(1)} %get-tuple-element.255, f32[8,16]{1,0:T(8,128)S(1)} %get-tuple-element.256, ...), kind=kLoop, calls=%fused_computation.2.clone.1 | loop fusion | flops 8896512 | bytes 4395520 | tf_op jit(solution)/shard_map/while/body/eval_jaxpr/reduce_sum | solution.py:98
  110.6 1.8 %multiply_reduce_fusion.13 = (f32[8,2048]{1,0:T(8,128)S(1)}, f32[8,2048]{1,0:T(8,128)S(1)}, f32[8,2048]{1,0:T(8,128)S(1)}, f32[8,2048]{1,0:T(8,128)S(1)}) fusion(f32[8,16]{1,0:T(8,128)S(1)} %get-tuple-element.285, f32[8,16]{1,0:T(8,128)S(1)} %get-tuple-element.256, f32[8,2048]{1,0:T(8,128)S(1)} %get-tuple-element.257, ...), kind=kLoop, calls=%fused_computation.3.clone.1 | loop fusion | flops 5177344 | bytes 1838592 | tf_op jit(solution)/shard_map/while/body/eval_jaxpr/reduce_sum | solution.py:98
  121.5 1.5 %multiply_reduce_fusion.12 = (f32[8,2048]{1,0:T(8,128)S(1)}, f32[8,2048]{1,0:T(8,128)S(1)}, f32[8,2048]{1,0:T(8,128)S(1)}) fusion(f32[8,16]{1,0:T(8,128)S(1)} %get-tuple-element.279, f32[8,16]{1,0:T(8,128)S(1)} %get-tuple-element.268, f32[8,2048]{1,0:T(8,128)S(1)} %get-tuple-element.269, f32[8,2048]{1,0:T(8,128)S(1)} %get-tuple-element.276, ...), kind=kLoop, calls=%fused_computation.7.clone.1 | loop fusion | flops 4669440 | bytes 1772544 | tf_op jit(solution)/shard_map/while/body/eval_jaxpr/reduce_sum | solution.py:98
  123.0 2.5 %multiply_reduce_fusion.11 = (f32[8,2048]{1,0:T(8,128)S(1)}, f32[8,16,2048]{2,1,0:T(8,128)S(1)}, f32[8,16,2048]{2,1,0:T(8,128)S(1)}) fusion(f32[8,16]{1,0:T(8,128)S(1)} %get-tuple-element.253, f32[8,16]{1,0:T(8,128)S(1)} %get-tuple-element.254, f32[8,2048]{1,0:T(8,128)S(1)} %get-tuple-element.255, f32[8,16]{1,0:T(8,128)S(1)} %get-tuple-element.256, ...), kind=kLoop, calls=%fused_computation.2.clone.1 | loop fusion | flops 8896512 | bytes 4395520 | tf_op jit(solution)/shard_map/while/body/eval_jaxpr/reduce_sum | solution.py:98
  125.6 1.8 %multiply_reduce_fusion.13 = (f32[8,2048]{1,0:T(8,128)S(1)}, f32[8,2048]{1,0:T(8,128)S(1)}, f32[8,2048]{1,0:T(8,128)S(1)}, f32[8,2048]{1,0:T(8,128)S(1)}) fusion(f32[8,16]{1,0:T(8,128)S(1)} %get-tuple-element.285, f32[8,16]{1,0:T(8,128)S(1)} %get-tuple-element.256, f32[8,2048]{1,0:T(8,128)S(1)} %get-tuple-element.257, ...), kind=kLoop, calls=%fused_computation.3.clone.1 | loop fusion | flops 5177344 | bytes 1838592 | tf_op jit(solution)/shard_map/while/body/eval_jaxpr/reduce_sum | solution.py:98
  135.1 2.9 %copy.36 = f32[32,8,2048]{2,0,1:T(8,128)S(1)} copy(f32[32,8,2048]{2,1,0:T(8,128)} %bitcast.224) | data formatting | bytes 4194304 | tf_op jit(solution)/shard_map/reshape | solution.py:109
  138.9 1.6 %fusion.44 = bf16[256,2048]{1,0:T(8,128)(2,1)} fusion(bf16[256,2048]{1,0:T(8,128)(2,1)S(1)} %copy-done.2, f32[32,8,2048]{2,0,1:T(8,128)S(1)} %copy.36), kind=kLoop, calls=%fused_computation.110 | loop fusion | flops 3670016 | bytes 4194304 | tf_op jit(solution)/shard_map/convert_element_type | solution.py:111
  (78 shorter events, 45.1 us)
Async XLA Ops:
  7.2 24.0 %copy-start = (bf16[2048,288]{0,1:T(8,128)(2,1)S(1)}, bf16[2048,288]{0,1:T(8,128)(2,1)}, u32[]{:S(2)}) copy-start(bf16[2048,288]{0,1:T(8,128)(2,1)} %param.20) | copy-start | bytes 3538948
  7.2 58.9 %all-reduce.2.cloned.1.call-start = ((), (), s32[]{:S(2)}) async-start(), calls=%async_computation | async-start | bytes 589824 | tf_op jit(solution)/shard_map/psum | solution.py:76
  31.1 1.3 copy-start.3
  32.3 18.8 %copy-start.4 = (f32[16,2048]{1,0:T(8,128)S(1)}, f32[16,2048]{1,0:T(8,128)}, u32[]{:S(2)}) copy-start(f32[16,2048]{1,0:T(8,128)} %param.23) | copy-start | bytes 393220
  51.2 14.9 %copy-start.5 = (f32[2048]{0:T(1024)S(1)}, f32[2048]{0:T(1024)}, u32[]{:S(2)}) copy-start(f32[2048]{0:T(1024)} %param.22) | copy-start | bytes 24580
  71.4 3.7 %copy-start.1 = (f32[2048]{0:T(1024)S(1)}, f32[2048]{0:T(1024)}, u32[]{:S(2)}) copy-start(f32[2048]{0:T(1024)} %param.24) | copy-start | bytes 24580
  135.1 3.8 %copy-start.2 = (bf16[256,2048]{1,0:T(8,128)(2,1)S(1)}, bf16[256,2048]{1,0:T(8,128)(2,1)}, u32[]{:S(2)}) copy-start(bf16[256,2048]{1,0:T(8,128)(2,1)} %param.17) | copy-start | bytes 3145732
Sparse Core Ops, SparseCore 0:
  32.5 33.4 all-reduce.1
where the time goes:
time: 150 us; the launch traced here: 147 us
  other arithmetic  62 us (41%)
  blocking collectives  31.2 us (21%)
  local copies, waits for them, and re-layouts  24.9 us (17%)
  between operations  14.2 us (9%)
  waiting for transfers between devices  10.7 us (7%)
  matrix products  4.07 us (3%)
    while x28, other arithmetic  24.1 us
    reduce_sum x12, other arithmetic, advance_block(): jnp.sum(c_values[:, :, None] * state_now, axis=1) + d_skip * mixed_now  23.3 us
    all_gather x1, blocking collectives, shards(): lax.all_gather(cache_ssm, 'replica', axis=0, tiled=True)  16.1 us
    all_gather x1, blocking collectives, shards(): lax.all_gather(cache_conv, 'replica', axis=0, tiled=True)  15.1 us
    psum x1, waiting for transfers between devices, shards(): projected = lax.psum(partial_sum, 'tensor')  10.7 us
    mul x8, local copies, waits for them, and re-layouts, advance_block(): drive_now[:, None, :] * b_values[:, :, None]  5.39 us
    transpose x4, local copies, waits for them, and re-layouts, time_blocks(): ordered = values.reshape(per_dev, NEW, -1).transpose(1, 0, 2)  5.3 us
    reshape x1, other arithmetic, time_blocks(): return ordered.reshape((NEW // block_len, block_len) + ordered.shape[1:])  4.66 us
  transfers between devices with their start and end apart: 1, of which 1 were waited for; matrix products, arithmetic and copies ran while one was open for 5% of the time, Pallas kernels for 0%

commit v1 on v0

v1 whole, which is shorter than its diff:
```python
import functools

import jax
import jax.numpy as jnp
from jax import lax
from jax.experimental import pallas as pl
from jax.experimental.pallas import tpu as pltpu
from jax.sharding import PartitionSpec as P

NEW = 32
LOG2E = 1.4426950408889634
VMEM_LIMIT = 40 * 1024 * 1024
NT = (((1,), (1,)), ((), ()))


def silu(v):
    half = 0.5 * v
    return half + half * jnp.tanh(half)


def softplus(v):
    u = jnp.exp(-jnp.abs(v))
    small = u * (1.0 - u * (0.5 - u * (1.0 / 3.0)))
    return jnp.maximum(v, 0.0) + jnp.where(u < 0.004, small, jnp.log(1.0 + u))


def one_hot_rows(count, outer, inner):
    row = lax.broadcasted_iota(jnp.int32, (count, count), 0)
    col = lax.broadcasted_iota(jnp.int32, (count, count), 1)
    source = lax.rem(row, outer) * inner + lax.div(row, outer)
    return jnp.where(col == source, 1.0, 0.0).astype(jnp.bfloat16)


def project_kernel(dims, holder, slot_id, prefix_len, *refs):
    per_dev, n_replica, slots, relative, n_pieces = dims
    x_ref, wt_ref, cw_ref, cb_ref = refs[:4]
    pieces = refs[4 : 4 + n_pieces]
    mixed_ref, part_ref = refs[4 + n_pieces : 6 + n_pieces]
    joined, order = refs[6 + n_pieces :]
    step = pl.program_id(0)
    me = lax.axis_index("replica")
    rows = per_dev * NEW
    taps = cw_ref.shape[0]
    piece_rows = pieces[0].shape[0]

    @pl.when(step == 0)
    def _():
        order[...] = one_hot_rows(rows, per_dev, NEW)

    for r in range(per_dev):
        request = me * per_dev + r
        base = me if relative else 0
        index = lax.rem(holder[request] - base + n_replica, n_replica) * slots + slot_id[request]
        length = prefix_len[request]
        value = jnp.zeros(pieces[0].shape[1:], jnp.float32)
        for p in range(n_pieces):
            row = jnp.clip(index - p * piece_rows, 0, piece_rows - 1)
            here = (index >= p * piece_rows) & (index < (p + 1) * piece_rows)
            value = jnp.where(here, pieces[p][row].astype(jnp.float32), value)
        for j in range(taps - 1):
            live = taps - 1 - j <= length
            line = value[j : j + 1, :]
            joined[j * per_dev + r : j * per_dev + r + 1, :] = jnp.where(live, line, jnp.zeros_like(line))

    joined[(taps - 1) * per_dev :, :] = jnp.dot(
        order[...], x_ref[...], preferred_element_type=jnp.float32
    )
    summed = jnp.broadcast_to(cb_ref[...], x_ref.shape)
    for k in range(taps):
        weight = cw_ref[k : k + 1, :].astype(jnp.float32)
        summed = summed + joined[k * per_dev : k * per_dev + rows, :] * weight
    mixed = silu(summed).astype(jnp.bfloat16)
    mixed_ref[...] = mixed
    part = lax.dot_general(mixed, wt_ref[...], NT, preferred_element_type=jnp.float32)

    @pl.when(step == 0)
    def _():
        part_ref[...] = part

    @pl.when(step > 0)
    def _():
        part_ref[...] += part


def scan_kernel(dims, holder, slot_id, prefix_len, *refs):
    per_dev, n_replica, slots, relative, n_pieces, n_parts = dims
    mixed_ref, z_ref, dtw_ref, dtb_ref, al_ref, skip_ref = refs[:6]
    parts = refs[6 : 6 + n_parts]
    pieces = refs[6 + n_parts : 6 + n_parts + n_pieces]
    out_ref, state_ref = refs[6 + n_parts + n_pieces : 8 + n_parts + n_pieces]
    (order, back, order_s, back_s, dt_low, b_tab, c_tab, dt_buf, gate_buf, y_buf, a_buf, start_rm, start_tm,
     final_tm, sems) = refs[8 + n_parts + n_pieces :]
    step = pl.program_id(0)
    me = lax.axis_index("replica")
    rows = per_dev * NEW
    states = al_ref.shape[0]
    rank = dtw_ref.shape[0]
    width = z_ref.shape[1]
    piece_rows = pieces[0].shape[0]

    def fetch(r, do):
        request = me * per_dev + r
        base = me if relative else 0
        index = lax.rem(holder[request] - base + n_replica, n_replica) * slots + slot_id[request]
        for p in range(n_pieces):
            row = jnp.clip(index - p * piece_rows, 0, piece_rows - 1)
            here = (index >= p * piece_rows) & (index < (p + 1) * piece_rows)

            @pl.when(here)
            def _():
                do(pltpu.make_async_copy(pieces[p].at[row], start_rm.at[r], sems.at[r]))

    @pl.when(step == 0)
    def _():
        for r in range(per_dev):
            fetch(r, lambda copy: copy.start())
        order[...] = one_hot_rows(rows, per_dev, NEW)
        back[...] = one_hot_rows(rows, NEW, per_dev)
        order_s[...] = one_hot_rows(per_dev * states, per_dev, states)
        back_s[...] = one_hot_rows(per_dev * states, states, per_dev)
        projected = parts[0][...]
        for p in range(1, n_parts):
            projected = projected + parts[p][...]
        dt_low[...] = projected[:, :rank].astype(jnp.bfloat16)
        for n in range(states):
            b_tab[n] = jnp.broadcast_to(projected[:, rank + n : rank + n + 1], (rows, 128))
            c_tab[n] = jnp.broadcast_to(
                projected[:, rank + states + n : rank + states + n + 1], (rows, 128)
            )
        for r in range(per_dev):
            fetch(r, lambda copy: copy.wait())
        for r in range(per_dev):
            has = prefix_len[me * per_dev + r] > 0
            value = start_rm[r]
            start_rm[r] = jnp.where(has, value, jnp.zeros_like(value))

    columns = pl.ds(pl.multiple_of(step * width, 128), width)
    dt_buf[...] = softplus(
        jnp.dot(dt_low[...], dtw_ref[...], preferred_element_type=jnp.float32) + dtb_ref[...]
    )
    gate_buf[...] = silu(jnp.dot(order[...], z_ref[...], preferred_element_type=jnp.float32))
    a_buf[...] = jnp.exp(al_ref[...]) * (-LOG2E)
    start = start_rm[:, :, columns].reshape(per_dev * states, width)
    start_tm[...] = jnp.dot(order_s[...], start, preferred_element_type=jnp.float32)

    for tile in range(width // 128):
        lanes = slice(tile * 128, (tile + 1) * 128)
        rates = [jnp.broadcast_to(a_buf[n : n + 1, lanes], (per_dev, 128)) for n in range(states)]
        skip = jnp.broadcast_to(skip_ref[:, lanes], (per_dev, 128))

        def advance(t, state):
            now = pl.ds(pl.multiple_of(t * per_dev, per_dev), per_dev)
            dt = dt_buf[now, lanes]
            mixed = mixed_ref[now, lanes].astype(jnp.float32)
            drive = dt * mixed
            later = []
            terms = []
            for n in range(states):
                value = jnp.exp2(dt * rates[n]) * state[n] + drive * b_tab[n, now, :]
                later.append(value)
                terms.append(value * c_tab[n, now, :])
            while len(terms) > 1:
                terms = [terms[i] + terms[i + 1] for i in range(0, len(terms) - 1, 2)] + (
                    [terms[-1]] if len(terms) % 2 else []
                )
            y_buf[now, lanes] = (terms[0] + skip * mixed) * gate_buf[now, lanes]
            return tuple(later)

        state = tuple(start_tm[n * per_dev : (n + 1) * per_dev, lanes] for n in range(states))
        state = lax.fori_loop(0, NEW, advance, state, unroll=2)
        for n in range(states):
            final_tm[n * per_dev : (n + 1) * per_dev, lanes] = state[n]

    out_ref[...] = jnp.dot(
        back[...], y_buf[...].astype(jnp.bfloat16), preferred_element_type=jnp.float32
    ).astype(jnp.bfloat16)
    final = jnp.dot(back_s[...], final_tm[...].astype(jnp.bfloat16), preferred_element_type=jnp.float32)
    state_ref[...] = final.astype(jnp.bfloat16).reshape(per_dev, states, width)


def from_offset(value, axis, size, offset):
    return lax.ppermute(value, axis, [((i + offset) % size, i) for i in range(size)])


def gather_pieces(value, axis, size):
    if size <= 8:
        return [value] + [from_offset(value, axis, size, k) for k in range(1, size)], True
    return [lax.all_gather(value, axis, axis=0, tiled=True)], False


def shards(mesh, x_new, z_new, conv_weight, conv_bias, x_proj_weight, dt_proj_weight, dt_bias, a_log, d_skip,
           cache_ssm, cache_conv, holder, slot_id, prefix_len):
    n_replica, n_tensor = mesh.shape["replica"], mesh.shape["tensor"]
    rows, channels = x_new.shape
    per_dev = rows // NEW
    states = a_log.shape[0]
    rank = dt_proj_weight.shape[0]
    taps = conv_weight.shape[0]
    slots = cache_ssm.shape[0]
    out_cols = x_proj_weight.shape[1]

    conv_pieces, relative = gather_pieces(cache_conv, "replica", n_replica)
    ssm_pieces, _ = gather_pieces(cache_ssm, "replica", n_replica)

    width = min(512, channels)
    smem = pl.BlockSpec(memory_space=pltpu.SMEM)

    def cols(count):
        return pl.BlockSpec((count, width), lambda i: (0, i))

    def whole(shape):
        return pl.BlockSpec(shape, lambda i: (0,) * len(shape))

    params = pltpu.CompilerParams(vmem_limit_bytes=VMEM_LIMIT)
    dims = (per_dev, n_replica, slots, relative, len(conv_pieces))
    mixed, part = pl.pallas_call(
        functools.partial(project_kernel, dims),
        grid=(channels // width,),
        in_specs=[smem] * 3
        + [cols(rows), cols(out_cols), cols(taps), cols(1)]
        + [pl.BlockSpec(piece.shape[:2] + (width,), lambda i: (0, 0, i)) for piece in conv_pieces],
        out_specs=[cols(rows), whole((rows, out_cols))],
        out_shape=[
            jax.ShapeDtypeStruct((rows, channels), jnp.bfloat16),
            jax.ShapeDtypeStruct((rows, out_cols), jnp.float32),
        ],
        scratch_shapes=[
            pltpu.VMEM((rows + (taps - 1) * per_dev, width), jnp.float32),
            pltpu.VMEM((rows, rows), jnp.bfloat16),
        ],
        compiler_params=params,
        name="conv_project",
    )(holder, slot_id, prefix_len, x_new, x_proj_weight.T, conv_weight, conv_bias[None, :], *conv_pieces)

    parts = [part] + [from_offset(part, "tensor", n_tensor, k) for k in range(1, n_tensor)]

    dims = (per_dev, n_replica, slots, relative, len(ssm_pieces), n_tensor)
    f32, bf16 = jnp.float32, jnp.bfloat16
    return pl.pallas_call(
        functools.partial(scan_kernel, dims),
        grid=(channels // width,),
        in_specs=[smem] * 3
        + [cols(rows), cols(rows), cols(rank), cols(1), cols(states), cols(1)]
        + [whole((rows, out_cols))] * n_tensor
        + [pl.BlockSpec(memory_space=pl.ANY)] * len(ssm_pieces),
        out_specs=[cols(rows), pl.BlockSpec((per_dev, states, width), lambda i: (0, 0, i))],
        out_shape=[
            jax.ShapeDtypeStruct((rows, channels), bf16),
            jax.ShapeDtypeStruct((per_dev, states, channels), bf16),
        ],
        scratch_shapes=[
            pltpu.VMEM((rows, rows), bf16),
            pltpu.VMEM((rows, rows), bf16),
            pltpu.VMEM((per_dev * states, per_dev * states), bf16),
            pltpu.VMEM((per_dev * states, per_dev * states), bf16),
            pltpu.VMEM((rows, rank), bf16),
            pltpu.VMEM((states, rows, 128), f32),
            pltpu.VMEM((states, rows, 128), f32),
            pltpu.VMEM((rows, width), f32),
            pltpu.VMEM((rows, width), f32),
            pltpu.VMEM((rows, width), f32),
            pltpu.VMEM((states, width), f32),
            pltpu.VMEM((per_dev, states, channels), bf16),
            pltpu.VMEM((per_dev * states, width), f32),
            pltpu.VMEM((per_dev * states, width), f32),
            pltpu.SemaphoreType.DMA((per_dev,)),
        ],
        compiler_params=params,
        name="dt_scan_gate",
    )(holder, slot_id, prefix_len, mixed, z_new, dt_proj_weight, dt_bias[None, :], a_log, d_skip[None, :],
      *parts, *ssm_pieces)


def solution(mesh):
    placed = (
        P(("groups", "replica"), "tensor"),
        P(("groups", "replica"), "tensor"),
        P(None, "tensor"),
        P("tensor"),
        P("tensor", None),
        P(None, "tensor"),
        P("tensor"),
        P(None, "tensor"),
        P("tensor"),
        P(("groups", "replica"), None, "tensor"),
        P(("groups", "replica"), None, "tensor"),
        P("groups"),
        P("groups"),
        P("groups"),
    )
    return jax.shard_map(
        functools.partial(shards, mesh),
        mesh=mesh,
        in_specs=placed,
        out_specs=(P(("groups", "replica"), "tensor"), P(("groups", "replica"), None, "tensor")),
        check_vma=False,
    )
```

time: 150 us -> 59.2 us (0.39); the launches traced: 147 us -> 58.7 us
  other arithmetic: 62 us -> 0 us
  blocking collectives: 31.2 us -> 0 us
  Pallas kernels: 0 us -> 22.7 us
  local copies, waits for them, and re-layouts: 24.9 us -> 6.66 us
  starting transfers between devices: 0.04 us -> 14.3 us
  between operations: 14.2 us -> 0.73 us
  matrix products: 4.07 us -> 0 us
  waiting for transfers between devices: 10.7 us -> 14.4 us
    all_gather x2 -> x0, blocking collectives: 31.2 us -> none  [the longest x1 16.1 us: shards(): lax.all_gather(cache_ssm, 'replica', axis=0, tiled=True)]
    while x28 -> x0, other arithmetic: 24.1 us -> none
    reduce_sum x12 -> x0, other arithmetic: 23.3 us -> none  [advance_block(): jnp.sum(c_values[:, :, None] * state_now, axis=1) + d_skip * mixed_now]
    pallas_call x0 -> x2, Pallas kernels: none -> 22.7 us  [the longest x1 19 us: shards(): pl.pallas_call(functools.partial(scan_kernel, dims), grid=(channels // wi...]
    ppermute x0 -> x9, waiting for transfers between devices: none -> 14.4 us  [from_offset(): lax.ppermute(value, axis, [((i + offset) % size, i) for i in range(size)])]
    ppermute x0 -> x9, starting transfers between devices: none -> 14.3 us  [from_offset(): lax.ppermute(value, axis, [((i + offset) % size, i) for i in range(size)])]
    psum x1 -> x0, waiting for transfers between devices: 10.7 us -> none  [shards(): projected = lax.psum(partial_sum, 'tensor')]
    reshape x4 -> x0, local copies, waits for them, and re-layouts: 7.21 us -> none  [the longest x1 4.16 us: time_blocks(): return ordered.reshape((NEW // block_len, block_len) + ordered.shape[1:])]
  transfers between devices with their start and end apart: 1 -> 9, of which waited for: 1 -> 4; matrix products, arithmetic and copies ran while one was open for 5% -> 0% of each run, Pallas kernels for 0% -> 0%
where the time goes in v1:
time: 59.2 us; the launch traced here: 58.7 us
  Pallas kernels  22.7 us (38%)
  waiting for transfers between devices  14.4 us (24%)
  starting transfers between devices  14.3 us (24%)
  local copies, waits for them, and re-layouts  6.66 us (11%)
  between operations  0.73 us (1%)
    pallas_call x1, Pallas kernels, shards(): pl.pallas_call(functools.partial(scan_kernel, dims), grid=(channels // wi...  19 us
    ppermute x9, waiting for transfers between devices, from_offset(): lax.ppermute(value, axis, [((i + offset) % size, i) for i in range(size)])  14.4 us
    ppermute x9, starting transfers between devices, from_offset(): lax.ppermute(value, axis, [((i + offset) % size, i) for i in range(size)])  14.3 us
    unnamed x27, local copies, waits for them, and re-layouts  6.66 us
    pallas_call x1, Pallas kernels, shards(): pl.pallas_call(functools.partial(project_kernel, dims), grid=(channels //...  3.61 us
  transfers between devices with their start and end apart: 9, of which 4 were waited for; matrix products, arithmetic and copies ran while one was open for 0% of the time, Pallas kernels for 0%

profile of v1, /device:TPU:0, one launch (start us, length us, event | category | flops | bytes accessed | tf_op | source)
XLA Modules:
  0.0 58.7 jit_solution(16838982302536880356)
XLA Ops:
  0.6 0.8 %copy.19.refs_4_ = bf16[2,3,2048]{2,1,0:T(4,128)(2,1)S(1)} copy(bf16[2,3,2048]{2,0,1:T(2,128)(2,1)} %param.24) | data formatting | bytes 49152 | tf_op args[10]
  1.4 3.1 %collective-permute-start.2 = (bf16[2,3,2048]{2,1,0:T(4,128)(2,1)S(1)}, bf16[2,3,2048]{2,1,0:T(4,128)(2,1)S(1)}, u32[]{:S(2)}, u32[]{:S(2)}) collective-permute-start(bf16[2,3,2048]{2,1,0:T(4,128)(2,1)S(1)} %copy.19.refs_4_), channel_id=1, source_target_pairs={{12,0},{0,4},{4,8},{8,12},{13,1},{1,5},{5,9},{9,13},{14,2},{2,6},{... | collective-permute-start | bytes 73736 | tf_op jit(solution)/shard_map/ppermute | solution.py:182
  4.5 2.6 %collective-permute-start.1 = (bf16[2,3,2048]{2,1,0:T(4,128)(2,1)S(1)}, bf16[2,3,2048]{2,1,0:T(4,128)(2,1)S(1)}, u32[]{:S(2)}, u32[]{:S(2)}) collective-permute-start(bf16[2,3,2048]{2,1,0:T(4,128)(2,1)S(1)} %copy.19.refs_4_), channel_id=1, source_target_pairs={{8,0},{12,4},{0,8},{4,12},{9,1},{13,5},{1,9},{5,13},{10,2},{14,6},... | collective-permute-start | bytes 73736 | tf_op jit(solution)/shard_map/ppermute | solution.py:182
  7.1 1.3 %collective-permute-start = (bf16[2,3,2048]{2,1,0:T(4,128)(2,1)S(1)}, bf16[2,3,2048]{2,1,0:T(4,128)(2,1)S(1)}, u32[]{:S(2)}, u32[]{:S(2)}) collective-permute-start(bf16[2,3,2048]{2,1,0:T(4,128)(2,1)S(1)} %copy.19.refs_4_), channel_id=1, source_target_pairs={{4,0},{8,4},{12,8},{0,12},{5,1},{9,5},{13,9},{1,13},{6,2},{10,6},{... | collective-permute-start | bytes 73736 | tf_op jit(solution)/shard_map/ppermute | solution.py:182
  8.4 1.2 %collective-permute-done.1.refs_6_ = bf16[2,3,2048]{2,1,0:T(4,128)(2,1)S(1)} collective-permute-done((bf16[2,3,2048]{2,1,0:T(4,128)(2,1)S(1)}, bf16[2,3,2048]{2,1,0:T(4,128)(2,1)S(1)}, u32[]{:S(2)}, u32[]{:S(2)}) %collective-permute-start.1) | collective-permute-done | bytes 24608 | tf_op jit(solution)/shard_map/ppermute | solution.py:182
  9.6 1.3 %collective-permute-done.refs_5_ = bf16[2,3,2048]{2,1,0:T(4,128)(2,1)S(1)} collective-permute-done((bf16[2,3,2048]{2,1,0:T(4,128)(2,1)S(1)}, bf16[2,3,2048]{2,1,0:T(4,128)(2,1)S(1)}, u32[]{:S(2)}, u32[]{:S(2)}) %collective-permute-start) | collective-permute-done | bytes 24608 | tf_op jit(solution)/shard_map/ppermute | solution.py:182
  11.0 1.3 %copy-done = bf16[2048,288]{0,1:T(8,128)(2,1)S(1)} copy-done((bf16[2048,288]{0,1:T(8,128)(2,1)S(1)}, bf16[2048,288]{0,1:T(8,128)(2,1)}, u32[]{:S(2)}) %copy-start) | copy-done | bytes 1179672
  12.2 1.2 %copy-done.1 = bf16[256,2048]{1,0:T(8,128)(2,1)S(1)} copy-done((bf16[256,2048]{1,0:T(8,128)(2,1)S(1)}, bf16[256,2048]{1,0:T(8,128)(2,1)}, u32[]{:S(2)}) %copy-start.1) | copy-done | bytes 1048600
  13.5 0.7 %copy-done.6 = bf16[4,2048]{1,0:T(4,128)(2,1)S(1)} copy-done((bf16[4,2048]{1,0:T(4,128)(2,1)S(1)}, bf16[4,2048]{1,0:T(4,128)(2,1)}, u32[]{:S(2)}) %copy-start.6) | copy-done | bytes 16408
  14.2 0.7 %copy-done.7 = f32[2048]{0:T(1024)S(1)} copy-done((f32[2048]{0:T(1024)S(1)}, f32[2048]{0:T(1024)}, u32[]{:S(2)}) %copy-start.7) | copy-done | bytes 8216
  14.9 0.7 %copy-done.10 = s32[32]{0:T(128)S(1)} copy-done((s32[32]{0:T(128)S(1)}, s32[32]{0:T(128)}, u32[]{:S(2)}) %copy-start.10) | copy-done | bytes 152
  15.5 0.7 %copy-done.11 = s32[32]{0:T(128)S(1)} copy-done((s32[32]{0:T(128)S(1)}, s32[32]{0:T(128)}, u32[]{:S(2)}) %copy-start.11) | copy-done | bytes 152
  16.2 0.7 %copy-done.12 = s32[32]{0:T(128)S(1)} copy-done((s32[32]{0:T(128)S(1)}, s32[32]{0:T(128)}, u32[]{:S(2)}) %copy-start.12) | copy-done | bytes 152
  16.9 0.0 copy-start.8
  16.9 3.6 %conv_project.1 = (bf16[256,2048]{1,0:T(8,128)(2,1)S(1)}, f32[256,288]{1,0:T(8,128)S(1)}) custom-call(s32[32]{0:T(128)S(1)} %copy-done.10, s32[32]{0:T(128)S(1)} %copy-done.11, s32[32]{0:T(128)S(1)} %copy-done.12, bf16[256,2048]{1,0:T(8,128)(2,1)S(1)} %copy-done.1, bf16[288,2048]{1,0:T(8,128)(2,1)S(1)} %bitcast.4, bf16[4,2048]{1,0:T(4,128)(2,1)S(1)} %copy-done.6, ...), custom_call_target="tpu_custom_call" | custom-call | tf_op jit(solution)/shard_map/conv_project/pallas_call | solution.py:216
  20.5 0.1 collective-permute-start.5
  20.6 1.6 %collective-permute-start.4 = (f32[256,288]{1,0:T(8,128)S(1)}, f32[256,288]{1,0:T(8,128)S(1)}, u32[]{:S(2)}, u32[]{:S(2)}) collective-permute-start(f32[256,288]{1,0:T(8,128)S(1)} %get-tuple-element.5.refs_6_), channel_id=1, source_target_pairs={{2,0},{3,1},{0,2},{1,3},{6,4},{7,5},{4,6},{5,7},{10,8},{11,9},{8,1... | collective-permute-start | bytes 884744 | tf_op jit(solution)/shard_map/ppermute | solution.py:182
  22.1 1.4 %collective-permute-start.3 = (f32[256,288]{1,0:T(8,128)S(1)}, f32[256,288]{1,0:T(8,128)S(1)}, u32[]{:S(2)}, u32[]{:S(2)}) collective-permute-start(f32[256,288]{1,0:T(8,128)S(1)} %get-tuple-element.5.refs_6_), channel_id=1, source_target_pairs={{1,0},{2,1},{3,2},{0,3},{5,4},{6,5},{7,6},{4,7},{9,8},{10,9},{11,1... | collective-permute-start | bytes 884744 | tf_op jit(solution)/shard_map/ppermute | solution.py:182
  23.5 0.9 %collective-permute-start.7 = (bf16[2,16,2048]{2,1,0:T(8,128)(2,1)S(1)}, bf16[2,16,2048]{2,1,0:T(8,128)(2,1)S(1)}, u32[]{:S(2)}, u32[]{:S(2)}) collective-permute-start(bf16[2,16,2048]{2,1,0:T(8,128)(2,1)S(1)} %copy-done.5), channel_id=1, source_target_pairs={{8,0},{12,4},{0,8},{4,12},{9,1},{13,5},{1,9},{5,13},{10,2},{14,6},... | collective-permute-start | bytes 393224 | tf_op jit(solution)/shard_map/ppermute | solution.py:182
  24.4 2.2 %collective-permute-start.6 = (bf16[2,16,2048]{2,1,0:T(8,128)(2,1)S(1)}, bf16[2,16,2048]{2,1,0:T(8,128)(2,1)S(1)}, u32[]{:S(2)}, u32[]{:S(2)}) collective-permute-start(bf16[2,16,2048]{2,1,0:T(8,128)(2,1)S(1)} %copy-done.5), channel_id=1, source_target_pairs={{4,0},{8,4},{12,8},{0,12},{5,1},{9,5},{13,9},{1,13},{6,2},{10,6},{... | collective-permute-start | bytes 393224 | tf_op jit(solution)/shard_map/ppermute | solution.py:182
  26.7 5.7 %collective-permute-done.7.refs_12_ = bf16[2,16,2048]{2,1,0:T(8,128)(2,1)S(1)} collective-permute-done((bf16[2,16,2048]{2,1,0:T(8,128)(2,1)S(1)}, bf16[2,16,2048]{2,1,0:T(8,128)(2,1)S(1)}, u32[]{:S(2)}, u32[]{:S(2)}) %collective-permute-start.7) | collective-permute-done | bytes 131104 | tf_op jit(solution)/shard_map/ppermute | solution.py:182
  32.4 1.1 %collective-permute-start.8 = (bf16[2,16,2048]{2,1,0:T(8,128)(2,1)S(1)}, bf16[2,16,2048]{2,1,0:T(8,128)(2,1)S(1)}, u32[]{:S(2)}, u32[]{:S(2)}) collective-permute-start(bf16[2,16,2048]{2,1,0:T(8,128)(2,1)S(1)} %copy-done.5), channel_id=1, source_target_pairs={{12,0},{0,4},{4,8},{8,12},{13,1},{1,5},{5,9},{9,13},{14,2},{2,6},{... | collective-permute-start | bytes 393224 | tf_op jit(solution)/shard_map/ppermute | solution.py:182
  33.6 6.1 %collective-permute-done.8.refs_13_ = bf16[2,16,2048]{2,1,0:T(8,128)(2,1)S(1)} collective-permute-done((bf16[2,16,2048]{2,1,0:T(8,128)(2,1)S(1)}, bf16[2,16,2048]{2,1,0:T(8,128)(2,1)S(1)}, u32[]{:S(2)}, u32[]{:S(2)}) %collective-permute-start.8) | collective-permute-done | bytes 131104 | tf_op jit(solution)/shard_map/ppermute | solution.py:182
  39.7 19.0 %dt_scan_gate.1 = (bf16[256,2048]{1,0:T(8,128)(2,1)}, bf16[8,16,2048]{2,1,0:T(8,128)(2,1)}) custom-call(s32[32]{0:T(128)S(1)} %copy-done.10, s32[32]{0:T(128)S(1)} %copy-done.11, s32[32]{0:T(128)S(1)} %copy-done.12, bf16[256,2048]{1,0:T(8,128)(2,1)S(1)} %get-tuple-element.4.refs_0_, bf16[256,2048]{1,0:T(8,128)(2,1)S(1)} %copy-done.2, ...), custom_call_target="tpu_custom_call" | custom-call | tf_op jit(solution)/shard_map/dt_scan_gate/pallas_call | solution.py:239
  (23 shorter events, 0.0 us)
Async XLA Ops:
  1.4 7.0 %collective-permute-start.2 = (bf16[2,3,2048]{2,1,0:T(4,128)(2,1)S(1)}, bf16[2,3,2048]{2,1,0:T(4,128)(2,1)S(1)}, u32[]{:S(2)}, u32[]{:S(2)}) collective-permute-start(bf16[2,3,2048]{2,1,0:T(4,128)(2,1)S(1)} %copy.19.refs_4_), channel_id=1, source_target_pairs={{12,0},{0,4},{4,8},{8,12},{13,1},{1,5},{5,9},{9,13},{14,2},{2,6},{... | collective-permute-start | bytes 73736 | tf_op jit(solution)/shard_map/ppermute | solution.py:182
  4.5 5.2 %collective-permute-start.1 = (bf16[2,3,2048]{2,1,0:T(4,128)(2,1)S(1)}, bf16[2,3,2048]{2,1,0:T(4,128)(2,1)S(1)}, u32[]{:S(2)}, u32[]{:S(2)}) collective-permute-start(bf16[2,3,2048]{2,1,0:T(4,128)(2,1)S(1)} %copy.19.refs_4_), channel_id=1, source_target_pairs={{8,0},{12,4},{0,8},{4,12},{9,1},{13,5},{1,9},{5,13},{10,2},{14,6},... | collective-permute-start | bytes 73736 | tf_op jit(solution)/shard_map/ppermute | solution.py:182
  7.1 3.9 %collective-permute-start = (bf16[2,3,2048]{2,1,0:T(4,128)(2,1)S(1)}, bf16[2,3,2048]{2,1,0:T(4,128)(2,1)S(1)}, u32[]{:S(2)}, u32[]{:S(2)}) collective-permute-start(bf16[2,3,2048]{2,1,0:T(4,128)(2,1)S(1)} %copy.19.refs_4_), channel_id=1, source_target_pairs={{4,0},{8,4},{12,8},{0,12},{5,1},{9,5},{13,9},{1,13},{6,2},{10,6},{... | collective-permute-start | bytes 73736 | tf_op jit(solution)/shard_map/ppermute | solution.py:182
  11.0 1.3 %copy-start = (bf16[2048,288]{0,1:T(8,128)(2,1)S(1)}, bf16[2048,288]{0,1:T(8,128)(2,1)}, u32[]{:S(2)}) copy-start(bf16[2048,288]{0,1:T(8,128)(2,1)} %param.18) | copy-start | bytes 3538948
  12.2 1.2 %copy-start.1 = (bf16[256,2048]{1,0:T(8,128)(2,1)S(1)}, bf16[256,2048]{1,0:T(8,128)(2,1)}, u32[]{:S(2)}) copy-start(bf16[256,2048]{1,0:T(8,128)(2,1)} %refs_0_.1) | copy-start | bytes 3145732
  13.5 0.7 %copy-start.6 = (bf16[4,2048]{1,0:T(4,128)(2,1)S(1)}, bf16[4,2048]{1,0:T(4,128)(2,1)}, u32[]{:S(2)}) copy-start(bf16[4,2048]{1,0:T(4,128)(2,1)} %refs_2_.2) | copy-start | bytes 49156
  14.2 0.7 %copy-start.7 = (f32[2048]{0:T(1024)S(1)}, f32[2048]{0:T(1024)}, u32[]{:S(2)}) copy-start(f32[2048]{0:T(1024)} %param.17) | copy-start | bytes 24580
  14.9 0.7 %copy-start.10 = (s32[32]{0:T(128)S(1)}, s32[32]{0:T(128)}, u32[]{:S(2)}) copy-start(s32[32]{0:T(128)} %holder.3) | copy-start | bytes 388
  15.5 0.7 %copy-start.11 = (s32[32]{0:T(128)S(1)}, s32[32]{0:T(128)}, u32[]{:S(2)}) copy-start(s32[32]{0:T(128)} %slot_id.3) | copy-start | bytes 388
  16.2 0.7 %copy-start.12 = (s32[32]{0:T(128)S(1)}, s32[32]{0:T(128)}, u32[]{:S(2)}) copy-start(s32[32]{0:T(128)} %prefix_len.3) | copy-start | bytes 388
  16.8 6.7 %copy-start.5 = (bf16[2,16,2048]{2,1,0:T(8,128)(2,1)S(1)}, bf16[2,16,2048]{2,1,0:T(8,128)(2,1)}, u32[]{:S(2)}) copy-start(bf16[2,16,2048]{2,1,0:T(8,128)(2,1)} %refs_10_.1) | copy-start | bytes 393220
  16.9 22.8 %copy-start.2 = (bf16[256,2048]{1,0:T(8,128)(2,1)S(1)}, bf16[256,2048]{1,0:T(8,128)(2,1)}, u32[]{:S(2)}) copy-start(bf16[256,2048]{1,0:T(8,128)(2,1)} %refs_1_.1) | copy-start | bytes 3145732
  16.9 22.8 %copy-start.3 = (bf16[256,2048]{1,0:T(8,128)(2,1)S(1)}, bf16[256,2048]{1,0:T(8,128)(2,1)}, u32[]{:S(2)}) copy-start(bf16[256,2048]{1,0:T(8,128)(2,1)} %refs_2_.3) | copy-start | bytes 3145732
  16.9 22.8 %copy-start.4 = (f32[16,2048]{1,0:T(8,128)S(1)}, f32[16,2048]{1,0:T(8,128)}, u32[]{:S(2)}) copy-start(f32[16,2048]{1,0:T(8,128)} %refs_4_.2) | copy-start | bytes 393220
  16.9 22.8 %copy-start.8 = (f32[2048]{0:T(1024)S(1)}, f32[2048]{0:T(1024)}, u32[]{:S(2)}) copy-start(f32[2048]{0:T(1024)} %param.20) | copy-start | bytes 24580
  16.9 22.8 %copy-start.9 = (f32[2048]{0:T(1024)S(1)}, f32[2048]{0:T(1024)}, u32[]{:S(2)}) copy-start(f32[2048]{0:T(1024)} %param.22) | copy-start | bytes 24580
  20.5 19.1 %collective-permute-start.5 = (f32[256,288]{1,0:T(8,128)S(1)}, f32[256,288]{1,0:T(8,128)S(1)}, u32[]{:S(2)}, u32[]{:S(2)}) collective-permute-start(f32[256,288]{1,0:T(8,128)S(1)} %get-tuple-element.5.refs_6_), channel_id=1, source_target_pairs={{3,0},{0,1},{1,2},{2,3},{7,4},{4,5},{5,6},{6,7},{11,8},{8,9},{9,10... | collective-permute-start | bytes 884744 | tf_op jit(solution)/shard_map/ppermute | solution.py:182
  20.6 19.1 %collective-permute-start.4 = (f32[256,288]{1,0:T(8,128)S(1)}, f32[256,288]{1,0:T(8,128)S(1)}, u32[]{:S(2)}, u32[]{:S(2)}) collective-permute-start(f32[256,288]{1,0:T(8,128)S(1)} %get-tuple-element.5.refs_6_), channel_id=1, source_target_pairs={{2,0},{3,1},{0,2},{1,3},{6,4},{7,5},{4,6},{5,7},{10,8},{11,9},{8,1... | collective-permute-start | bytes 884744 | tf_op jit(solution)/shard_map/ppermute | solution.py:182
  22.1 17.5 %collective-permute-start.3 = (f32[256,288]{1,0:T(8,128)S(1)}, f32[256,288]{1,0:T(8,128)S(1)}, u32[]{:S(2)}, u32[]{:S(2)}) collective-permute-start(f32[256,288]{1,0:T(8,128)S(1)} %get-tuple-element.5.refs_6_), channel_id=1, source_target_pairs={{1,0},{2,1},{3,2},{0,3},{5,4},{6,5},{7,6},{4,7},{9,8},{10,9},{11,1... | collective-permute-start | bytes 884744 | tf_op jit(solution)/shard_map/ppermute | solution.py:182
  23.5 8.9 %collective-permute-start.7 = (bf16[2,16,2048]{2,1,0:T(8,128)(2,1)S(1)}, bf16[2,16,2048]{2,1,0:T(8,128)(2,1)S(1)}, u32[]{:S(2)}, u32[]{:S(2)}) collective-permute-start(bf16[2,16,2048]{2,1,0:T(8,128)(2,1)S(1)} %copy-done.5), channel_id=1, source_target_pairs={{8,0},{12,4},{0,8},{4,12},{9,1},{13,5},{1,9},{5,13},{10,2},{14,6},... | collective-permute-start | bytes 393224 | tf_op jit(solution)/shard_map/ppermute | solution.py:182
  24.4 9.1 %collective-permute-start.6 = (bf16[2,16,2048]{2,1,0:T(8,128)(2,1)S(1)}, bf16[2,16,2048]{2,1,0:T(8,128)(2,1)S(1)}, u32[]{:S(2)}, u32[]{:S(2)}) collective-permute-start(bf16[2,16,2048]{2,1,0:T(8,128)(2,1)S(1)} %copy-done.5), channel_id=1, source_target_pairs={{4,0},{8,4},{12,8},{0,12},{5,1},{9,5},{13,9},{1,13},{6,2},{10,6},{... | collective-permute-start | bytes 393224 | tf_op jit(solution)/shard_map/ppermute | solution.py:182
  32.4 7.2 %collective-permute-start.8 = (bf16[2,16,2048]{2,1,0:T(8,128)(2,1)S(1)}, bf16[2,16,2048]{2,1,0:T(8,128)(2,1)S(1)}, u32[]{:S(2)}, u32[]{:S(2)}) collective-permute-start(bf16[2,16,2048]{2,1,0:T(8,128)(2,1)S(1)} %copy-done.5), channel_id=1, source_target_pairs={{12,0},{0,4},{4,8},{8,12},{13,1},{1,5},{5,9},{9,13},{14,2},{2,6},{... | collective-permute-start | bytes 393224 | tf_op jit(solution)/shard_map/ppermute | solution.py:182

commit v2 on v0

v2 whole, which is shorter than its diff:
```python
import functools

import jax
import jax.numpy as jnp
from jax import lax
from jax.experimental import pallas as pl
from jax.experimental.pallas import tpu as pltpu
from jax.sharding import PartitionSpec as P

NEW = 32
LANES = 128
LOG2E = 1.4426950408889634
VMEM_LIMIT = 60 * 1024 * 1024
UNROLL = 8
F32, BF16 = jnp.float32, jnp.bfloat16
NT = (((1,), (1,)), ((), ()))
TN = (((0,), (0,)), ((), ()))


def silu(v):
    half = 0.5 * v
    return half + half * jnp.tanh(half)


def softplus(v):
    u = jnp.exp(-jnp.abs(v))
    small = u * (1.0 - u * (0.5 - u * (1.0 / 3.0)))
    return jnp.maximum(v, 0.0) + jnp.where(u < 0.004, small, jnp.log(1.0 + u))


def split_index(value, inner):
    assert inner & (inner - 1) == 0
    return value >> (inner.bit_length() - 1), value & (inner - 1)


def one_hot_rows(outer, inner):
    count = outer * inner
    row = lax.broadcasted_iota(jnp.int32, (count, count), 0)
    col = lax.broadcasted_iota(jnp.int32, (count, count), 1)
    high, low = split_index(row, outer)
    return jnp.where(col == low * inner + high, 1.0, 0.0).astype(BF16)


def pick_rows(values, row_low, count):
    out = jnp.zeros(row_low.shape, jnp.int32)
    for r in range(count):
        out = jnp.where(row_low == r, values[r], out)
    return out


def request_slots(dims, ints, me):
    per_dev, n_replica, slots, relative = dims
    found, lengths = [], []
    for r in range(per_dev):
        request = me * per_dev + r
        base = me if relative else 0
        place = lax.rem(ints[0][request] - base + n_replica, n_replica)
        found.append(place * slots + ints[1][request])
        lengths.append(ints[2][request])
    return found, lengths


def project_kernel(dims, refs_in, refs_out, scratch):
    per_dev, n_replica, slots, _ = dims
    holder, slot_id, prefix_len, x_hbm, wt_hbm, cw_hbm, cb_hbm, conv_hbm = refs_in
    mixed_hbm, part_hbm = refs_out
    h_s, s_s, l_s, x_v, wt_v, cw_v, cb_v, conv_v, joined, mixed_v, part_f, part_v, sems, out_sems = scratch
    rows, channels = x_v.shape
    taps = cw_v.shape[0]
    copies = []
    for src, dst in ((holder, h_s), (slot_id, s_s), (prefix_len, l_s), (conv_hbm, conv_v), (cw_hbm, cw_v), (cb_hbm, cb_v)):
        copies.append(pltpu.make_async_copy(src, dst, sems.at[len(copies)]))
    small = len(copies)
    width = min(512, channels)
    chunks = [slice(c * width, (c + 1) * width) for c in range(channels // width)]
    for chunk in chunks:
        copies.append(pltpu.make_async_copy(x_hbm.at[:, chunk], x_v.at[:, chunk], sems.at[len(copies)]))
        copies.append(pltpu.make_async_copy(wt_hbm.at[:, chunk], wt_v.at[:, chunk], sems.at[len(copies)]))
    for copy in copies:
        copy.start()

    order = one_hot_rows(per_dev, NEW)
    for copy in copies[:small]:
        copy.wait()

    me = lax.axis_index("replica")
    found, lengths = request_slots(dims, (h_s, s_s, l_s), me)
    lines = (taps - 1) * per_dev
    shape = (per_dev * taps, conv_v.shape[0])
    tap, request = split_index(lax.broadcasted_iota(jnp.int32, shape, 0), per_dev)
    slot, col_tap = split_index(lax.broadcasted_iota(jnp.int32, shape, 1), taps)
    live = (taps - 1 - tap <= pick_rows(lengths, request, per_dev)) & (tap == col_tap)
    chosen = live & (slot == pick_rows(found, request, per_dev))
    select = jnp.where(chosen, 1.0, 0.0).astype(BF16)

    outs = []
    for c, chunk in enumerate(chunks):
        copies[small + 2 * c].wait()
        history = jnp.dot(select, conv_v[:, chunk], preferred_element_type=F32)
        joined[:lines, chunk] = history[:lines]
        joined[lines:, chunk] = jnp.dot(order, x_v[:, chunk], preferred_element_type=F32)
        summed = jnp.broadcast_to(cb_v[:, chunk], (rows, width))
        for k in range(taps):
            weight = cw_v[k : k + 1, chunk].astype(F32)
            summed = summed + joined[k * per_dev : k * per_dev + rows, chunk] * weight
        mixed = silu(summed).astype(BF16)
        mixed_v[:, chunk] = mixed
        copies[small + 2 * c + 1].wait()
        part = lax.dot_general(wt_v[:, chunk], mixed, NT, preferred_element_type=F32)
        if c == 0:
            part_f[...] = part
        else:
            part_f[...] += part
        outs.append(pltpu.make_async_copy(mixed_v.at[:, chunk], mixed_hbm.at[:, chunk], out_sems.at[c]))
        outs[-1].start()
    part_v[...] = part_f[...].astype(BF16)
    for k in range(part_hbm.shape[0]):
        outs.append(pltpu.make_async_copy(part_v, part_hbm.at[k], out_sems.at[len(outs)]))
        outs[-1].start()
    for copy in outs:
        copy.wait()


def scan_kernel(dims, refs_in, refs_out, scratch):
    per_dev, n_replica, slots, _ = dims
    holder, slot_id, prefix_len, mixed_hbm, z_hbm, dtw_hbm, dtb_hbm, al_hbm, skip_hbm, parts_hbm = refs_in[:10]
    pieces = refs_in[10:]
    out_hbm, state_hbm = refs_out
    (h_s, s_s, l_s, mixed_v, z_v, dtw_v, dtb_v, al_v, skip_v, parts_v, cache_v, b_tab, c_tab, dt_v, gate_v,
     a_v, start_tm, final_tm, y_v, out_v, state_v, sems, out_sems) = scratch
    rows, channels = z_v.shape
    states = al_v.shape[0]
    rank = dtw_v.shape[0]
    pairs = (
        (z_hbm, z_v), (parts_hbm, parts_v), (dtw_hbm, dtw_v), (dtb_hbm, dtb_v), (al_hbm, al_v), (holder, h_s),
        (slot_id, s_s), (prefix_len, l_s), (skip_hbm, skip_v), (mixed_hbm, mixed_v),
    )
    copies = [pltpu.make_async_copy(src, dst, sems.at[i]) for i, (src, dst) in enumerate(pairs)]
    piece_rows = cache_v.shape[0] // len(pieces)
    for p, piece in enumerate(pieces):
        target = cache_v.at[p * piece_rows : (p + 1) * piece_rows]
        copies.append(pltpu.make_async_copy(piece, target, sems.at[len(copies)]))
    for copy in copies:
        copy.start()

    order = one_hot_rows(per_dev, NEW)
    copies[0].wait()
    gate_v[...] = silu(jnp.dot(order, z_v[...], preferred_element_type=F32))

    copies[1].wait()
    projected = parts_v[0].astype(F32)
    for p in range(1, parts_v.shape[0]):
        projected = projected + parts_v[p].astype(F32)
    dt_low = projected[:rank].astype(BF16)
    late = projected[rank:].T
    for n in range(states):
        b_tab[n] = jnp.broadcast_to(late[:, n : n + 1], (rows, LANES))
        c_tab[n] = jnp.broadcast_to(late[:, states + n : states + n + 1], (rows, LANES))
    for copy in copies[2:]:
        copy.wait()
    dt_v[...] = softplus(
        lax.dot_general(dt_low, dtw_v[...], TN, preferred_element_type=F32) + dtb_v[...]
    )
    a_v[...] = jnp.exp(al_v[...]) * (-LOG2E)

    me = lax.axis_index("replica")
    found, lengths = request_slots(dims, (h_s, s_s, l_s), me)
    shape = (per_dev * states, cache_v.shape[0])
    state_id, request = split_index(lax.broadcasted_iota(jnp.int32, shape, 0), per_dev)
    slot, col_state = split_index(lax.broadcasted_iota(jnp.int32, shape, 1), states)
    chosen = (pick_rows(lengths, request, per_dev) > 0) & (state_id == col_state)
    chosen = chosen & (slot == pick_rows(found, request, per_dev))
    select = jnp.where(chosen, 1.0, 0.0).astype(BF16)
    start_tm[...] = jnp.dot(select, cache_v[...], preferred_element_type=F32)

    back = one_hot_rows(NEW, per_dev)
    back_s = one_hot_rows(states, per_dev)
    width = min(512, channels)
    outs = []
    for c in range(channels // width):

        def one_tile(i, carry):
            lanes = pl.ds(pl.multiple_of(c * width + i * LANES, LANES), LANES)
            rates = [jnp.broadcast_to(a_v[n : n + 1, lanes], (per_dev, LANES)) for n in range(states)]
            skip = jnp.broadcast_to(skip_v[:, lanes], (per_dev, LANES))

            def advance(block, state):
                state = list(state)
                for u in range(UNROLL):
                    now = pl.ds(pl.multiple_of((block * UNROLL + u) * per_dev, per_dev), per_dev)
                    dt = dt_v[now, lanes]
                    if u % 2 == 0:
                        both = pl.ds(pl.multiple_of((block * UNROLL + u) * per_dev, 2 * per_dev), 2 * per_dev)
                        pair = mixed_v[both, lanes].astype(F32)
                    mixed = pair[u % 2 * per_dev : (u % 2 + 1) * per_dev]
                    drive = dt * mixed
                    sums = [skip * mixed, None]
                    for n in range(states):
                        state[n] = jnp.exp2(dt * rates[n]) * state[n] + drive * b_tab[n, now, :]
                        term = state[n] * c_tab[n, now, :]
                        sums[n % 2] = term if sums[n % 2] is None else sums[n % 2] + term
                    y_v[now, lanes] = (sums[0] + sums[1]) * gate_v[now, lanes]
                return tuple(state)

            state = tuple(start_tm[n * per_dev : (n + 1) * per_dev, lanes] for n in range(states))
            state = lax.fori_loop(0, NEW // UNROLL, advance, state)
            for n in range(states):
                final_tm[n * per_dev : (n + 1) * per_dev, lanes] = state[n]
            return carry

        lax.fori_loop(0, width // LANES, one_tile, 0)
        chunk = slice(c * width, (c + 1) * width)
        gated = y_v[:, chunk].astype(BF16)
        out_v[:, chunk] = jnp.dot(back, gated, preferred_element_type=F32).astype(BF16)
        final = jnp.dot(back_s, final_tm[:, chunk].astype(BF16), preferred_element_type=F32)
        state_v[:, chunk] = final.astype(BF16)
        for src, dst in ((out_v, out_hbm), (state_v, state_hbm)):
            outs.append(pltpu.make_async_copy(src.at[:, chunk], dst.at[:, chunk], out_sems.at[len(outs)]))
            outs[-1].start()
    for copy in outs:
        copy.wait()


def split_refs(kernel, dims, n_in, n_out):
    def body(*refs):
        kernel(dims, refs[:n_in], refs[n_in : n_in + n_out], refs[n_in + n_out :])

    return body


def call(kernel, dims, name, ins, outs, scratch):
    hbm = pl.BlockSpec(memory_space=pltpu.HBM)
    anywhere = pl.BlockSpec(memory_space=pl.ANY)
    return pl.pallas_call(
        split_refs(kernel, dims, len(ins), len(outs)),
        in_specs=[hbm if fixed else anywhere for _, fixed in ins],
        out_specs=[anywhere] * len(outs),
        out_shape=[jax.ShapeDtypeStruct(*out) for out in outs],
        scratch_shapes=scratch,
        compiler_params=pltpu.CompilerParams(vmem_limit_bytes=VMEM_LIMIT),
        name=name,
    )(*[value for value, _ in ins])


def to_all(value, axis):
    return lax.all_to_all(value, axis, 0, 0)


def from_offset(value, axis, size, offset):
    return lax.ppermute(value, axis, [((i + offset) % size, i) for i in range(size)])


def shards(mesh, x_new, z_new, conv_weight, conv_bias, x_proj_weight, dt_proj_weight, dt_bias, a_log, d_skip,
           cache_ssm, cache_conv, holder, slot_id, prefix_len):
    n_replica, n_tensor = mesh.shape["replica"], mesh.shape["tensor"]
    rows, channels = x_new.shape
    per_dev = rows // NEW
    states = a_log.shape[0]
    rank = dt_proj_weight.shape[0]
    taps = conv_weight.shape[0]
    slots = cache_ssm.shape[0]
    out_cols = x_proj_weight.shape[1]
    requests = holder.shape[0]

    conv_rows = jnp.pad(cache_conv, ((0, 0), (0, 1), (0, 0))).reshape(slots * taps, channels)
    ssm_rows = cache_ssm.reshape(slots * states, channels)
    relative = n_replica <= 8
    if relative:
        conv_all = to_all(jnp.broadcast_to(conv_rows[None], (n_replica,) + conv_rows.shape), "replica")
        conv_all = conv_all.reshape(n_replica * slots * taps, channels)
        ssm_pieces = [ssm_rows] + [from_offset(ssm_rows, "replica", n_replica, k) for k in range(1, n_replica)]
    else:
        conv_all = lax.all_gather(conv_rows, "replica", axis=0, tiled=True)
        ssm_pieces = [lax.all_gather(ssm_rows, "replica", axis=0, tiled=True)]

    vmem, dma = pltpu.VMEM, pltpu.SemaphoreType.DMA
    ints = [pltpu.SMEM((requests,), jnp.int32)] * 3
    n_chunks = channels // min(512, channels)

    mixed, parts = call(
        project_kernel, (per_dev, n_replica, slots, False), "conv_project",
        [(holder, True), (slot_id, True), (prefix_len, True), (x_new, True), (x_proj_weight.T, True),
         (conv_weight, True), (conv_bias[None, :], True), (conv_all, False)],
        [((rows, channels), BF16), ((n_tensor, out_cols, rows), BF16)],
        ints + [
            vmem((rows, channels), BF16),
            vmem((out_cols, channels), BF16),
            vmem((taps, channels), BF16),
            vmem((1, channels), F32),
            vmem(conv_all.shape, BF16),
            vmem((rows + (taps - 1) * per_dev, channels), F32),
            vmem((rows, channels), BF16),
            vmem((out_cols, rows), F32),
            vmem((out_cols, rows), BF16),
            dma((6 + 2 * n_chunks,)),
            dma((n_chunks + n_tensor,)),
        ],
    )
    parts = to_all(parts, "tensor")

    out, state = call(
        scan_kernel, (per_dev, n_replica, slots, relative), "dt_scan_gate",
        [(holder, True), (slot_id, True), (prefix_len, True), (mixed, False), (z_new, True), (dt_proj_weight, True),
         (dt_bias[None, :], True), (a_log, True), (d_skip[None, :], True), (parts, False)]
        + [(piece, False) for piece in ssm_pieces],
        [((rows, channels), BF16), ((per_dev * states, channels), BF16)],
        ints + [
            vmem((rows, channels), BF16),
            vmem((rows, channels), BF16),
            vmem((rank, channels), BF16),
            vmem((1, channels), F32),
            vmem((states, channels), F32),
            vmem((1, channels), F32),
            vmem((n_tensor, out_cols, rows), BF16),
            vmem((n_replica * slots * states, channels), BF16),
            vmem((states, rows, LANES), F32),
            vmem((states, rows, LANES), F32),
            vmem((rows, channels), F32),
            vmem((rows, channels), F32),
            vmem((states, channels), F32),
            vmem((per_dev * states, channels), F32),
            vmem((per_dev * states, channels), F32),
            vmem((rows, channels), F32),
            vmem((rows, channels), BF16),
            vmem((per_dev * states, channels), BF16),
            dma((10 + len(ssm_pieces),)),
            dma((2 * n_chunks,)),
        ],
    )
    return out, state.reshape(per_dev, states, channels)


def solution(mesh):
    placed = (
        P(("groups", "replica"), "tensor"),
        P(("groups", "replica"), "tensor"),
        P(None, "tensor"),
        P("tensor"),
        P("tensor", None),
        P(None, "tensor"),
        P("tensor"),
        P(None, "tensor"),
        P("tensor"),
        P(("groups", "replica"), None, "tensor"),
        P(("groups", "replica"), None, "tensor"),
        P("groups"),
        P("groups"),
        P("groups"),
    )
    return jax.shard_map(
        functools.partial(shards, mesh),
        mesh=mesh,
        in_specs=placed,
        out_specs=(P(("groups", "replica"), "tensor"), P(("groups", "replica"), None, "tensor")),
        check_vma=False,
    )
```

time: 150 us -> 53.5 us (0.36); the launches traced: 147 us -> 52.8 us
  other arithmetic: 62 us -> 0 us
  local copies, waits for them, and re-layouts: 24.9 us -> 1.73 us
  Pallas kernels: 0 us -> 21 us
  blocking collectives: 31.2 us -> 12.3 us
  between operations: 14.2 us -> 0.71 us
  starting transfers between devices: 0.04 us -> 7.5 us
  matrix products: 4.07 us -> 0 us
    all_gather x2 -> x0, blocking collectives: 31.2 us -> none  [the longest x1 16.1 us: shards(): lax.all_gather(cache_ssm, 'replica', axis=0, tiled=True)]
    while x28 -> x0, other arithmetic: 24.1 us -> none
    reduce_sum x12 -> x0, other arithmetic: 23.3 us -> none  [advance_block(): jnp.sum(c_values[:, :, None] * state_now, axis=1) + d_skip * mixed_now]
    pallas_call x0 -> x2, Pallas kernels: none -> 21 us  [call(): pl.pallas_call(split_refs(kernel, dims, len(ins), len(outs)), in_specs=[h...]
    all_to_all x0 -> x1, blocking collectives: none -> 12.3 us  [to_all(): return lax.all_to_all(value, axis, 0, 0)]
    psum x1 -> x0, waiting for transfers between devices: 10.7 us -> none  [shards(): projected = lax.psum(partial_sum, 'tensor')]
    ppermute x0 -> x3, waiting for transfers between devices: none -> 9.56 us  [from_offset(): lax.ppermute(value, axis, [((i + offset) % size, i) for i in range(size)])]
    reshape x4 -> x0, local copies, waits for them, and re-layouts: 7.21 us -> none  [the longest x1 4.16 us: time_blocks(): return ordered.reshape((NEW // block_len, block_len) + ordered.shape[1:])]
  transfers between devices with their start and end apart: 1 -> 4, of which waited for: 1 -> 2; matrix products, arithmetic and copies ran while one was open for 5% -> 0% of each run, Pallas kernels for 0% -> 0%
where the time goes in v2:
time: 53.5 us; the launch traced here: 52.8 us
  Pallas kernels  21 us (39%)
  blocking collectives  12.3 us (23%)
  waiting for transfers between devices  9.56 us (18%)
  starting transfers between devices  7.5 us (14%)
  local copies, waits for them, and re-layouts  1.73 us (3%)
  between operations  0.71 us (1%)
    pallas_call x2, Pallas kernels, call(): pl.pallas_call(split_refs(kernel, dims, len(ins), len(outs)), in_specs=[h...  21 us
    all_to_all x1, blocking collectives, to_all(): return lax.all_to_all(value, axis, 0, 0)  12.3 us
    ppermute x3, waiting for transfers between devices, from_offset(): lax.ppermute(value, axis, [((i + offset) % size, i) for i in range(size)])  9.56 us
    ppermute x3, starting transfers between devices, from_offset(): lax.ppermute(value, axis, [((i + offset) % size, i) for i in range(size)])  3.88 us
    all_to_all x1, starting transfers between devices, to_all(): return lax.all_to_all(value, axis, 0, 0)  3.62 us
    unnamed x11, local copies, waits for them, and re-layouts  1.69 us
  transfers between devices with their start and end apart: 4, of which 2 were waited for; matrix products, arithmetic and copies ran while one was open for 0% of the time, Pallas kernels for 0%

profile of v2, /device:TPU:0, one launch (start us, length us, event | category | flops | bytes accessed | tf_op | source)
XLA Modules:
  0.0 52.8 jit_solution(2419119912160479309)
XLA Ops:
  0.6 0.8 %copy.17 = bf16[2,3,2048]{2,1,0:T(4,128)(2,1)S(1)} copy(bf16[2,3,2048]{2,0,1:T(2,128)(2,1)} %param.24) | data formatting | bytes 49152
  1.5 12.3 %all_to_all.10 = bf16[4,8,2048]{2,1,0:T(8,128)(2,1)} all-to-all(bf16[4,8,2048]{2,1,0:T(8,128)(2,1)S(1)} %broadcast_in_dim.18), channel_id=1, replica_groups=mesh['groups'=2,'replica'=4,'tensor'=4] {'replica'}, dimensions={0} | all-to-all | bytes 262144 | tf_op jit(solution)/shard_map/all_to_all | solution.py:246
  13.8 4.8 %conv_project.1 = (bf16[256,2048]{1,0:T(8,128)(2,1)}, bf16[4,288,256]{2,1,0:T(8,128)(2,1)}) custom-call(s32[32]{0:T(128)} %refs_0_.3, s32[32]{0:T(128)} %refs_1_.3, s32[32]{0:T(128)} %refs_2_.3, bf16[256,2048]{1,0:T(8,128)(2,1)} %refs_3_.1, bf16[288,2048]{1,0:T(8,128)(2,1)} %bitcast.7, bf16[4,2048]{1,0:T(4,128)(2,1)} %refs_5_.2, f32[1,2048]{1,0:T(1,128)} %bitcast.13, ...), custom_call_target="tpu_custom_call" | custom-call | tf_op jit(solution)/shard_map/conv_project/pallas_call | solution.py:234
  18.5 0.0 copy-start.1
  18.6 3.6 %all-to-all-start.1 = ((bf16[4,288,256]{2,1,0:T(8,128)(2,1)}), bf16[4,288,256]{2,1,0:T(8,128)(2,1)S(1)}, u32[]{:S(2)}, u32[]{:S(2)}) async-start(bf16[4,288,256]{2,1,0:T(8,128)(2,1)} %get-tuple-element.7), calls=%async_computation.1 | async-start | bytes 1179648 | tf_op jit(solution)/shard_map/all_to_all | solution.py:246
  22.2 0.0 copy-done.1
  22.2 1.2 %collective-permute-start.2 = (bf16[32,2048]{1,0:T(8,128)(2,1)S(1)}, bf16[32,2048]{1,0:T(8,128)(2,1)S(1)}, u32[]{:S(2)}, u32[]{:S(2)}) collective-permute-start(bf16[32,2048]{1,0:T(8,128)(2,1)S(1)} %bitcast.10), channel_id=1, source_target_pairs={{12,0},{0,4},{4,8},{8,12},{13,1},{1,5},{5,9},{9,13},{14,2},{2,6},{... | collective-permute-start | bytes 393224 | tf_op jit(solution)/shard_map/ppermute | solution.py:250
  23.4 0.9 %collective-permute-start.1 = (bf16[32,2048]{1,0:T(8,128)(2,1)S(1)}, bf16[32,2048]{1,0:T(8,128)(2,1)S(1)}, u32[]{:S(2)}, u32[]{:S(2)}) collective-permute-start(bf16[32,2048]{1,0:T(8,128)(2,1)S(1)} %bitcast.11), channel_id=1, source_target_pairs={{8,0},{12,4},{0,8},{4,12},{9,1},{13,5},{1,9},{5,13},{10,2},{14,6},... | collective-permute-start | bytes 393224 | tf_op jit(solution)/shard_map/ppermute | solution.py:250
  24.3 1.8 %collective-permute-start = (bf16[32,2048]{1,0:T(8,128)(2,1)S(1)}, bf16[32,2048]{1,0:T(8,128)(2,1)S(1)}, u32[]{:S(2)}, u32[]{:S(2)}) collective-permute-start(bf16[32,2048]{1,0:T(8,128)(2,1)S(1)} %bitcast.12), channel_id=1, source_target_pairs={{4,0},{8,4},{12,8},{0,12},{5,1},{9,5},{13,9},{1,13},{6,2},{10,6},{... | collective-permute-start | bytes 393224 | tf_op jit(solution)/shard_map/ppermute | solution.py:250
  26.1 4.4 %collective-permute-done.2.refs_13_ = bf16[32,2048]{1,0:T(8,128)(2,1)S(1)} collective-permute-done((bf16[32,2048]{1,0:T(8,128)(2,1)S(1)}, bf16[32,2048]{1,0:T(8,128)(2,1)S(1)}, u32[]{:S(2)}, u32[]{:S(2)}) %collective-permute-start.2) | collective-permute-done | bytes 131104 | tf_op jit(solution)/shard_map/ppermute | solution.py:250
  30.5 0.0 copy-start.2
  30.5 5.1 %collective-permute-done.1.refs_12_ = bf16[32,2048]{1,0:T(8,128)(2,1)S(1)} collective-permute-done((bf16[32,2048]{1,0:T(8,128)(2,1)S(1)}, bf16[32,2048]{1,0:T(8,128)(2,1)S(1)}, u32[]{:S(2)}, u32[]{:S(2)}) %collective-permute-start.1) | collective-permute-done | bytes 131104 | tf_op jit(solution)/shard_map/ppermute | solution.py:250
  35.6 0.0 copy-start.3
  35.6 0.0 collective-permute-done.refs_11_
  35.6 0.0 copy-start.4
  35.6 0.0 all-to-all-done.1.refs_9_
  35.6 0.0 copy-start
  35.7 0.0 copy-done.2
  35.7 0.6 %copy-done.3 = bf16[32,2048]{1,0:T(8,128)(2,1)} copy-done((bf16[32,2048]{1,0:T(8,128)(2,1)}, bf16[32,2048]{1,0:T(8,128)(2,1)S(1)}, u32[]{:S(2)}) %copy-start.3) | copy-done | bytes 131096
  36.3 0.0 copy-done.4
  36.3 0.3 copy-done
  36.6 16.2 %dt_scan_gate.1 = (bf16[256,2048]{1,0:T(8,128)(2,1)}, bf16[128,2048]{1,0:T(8,128)(2,1)}) custom-call(s32[32]{0:T(128)} %refs_0_.3, s32[32]{0:T(128)} %refs_1_.3, s32[32]{0:T(128)} %refs_2_.3, bf16[256,2048]{1,0:T(8,128)(2,1)} %get-tuple-element.6.refs_3_, bf16[256,2048]{1,0:T(8,128)(2,1)} %refs_4_.1, bf16[256,2048]{1,0:T(8,128)(2,1)} %refs_5_.3, ...), custom_call_target="tpu_custom_call" | custom-call | tf_op jit(solution)/shard_map/dt_scan_gate/pallas_call | solution.py:234
  (3 shorter events, 0.0 us)
Async XLA Ops:
  18.5 3.6 %copy-start.1 = (bf16[2,16,2048]{2,1,0:T(8,128)(2,1)S(1)}, bf16[2,16,2048]{2,1,0:T(8,128)(2,1)}, u32[]{:S(2)}) copy-start(bf16[2,16,2048]{2,1,0:T(8,128)(2,1)} %param.23) | copy-start | bytes 393220
  18.6 17.1 %all-to-all-start.1 = ((bf16[4,288,256]{2,1,0:T(8,128)(2,1)}), bf16[4,288,256]{2,1,0:T(8,128)(2,1)S(1)}, u32[]{:S(2)}, u32[]{:S(2)}) async-start(bf16[4,288,256]{2,1,0:T(8,128)(2,1)} %get-tuple-element.7), calls=%async_computation.1 | async-start | bytes 1179648 | tf_op jit(solution)/shard_map/all_to_all | solution.py:246
  22.2 8.3 %collective-permute-start.2 = (bf16[32,2048]{1,0:T(8,128)(2,1)S(1)}, bf16[32,2048]{1,0:T(8,128)(2,1)S(1)}, u32[]{:S(2)}, u32[]{:S(2)}) collective-permute-start(bf16[32,2048]{1,0:T(8,128)(2,1)S(1)} %bitcast.10), channel_id=1, source_target_pairs={{12,0},{0,4},{4,8},{8,12},{13,1},{1,5},{5,9},{9,13},{14,2},{2,6},{... | collective-permute-start | bytes 393224 | tf_op jit(solution)/shard_map/ppermute | solution.py:250
  23.4 12.3 %collective-permute-start.1 = (bf16[32,2048]{1,0:T(8,128)(2,1)S(1)}, bf16[32,2048]{1,0:T(8,128)(2,1)S(1)}, u32[]{:S(2)}, u32[]{:S(2)}) collective-permute-start(bf16[32,2048]{1,0:T(8,128)(2,1)S(1)} %bitcast.11), channel_id=1, source_target_pairs={{8,0},{12,4},{0,8},{4,12},{9,1},{13,5},{1,9},{5,13},{10,2},{14,6},... | collective-permute-start | bytes 393224 | tf_op jit(solution)/shard_map/ppermute | solution.py:250
  24.3 11.4 %collective-permute-start = (bf16[32,2048]{1,0:T(8,128)(2,1)S(1)}, bf16[32,2048]{1,0:T(8,128)(2,1)S(1)}, u32[]{:S(2)}, u32[]{:S(2)}) collective-permute-start(bf16[32,2048]{1,0:T(8,128)(2,1)S(1)} %bitcast.12), channel_id=1, source_target_pairs={{4,0},{8,4},{12,8},{0,12},{5,1},{9,5},{13,9},{1,13},{6,2},{10,6},{... | collective-permute-start | bytes 393224 | tf_op jit(solution)/shard_map/ppermute | solution.py:250
  30.5 5.2 %copy-start.2 = (bf16[32,2048]{1,0:T(8,128)(2,1)}, bf16[32,2048]{1,0:T(8,128)(2,1)S(1)}, u32[]{:S(2)}) copy-start(bf16[32,2048]{1,0:T(8,128)(2,1)S(1)} %collective-permute-done.2.refs_13_) | copy-start | bytes 393220
  35.6 0.7 %copy-start.3 = (bf16[32,2048]{1,0:T(8,128)(2,1)}, bf16[32,2048]{1,0:T(8,128)(2,1)S(1)}, u32[]{:S(2)}) copy-start(bf16[32,2048]{1,0:T(8,128)(2,1)S(1)} %collective-permute-done.1.refs_12_) | copy-start | bytes 393220
  35.6 0.7 %copy-start.4 = (bf16[32,2048]{1,0:T(8,128)(2,1)}, bf16[32,2048]{1,0:T(8,128)(2,1)S(1)}, u32[]{:S(2)}) copy-start(bf16[32,2048]{1,0:T(8,128)(2,1)S(1)} %collective-permute-done.refs_11_) | copy-start | bytes 393220
  35.6 0.9 %copy-start = (bf16[4,288,256]{2,1,0:T(8,128)(2,1)}, bf16[4,288,256]{2,1,0:T(8,128)(2,1)S(1)}, u32[]{:S(2)}) copy-start(bf16[4,288,256]{2,1,0:T(8,128)(2,1)S(1)} %all-to-all-done.1.refs_9_) | copy-start | bytes 1769476

commit v3 on v2

v3 whole, which is shorter than its diff:
```python
import functools

import jax
import jax.numpy as jnp
from jax import lax
from jax.experimental import pallas as pl
from jax.experimental.pallas import tpu as pltpu
from jax.sharding import PartitionSpec as P

NEW = 32
LANES = 128
LOG2E = 1.4426950408889634
MIB = 1024 * 1024
UNROLL = 8
F32, BF16 = jnp.float32, jnp.bfloat16
NT = (((1,), (1,)), ((), ()))
TN = (((0,), (0,)), ((), ()))


def silu(v):
    half = 0.5 * v
    return half + half * jnp.tanh(half)


def softplus(v):
    u = jnp.exp(-jnp.abs(v))
    small = u * (1.0 - u * (0.5 - u * (1.0 / 3.0)))
    return jnp.maximum(v, 0.0) + jnp.where(u < 0.004, small, jnp.log(1.0 + u))


def split_index(value, inner):
    assert inner & (inner - 1) == 0
    return value >> (inner.bit_length() - 1), value & (inner - 1)


def one_hot_rows(outer, inner):
    count = outer * inner
    row = lax.broadcasted_iota(jnp.int32, (count, count), 0)
    col = lax.broadcasted_iota(jnp.int32, (count, count), 1)
    high, low = split_index(row, outer)
    return jnp.where(col == low * inner + high, 1.0, 0.0).astype(BF16)


def pick_rows(values, row_low, count):
    out = jnp.zeros(row_low.shape, jnp.int32)
    for r in range(count):
        out = jnp.where(row_low == r, values[r], out)
    return out


def request_slots(dims, ints, me, gray):
    per_dev, n_replica, slots, relative = dims
    found, lengths = [], []
    for r in range(per_dev):
        request = me * per_dev + r
        place = ints[0][request]
        if relative:
            place = place ^ me
            place = place ^ (place >> 1) if gray else place
        found.append(place * slots + ints[1][request])
        lengths.append(ints[2][request])
    return found, lengths


def project_kernel(dims, refs_in, refs_out, scratch):
    per_dev, n_replica, slots, _ = dims
    holder, slot_id, prefix_len, x_hbm, wt_hbm, cw_hbm, cb_hbm = refs_in[:7]
    mixed_hbm, part_hbm = refs_out
    h_s, s_s, l_s, x_v, wt_v, cw_v, cb_v, conv_v, joined, mixed_v, part_f, part_v, sems, out_sems = scratch
    n_pieces = conv_v.shape[0]
    pieces = refs_in[7 : 7 + n_pieces]
    rows, channels = x_v.shape
    taps = cw_v.shape[0]
    copies = []
    pairs = [(cw_hbm, cw_v), (cb_hbm, cb_v), (holder, h_s), (slot_id, s_s), (prefix_len, l_s)]
    pairs += [(piece, conv_v.at[p]) for p, piece in enumerate(pieces)]
    for src, dst in pairs:
        copies.append(pltpu.make_async_copy(src, dst, sems.at[len(copies)]))
    small = len(copies)
    width = min(512, channels)
    chunks = [slice(c * width, (c + 1) * width) for c in range(channels // width)]
    for chunk in chunks:
        copies.append(pltpu.make_async_copy(x_hbm.at[:, chunk], x_v.at[:, chunk], sems.at[len(copies)]))
        copies.append(pltpu.make_async_copy(wt_hbm.at[:, chunk], wt_v.at[:, chunk], sems.at[len(copies)]))
    for copy in copies:
        copy.start()

    order = one_hot_rows(per_dev, NEW)
    for copy in copies[:small]:
        copy.wait()

    me = lax.axis_index("replica")
    found, lengths = request_slots(dims, (h_s, s_s, l_s), me, False)
    lines = (taps - 1) * per_dev
    piece_rows = conv_v.shape[1]
    shape = (per_dev * taps, n_pieces * piece_rows)
    tap, request = split_index(lax.broadcasted_iota(jnp.int32, shape, 0), per_dev)
    slot, col_tap = split_index(lax.broadcasted_iota(jnp.int32, shape, 1), taps)
    live = (taps - 1 - tap <= pick_rows(lengths, request, per_dev)) & (tap == col_tap)
    chosen = live & (slot == pick_rows(found, request, per_dev))
    select = jnp.where(chosen, 1.0, 0.0).astype(BF16)

    outs = []
    for c, chunk in enumerate(chunks):
        copies[small + 2 * c].wait()
        history = jnp.dot(select[:, :piece_rows], conv_v[0, :, chunk], preferred_element_type=F32)
        for p in range(1, n_pieces):
            picked = select[:, p * piece_rows : (p + 1) * piece_rows]
            history = history + jnp.dot(picked, conv_v[p, :, chunk], preferred_element_type=F32)
        joined[:lines, chunk] = history[:lines]
        joined[lines:, chunk] = jnp.dot(order, x_v[:, chunk], preferred_element_type=F32)
        summed = jnp.broadcast_to(cb_v[:, chunk], (rows, width))
        for k in range(taps):
            weight = cw_v[k : k + 1, chunk].astype(F32)
            summed = summed + joined[k * per_dev : k * per_dev + rows, chunk] * weight
        mixed = silu(summed).astype(BF16)
        mixed_v[:, chunk] = mixed
        copies[small + 2 * c + 1].wait()
        part = lax.dot_general(wt_v[:, chunk], mixed, NT, preferred_element_type=F32)
        if c == 0:
            part_f[...] = part
        else:
            part_f[...] += part
        outs.append(pltpu.make_async_copy(mixed_v.at[:, chunk], mixed_hbm.at[:, chunk], out_sems.at[c]))
        outs[-1].start()
    part_v[...] = part_f[...].astype(BF16)
    outs.append(pltpu.make_async_copy(part_v, part_hbm, out_sems.at[len(outs)]))
    outs[-1].start()
    for copy in outs:
        copy.wait()


def scan_kernel(dims, refs_in, refs_out, scratch):
    per_dev, n_replica, slots, _ = dims
    holder, slot_id, prefix_len, mixed_hbm, z_hbm, dtw_hbm, dtb_hbm, al_hbm, skip_hbm = refs_in[:9]
    out_hbm, state_hbm = refs_out
    (h_s, s_s, l_s, mixed_v, z_v, dtw_v, dtb_v, al_v, skip_v, parts_v, cache_v, b_tab, c_big, dt_v, gate_v,
     a_v, start_tm, final_tm, h_v, y_v, out_v, state_v, sems, out_sems) = scratch
    n_parts = parts_v.shape[0]
    parts, pieces = refs_in[9 : 9 + n_parts], refs_in[9 + n_parts :]
    rows, channels = z_v.shape
    states = al_v.shape[0]
    rank = dtw_v.shape[0]
    group = h_v.shape[2]
    pair_rows = 2 * per_dev
    depth = 2 * states * per_dev
    piece_rows = cache_v.shape[0] // len(pieces)
    pairs = [(z_hbm, z_v)] + [(part, parts_v.at[p]) for p, part in enumerate(parts)]
    pairs += [(dtw_hbm, dtw_v), (dtb_hbm, dtb_v), (al_hbm, al_v), (holder, h_s), (slot_id, s_s), (prefix_len, l_s),
              (skip_hbm, skip_v), (mixed_hbm, mixed_v)]
    pairs += [(piece, cache_v.at[p * piece_rows : (p + 1) * piece_rows]) for p, piece in enumerate(pieces)]
    copies = [pltpu.make_async_copy(src, dst, sems.at[i]) for i, (src, dst) in enumerate(pairs)]
    for copy in copies:
        copy.start()

    order = one_hot_rows(per_dev, NEW)
    copies[0].wait()
    gate_v[...] = silu(jnp.dot(order, z_v[...], preferred_element_type=F32))

    for copy in copies[1 : 1 + n_parts]:
        copy.wait()
    projected = parts_v[0].astype(F32)
    for p in range(1, n_parts):
        projected = projected + parts_v[p].astype(F32)
    dt_low = projected[:rank].astype(BF16)
    late = projected[rank:].T
    for n in range(states):
        b_tab[n] = jnp.broadcast_to(late[:, n : n + 1], (rows, LANES))
    shape = (states, depth)
    col_state = split_index(lax.broadcasted_iota(jnp.int32, shape, 1), per_dev)[0] & (states - 1)
    spread = jnp.where(lax.broadcasted_iota(jnp.int32, shape, 0) == col_state, 1.0, 0.0).astype(BF16)
    c_wide = jnp.dot(late[:, states:].astype(BF16), spread, preferred_element_type=F32)
    row = lax.broadcasted_iota(jnp.int32, (rows, depth), 0)
    col = lax.broadcasted_iota(jnp.int32, (rows, depth), 1)
    row_token, row_request = split_index(row, per_dev)
    col_token, col_rest = split_index(col, states * per_dev)
    fits = (row_request == (col_rest & (per_dev - 1))) & ((row_token & 1) == col_token)
    c_big[...] = jnp.where(fits, c_wide, 0.0).astype(BF16)

    for copy in copies[1 + n_parts :]:
        copy.wait()
    dt_v[...] = softplus(
        lax.dot_general(dt_low, dtw_v[...], TN, preferred_element_type=F32) + dtb_v[...]
    )
    a_v[...] = jnp.exp(al_v[...]) * (-LOG2E)

    me = lax.axis_index("replica")
    found, lengths = request_slots(dims, (h_s, s_s, l_s), me, True)
    shape = (per_dev * states, cache_v.shape[0])
    state_id, request = split_index(lax.broadcasted_iota(jnp.int32, shape, 0), per_dev)
    slot, col_state = split_index(lax.broadcasted_iota(jnp.int32, shape, 1), states)
    chosen = (pick_rows(lengths, request, per_dev) > 0) & (state_id == col_state)
    chosen = chosen & (slot == pick_rows(found, request, per_dev))
    select = jnp.where(chosen, 1.0, 0.0).astype(BF16)
    start_tm[...] = jnp.dot(select, cache_v[...], preferred_element_type=F32)

    n_groups = channels // group
    n_tiles = group // LANES
    n_blocks = NEW // UNROLL
    pairs_each = NEW // 2 // (n_tiles * n_blocks)

    def group_lanes(g):
        return pl.ds(pl.multiple_of(g * group, group), group)

    def finish_pair(g, pair):
        lanes = group_lanes(g)
        now = pl.ds(pl.multiple_of(pair * pair_rows, pair_rows), pair_rows)
        held = h_v[g & 1, pl.ds(pl.multiple_of(pair * depth, depth), depth), :]
        total = jnp.dot(c_big[now, :], held, preferred_element_type=F32)
        mixed = mixed_v[now, lanes].astype(F32)
        y_v[now, lanes] = ((total + skip_v[:, lanes] * mixed) * gate_v[now, lanes]).astype(BF16)

    def out_copies(g):
        lanes = group_lanes(g)
        return [
            pltpu.make_async_copy(src.at[:, lanes], dst.at[:, lanes], out_sems.at[i, g])
            for i, (src, dst) in enumerate(((out_v, out_hbm), (state_v, state_hbm)))
        ]

    def finish_group(g):
        lanes = group_lanes(g)
        back = one_hot_rows(NEW, per_dev)
        back_s = one_hot_rows(states, per_dev)
        out_v[:, lanes] = jnp.dot(back, y_v[:, lanes], preferred_element_type=F32).astype(BF16)
        final = jnp.dot(back_s, final_tm[:, lanes].astype(BF16), preferred_element_type=F32)
        state_v[:, lanes] = final.astype(BF16)
        for copy in out_copies(g):
            copy.start()

    def one_group(g, carry):
        before = jnp.maximum(g - 1, 0)

        def one_tile(i, carry):
            lanes = pl.ds(pl.multiple_of(g * group + i * LANES, LANES), LANES)
            part = pl.ds(pl.multiple_of(i * LANES, LANES), LANES)
            rates = [jnp.broadcast_to(a_v[n : n + 1, lanes], (per_dev, LANES)) for n in range(states)]

            def advance(block, state):
                state = list(state)
                for u in range(UNROLL):
                    t = block * UNROLL + u
                    now = pl.ds(pl.multiple_of(t * per_dev, per_dev), per_dev)
                    dt = dt_v[now, lanes]
                    if u % 2 == 0:
                        both = pl.ds(pl.multiple_of(t * per_dev, pair_rows), pair_rows)
                        pair = mixed_v[both, lanes].astype(F32)
                    drive = dt * pair[u % 2 * per_dev : (u % 2 + 1) * per_dev]
                    for n in range(states):
                        state[n] = jnp.exp2(dt * rates[n]) * state[n] + drive * b_tab[n, now, :]
                        if n % 2:
                            spot = pl.multiple_of((t * states + n - 1) * per_dev, pair_rows)
                            packed = jnp.concatenate([state[n - 1], state[n]], axis=0).astype(BF16)
                            h_v[g & 1, pl.ds(spot, pair_rows), part] = packed
                for k in range(pairs_each):
                    finish_pair(before, (i * n_blocks + block) * pairs_each + k)
                return tuple(state)

            state = tuple(start_tm[n * per_dev : (n + 1) * per_dev, lanes] for n in range(states))
            state = lax.fori_loop(0, n_blocks, advance, state)
            for n in range(states):
                final_tm[n * per_dev : (n + 1) * per_dev, lanes] = state[n]
            return carry

        lax.fori_loop(0, n_tiles, one_tile, 0)

        @pl.when(g > 0)
        def _():
            finish_group(before)

        return carry

    lax.fori_loop(0, n_groups, one_group, 0)

    def last_pair(pair, carry):
        finish_pair(n_groups - 1, pair)
        return carry

    lax.fori_loop(0, NEW // 2, last_pair, 0, unroll=4)
    finish_group(n_groups - 1)

    def last_wait(g, carry):
        for copy in out_copies(g):
            copy.wait()
        return carry

    lax.fori_loop(0, n_groups, last_wait, 0)


def split_refs(kernel, dims, n_in, n_out):
    def body(*refs):
        kernel(dims, refs[:n_in], refs[n_in : n_in + n_out], refs[n_in + n_out :])

    return body


def call(kernel, dims, name, limit, ins, outs, scratch):
    hbm = pl.BlockSpec(memory_space=pltpu.HBM)
    anywhere = pl.BlockSpec(memory_space=pl.ANY)
    return pl.pallas_call(
        split_refs(kernel, dims, len(ins), len(outs)),
        in_specs=[hbm if fixed else anywhere for _, fixed in ins],
        out_specs=[anywhere] * len(outs),
        out_shape=[jax.ShapeDtypeStruct(*out) for out in outs],
        scratch_shapes=scratch,
        compiler_params=pltpu.CompilerParams(vmem_limit_bytes=limit * MIB),
        name=name,
    )(*[value for value, _ in ins])


def swap(value, axis, size, mask):
    return lax.ppermute(value, axis, [(i, i ^ mask) for i in range(size)])


def shards(mesh, x_new, z_new, conv_weight, conv_bias, x_proj_weight, dt_proj_weight, dt_bias, a_log, d_skip,
           cache_ssm, cache_conv, holder, slot_id, prefix_len):
    n_replica, n_tensor = mesh.shape["replica"], mesh.shape["tensor"]
    rows, channels = x_new.shape
    per_dev = rows // NEW
    states = a_log.shape[0]
    rank = dt_proj_weight.shape[0]
    taps = conv_weight.shape[0]
    slots = cache_ssm.shape[0]
    out_cols = x_proj_weight.shape[1]
    requests = holder.shape[0]

    conv_rows = jnp.pad(cache_conv, ((0, 0), (0, 1), (0, 0))).reshape(slots * taps, channels)
    ssm_rows = cache_ssm.reshape(slots * states, channels)
    relative = n_replica == 4
    if relative:
        conv_pieces = [conv_rows] + [swap(conv_rows, "replica", n_replica, k) for k in range(1, n_replica)]
        early = [swap(ssm_rows, "replica", n_replica, 3), swap(ssm_rows, "replica", n_replica, 1)]
        ssm_pieces = [ssm_rows, early[1], early[0], swap(early[0], "replica", n_replica, 1)]
    else:
        conv_pieces = [lax.all_gather(conv_rows, "replica", axis=0, tiled=True)]
        ssm_pieces = [lax.all_gather(ssm_rows, "replica", axis=0, tiled=True)]
        early = []

    vmem, dma = pltpu.VMEM, pltpu.SemaphoreType.DMA
    ints = [pltpu.SMEM((requests,), jnp.int32)] * 3
    n_chunks = channels // min(512, channels)
    dims = (per_dev, n_replica, slots, relative)

    mixed, part = call(
        project_kernel, dims, "conv_project", 60,
        [(holder, True), (slot_id, True), (prefix_len, True), (x_new, True), (x_proj_weight.T, True),
         (conv_weight, True), (conv_bias[None, :], True)]
        + [(piece, False) for piece in conv_pieces + early],
        [((rows, channels), BF16), ((out_cols, rows), BF16)],
        ints + [
            vmem((rows, channels), BF16),
            vmem((out_cols, channels), BF16),
            vmem((taps, channels), BF16),
            vmem((1, channels), F32),
            vmem((len(conv_pieces),) + conv_pieces[0].shape, BF16),
            vmem((rows + (taps - 1) * per_dev, channels), F32),
            vmem((rows, channels), BF16),
            vmem((out_cols, rows), F32),
            vmem((out_cols, rows), BF16),
            dma((5 + len(conv_pieces) + 2 * n_chunks,)),
            dma((n_chunks + 1,)),
        ],
    )
    parts = [swap(part, "tensor", n_tensor, k) for k in reversed(range(1, n_tensor))] + [part]

    group = 2 * LANES
    out, state = call(
        scan_kernel, dims, "dt_scan_gate", 32,
        [(holder, True), (slot_id, True), (prefix_len, True), (mixed, False), (z_new, True), (dt_proj_weight, True),
         (dt_bias[None, :], True), (a_log, True), (d_skip[None, :], True)]
        + [(piece, False) for piece in parts + ssm_pieces],
        [((rows, channels), BF16), ((per_dev * states, channels), BF16)],
        ints + [
            vmem((rows, channels), BF16),
            vmem((rows, channels), BF16),
            vmem((rank, channels), BF16),
            vmem((1, channels), F32),
            vmem((states, channels), F32),
            vmem((1, channels), F32),
            vmem((n_tensor, out_cols, rows), BF16),
            vmem((n_replica * slots * states, channels), BF16),
            vmem((states, rows, LANES), F32),
            vmem((rows, 2 * states * per_dev), BF16),
            vmem((rows, channels), F32),
            vmem((rows, channels), F32),
            vmem((states, channels), F32),
            vmem((per_dev * states, channels), F32),
            vmem((per_dev * states, channels), F32),
            vmem((2, rows * states, group), BF16),
            vmem((rows, channels), BF16),
            vmem((rows, channels), BF16),
            vmem((per_dev * states, channels), BF16),
            dma((9 + n_tensor + len(ssm_pieces),)),
            dma((2, channels // group)),
        ],
    )
    return out, state.reshape(per_dev, states, channels)


def solution(mesh):
    placed = (
        P(("groups", "replica"), "tensor"),
        P(("groups", "replica"), "tensor"),
        P(None, "tensor"),
        P("tensor"),
        P("tensor", None),
        P(None, "tensor"),
        P("tensor"),
        P(None, "tensor"),
        P("tensor"),
        P(("groups", "replica"), None, "tensor"),
        P(("groups", "replica"), None, "tensor"),
        P("groups"),
        P("groups"),
        P("groups"),
    )
    return jax.shard_map(
        functools.partial(shards, mesh),
        mesh=mesh,
        in_specs=placed,
        out_specs=(P(("groups", "replica"), "tensor"), P(("groups", "replica"), None, "tensor")),
        check_vma=False,
    )
```

time: 53.5 us -> 62.1 us (1.16)
  blocking collectives: 12.3 us -> 0 us
  Pallas kernels: 21 us -> 32.3 us
  starting transfers between devices: 7.5 us -> 12.2 us
  local copies, waits for them, and re-layouts: 1.73 us -> 5.44 us
  waiting for transfers between devices: 9.56 us -> 11 us
    all_to_all x1 -> x0, blocking collectives: 12.3 us -> none  [to_all(): return lax.all_to_all(value, axis, 0, 0)]
    pallas_call x2, Pallas kernels: 21 us -> 32.3 us  [call(): pl.pallas_call(split_refs(kernel, dims, len(ins), len(outs)), in_specs=[h...]
    ppermute x3 -> x9, starting transfers between devices: 3.88 us -> 12.2 us  [swap(): return lax.ppermute(value, axis, [(i, i ^ mask) for i in range(size)])]
    unnamed x11 -> x39, local copies, waits for them, and re-layouts: 1.69 us -> 5.41 us
    all_to_all x1 -> x0, starting transfers between devices: 3.62 us -> none  [to_all(): return lax.all_to_all(value, axis, 0, 0)]
    ppermute x3 -> x9, waiting for transfers between devices: 9.56 us -> 11 us  [swap(): return lax.ppermute(value, axis, [(i, i ^ mask) for i in range(size)])]
  transfers between devices with their start and end apart: 4 -> 9, of which waited for: 2 -> 4; matrix products, arithmetic and copies ran while one was open for 0% -> 1% of each run, Pallas kernels for 0% -> 0%
where the time goes in v3:
time: 62.1 us; the launch traced here: 61.8 us
  Pallas kernels  32.3 us (52%)
  starting transfers between devices  12.2 us (20%)
  waiting for transfers between devices  11 us (18%)
  local copies, waits for them, and re-layouts  5.44 us (9%)
  between operations  0.83 us (1%)
    pallas_call x2, Pallas kernels, call(): pl.pallas_call(split_refs(kernel, dims, len(ins), len(outs)), in_specs=[h...  32.3 us
    ppermute x9, starting transfers between devices, swap(): return lax.ppermute(value, axis, [(i, i ^ mask) for i in range(size)])  12.2 us
    ppermute x9, waiting for transfers between devices, swap(): return lax.ppermute(value, axis, [(i, i ^ mask) for i in range(size)])  11 us
    unnamed x39, local copies, waits for them, and re-layouts  5.41 us
  transfers between devices with their start and end apart: 9, of which 4 were waited for; matrix products, arithmetic and copies ran while one was open for 1% of the time, Pallas kernels for 0%

profile of v3, /device:TPU:0, one launch (start us, length us, event | category | flops | bytes accessed | tf_op | source)
XLA Modules:
  0.0 61.8 jit_solution(2605759970818228429)
XLA Ops:
  0.6 3.1 %collective-permute-start.4 = (bf16[32,2048]{1,0:T(8,128)(2,1)}, bf16[32,2048]{1,0:T(8,128)(2,1)S(1)}, u32[]{:S(2)}, u32[]{:S(2)}) collective-permute-start(bf16[32,2048]{1,0:T(8,128)(2,1)} %bitcast.6), channel_id=1, source_target_pairs={{0,4},{4,0},{8,12},{12,8},{1,5},{5,1},{9,13},{13,9},{2,6},{6,2},{1... | collective-permute-start | bytes 393224 | tf_op jit(solution)/shard_map/ppermute | solution.py:311
  3.7 2.5 %collective-permute-start.3 = (bf16[32,2048]{1,0:T(8,128)(2,1)}, bf16[32,2048]{1,0:T(8,128)(2,1)S(1)}, u32[]{:S(2)}, u32[]{:S(2)}) collective-permute-start(bf16[32,2048]{1,0:T(8,128)(2,1)} %bitcast.7), channel_id=1, source_target_pairs={{0,12},{4,8},{8,4},{12,0},{1,13},{5,9},{9,5},{13,1},{2,14},{6,10},... | collective-permute-start | bytes 393224 | tf_op jit(solution)/shard_map/ppermute | solution.py:311
  6.2 0.8 %copy.17 = bf16[2,3,2048]{2,1,0:T(4,128)(2,1)S(1)} copy(bf16[2,3,2048]{2,0,1:T(2,128)(2,1)} %param.24) | data formatting | bytes 49152
  7.0 1.4 %collective-permute-start.2 = (bf16[8,2048]{1,0:T(8,128)(2,1)S(1)}, bf16[8,2048]{1,0:T(8,128)(2,1)S(1)}, u32[]{:S(2)}, u32[]{:S(2)}) collective-permute-start(bf16[8,2048]{1,0:T(8,128)(2,1)S(1)} %reshape.13.refs_7_), channel_id=1, source_target_pairs={{0,12},{4,8},{8,4},{12,0},{1,13},{5,9},{9,5},{13,1},{2,14},{6,10},... | collective-permute-start | bytes 98312 | tf_op jit(solution)/shard_map/ppermute | solution.py:311
  8.4 0.8 %collective-permute-start.1 = (bf16[8,2048]{1,0:T(8,128)(2,1)S(1)}, bf16[8,2048]{1,0:T(8,128)(2,1)S(1)}, u32[]{:S(2)}, u32[]{:S(2)}) collective-permute-start(bf16[8,2048]{1,0:T(8,128)(2,1)S(1)} %reshape.13.refs_7_), channel_id=1, source_target_pairs={{0,8},{4,12},{8,0},{12,4},{1,9},{5,13},{9,1},{13,5},{2,10},{6,14},... | collective-permute-start | bytes 98312 | tf_op jit(solution)/shard_map/ppermute | solution.py:311
  9.2 2.2 %collective-permute-start = (bf16[8,2048]{1,0:T(8,128)(2,1)S(1)}, bf16[8,2048]{1,0:T(8,128)(2,1)S(1)}, u32[]{:S(2)}, u32[]{:S(2)}) collective-permute-start(bf16[8,2048]{1,0:T(8,128)(2,1)S(1)} %reshape.13.refs_7_), channel_id=1, source_target_pairs={{0,4},{4,0},{8,12},{12,8},{1,5},{5,1},{9,13},{13,9},{2,6},{6,2},{1... | collective-permute-start | bytes 98312 | tf_op jit(solution)/shard_map/ppermute | solution.py:311
  11.5 2.5 %collective-permute-done.2.refs_10_ = bf16[8,2048]{1,0:T(8,128)(2,1)S(1)} collective-permute-done((bf16[8,2048]{1,0:T(8,128)(2,1)S(1)}, bf16[8,2048]{1,0:T(8,128)(2,1)S(1)}, u32[]{:S(2)}, u32[]{:S(2)}) %collective-permute-start.2) | collective-permute-done | bytes 32800 | tf_op jit(solution)/shard_map/ppermute | solution.py:311
  13.9 1.5 %collective-permute-done.1.refs_9_ = bf16[8,2048]{1,0:T(8,128)(2,1)S(1)} collective-permute-done((bf16[8,2048]{1,0:T(8,128)(2,1)S(1)}, bf16[8,2048]{1,0:T(8,128)(2,1)S(1)}, u32[]{:S(2)}, u32[]{:S(2)}) %collective-permute-start.1) | collective-permute-done | bytes 32800 | tf_op jit(solution)/shard_map/ppermute | solution.py:311
  15.4 0.5 copy-done.17
  16.0 0.0 copy-done.18
  16.0 0.1 copy-done.3
  16.1 0.1 copy-done.5
  16.2 4.9 %conv_project.1 = (bf16[256,2048]{1,0:T(8,128)(2,1)}, bf16[288,256]{1,0:T(8,128)(2,1)}) custom-call(s32[32]{0:T(128)} %refs_0_.3, s32[32]{0:T(128)} %refs_1_.3, s32[32]{0:T(128)} %refs_2_.3, bf16[256,2048]{1,0:T(8,128)(2,1)} %refs_3_.1, bf16[288,2048]{1,0:T(8,128)(2,1)} %bitcast.11, bf16[4,2048]{1,0:T(4,128)(2,1)} %refs_5_.2, f32[1,2048]{1,0:T(1,128)} %bitcast.12, ...), custom_call_target="tpu_custom_call" | custom-call | tf_op jit(solution)/shard_map/conv_project/pallas_call | solution.py:299
  21.0 0.1 collective-permute-start.7
  21.1 1.6 %collective-permute-start.6 = (bf16[288,256]{1,0:T(8,128)(2,1)}, bf16[288,256]{1,0:T(8,128)(2,1)S(1)}, u32[]{:S(2)}, u32[]{:S(2)}) collective-permute-start(bf16[288,256]{1,0:T(8,128)(2,1)} %get-tuple-element.7.refs_12_), channel_id=1, source_target_pairs={{0,2},{1,3},{2,0},{3,1},{4,6},{5,7},{6,4},{7,5},{8,10},{9,11},{10,... | collective-permute-start | bytes 442376 | tf_op jit(solution)/shard_map/ppermute | solution.py:311
  22.7 0.3 collective-permute-start.5
  23.0 0.2 collective-permute-start.8
  23.2 5.7 %collective-permute-done.8.refs_16_ = bf16[32,2048]{1,0:T(8,128)(2,1)S(1)} collective-permute-done((bf16[32,2048]{1,0:T(8,128)(2,1)}, bf16[32,2048]{1,0:T(8,128)(2,1)S(1)}, u32[]{:S(2)}, u32[]{:S(2)}) %collective-permute-start.8) | collective-permute-done | bytes 131104 | tf_op jit(solution)/shard_map/ppermute | solution.py:311
  29.0 1.4 %collective-permute-done.5.refs_9_ = bf16[288,256]{1,0:T(8,128)(2,1)S(1)} collective-permute-done((bf16[288,256]{1,0:T(8,128)(2,1)}, bf16[288,256]{1,0:T(8,128)(2,1)S(1)}, u32[]{:S(2)}, u32[]{:S(2)}) %collective-permute-start.5) | collective-permute-done | bytes 147488 | tf_op jit(solution)/shard_map/ppermute | solution.py:311
  30.4 1.2 %copy-done.2 = bf16[256,2048]{1,0:T(8,128)(2,1)S(1)} copy-done((bf16[256,2048]{1,0:T(8,128)(2,1)S(1)}, bf16[256,2048]{1,0:T(8,128)(2,1)}, u32[]{:S(2)}) %copy-start.2) | copy-done | bytes 1048600
  31.6 0.9 %copy-done.4 = bf16[32,2048]{1,0:T(8,128)(2,1)S(1)} copy-done((bf16[32,2048]{1,0:T(8,128)(2,1)S(1)}, bf16[32,2048]{1,0:T(8,128)(2,1)}, u32[]{:S(2)}) %copy-start.4) | copy-done | bytes 131096
  32.5 0.9 %copy-done.6 = bf16[32,2048]{1,0:T(8,128)(2,1)S(1)} copy-done((bf16[32,2048]{1,0:T(8,128)(2,1)S(1)}, bf16[32,2048]{1,0:T(8,128)(2,1)}, u32[]{:S(2)}) %copy-start.6) | copy-done | bytes 131096
  33.4 0.9 %copy-done.7 = bf16[288,256]{1,0:T(8,128)(2,1)S(1)} copy-done((bf16[288,256]{1,0:T(8,128)(2,1)S(1)}, bf16[288,256]{1,0:T(8,128)(2,1)}, u32[]{:S(2)}) %copy-start.7) | copy-done | bytes 147480
  34.3 27.5 %dt_scan_gate.1 = (bf16[256,2048]{1,0:T(8,128)(2,1)}, bf16[128,2048]{1,0:T(8,128)(2,1)}) custom-call(s32[32]{0:T(128)S(1)} %copy-done.12, s32[32]{0:T(128)S(1)} %copy-done.13, s32[32]{0:T(128)S(1)} %copy-done.14, bf16[256,2048]{1,0:T(8,128)(2,1)S(1)} %copy-done.2, bf16[256,2048]{1,0:T(8,128)(2,1)S(1)} %copy-done, bf16[256,2048]{1,0:T(8,128)(2,1)S(1)} %copy-done.1, ...), custom_call_target="tpu_custom_call" | custom-call | tf_op jit(solution)/shard_map/dt_scan_gate/pallas_call | solution.py:299
  (37 shorter events, 0.1 us)
Async XLA Ops:
  0.6 14.8 %collective-permute-start.4 = (bf16[32,2048]{1,0:T(8,128)(2,1)}, bf16[32,2048]{1,0:T(8,128)(2,1)S(1)}, u32[]{:S(2)}, u32[]{:S(2)}) collective-permute-start(bf16[32,2048]{1,0:T(8,128)(2,1)} %bitcast.6), channel_id=1, source_target_pairs={{0,4},{4,0},{8,12},{12,8},{1,5},{5,1},{9,13},{13,9},{2,6},{6,2},{1... | collective-permute-start | bytes 393224 | tf_op jit(solution)/shard_map/ppermute | solution.py:311
  3.7 11.7 %collective-permute-start.3 = (bf16[32,2048]{1,0:T(8,128)(2,1)}, bf16[32,2048]{1,0:T(8,128)(2,1)S(1)}, u32[]{:S(2)}, u32[]{:S(2)}) collective-permute-start(bf16[32,2048]{1,0:T(8,128)(2,1)} %bitcast.7), channel_id=1, source_target_pairs={{0,12},{4,8},{8,4},{12,0},{1,13},{5,9},{9,5},{13,1},{2,14},{6,10},... | collective-permute-start | bytes 393224 | tf_op jit(solution)/shard_map/ppermute | solution.py:311
  7.0 8.4 %copy-start.15 = (bf16[8,2048]{1,0:T(8,128)(2,1)}, bf16[8,2048]{1,0:T(8,128)(2,1)S(1)}, u32[]{:S(2)}) copy-start(bf16[8,2048]{1,0:T(8,128)(2,1)S(1)} %reshape.13.refs_7_) | copy-start | bytes 98308
  7.0 6.9 %collective-permute-start.2 = (bf16[8,2048]{1,0:T(8,128)(2,1)S(1)}, bf16[8,2048]{1,0:T(8,128)(2,1)S(1)}, u32[]{:S(2)}, u32[]{:S(2)}) collective-permute-start(bf16[8,2048]{1,0:T(8,128)(2,1)S(1)} %reshape.13.refs_7_), channel_id=1, source_target_pairs={{0,12},{4,8},{8,4},{12,0},{1,13},{5,9},{9,5},{13,1},{2,14},{6,10},... | collective-permute-start | bytes 98312 | tf_op jit(solution)/shard_map/ppermute | solution.py:311
  8.4 7.0 %collective-permute-start.1 = (bf16[8,2048]{1,0:T(8,128)(2,1)S(1)}, bf16[8,2048]{1,0:T(8,128)(2,1)S(1)}, u32[]{:S(2)}, u32[]{:S(2)}) collective-permute-start(bf16[8,2048]{1,0:T(8,128)(2,1)S(1)} %reshape.13.refs_7_), channel_id=1, source_target_pairs={{0,8},{4,12},{8,0},{12,4},{1,9},{5,13},{9,1},{13,5},{2,10},{6,14},... | collective-permute-start | bytes 98312 | tf_op jit(solution)/shard_map/ppermute | solution.py:311
  9.2 6.2 %collective-permute-start = (bf16[8,2048]{1,0:T(8,128)(2,1)S(1)}, bf16[8,2048]{1,0:T(8,128)(2,1)S(1)}, u32[]{:S(2)}, u32[]{:S(2)}) collective-permute-start(bf16[8,2048]{1,0:T(8,128)(2,1)S(1)} %reshape.13.refs_7_), channel_id=1, source_target_pairs={{0,4},{4,0},{8,12},{12,8},{1,5},{5,1},{9,13},{13,9},{2,6},{6,2},{1... | collective-permute-start | bytes 98312 | tf_op jit(solution)/shard_map/ppermute | solution.py:311
  13.9 1.5 %copy-start.16 = (bf16[8,2048]{1,0:T(8,128)(2,1)}, bf16[8,2048]{1,0:T(8,128)(2,1)S(1)}, u32[]{:S(2)}) copy-start(bf16[8,2048]{1,0:T(8,128)(2,1)S(1)} %collective-permute-done.2.refs_10_) | copy-start | bytes 98308
  16.1 14.2 %copy-start = (bf16[256,2048]{1,0:T(8,128)(2,1)S(1)}, bf16[256,2048]{1,0:T(8,128)(2,1)}, u32[]{:S(2)}) copy-start(bf16[256,2048]{1,0:T(8,128)(2,1)} %refs_4_.1) | copy-start | bytes 3145732
  16.1 14.2 %copy-start.1 = (bf16[256,2048]{1,0:T(8,128)(2,1)S(1)}, bf16[256,2048]{1,0:T(8,128)(2,1)}, u32[]{:S(2)}) copy-start(bf16[256,2048]{1,0:T(8,128)(2,1)} %refs_5_.3) | copy-start | bytes 3145732
  16.1 14.2 %copy-start.8 = (bf16[2,16,2048]{2,1,0:T(8,128)(2,1)S(1)}, bf16[2,16,2048]{2,1,0:T(8,128)(2,1)}, u32[]{:S(2)}) copy-start(bf16[2,16,2048]{2,1,0:T(8,128)(2,1)} %param.23) | copy-start | bytes 393220
  16.1 14.2 %copy-start.9 = (f32[16,2048]{1,0:T(8,128)S(1)}, f32[16,2048]{1,0:T(8,128)}, u32[]{:S(2)}) copy-start(f32[16,2048]{1,0:T(8,128)} %refs_7_.1) | copy-start | bytes 393220
  16.1 14.2 %copy-start.10 = (f32[2048]{0:T(1024)S(1)}, f32[2048]{0:T(1024)}, u32[]{:S(2)}) copy-start(f32[2048]{0:T(1024)} %param.20) | copy-start | bytes 24580
  16.1 14.2 %copy-start.11 = (f32[2048]{0:T(1024)S(1)}, f32[2048]{0:T(1024)}, u32[]{:S(2)}) copy-start(f32[2048]{0:T(1024)} %param.22) | copy-start | bytes 24580
  16.1 14.2 %copy-start.12 = (s32[32]{0:T(128)S(1)}, s32[32]{0:T(128)}, u32[]{:S(2)}) copy-start(s32[32]{0:T(128)} %refs_0_.3) | copy-start | bytes 388
  16.2 14.2 %copy-start.13 = (s32[32]{0:T(128)S(1)}, s32[32]{0:T(128)}, u32[]{:S(2)}) copy-start(s32[32]{0:T(128)} %refs_1_.3) | copy-start | bytes 388
  16.2 14.2 %copy-start.14 = (s32[32]{0:T(128)S(1)}, s32[32]{0:T(128)}, u32[]{:S(2)}) copy-start(s32[32]{0:T(128)} %refs_2_.3) | copy-start | bytes 388
  21.0 7.9 %collective-permute-start.7 = (bf16[288,256]{1,0:T(8,128)(2,1)}, bf16[288,256]{1,0:T(8,128)(2,1)S(1)}, u32[]{:S(2)}, u32[]{:S(2)}) collective-permute-start(bf16[288,256]{1,0:T(8,128)(2,1)} %get-tuple-element.7.refs_12_), channel_id=1, source_target_pairs={{0,1},{1,0},{2,3},{3,2},{4,5},{5,4},{6,7},{7,6},{8,9},{9,8},{10,11... | collective-permute-start | bytes 442376 | tf_op jit(solution)/shard_map/ppermute | solution.py:311
  21.1 7.8 %collective-permute-start.6 = (bf16[288,256]{1,0:T(8,128)(2,1)}, bf16[288,256]{1,0:T(8,128)(2,1)S(1)}, u32[]{:S(2)}, u32[]{:S(2)}) collective-permute-start(bf16[288,256]{1,0:T(8,128)(2,1)} %get-tuple-element.7.refs_12_), channel_id=1, source_target_pairs={{0,2},{1,3},{2,0},{3,1},{4,6},{5,7},{6,4},{7,5},{8,10},{9,11},{10,... | collective-permute-start | bytes 442376 | tf_op jit(solution)/shard_map/ppermute | solution.py:311
  22.7 7.6 %collective-permute-start.5 = (bf16[288,256]{1,0:T(8,128)(2,1)}, bf16[288,256]{1,0:T(8,128)(2,1)S(1)}, u32[]{:S(2)}, u32[]{:S(2)}) collective-permute-start(bf16[288,256]{1,0:T(8,128)(2,1)} %get-tuple-element.7.refs_12_), channel_id=1, source_target_pairs={{0,3},{1,2},{2,1},{3,0},{4,7},{5,6},{6,5},{7,4},{8,11},{9,10},{10,... | collective-permute-start | bytes 442376 | tf_op jit(solution)/shard_map/ppermute | solution.py:311
  23.0 6.0 %collective-permute-start.8 = (bf16[32,2048]{1,0:T(8,128)(2,1)}, bf16[32,2048]{1,0:T(8,128)(2,1)S(1)}, u32[]{:S(2)}, u32[]{:S(2)}) collective-permute-start(bf16[32,2048]{1,0:T(8,128)(2,1)} %copy-done.5), channel_id=1, source_target_pairs={{0,4},{4,0},{8,12},{12,8},{1,5},{5,1},{9,13},{13,9},{2,6},{6,2},{1... | collective-permute-start | bytes 393224 | tf_op jit(solution)/shard_map/ppermute | solution.py:311
  30.4 1.2 %copy-start.2 = (bf16[256,2048]{1,0:T(8,128)(2,1)S(1)}, bf16[256,2048]{1,0:T(8,128)(2,1)}, u32[]{:S(2)}) copy-start(bf16[256,2048]{1,0:T(8,128)(2,1)} %get-tuple-element.6.refs_3_) | copy-start | bytes 3145732
  31.6 0.9 %copy-start.4 = (bf16[32,2048]{1,0:T(8,128)(2,1)S(1)}, bf16[32,2048]{1,0:T(8,128)(2,1)}, u32[]{:S(2)}) copy-start(bf16[32,2048]{1,0:T(8,128)(2,1)} %copy-done.3) | copy-start | bytes 393220
  32.5 0.9 %copy-start.6 = (bf16[32,2048]{1,0:T(8,128)(2,1)S(1)}, bf16[32,2048]{1,0:T(8,128)(2,1)}, u32[]{:S(2)}) copy-start(bf16[32,2048]{1,0:T(8,128)(2,1)} %copy-done.5) | copy-start | bytes 393220
  33.4 0.9 %copy-start.7 = (bf16[288,256]{1,0:T(8,128)(2,1)S(1)}, bf16[288,256]{1,0:T(8,128)(2,1)}, u32[]{:S(2)}) copy-start(bf16[288,256]{1,0:T(8,128)(2,1)} %get-tuple-element.7.refs_12_) | copy-start | bytes 442372
  (4 other events, 2.6 us)

commit v4 on v3

v4 whole, which is shorter than its diff:
```python
import functools

import jax
import jax.numpy as jnp
from jax import lax
from jax.experimental import pallas as pl
from jax.experimental.pallas import tpu as pltpu
from jax.sharding import PartitionSpec as P

NEW = 32
LANES = 128
LOG2E = 1.4426950408889634
MIB = 1024 * 1024
UNROLL = 8
F32, BF16 = jnp.float32, jnp.bfloat16
NT = (((1,), (1,)), ((), ()))
TN = (((0,), (0,)), ((), ()))


def silu(v):
    half = 0.5 * v
    return half + half * jnp.tanh(half)


def softplus(v):
    u = jnp.exp(-jnp.abs(v))
    small = u * (1.0 - u * (0.5 - u * (1.0 / 3.0)))
    return jnp.maximum(v, 0.0) + jnp.where(u < 0.004, small, jnp.log(1.0 + u))


def split_index(value, inner):
    assert inner & (inner - 1) == 0
    return value >> (inner.bit_length() - 1), value & (inner - 1)


def one_hot_rows(outer, inner):
    count = outer * inner
    row = lax.broadcasted_iota(jnp.int32, (count, count), 0)
    col = lax.broadcasted_iota(jnp.int32, (count, count), 1)
    high, low = split_index(row, outer)
    return jnp.where(col == low * inner + high, 1.0, 0.0).astype(BF16)


def pick_rows(values, row_low, count):
    out = jnp.zeros(row_low.shape, jnp.int32)
    for r in range(count):
        out = jnp.where(row_low == r, values[r], out)
    return out


def request_places(dims, ints, me):
    per_dev, n_replica, _, relative = dims
    places, slot_ids, lengths = [], [], []
    for r in range(per_dev):
        request = me * per_dev + r
        place = ints[0][request]
        if relative:
            place = place ^ me
            place = place ^ (place >> 1)
        places.append(place)
        slot_ids.append(ints[1][request])
        lengths.append(ints[2][request])
    return places, slot_ids, lengths


def fetch_rows(target, live, pieces):
    total = None
    for first, value in pieces:
        col = lax.broadcasted_iota(jnp.int32, (target.shape[0], value.shape[0]), 1) + first
        select = jnp.where((col == target) & live, 1.0, 0.0).astype(BF16)
        part = jnp.dot(select, value, preferred_element_type=F32)
        total = part if total is None else total + part
    return total


def project_kernel(dims, refs_in, refs_out, scratch):
    dims, block, firsts = dims
    per_dev, n_replica, slots, _ = dims
    holder, slot_id, prefix_len, x_hbm, wt_hbm, cw_hbm, cb_hbm = refs_in[:7]
    mixed_hbm, part_hbm = refs_out
    h_s, s_s, l_s, x_v, wt_v, cw_v, cb_v, joined, mixed_v, part_f, part_v, sems, out_sems = scratch[:13]
    held = scratch[13:]
    pieces = refs_in[7:]
    rows, channels = x_v.shape
    taps = cw_v.shape[0]
    copies = []
    pairs = [(cw_hbm, cw_v), (cb_hbm, cb_v), (holder, h_s), (slot_id, s_s), (prefix_len, l_s)]
    pairs += list(zip(pieces, held))
    for src, dst in pairs:
        copies.append(pltpu.make_async_copy(src, dst, sems.at[len(copies)]))
    small = len(copies)
    width = min(512, channels)
    chunks = [slice(c * width, (c + 1) * width) for c in range(channels // width)]
    for chunk in chunks:
        copies.append(pltpu.make_async_copy(x_hbm.at[:, chunk], x_v.at[:, chunk], sems.at[len(copies)]))
        copies.append(pltpu.make_async_copy(wt_hbm.at[:, chunk], wt_v.at[:, chunk], sems.at[len(copies)]))
    for copy in copies:
        copy.start()

    order = one_hot_rows(per_dev, NEW)
    for copy in copies[:small]:
        copy.wait()

    me = lax.axis_index("replica")
    places, slot_ids, lengths = request_places(dims, (h_s, s_s, l_s), me)
    lines = (taps - 1) * per_dev
    tap, request = split_index(lax.broadcasted_iota(jnp.int32, (per_dev * taps, 1), 0), per_dev)
    starts = [places[r] * block + (block - slots * taps) + slot_ids[r] * taps for r in range(per_dev)]
    target = pick_rows(starts, request, per_dev) + tap
    live = (tap < taps - 1) & (taps - 1 - tap <= pick_rows(lengths, request, per_dev))

    outs = []
    for c, chunk in enumerate(chunks):
        copies[small + 2 * c].wait()
        found = [(first, ref[:, chunk]) for first, ref in zip(firsts, held)]
        history = fetch_rows(target, live, found)
        joined[:lines, chunk] = history[:lines]
        joined[lines:, chunk] = jnp.dot(order, x_v[:, chunk], preferred_element_type=F32)
        summed = jnp.broadcast_to(cb_v[:, chunk], (rows, width))
        for k in range(taps):
            weight = cw_v[k : k + 1, chunk].astype(F32)
            summed = summed + joined[k * per_dev : k * per_dev + rows, chunk] * weight
        mixed = silu(summed).astype(BF16)
        mixed_v[:, chunk] = mixed
        copies[small + 2 * c + 1].wait()
        part = lax.dot_general(wt_v[:, chunk], mixed, NT, preferred_element_type=F32)
        if c == 0:
            part_f[...] = part
        else:
            part_f[...] += part
        outs.append(pltpu.make_async_copy(mixed_v.at[:, chunk], mixed_hbm.at[:, chunk], out_sems.at[c]))
        outs[-1].start()
    part_v[...] = part_f[...].astype(BF16)
    outs.append(pltpu.make_async_copy(part_v, part_hbm, out_sems.at[len(outs)]))
    outs[-1].start()
    for copy in outs:
        copy.wait()


def scan_kernel(dims, refs_in, refs_out, scratch):
    dims, block = dims
    per_dev, n_replica, slots, _ = dims
    holder, slot_id, prefix_len, mixed_hbm, z_hbm, dtw_hbm, dtb_hbm, al_hbm, skip_hbm = refs_in[:9]
    out_hbm, state_hbm = refs_out
    (h_s, s_s, l_s, mixed_v, z_v, dtw_v, dtb_v, al_v, skip_v, parts_v, cache_v, b_tab, c_tab, dt_v, drive_v, gate_v,
     a_v, start_tm, final_tm, y_v, out_v, state_v, sems, out_sems) = scratch
    n_parts, n_pieces = parts_v.shape[0], cache_v.shape[0]
    parts, pieces = refs_in[9 : 9 + n_parts], refs_in[9 + n_parts :]
    rows, channels = z_v.shape
    states = al_v.shape[0]
    rank = dtw_v.shape[0]
    pairs = [(z_hbm, z_v)] + [(part, parts_v.at[p]) for p, part in enumerate(parts)]
    pairs += [(dtw_hbm, dtw_v), (dtb_hbm, dtb_v), (al_hbm, al_v), (holder, h_s), (slot_id, s_s), (prefix_len, l_s),
              (skip_hbm, skip_v), (mixed_hbm, mixed_v)]
    pairs += [(piece, cache_v.at[p]) for p, piece in enumerate(pieces)]
    copies = [pltpu.make_async_copy(src, dst, sems.at[i]) for i, (src, dst) in enumerate(pairs)]
    for copy in copies:
        copy.start()

    order = one_hot_rows(per_dev, NEW)
    copies[0].wait()
    gate_v[...] = silu(jnp.dot(order, z_v[...], preferred_element_type=F32))

    for copy in copies[1 : 1 + n_parts]:
        copy.wait()
    projected = parts_v[0].astype(F32)
    for p in range(1, n_parts):
        projected = projected + parts_v[p].astype(F32)
    dt_low = projected[:rank].astype(BF16)
    late = projected[rank:].T
    for n in range(states):
        b_tab[n] = jnp.broadcast_to(late[:, n : n + 1], (rows, LANES))
        c_tab[n] = jnp.broadcast_to(late[:, states + n : states + n + 1], (rows, LANES))
    for copy in copies[1 + n_parts :]:
        copy.wait()
    dt = softplus(lax.dot_general(dt_low, dtw_v[...], TN, preferred_element_type=F32) + dtb_v[...])
    dt_v[...] = dt
    drive_v[...] = dt * mixed_v[...].astype(F32)
    a_v[...] = jnp.exp(al_v[...]) * (-LOG2E)

    me = lax.axis_index("replica")
    places, slot_ids, lengths = request_places(dims, (h_s, s_s, l_s), me)
    state_id, request = split_index(lax.broadcasted_iota(jnp.int32, (per_dev * states, 1), 0), per_dev)
    starts = [places[r] * block + slot_ids[r] * states for r in range(per_dev)]
    target = pick_rows(starts, request, per_dev) + state_id
    live = pick_rows(lengths, request, per_dev) > 0
    found = [(p * cache_v.shape[1], cache_v[p]) for p in range(n_pieces)]
    start_tm[...] = fetch_rows(target, live, found)

    tiles = 2
    half = states // 2
    width = 2 * tiles * LANES
    n_chunks = channels // width

    def out_copies(c):
        lanes = pl.ds(pl.multiple_of(c * width, width), width)
        return [
            pltpu.make_async_copy(src.at[:, lanes], dst.at[:, lanes], out_sems.at[i, c])
            for i, (src, dst) in enumerate(((out_v, out_hbm), (state_v, state_hbm)))
        ]

    def scan_group(g, carry):
        lanes = [pl.ds(pl.multiple_of((g * tiles + j) * LANES, LANES), LANES) for j in range(tiles)]
        for first in range(0, states, half):
            ids = range(first, first + half)
            rates = [[jnp.broadcast_to(a_v[n : n + 1, lane], (per_dev, LANES)) for n in ids] for lane in lanes]

            def advance(step, state):
                state = list(state)
                for u in range(UNROLL):
                    now = pl.ds(pl.multiple_of((step * UNROLL + u) * per_dev, per_dev), per_dev)
                    dt = [dt_v[now, lane] for lane in lanes]
                    drive = [drive_v[now, lane] for lane in lanes]
                    sums = [None] * tiles
                    for k, n in enumerate(ids):
                        b, c = b_tab[n, now, :], c_tab[n, now, :]
                        for j in range(tiles):
                            i = j * half + k
                            state[i] = jnp.exp2(dt[j] * rates[j][k]) * state[i] + drive[j] * b
                            term = state[i] * c
                            sums[j] = term if sums[j] is None else sums[j] + term
                    for j, lane in enumerate(lanes):
                        y_v[now, lane] = sums[j] if first == 0 else y_v[now, lane] + sums[j]
                return tuple(state)

            state = tuple(start_tm[n * per_dev : (n + 1) * per_dev, lane] for lane in lanes for n in ids)
            state = lax.fori_loop(0, NEW // UNROLL, advance, state)
            for j, lane in enumerate(lanes):
                for k, n in enumerate(ids):
                    final_tm[n * per_dev : (n + 1) * per_dev, lane] = state[j * half + k]
        return carry

    def one_chunk(c, carry):
        lax.fori_loop(c * 2, c * 2 + 2, scan_group, 0)
        lanes = pl.ds(pl.multiple_of(c * width, width), width)
        total = y_v[:, lanes] + skip_v[:, lanes] * mixed_v[:, lanes].astype(F32)
        gated = (total * gate_v[:, lanes]).astype(BF16)
        back = one_hot_rows(NEW, per_dev)
        back_s = one_hot_rows(states, per_dev)
        out_v[:, lanes] = jnp.dot(back, gated, preferred_element_type=F32).astype(BF16)
        final = jnp.dot(back_s, final_tm[:, lanes].astype(BF16), preferred_element_type=F32)
        state_v[:, lanes] = final.astype(BF16)
        for copy in out_copies(c):
            copy.start()
        return carry

    lax.fori_loop(0, n_chunks, one_chunk, 0)

    def last_wait(c, carry):
        for copy in out_copies(c):
            copy.wait()
        return carry

    lax.fori_loop(0, n_chunks, last_wait, 0)


def split_refs(kernel, dims, n_in, n_out):
    def body(*refs):
        kernel(dims, refs[:n_in], refs[n_in : n_in + n_out], refs[n_in + n_out :])

    return body


def call(kernel, dims, name, limit, ins, outs, scratch):
    hbm = pl.BlockSpec(memory_space=pltpu.HBM)
    anywhere = pl.BlockSpec(memory_space=pl.ANY)
    return pl.pallas_call(
        split_refs(kernel, dims, len(ins), len(outs)),
        in_specs=[hbm if fixed else anywhere for _, fixed in ins],
        out_specs=[anywhere] * len(outs),
        out_shape=[jax.ShapeDtypeStruct(*out) for out in outs],
        scratch_shapes=scratch,
        compiler_params=pltpu.CompilerParams(vmem_limit_bytes=limit * MIB),
        name=name,
    )(*[value for value, _ in ins])


def swap(value, axis, size, mask):
    return lax.ppermute(value, axis, [(i, i ^ mask) for i in range(size)])


def shards(mesh, x_new, z_new, conv_weight, conv_bias, x_proj_weight, dt_proj_weight, dt_bias, a_log, d_skip,
           cache_ssm, cache_conv, holder, slot_id, prefix_len):
    n_replica, n_tensor = mesh.shape["replica"], mesh.shape["tensor"]
    rows, channels = x_new.shape
    per_dev = rows // NEW
    states = a_log.shape[0]
    rank = dt_proj_weight.shape[0]
    taps = conv_weight.shape[0]
    slots = cache_ssm.shape[0]
    out_cols = x_proj_weight.shape[1]
    requests = holder.shape[0]

    conv_rows = jnp.pad(cache_conv, ((0, 0), (0, 1), (0, 0))).reshape(slots * taps, channels)
    rows_all = jnp.concatenate([cache_ssm.reshape(slots * states, channels), conv_rows])
    block = rows_all.shape[0]
    relative = n_replica == 4
    if relative:
        far = swap(rows_all, "replica", n_replica, 3)
        near = swap(rows_all, "replica", n_replica, 1)
        conv_two = swap(conv_rows, "replica", n_replica, 2)
        conv_pieces = [rows_all, near, far, conv_two]
        firsts = (0, block, 2 * block, 4 * block - slots * taps)
        ssm_pieces = [rows_all, near, far, swap(far, "replica", n_replica, 1)]
    else:
        ssm_pieces = [lax.all_gather(rows_all, "replica", axis=0, tiled=True)]
        conv_pieces, firsts = ssm_pieces, (0,)

    vmem, dma = pltpu.VMEM, pltpu.SemaphoreType.DMA
    ints = [pltpu.SMEM((requests,), jnp.int32)] * 3
    n_chunks = channels // min(512, channels)
    dims = (per_dev, n_replica, slots, relative)

    mixed, part = call(
        project_kernel, (dims, block, firsts), "conv_project", 60,
        [(holder, True), (slot_id, True), (prefix_len, True), (x_new, True), (x_proj_weight.T, True),
         (conv_weight, True), (conv_bias[None, :], True)]
        + [(piece, False) for piece in conv_pieces],
        [((rows, channels), BF16), ((out_cols, rows), BF16)],
        ints + [
            vmem((rows, channels), BF16),
            vmem((out_cols, channels), BF16),
            vmem((taps, channels), BF16),
            vmem((1, channels), F32),
            vmem((rows + (taps - 1) * per_dev, channels), F32),
            vmem((rows, channels), BF16),
            vmem((out_cols, rows), F32),
            vmem((out_cols, rows), BF16),
            dma((5 + len(conv_pieces) + 2 * n_chunks,)),
            dma((n_chunks + 1,)),
        ] + [vmem(piece.shape, BF16) for piece in conv_pieces],
    )
    parts = [swap(part, "tensor", n_tensor, k) for k in reversed(range(1, n_tensor))] + [part]

    blocks = (len(ssm_pieces),) + ssm_pieces[0].shape
    out, state = call(
        scan_kernel, (dims, block), "dt_scan_gate", 60,
        [(holder, True), (slot_id, True), (prefix_len, True), (mixed, False), (z_new, True), (dt_proj_weight, True),
         (dt_bias[None, :], True), (a_log, True), (d_skip[None, :], True)]
        + [(piece, False) for piece in parts + ssm_pieces],
        [((rows, channels), BF16), ((per_dev * states, channels), BF16)],
        ints + [
            vmem((rows, channels), BF16),
            vmem((rows, channels), BF16),
            vmem((rank, channels), BF16),
            vmem((1, channels), F32),
            vmem((states, channels), F32),
            vmem((1, channels), F32),
            vmem((n_tensor, out_cols, rows), BF16),
            vmem(blocks, BF16),
            vmem((states, rows, LANES), F32),
            vmem((states, rows, LANES), F32),
            vmem((rows, channels), F32),
            vmem((rows, channels), F32),
            vmem((rows, channels), F32),
            vmem((states, channels), F32),
            vmem((per_dev * states, channels), F32),
            vmem((per_dev * states, channels), F32),
            vmem((rows, channels), F32),
            vmem((rows, channels), BF16),
            vmem((per_dev * states, channels), BF16),
            dma((9 + n_tensor + len(ssm_pieces),)),
            dma((2, n_chunks)),
        ],
    )
    return out, state.reshape(per_dev, states, channels)


def solution(mesh):
    placed = (
        P(("groups", "replica"), "tensor"),
        P(("groups", "replica"), "tensor"),
        P(None, "tensor"),
        P("tensor"),
        P("tensor", None),
        P(None, "tensor"),
        P("tensor"),
        P(None, "tensor"),
        P("tensor"),
        P(("groups", "replica"), None, "tensor"),
        P(("groups", "replica"), None, "tensor"),
        P("groups"),
        P("groups"),
        P("groups"),
    )
    return jax.shard_map(
        functools.partial(shards, mesh),
        mesh=mesh,
        in_specs=placed,
        out_specs=(P(("groups", "replica"), "tensor"), P(("groups", "replica"), None, "tensor")),
        check_vma=False,
    )
```

time: 62.1 us -> 48.4 us (0.78)
  Pallas kernels: 32.3 us -> 21.4 us
  local copies, waits for them, and re-layouts: 5.44 us -> 2.15 us
  starting transfers between devices: 12.2 us -> 10.7 us
  waiting for transfers between devices: 11 us -> 12.4 us
  other arithmetic: 0 us -> 0.92 us
    pallas_call x2, Pallas kernels: 32.3 us -> 21.4 us  [call(): pl.pallas_call(split_refs(kernel, dims, len(ins), len(outs)), in_specs=[h...]
    unnamed x39 -> x17, local copies, waits for them, and re-layouts: 5.41 us -> 2.11 us
    ppermute x9 -> x7, starting transfers between devices: 12.2 us -> 10.7 us  [swap(): return lax.ppermute(value, axis, [(i, i ^ mask) for i in range(size)])]
    ppermute x9 -> x7, waiting for transfers between devices: 11 us -> 12.4 us  [swap(): return lax.ppermute(value, axis, [(i, i ^ mask) for i in range(size)])]
    concatenate x0 -> x1, other arithmetic: none -> 0.92 us  [shards(): jnp.concatenate([cache_ssm.reshape(slots * states, channels), conv_rows])]
  transfers between devices with their start and end apart: 9 -> 7, of which waited for: 4 -> 4; matrix products, arithmetic and copies ran while one was open for 1% -> 0% of each run, Pallas kernels for 0% -> 10%
where the time goes in v4:
time: 48.4 us; the launch traced here: 48.2 us
  Pallas kernels  21.4 us (44%)
  waiting for transfers between devices  12.4 us (26%)
  starting transfers between devices  10.7 us (22%)
  local copies, waits for them, and re-layouts  2.15 us (4%)
  other arithmetic  0.92 us (2%)
  between operations  0.71 us (1%)
    pallas_call x2, Pallas kernels, call(): pl.pallas_call(split_refs(kernel, dims, len(ins), len(outs)), in_specs=[h...  21.4 us
    ppermute x7, waiting for transfers between devices, swap(): return lax.ppermute(value, axis, [(i, i ^ mask) for i in range(size)])  12.4 us
    ppermute x7, starting transfers between devices, swap(): return lax.ppermute(value, axis, [(i, i ^ mask) for i in range(size)])  10.7 us
    unnamed x17, local copies, waits for them, and re-layouts  2.11 us
  transfers between devices with their start and end apart: 7, of which 4 were waited for; matrix products, arithmetic and copies ran while one was open for 0% of the time, Pallas kernels for 10%

profile of v4, /device:TPU:0, one launch (start us, length us, event | category | flops | bytes accessed | tf_op | source)
XLA Modules:
  0.0 48.2 jit_solution(16165061127810488073)
XLA Ops:
  0.6 0.8 %copy.17 = bf16[2,3,2048]{2,1,0:T(4,128)(2,1)S(1)} copy(bf16[2,3,2048]{2,0,1:T(2,128)(2,1)} %param.24) | data formatting | bytes 49152
  1.4 0.9 %pad_maximum_fusion.refs_7_.refs_13_ = bf16[40,2048]{1,0:T(8,128)(2,1)S(1)} fusion(bf16[8,2048]{1,0:T(8,128)(2,1)S(1)} %reshape.14, bf16[32,2048]{1,0:T(8,128)(2,1)} %bitcast.7), kind=kLoop, calls=%fused_computation | loop fusion | flops 327680 | bytes 327680 | tf_op jit(solution)/shard_map/concatenate | solution.py:295
  2.4 0.0 copy-start
  2.4 5.1 %collective-permute-start.1 = (bf16[40,2048]{1,0:T(8,128)(2,1)S(1)}, bf16[40,2048]{1,0:T(8,128)(2,1)S(1)}, u32[]{:S(2)}, u32[]{:S(2)}) collective-permute-start(bf16[40,2048]{1,0:T(8,128)(2,1)S(1)} %pad_maximum_fusion.refs_7_.refs_13_), channel_id=1, source_target_pairs={{0,12},{4,8},{8,4},{12,0},{1,13},{5,9},{9,5},{13,1},{2,14},{6,10},... | collective-permute-start | bytes 491528 | tf_op jit(solution)/shard_map/ppermute | solution.py:279
  7.5 0.0 collective-permute-start
  7.5 0.6 %collective-permute-start.2 = (bf16[8,2048]{1,0:T(8,128)(2,1)S(1)}, bf16[8,2048]{1,0:T(8,128)(2,1)S(1)}, u32[]{:S(2)}, u32[]{:S(2)}) collective-permute-start(bf16[8,2048]{1,0:T(8,128)(2,1)S(1)} %reshape.14), channel_id=1, source_target_pairs={{0,8},{4,12},{8,0},{12,4},{1,9},{5,13},{9,1},{13,5},{2,10},{6,14},... | collective-permute-start | bytes 98312 | tf_op jit(solution)/shard_map/ppermute | solution.py:279
  8.1 4.4 %collective-permute-done.1.refs_9_.refs_15_ = bf16[40,2048]{1,0:T(8,128)(2,1)S(1)} collective-permute-done((bf16[40,2048]{1,0:T(8,128)(2,1)S(1)}, bf16[40,2048]{1,0:T(8,128)(2,1)S(1)}, u32[]{:S(2)}, u32[]{:S(2)}) %collective-permute-start.1) | collective-permute-done | bytes 163872 | tf_op jit(solution)/shard_map/ppermute | solution.py:279
  12.6 3.0 %collective-permute-start.6 = (bf16[40,2048]{1,0:T(8,128)(2,1)S(1)}, bf16[40,2048]{1,0:T(8,128)(2,1)S(1)}, u32[]{:S(2)}, u32[]{:S(2)}) collective-permute-start(bf16[40,2048]{1,0:T(8,128)(2,1)S(1)} %collective-permute-done.1.refs_9_.refs_15_), channel_id=1, source_target_pairs={{0,4},{4,0},{8,12},{12,8},{1,5},{5,1},{9,13},{13,9},{2,6},{6,2},{1... | collective-permute-start | bytes 491528 | tf_op jit(solution)/shard_map/ppermute | solution.py:279
  15.5 0.6 %collective-permute-done.2.refs_10_ = bf16[8,2048]{1,0:T(8,128)(2,1)S(1)} collective-permute-done((bf16[8,2048]{1,0:T(8,128)(2,1)S(1)}, bf16[8,2048]{1,0:T(8,128)(2,1)S(1)}, u32[]{:S(2)}, u32[]{:S(2)}) %collective-permute-start.2) | collective-permute-done | bytes 32800 | tf_op jit(solution)/shard_map/ppermute | solution.py:279
  16.2 0.0 collective-permute-done.refs_8_.refs_14_
  16.2 0.0 copy-done
  16.2 0.6 %copy-done.7 = bf16[8,2048]{1,0:T(8,128)(2,1)} copy-done((bf16[8,2048]{1,0:T(8,128)(2,1)}, bf16[8,2048]{1,0:T(8,128)(2,1)S(1)}, u32[]{:S(2)}) %copy-start.7) | copy-done | bytes 32792
  16.8 0.1 copy-done.2
  16.8 4.9 %conv_project.1 = (bf16[256,2048]{1,0:T(8,128)(2,1)}, bf16[288,256]{1,0:T(8,128)(2,1)}) custom-call(s32[32]{0:T(128)} %refs_0_.3, s32[32]{0:T(128)} %refs_1_.3, s32[32]{0:T(128)} %refs_2_.3, bf16[256,2048]{1,0:T(8,128)(2,1)} %refs_3_.1, bf16[288,2048]{1,0:T(8,128)(2,1)} %bitcast.6, bf16[4,2048]{1,0:T(4,128)(2,1)} %refs_5_.2, f32[1,2048]{1,0:T(1,128)} %bitcast.8, ...), custom_call_target="tpu_custom_call" | custom-call | tf_op jit(solution)/shard_map/conv_project/pallas_call | solution.py:267
  21.7 0.1 collective-permute-start.5
  21.8 1.6 %collective-permute-start.4 = (bf16[288,256]{1,0:T(8,128)(2,1)}, bf16[288,256]{1,0:T(8,128)(2,1)S(1)}, u32[]{:S(2)}, u32[]{:S(2)}) collective-permute-start(bf16[288,256]{1,0:T(8,128)(2,1)} %get-tuple-element.7.refs_12_), channel_id=1, source_target_pairs={{0,2},{1,3},{2,0},{3,1},{4,6},{5,7},{6,4},{7,5},{8,10},{9,11},{10,... | collective-permute-start | bytes 442376 | tf_op jit(solution)/shard_map/ppermute | solution.py:279
  23.3 0.3 collective-permute-start.3
  23.6 0.0 collective-permute-done.5.refs_11_
  23.6 5.1 %collective-permute-done.4.refs_10_ = bf16[288,256]{1,0:T(8,128)(2,1)S(1)} collective-permute-done((bf16[288,256]{1,0:T(8,128)(2,1)}, bf16[288,256]{1,0:T(8,128)(2,1)S(1)}, u32[]{:S(2)}, u32[]{:S(2)}) %collective-permute-start.4) | collective-permute-done | bytes 147488 | tf_op jit(solution)/shard_map/ppermute | solution.py:279
  28.7 2.3 %collective-permute-done.3.refs_9_ = bf16[288,256]{1,0:T(8,128)(2,1)S(1)} collective-permute-done((bf16[288,256]{1,0:T(8,128)(2,1)}, bf16[288,256]{1,0:T(8,128)(2,1)S(1)}, u32[]{:S(2)}, u32[]{:S(2)}) %collective-permute-start.3) | collective-permute-done | bytes 147488 | tf_op jit(solution)/shard_map/ppermute | solution.py:279
  31.0 0.0 collective-permute-done.6.refs_16_
  31.0 0.7 %copy-done.6 = bf16[288,256]{1,0:T(8,128)(2,1)} copy-done((bf16[288,256]{1,0:T(8,128)(2,1)}, bf16[288,256]{1,0:T(8,128)(2,1)S(1)}, u32[]{:S(2)}) %copy-start.6) | copy-done | bytes 147480
  31.6 0.0 copy-done.3
  31.7 16.5 %dt_scan_gate.1 = (bf16[256,2048]{1,0:T(8,128)(2,1)}, bf16[128,2048]{1,0:T(8,128)(2,1)}) custom-call(s32[32]{0:T(128)} %refs_0_.3, s32[32]{0:T(128)} %refs_1_.3, s32[32]{0:T(128)} %refs_2_.3, bf16[256,2048]{1,0:T(8,128)(2,1)} %get-tuple-element.6.refs_3_, bf16[256,2048]{1,0:T(8,128)(2,1)} %refs_4_.1, bf16[256,2048]{1,0:T(8,128)(2,1)} %refs_5_.3, ...), custom_call_target="tpu_custom_call" | custom-call | tf_op jit(solution)/shard_map/dt_scan_gate/pallas_call | solution.py:267
  (12 shorter events, 0.0 us)
Async XLA Ops:
  2.4 13.8 %copy-start = (bf16[40,2048]{1,0:T(8,128)(2,1)}, bf16[40,2048]{1,0:T(8,128)(2,1)S(1)}, u32[]{:S(2)}) copy-start(bf16[40,2048]{1,0:T(8,128)(2,1)S(1)} %pad_maximum_fusion.refs_7_.refs_13_) | copy-start | bytes 491524
  2.4 10.2 %collective-permute-start.1 = (bf16[40,2048]{1,0:T(8,128)(2,1)S(1)}, bf16[40,2048]{1,0:T(8,128)(2,1)S(1)}, u32[]{:S(2)}, u32[]{:S(2)}) collective-permute-start(bf16[40,2048]{1,0:T(8,128)(2,1)S(1)} %pad_maximum_fusion.refs_7_.refs_13_), channel_id=1, source_target_pairs={{0,12},{4,8},{8,4},{12,0},{1,13},{5,9},{9,5},{13,1},{2,14},{6,10},... | collective-permute-start | bytes 491528 | tf_op jit(solution)/shard_map/ppermute | solution.py:279
  7.5 8.7 %collective-permute-start = (bf16[40,2048]{1,0:T(8,128)(2,1)S(1)}, bf16[40,2048]{1,0:T(8,128)(2,1)S(1)}, u32[]{:S(2)}, u32[]{:S(2)}) collective-permute-start(bf16[40,2048]{1,0:T(8,128)(2,1)S(1)} %pad_maximum_fusion.refs_7_.refs_13_), channel_id=1, source_target_pairs={{0,4},{4,0},{8,12},{12,8},{1,5},{5,1},{9,13},{13,9},{2,6},{6,2},{1... | collective-permute-start | bytes 491528 | tf_op jit(solution)/shard_map/ppermute | solution.py:279
  7.5 8.7 %collective-permute-start.2 = (bf16[8,2048]{1,0:T(8,128)(2,1)S(1)}, bf16[8,2048]{1,0:T(8,128)(2,1)S(1)}, u32[]{:S(2)}, u32[]{:S(2)}) collective-permute-start(bf16[8,2048]{1,0:T(8,128)(2,1)S(1)} %reshape.14), channel_id=1, source_target_pairs={{0,8},{4,12},{8,0},{12,4},{1,9},{5,13},{9,1},{13,5},{2,10},{6,14},... | collective-permute-start | bytes 98312 | tf_op jit(solution)/shard_map/ppermute | solution.py:279
  12.6 3.6 %copy-start.1 = (bf16[40,2048]{1,0:T(8,128)(2,1)}, bf16[40,2048]{1,0:T(8,128)(2,1)S(1)}, u32[]{:S(2)}) copy-start(bf16[40,2048]{1,0:T(8,128)(2,1)S(1)} %collective-permute-done.1.refs_9_.refs_15_) | copy-start | bytes 491524
  12.6 18.4 %collective-permute-start.6 = (bf16[40,2048]{1,0:T(8,128)(2,1)S(1)}, bf16[40,2048]{1,0:T(8,128)(2,1)S(1)}, u32[]{:S(2)}, u32[]{:S(2)}) collective-permute-start(bf16[40,2048]{1,0:T(8,128)(2,1)S(1)} %collective-permute-done.1.refs_9_.refs_15_), channel_id=1, source_target_pairs={{0,4},{4,0},{8,12},{12,8},{1,5},{5,1},{9,13},{13,9},{2,6},{6,2},{1... | collective-permute-start | bytes 491528 | tf_op jit(solution)/shard_map/ppermute | solution.py:279
  16.2 0.6 %copy-start.7 = (bf16[8,2048]{1,0:T(8,128)(2,1)}, bf16[8,2048]{1,0:T(8,128)(2,1)S(1)}, u32[]{:S(2)}) copy-start(bf16[8,2048]{1,0:T(8,128)(2,1)S(1)} %collective-permute-done.2.refs_10_) | copy-start | bytes 98308
  16.2 0.7 %copy-start.2 = (bf16[40,2048]{1,0:T(8,128)(2,1)}, bf16[40,2048]{1,0:T(8,128)(2,1)S(1)}, u32[]{:S(2)}) copy-start(bf16[40,2048]{1,0:T(8,128)(2,1)S(1)} %collective-permute-done.refs_8_.refs_14_) | copy-start | bytes 491524
  21.7 1.9 %collective-permute-start.5 = (bf16[288,256]{1,0:T(8,128)(2,1)}, bf16[288,256]{1,0:T(8,128)(2,1)S(1)}, u32[]{:S(2)}, u32[]{:S(2)}) collective-permute-start(bf16[288,256]{1,0:T(8,128)(2,1)} %get-tuple-element.7.refs_12_), channel_id=1, source_target_pairs={{0,1},{1,0},{2,3},{3,2},{4,5},{5,4},{6,7},{7,6},{8,9},{9,8},{10,11... | collective-permute-start | bytes 442376 | tf_op jit(solution)/shard_map/ppermute | solution.py:279
  21.8 6.9 %collective-permute-start.4 = (bf16[288,256]{1,0:T(8,128)(2,1)}, bf16[288,256]{1,0:T(8,128)(2,1)S(1)}, u32[]{:S(2)}, u32[]{:S(2)}) collective-permute-start(bf16[288,256]{1,0:T(8,128)(2,1)} %get-tuple-element.7.refs_12_), channel_id=1, source_target_pairs={{0,2},{1,3},{2,0},{3,1},{4,6},{5,7},{6,4},{7,5},{8,10},{9,11},{10,... | collective-permute-start | bytes 442376 | tf_op jit(solution)/shard_map/ppermute | solution.py:279
  23.3 7.6 %collective-permute-start.3 = (bf16[288,256]{1,0:T(8,128)(2,1)}, bf16[288,256]{1,0:T(8,128)(2,1)S(1)}, u32[]{:S(2)}, u32[]{:S(2)}) collective-permute-start(bf16[288,256]{1,0:T(8,128)(2,1)} %get-tuple-element.7.refs_12_), channel_id=1, source_target_pairs={{0,3},{1,2},{2,1},{3,0},{4,7},{5,6},{6,5},{7,4},{8,11},{9,10},{10,... | collective-permute-start | bytes 442376 | tf_op jit(solution)/shard_map/ppermute | solution.py:279
  23.6 7.3 %copy-start.4 = (bf16[288,256]{1,0:T(8,128)(2,1)}, bf16[288,256]{1,0:T(8,128)(2,1)S(1)}, u32[]{:S(2)}) copy-start(bf16[288,256]{1,0:T(8,128)(2,1)S(1)} %collective-permute-done.5.refs_11_) | copy-start | bytes 442372
  28.7 2.3 %copy-start.5 = (bf16[288,256]{1,0:T(8,128)(2,1)}, bf16[288,256]{1,0:T(8,128)(2,1)S(1)}, u32[]{:S(2)}) copy-start(bf16[288,256]{1,0:T(8,128)(2,1)S(1)} %collective-permute-done.4.refs_10_) | copy-start | bytes 442372
  31.0 0.7 %copy-start.6 = (bf16[288,256]{1,0:T(8,128)(2,1)}, bf16[288,256]{1,0:T(8,128)(2,1)S(1)}, u32[]{:S(2)}) copy-start(bf16[288,256]{1,0:T(8,128)(2,1)S(1)} %collective-permute-done.3.refs_9_) | copy-start | bytes 442372
  31.0 0.7 %copy-start.3 = (bf16[40,2048]{1,0:T(8,128)(2,1)}, bf16[40,2048]{1,0:T(8,128)(2,1)S(1)}, u32[]{:S(2)}) copy-start(bf16[40,2048]{1,0:T(8,128)(2,1)S(1)} %collective-permute-done.6.refs_16_) | copy-start | bytes 491524

commit v5 on v4

--- a/solution.py
+++ b/solution.py
@@ -9,7 +9,6 @@
 
 NEW = 32
 LANES = 128
-LOG2E = 1.4426950408889634
 MIB = 1024 * 1024
 UNROLL = 8
 F32, BF16 = jnp.float32, jnp.bfloat16
@@ -74,55 +73,38 @@
 
 
 def project_kernel(dims, refs_in, refs_out, scratch):
-    dims, block, firsts = dims
-    per_dev, n_replica, slots, _ = dims
-    holder, slot_id, prefix_len, x_hbm, wt_hbm, cw_hbm, cb_hbm = refs_in[:7]
-    mixed_hbm, part_hbm = refs_out
-    h_s, s_s, l_s, x_v, wt_v, cw_v, cb_v, joined, mixed_v, part_f, part_v, sems, out_sems = scratch[:13]
-    held = scratch[13:]
-    pieces = refs_in[7:]
+    per_dev = dims
+    x_hbm, wt_hbm, cw_hbm, cb_hbm = refs_in
+    mixed_hbm, head_hbm, part_hbm = refs_out
+    x_v, wt_v, cw_v, cb_v, joined, mixed_v, head_v, part_f, part_v, sems, out_sems = scratch
     rows, channels = x_v.shape
     taps = cw_v.shape[0]
-    copies = []
-    pairs = [(cw_hbm, cw_v), (cb_hbm, cb_v), (holder, h_s), (slot_id, s_s), (prefix_len, l_s)]
-    pairs += list(zip(pieces, held))
-    for src, dst in pairs:
-        copies.append(pltpu.make_async_copy(src, dst, sems.at[len(copies)]))
-    small = len(copies)
+    lines = (taps - 1) * per_dev
+    pairs = [(cw_hbm, cw_v), (cb_hbm, cb_v)]
     width = min(512, channels)
     chunks = [slice(c * width, (c + 1) * width) for c in range(channels // width)]
     for chunk in chunks:
-        copies.append(pltpu.make_async_copy(x_hbm.at[:, chunk], x_v.at[:, chunk], sems.at[len(copies)]))
-        copies.append(pltpu.make_async_copy(wt_hbm.at[:, chunk], wt_v.at[:, chunk], sems.at[len(copies)]))
+        pairs += [(x_hbm.at[:, chunk], x_v.at[:, chunk]), (wt_hbm.at[:, chunk], wt_v.at[:, chunk])]
+    copies = [pltpu.make_async_copy(src, dst, sems.at[i]) for i, (src, dst) in enumerate(pairs)]
     for copy in copies:
         copy.start()
 
     order = one_hot_rows(per_dev, NEW)
-    for copy in copies[:small]:
-        copy.wait()
-
-    me = lax.axis_index("replica")
-    places, slot_ids, lengths = request_places(dims, (h_s, s_s, l_s), me)
-    lines = (taps - 1) * per_dev
-    tap, request = split_index(lax.broadcasted_iota(jnp.int32, (per_dev * taps, 1), 0), per_dev)
-    starts = [places[r] * block + (block - slots * taps) + slot_ids[r] * taps for r in range(per_dev)]
-    target = pick_rows(starts, request, per_dev) + tap
-    live = (tap < taps - 1) & (taps - 1 - tap <= pick_rows(lengths, request, per_dev))
-
+    joined[:lines, :] = jnp.zeros((lines, channels), F32)
+    copies[0].wait()
+    copies[1].wait()
     outs = []
     for c, chunk in enumerate(chunks):
-        copies[small + 2 * c].wait()
-        found = [(first, ref[:, chunk]) for first, ref in zip(firsts, held)]
-        history = fetch_rows(target, live, found)
-        joined[:lines, chunk] = history[:lines]
+        copies[2 + 2 * c].wait()
         joined[lines:, chunk] = jnp.dot(order, x_v[:, chunk], preferred_element_type=F32)
         summed = jnp.broadcast_to(cb_v[:, chunk], (rows, width))
         for k in range(taps):
             weight = cw_v[k : k + 1, chunk].astype(F32)
             summed = summed + joined[k * per_dev : k * per_dev + rows, chunk] * weight
+        head_v[:, chunk] = summed[: head_v.shape[0]]
         mixed = silu(summed).astype(BF16)
         mixed_v[:, chunk] = mixed
-        copies[small + 2 * c + 1].wait()
+        copies[3 + 2 * c].wait()
         part = lax.dot_general(wt_v[:, chunk], mixed, NT, preferred_element_type=F32)
         if c == 0:
             part_f[...] = part
@@ -131,27 +113,74 @@
         outs.append(pltpu.make_async_copy(mixed_v.at[:, chunk], mixed_hbm.at[:, chunk], out_sems.at[c]))
         outs[-1].start()
     part_v[...] = part_f[...].astype(BF16)
-    outs.append(pltpu.make_async_copy(part_v, part_hbm, out_sems.at[len(outs)]))
-    outs[-1].start()
+    for src, dst in ((part_v, part_hbm), (head_v, head_hbm)):
+        outs.append(pltpu.make_async_copy(src, dst, out_sems.at[len(outs)]))
+        outs[-1].start()
     for copy in outs:
         copy.wait()
+
+
+def history_kernel(dims, refs_in, refs_out, scratch):
+    dims, block, firsts = dims
+    per_dev, n_replica, slots, _ = dims
+    holder, slot_id, prefix_len, head_hbm, part_hbm, wt_hbm, cw_hbm = refs_in[:7]
+    pieces = refs_in[7:]
+    mixed_hbm, fixed_hbm = refs_out
+    h_s, s_s, l_s, head_v, part_v, wt_v, cw_v, mixed_v, sems, out_sems = scratch[:10]
+    held = scratch[10:]
+    taps = cw_v.shape[0]
+    pairs = [(holder, h_s), (slot_id, s_s), (prefix_len, l_s), (cw_hbm, cw_v), (head_hbm, head_v)]
+    pairs += list(zip(pieces, held)) + [(wt_hbm, wt_v), (part_hbm, part_v)]
+    copies = [pltpu.make_async_copy(src, dst, sems.at[i]) for i, (src, dst) in enumerate(pairs)]
+    for copy in copies:
+        copy.start()
+    for copy in copies[:-2]:
+        copy.wait()
+
+    me = lax.axis_index("replica")
+    places, slot_ids, lengths = request_places(dims, (h_s, s_s, l_s), me)
+    tap, request = split_index(lax.broadcasted_iota(jnp.int32, (per_dev * taps, 1), 0), per_dev)
+    starts = [places[r] * block + (block - slots * taps) + slot_ids[r] * taps for r in range(per_dev)]
+    target = pick_rows(starts, request, per_dev) + tap
+    live = (tap < taps - 1) & (taps - 1 - tap <= pick_rows(lengths, request, per_dev))
+    history = fetch_rows(target, live, [(first, ref[...]) for first, ref in zip(firsts, held)])
+    for t in range(taps - 1):
+        now = slice(t * per_dev, (t + 1) * per_dev)
+        summed = head_v[now]
+        for k in range(taps - 1 - t):
+            weight = cw_v[k : k + 1].astype(F32)
+            summed = summed + history[(t + k) * per_dev : (t + k + 1) * per_dev] * weight
+        head_v[now] = summed
+    mixed = silu(head_v[...]).astype(BF16)
+    mixed_v[...] = mixed
+    mixed_out = pltpu.make_async_copy(mixed_v, mixed_hbm, out_sems.at[0])
+    mixed_out.start()
+    copies[-2].wait()
+    part = lax.dot_general(wt_v[...], mixed, NT, preferred_element_type=F32).astype(BF16)
+    copies[-1].wait()
+    part_v[:, : per_dev * taps] = part
+    part_out = pltpu.make_async_copy(part_v, fixed_hbm, out_sems.at[1])
+    part_out.start()
+    mixed_out.wait()
+    part_out.wait()
 
 
 def scan_kernel(dims, refs_in, refs_out, scratch):
     dims, block = dims
     per_dev, n_replica, slots, _ = dims
-    holder, slot_id, prefix_len, mixed_hbm, z_hbm, dtw_hbm, dtb_hbm, al_hbm, skip_hbm = refs_in[:9]
+    holder, slot_id, prefix_len, mixed_hbm, head_hbm, z_hbm, dtw_hbm, dtb_hbm, al_hbm, skip_hbm = refs_in[:10]
     out_hbm, state_hbm = refs_out
     (h_s, s_s, l_s, mixed_v, z_v, dtw_v, dtb_v, al_v, skip_v, parts_v, cache_v, b_tab, c_tab, dt_v, drive_v, gate_v,
      a_v, start_tm, final_tm, y_v, out_v, state_v, sems, out_sems) = scratch
     n_parts, n_pieces = parts_v.shape[0], cache_v.shape[0]
-    parts, pieces = refs_in[9 : 9 + n_parts], refs_in[9 + n_parts :]
+    parts, pieces = refs_in[10 : 10 + n_parts], refs_in[10 + n_parts :]
+    head = head_hbm.shape[0]
     rows, channels = z_v.shape
     states = al_v.shape[0]
     rank = dtw_v.shape[0]
     pairs = [(z_hbm, z_v)] + [(part, parts_v.at[p]) for p, part in enumerate(parts)]
     pairs += [(dtw_hbm, dtw_v), (dtb_hbm, dtb_v), (al_hbm, al_v), (holder, h_s), (slot_id, s_s), (prefix_len, l_s),
-              (skip_hbm, skip_v), (mixed_hbm, mixed_v)]
+              (skip_hbm, skip_v), (head_hbm, mixed_v.at[:head]), (mixed_hbm.at[head:], mixed_v.at[head:])]
     pairs += [(piece, cache_v.at[p]) for p, piece in enumerate(pieces)]
     copies = [pltpu.make_async_copy(src, dst, sems.at[i]) for i, (src, dst) in enumerate(pairs)]
     for copy in copies:
@@ -176,7 +205,7 @@
     dt = softplus(lax.dot_general(dt_low, dtw_v[...], TN, preferred_element_type=F32) + dtb_v[...])
     dt_v[...] = dt
     drive_v[...] = dt * mixed_v[...].astype(F32)
-    a_v[...] = jnp.exp(al_v[...]) * (-LOG2E)
+    a_v[...] = -jnp.exp(al_v[...])
 
     me = lax.axis_index("replica")
     places, slot_ids, lengths = request_places(dims, (h_s, s_s, l_s), me)
@@ -216,7 +245,7 @@
                         b, c = b_tab[n, now, :], c_tab[n, now, :]
                         for j in range(tiles):
                             i = j * half + k
-                            state[i] = jnp.exp2(dt[j] * rates[j][k]) * state[i] + drive[j] * b
+                            state[i] = jnp.exp(dt[j] * rates[j][k]) * state[i] + drive[j] * b
                             term = state[i] * c
                             sums[j] = term if sums[j] is None else sums[j] + term
                     for j, lane in enumerate(lanes):
@@ -311,31 +340,52 @@
     n_chunks = channels // min(512, channels)
     dims = (per_dev, n_replica, slots, relative)
 
-    mixed, part = call(
-        project_kernel, (dims, block, firsts), "conv_project", 60,
-        [(holder, True), (slot_id, True), (prefix_len, True), (x_new, True), (x_proj_weight.T, True),
-         (conv_weight, True), (conv_bias[None, :], True)]
-        + [(piece, False) for piece in conv_pieces],
-        [((rows, channels), BF16), ((out_cols, rows), BF16)],
-        ints + [
+    head = per_dev * taps
+    weights = x_proj_weight.T
+    mixed, head_sums, part = call(
+        project_kernel, per_dev, "conv_project", 60,
+        [(x_new, True), (weights, True), (conv_weight, True), (conv_bias[None, :], True)],
+        [((rows, channels), BF16), ((head, channels), F32), ((out_cols, rows), BF16)],
+        [
             vmem((rows, channels), BF16),
             vmem((out_cols, channels), BF16),
             vmem((taps, channels), BF16),
             vmem((1, channels), F32),
             vmem((rows + (taps - 1) * per_dev, channels), F32),
             vmem((rows, channels), BF16),
+            vmem((head, channels), F32),
             vmem((out_cols, rows), F32),
             vmem((out_cols, rows), BF16),
-            dma((5 + len(conv_pieces) + 2 * n_chunks,)),
-            dma((n_chunks + 1,)),
+            dma((2 + 2 * n_chunks,)),
+            dma((n_chunks + 2,)),
+        ],
+    )
+    mixed_head, part = call(
+        history_kernel, (dims, block, firsts), "history", 60,
+        [(holder, True), (slot_id, True), (prefix_len, True), (head_sums, False), (part, False), (weights, True),
+         (conv_weight, True)]
+        + [(piece, False) for piece in conv_pieces],
+        [((head, channels), BF16), ((out_cols, rows), BF16)],
+        ints + [
+            vmem((head, channels), F32),
+            vmem((out_cols, rows), BF16),
+            vmem((out_cols, channels), BF16),
+            vmem((taps, channels), BF16),
+            vmem((head, channels), BF16),
+            dma((7 + len(conv_pieces),)),
+            dma((2,)),
         ] + [vmem(piece.shape, BF16) for piece in conv_pieces],
     )
-    parts = [swap(part, "tensor", n_tensor, k) for k in reversed(range(1, n_tensor))] + [part]
+    parts = [part]
+    mask = n_tensor // 2
+    while mask:
+        parts = parts + [swap(value, "tensor", n_tensor, mask) for value in reversed(parts)]
+        mask //= 2
 
     blocks = (len(ssm_pieces),) + ssm_pieces[0].shape
     out, state = call(
         scan_kernel, (dims, block), "dt_scan_gate", 60,
-        [(holder, True), (slot_id, True), (prefix_len, True), (mixed, False), (z_new, True), (dt_proj_weight, True),
+        [(holder, True), (slot_id, True), (prefix_len, True), (mixed, False), (mixed_head, False), (z_new, True), (dt_proj_weight, True),
          (dt_bias[None, :], True), (a_log, True), (d_skip[None, :], True)]
         + [(piece, False) for piece in parts + ssm_pieces],
         [((rows, channels), BF16), ((per_dev * states, channels), BF16)],
@@ -359,7 +409,7 @@
             vmem((rows, channels), F32),
             vmem((rows, channels), BF16),
             vmem((per_dev * states, channels), BF16),
-            dma((9 + n_tensor + len(ssm_pieces),)),
+            dma((10 + n_tensor + len(ssm_pieces),)),
             dma((2, n_chunks)),
         ],
     )

time: 48.4 us -> 45.4 us (0.938)
  waiting for transfers between devices: 12.4 us -> 8.04 us
  Pallas kernels: 21.4 us -> 24.7 us
  starting transfers between devices: 10.7 us -> 8.65 us
    ppermute x7, waiting for transfers between devices: 12.4 us -> 8.04 us  [swap(): return lax.ppermute(value, axis, [(i, i ^ mask) for i in range(size)])]
    pallas_call x2 -> x3, Pallas kernels: 21.4 us -> 24.7 us  [call(): pl.pallas_call(split_refs(kernel, dims, len(ins), len(outs)), in_specs=[h...]
    ppermute x7, starting transfers between devices: 10.7 us -> 8.65 us  [swap(): return lax.ppermute(value, axis, [(i, i ^ mask) for i in range(size)])]
where the time goes in v5:
time: 45.4 us; the launch traced here: 45.2 us
  Pallas kernels  24.7 us (54%)
  starting transfers between devices  8.65 us (19%)
  waiting for transfers between devices  8.04 us (18%)
  local copies, waits for them, and re-layouts  2.14 us (5%)
  other arithmetic  0.92 us (2%)
  between operations  0.71 us (2%)
    pallas_call x3, Pallas kernels, call(): pl.pallas_call(split_refs(kernel, dims, len(ins), len(outs)), in_specs=[h...  24.7 us
    ppermute x7, starting transfers between devices, swap(): return lax.ppermute(value, axis, [(i, i ^ mask) for i in range(size)])  8.65 us
    ppermute x7, waiting for transfers between devices, swap(): return lax.ppermute(value, axis, [(i, i ^ mask) for i in range(size)])  8.04 us
    unnamed x17, local copies, waits for them, and re-layouts  2.1 us
    concatenate x1, other arithmetic, shards(): jnp.concatenate([cache_ssm.reshape(slots * states, channels), conv_rows])  0.92 us
  transfers between devices with their start and end apart: 7, of which 4 were waited for; matrix products, arithmetic and copies ran while one was open for 0% of the time, Pallas kernels for 10%

profile of v5, /device:TPU:0, one launch (start us, length us, event | category | flops | bytes accessed | tf_op | source)
XLA Modules:
  0.0 45.2 jit_solution(15616346630664671718)
XLA Ops:
  0.6 0.8 %copy.17 = bf16[2,3,2048]{2,1,0:T(4,128)(2,1)S(1)} copy(bf16[2,3,2048]{2,0,1:T(2,128)(2,1)} %param.24) | data formatting | bytes 49152
  1.4 0.9 %pad_maximum_fusion.refs_7_.refs_14_ = bf16[40,2048]{1,0:T(8,128)(2,1)S(1)} fusion(bf16[8,2048]{1,0:T(8,128)(2,1)S(1)} %reshape.14, bf16[32,2048]{1,0:T(8,128)(2,1)} %bitcast.8), kind=kLoop, calls=%fused_computation | loop fusion | flops 327680 | bytes 327680 | tf_op jit(solution)/shard_map/concatenate | solution.py:324
  2.4 5.1 %collective-permute-start.1 = (bf16[40,2048]{1,0:T(8,128)(2,1)S(1)}, bf16[40,2048]{1,0:T(8,128)(2,1)S(1)}, u32[]{:S(2)}, u32[]{:S(2)}) collective-permute-start(bf16[40,2048]{1,0:T(8,128)(2,1)S(1)} %pad_maximum_fusion.refs_7_.refs_14_), channel_id=1, source_target_pairs={{0,12},{4,8},{8,4},{12,0},{1,13},{5,9},{9,5},{13,1},{2,14},{6,10},... | collective-permute-start | bytes 491528 | tf_op jit(solution)/shard_map/ppermute | solution.py:308
  7.5 0.0 collective-permute-start
  7.5 0.6 %collective-permute-start.2 = (bf16[8,2048]{1,0:T(8,128)(2,1)S(1)}, bf16[8,2048]{1,0:T(8,128)(2,1)S(1)}, u32[]{:S(2)}, u32[]{:S(2)}) collective-permute-start(bf16[8,2048]{1,0:T(8,128)(2,1)S(1)} %reshape.14), channel_id=1, source_target_pairs={{0,8},{4,12},{8,0},{12,4},{1,9},{5,13},{9,1},{13,5},{2,10},{6,14},... | collective-permute-start | bytes 98312 | tf_op jit(solution)/shard_map/ppermute | solution.py:308
  8.1 4.5 %conv_project.1 = (bf16[256,2048]{1,0:T(8,128)(2,1)}, f32[32,2048]{1,0:T(8,128)}, bf16[288,256]{1,0:T(8,128)(2,1)}) custom-call(bf16[256,2048]{1,0:T(8,128)(2,1)} %refs_0_.3, bf16[288,2048]{1,0:T(8,128)(2,1)} %bitcast.6, bf16[4,2048]{1,0:T(4,128)(2,1)} %refs_6_.2, f32[1,2048]{1,0:T(1,128)} %bitcast.9), custom_call_target="tpu_custom_call" | custom-call | tf_op jit(solution)/shard_map/conv_project/pallas_call | solution.py:296
  12.6 2.9 %collective-permute-done.2.refs_10_ = bf16[8,2048]{1,0:T(8,128)(2,1)S(1)} collective-permute-done((bf16[8,2048]{1,0:T(8,128)(2,1)S(1)}, bf16[8,2048]{1,0:T(8,128)(2,1)S(1)}, u32[]{:S(2)}, u32[]{:S(2)}) %collective-permute-start.2) | collective-permute-done | bytes 32800 | tf_op jit(solution)/shard_map/ppermute | solution.py:308
  15.5 0.0 collective-permute-done.1.refs_9_.refs_16_
  15.5 0.5 %collective-permute-done.refs_8_.refs_15_ = bf16[40,2048]{1,0:T(8,128)(2,1)S(1)} collective-permute-done((bf16[40,2048]{1,0:T(8,128)(2,1)S(1)}, bf16[40,2048]{1,0:T(8,128)(2,1)S(1)}, u32[]{:S(2)}, u32[]{:S(2)}) %collective-permute-start) | collective-permute-done | bytes 163872 | tf_op jit(solution)/shard_map/ppermute | solution.py:308
  16.0 0.1 copy-done.7
  16.1 0.1 copy-done.1
  16.2 0.5 %copy-done.2 = bf16[40,2048]{1,0:T(8,128)(2,1)} copy-done((bf16[40,2048]{1,0:T(8,128)(2,1)}, bf16[40,2048]{1,0:T(8,128)(2,1)S(1)}, u32[]{:S(2)}) %copy-start.2) | copy-done | bytes 163864
  16.6 2.8 %history.1 = (bf16[32,2048]{1,0:T(8,128)(2,1)}, bf16[288,256]{1,0:T(8,128)(2,1)}) custom-call(s32[32]{0:T(128)} %refs_0_.5, s32[32]{0:T(128)} %refs_1_.3, s32[32]{0:T(128)} %refs_2_.5, f32[32,2048]{1,0:T(8,128)} %get-tuple-element.10.refs_3_, bf16[288,256]{1,0:T(8,128)(2,1)} %get-tuple-element.11.refs_4_, bf16[288,2048]{1,0:T(8,128)(2,1)} %bitcast.7, ...), custom_call_target="tpu_custom_call" | custom-call | tf_op jit(solution)/shard_map/history/pallas_call | solution.py:296
  19.5 1.6 %collective-permute-start.3 = (bf16[288,256]{1,0:T(8,128)(2,1)}, bf16[288,256]{1,0:T(8,128)(2,1)S(1)}, u32[]{:S(2)}, u32[]{:S(2)}) collective-permute-start(bf16[288,256]{1,0:T(8,128)(2,1)} %get-tuple-element.13.refs_10_), channel_id=1, source_target_pairs={{0,2},{1,3},{2,0},{3,1},{4,6},{5,7},{6,4},{7,5},{8,10},{9,11},{10,... | collective-permute-start | bytes 442376 | tf_op jit(solution)/shard_map/ppermute | solution.py:308
  21.0 1.3 %collective-permute-start.6 = (bf16[40,2048]{1,0:T(8,128)(2,1)}, bf16[40,2048]{1,0:T(8,128)(2,1)S(1)}, u32[]{:S(2)}, u32[]{:S(2)}) collective-permute-start(bf16[40,2048]{1,0:T(8,128)(2,1)} %copy-done.1), channel_id=1, source_target_pairs={{0,4},{4,0},{8,12},{12,8},{1,5},{5,1},{9,13},{13,9},{2,6},{6,2},{1... | collective-permute-start | bytes 491528 | tf_op jit(solution)/shard_map/ppermute | solution.py:308
  22.3 0.0 collective-permute-start.5
  22.4 3.1 %collective-permute-done.3.refs_11_ = bf16[288,256]{1,0:T(8,128)(2,1)S(1)} collective-permute-done((bf16[288,256]{1,0:T(8,128)(2,1)}, bf16[288,256]{1,0:T(8,128)(2,1)S(1)}, u32[]{:S(2)}, u32[]{:S(2)}) %collective-permute-start.3) | collective-permute-done | bytes 147488 | tf_op jit(solution)/shard_map/ppermute | solution.py:308
  25.5 0.0 collective-permute-start.4
  25.5 0.0 collective-permute-done.5.refs_13_
  25.5 1.5 %collective-permute-done.6.refs_17_ = bf16[40,2048]{1,0:T(8,128)(2,1)S(1)} collective-permute-done((bf16[40,2048]{1,0:T(8,128)(2,1)}, bf16[40,2048]{1,0:T(8,128)(2,1)S(1)}, u32[]{:S(2)}, u32[]{:S(2)}) %collective-permute-start.6) | collective-permute-done | bytes 163872 | tf_op jit(solution)/shard_map/ppermute | solution.py:308
  27.0 0.0 collective-permute-done.4.refs_12_
  27.1 0.6 %copy-done.3 = bf16[40,2048]{1,0:T(8,128)(2,1)} copy-done((bf16[40,2048]{1,0:T(8,128)(2,1)}, bf16[40,2048]{1,0:T(8,128)(2,1)S(1)}, u32[]{:S(2)}) %copy-start.3) | copy-done | bytes 163864
  27.7 0.1 copy-done.6
  27.8 17.4 %dt_scan_gate.1 = (bf16[256,2048]{1,0:T(8,128)(2,1)}, bf16[128,2048]{1,0:T(8,128)(2,1)}) custom-call(s32[32]{0:T(128)} %refs_0_.5, s32[32]{0:T(128)} %refs_1_.3, s32[32]{0:T(128)} %refs_2_.5, bf16[256,2048]{1,0:T(8,128)(2,1)} %get-tuple-element.9.refs_3_, bf16[32,2048]{1,0:T(8,128)(2,1)} %get-tuple-element.12.refs_4_, bf16[256,2048]{1,0:T(8,128)(2,1)} %refs_5_.1, ...), custom_call_target="tpu_custom_call" | custom-call | tf_op jit(solution)/shard_map/dt_scan_gate/pallas_call | solution.py:296
  (13 shorter events, 0.1 us)
Async XLA Ops:
  2.4 13.6 %copy-start = (bf16[40,2048]{1,0:T(8,128)(2,1)}, bf16[40,2048]{1,0:T(8,128)(2,1)S(1)}, u32[]{:S(2)}) copy-start(bf16[40,2048]{1,0:T(8,128)(2,1)S(1)} %pad_maximum_fusion.refs_7_.refs_14_) | copy-start | bytes 491524
  2.4 13.1 %collective-permute-start.1 = (bf16[40,2048]{1,0:T(8,128)(2,1)S(1)}, bf16[40,2048]{1,0:T(8,128)(2,1)S(1)}, u32[]{:S(2)}, u32[]{:S(2)}) collective-permute-start(bf16[40,2048]{1,0:T(8,128)(2,1)S(1)} %pad_maximum_fusion.refs_7_.refs_14_), channel_id=1, source_target_pairs={{0,12},{4,8},{8,4},{12,0},{1,13},{5,9},{9,5},{13,1},{2,14},{6,10},... | collective-permute-start | bytes 491528 | tf_op jit(solution)/shard_map/ppermute | solution.py:308
  7.5 8.5 %collective-permute-start = (bf16[40,2048]{1,0:T(8,128)(2,1)S(1)}, bf16[40,2048]{1,0:T(8,128)(2,1)S(1)}, u32[]{:S(2)}, u32[]{:S(2)}) collective-permute-start(bf16[40,2048]{1,0:T(8,128)(2,1)S(1)} %pad_maximum_fusion.refs_7_.refs_14_), channel_id=1, source_target_pairs={{0,4},{4,0},{8,12},{12,8},{1,5},{5,1},{9,13},{13,9},{2,6},{6,2},{1... | collective-permute-start | bytes 491528 | tf_op jit(solution)/shard_map/ppermute | solution.py:308
  7.5 8.0 %collective-permute-start.2 = (bf16[8,2048]{1,0:T(8,128)(2,1)S(1)}, bf16[8,2048]{1,0:T(8,128)(2,1)S(1)}, u32[]{:S(2)}, u32[]{:S(2)}) collective-permute-start(bf16[8,2048]{1,0:T(8,128)(2,1)S(1)} %reshape.14), channel_id=1, source_target_pairs={{0,8},{4,12},{8,0},{12,4},{1,9},{5,13},{9,1},{13,5},{2,10},{6,14},... | collective-permute-start | bytes 98312 | tf_op jit(solution)/shard_map/ppermute | solution.py:308
  15.5 0.6 %copy-start.7 = (bf16[8,2048]{1,0:T(8,128)(2,1)}, bf16[8,2048]{1,0:T(8,128)(2,1)S(1)}, u32[]{:S(2)}) copy-start(bf16[8,2048]{1,0:T(8,128)(2,1)S(1)} %collective-permute-done.2.refs_10_) | copy-start | bytes 98308
  15.5 0.7 %copy-start.1 = (bf16[40,2048]{1,0:T(8,128)(2,1)}, bf16[40,2048]{1,0:T(8,128)(2,1)S(1)}, u32[]{:S(2)}) copy-start(bf16[40,2048]{1,0:T(8,128)(2,1)S(1)} %collective-permute-done.1.refs_9_.refs_16_) | copy-start | bytes 491524
  16.0 0.6 %copy-start.2 = (bf16[40,2048]{1,0:T(8,128)(2,1)}, bf16[40,2048]{1,0:T(8,128)(2,1)S(1)}, u32[]{:S(2)}) copy-start(bf16[40,2048]{1,0:T(8,128)(2,1)S(1)} %collective-permute-done.refs_8_.refs_15_) | copy-start | bytes 491524
  19.5 6.0 %collective-permute-start.3 = (bf16[288,256]{1,0:T(8,128)(2,1)}, bf16[288,256]{1,0:T(8,128)(2,1)S(1)}, u32[]{:S(2)}, u32[]{:S(2)}) collective-permute-start(bf16[288,256]{1,0:T(8,128)(2,1)} %get-tuple-element.13.refs_10_), channel_id=1, source_target_pairs={{0,2},{1,3},{2,0},{3,1},{4,6},{5,7},{6,4},{7,5},{8,10},{9,11},{10,... | collective-permute-start | bytes 442376 | tf_op jit(solution)/shard_map/ppermute | solution.py:308
  21.0 6.0 %collective-permute-start.6 = (bf16[40,2048]{1,0:T(8,128)(2,1)}, bf16[40,2048]{1,0:T(8,128)(2,1)S(1)}, u32[]{:S(2)}, u32[]{:S(2)}) collective-permute-start(bf16[40,2048]{1,0:T(8,128)(2,1)} %copy-done.1), channel_id=1, source_target_pairs={{0,4},{4,0},{8,12},{12,8},{1,5},{5,1},{9,13},{13,9},{2,6},{6,2},{1... | collective-permute-start | bytes 491528 | tf_op jit(solution)/shard_map/ppermute | solution.py:308
  22.3 3.2 %collective-permute-start.5 = (bf16[288,256]{1,0:T(8,128)(2,1)}, bf16[288,256]{1,0:T(8,128)(2,1)S(1)}, u32[]{:S(2)}, u32[]{:S(2)}) collective-permute-start(bf16[288,256]{1,0:T(8,128)(2,1)} %get-tuple-element.13.refs_10_), channel_id=1, source_target_pairs={{0,1},{1,0},{2,3},{3,2},{4,5},{5,4},{6,7},{7,6},{8,9},{9,8},{10,11... | collective-permute-start | bytes 442376 | tf_op jit(solution)/shard_map/ppermute | solution.py:308
  25.5 1.6 %copy-start.4 = (bf16[288,256]{1,0:T(8,128)(2,1)}, bf16[288,256]{1,0:T(8,128)(2,1)S(1)}, u32[]{:S(2)}) copy-start(bf16[288,256]{1,0:T(8,128)(2,1)S(1)} %collective-permute-done.3.refs_11_) | copy-start | bytes 442372
  25.5 1.5 %collective-permute-start.4 = (bf16[288,256]{1,0:T(8,128)(2,1)S(1)}, bf16[288,256]{1,0:T(8,128)(2,1)S(1)}, u32[]{:S(2)}, u32[]{:S(2)}) collective-permute-start(bf16[288,256]{1,0:T(8,128)(2,1)S(1)} %collective-permute-done.3.refs_11_), channel_id=1, source_target_pairs={{0,1},{1,0},{2,3},{3,2},{4,5},{5,4},{6,7},{7,6},{8,9},{9,8},{10,11... | collective-permute-start | bytes 442376 | tf_op jit(solution)/shard_map/ppermute | solution.py:308
  25.5 1.5 %copy-start.5 = (bf16[288,256]{1,0:T(8,128)(2,1)}, bf16[288,256]{1,0:T(8,128)(2,1)S(1)}, u32[]{:S(2)}) copy-start(bf16[288,256]{1,0:T(8,128)(2,1)S(1)} %collective-permute-done.5.refs_13_) | copy-start | bytes 442372
  27.0 0.7 %copy-start.3 = (bf16[40,2048]{1,0:T(8,128)(2,1)}, bf16[40,2048]{1,0:T(8,128)(2,1)S(1)}, u32[]{:S(2)}) copy-start(bf16[40,2048]{1,0:T(8,128)(2,1)S(1)} %collective-permute-done.6.refs_17_) | copy-start | bytes 491524
  27.0 0.7 %copy-start.6 = (bf16[288,256]{1,0:T(8,128)(2,1)}, bf16[288,256]{1,0:T(8,128)(2,1)S(1)}, u32[]{:S(2)}) copy-start(bf16[288,256]{1,0:T(8,128)(2,1)S(1)} %collective-permute-done.4.refs_12_) | copy-start | bytes 442372

commit v6 on v5

--- a/solution.py
+++ b/solution.py
@@ -11,6 +11,7 @@
 LANES = 128
 MIB = 1024 * 1024
 UNROLL = 8
+LOG2E = 1.4426950408889634
 F32, BF16 = jnp.float32, jnp.bfloat16
 NT = (((1,), (1,)), ((), ()))
 TN = (((0,), (0,)), ((), ()))
@@ -30,14 +31,6 @@
 def split_index(value, inner):
     assert inner & (inner - 1) == 0
     return value >> (inner.bit_length() - 1), value & (inner - 1)
-
-
-def one_hot_rows(outer, inner):
-    count = outer * inner
-    row = lax.broadcasted_iota(jnp.int32, (count, count), 0)
-    col = lax.broadcasted_iota(jnp.int32, (count, count), 1)
-    high, low = split_index(row, outer)
-    return jnp.where(col == low * inner + high, 1.0, 0.0).astype(BF16)
 
 
 def pick_rows(values, row_low, count):
@@ -89,18 +82,24 @@
     for copy in copies:
         copy.start()
 
-    order = one_hot_rows(per_dev, NEW)
-    joined[:lines, :] = jnp.zeros((lines, channels), F32)
+    joined[:, :lines, :] = jnp.zeros((channels // LANES, lines, LANES), F32)
     copies[0].wait()
     copies[1].wait()
     outs = []
     for c, chunk in enumerate(chunks):
         copies[2 + 2 * c].wait()
-        joined[lines:, chunk] = jnp.dot(order, x_v[:, chunk], preferred_element_type=F32)
-        summed = jnp.broadcast_to(cb_v[:, chunk], (rows, width))
-        for k in range(taps):
-            weight = cw_v[k : k + 1, chunk].astype(F32)
-            summed = summed + joined[k * per_dev : k * per_dev + rows, chunk] * weight
+        sums = []
+        for tile in range(c * width // LANES, (c + 1) * width // LANES):
+            lanes = slice(tile * LANES, (tile + 1) * LANES)
+            for r in range(per_dev):
+                tokens = x_v[r * NEW : (r + 1) * NEW, lanes].astype(F32)
+                joined[tile, pl.ds(lines + r, NEW, stride=per_dev), :] = tokens
+            summed = jnp.broadcast_to(cb_v[:, lanes], (rows, LANES))
+            for k in range(taps):
+                weight = cw_v[k : k + 1, lanes].astype(F32)
+                summed = summed + joined[tile, k * per_dev : k * per_dev + rows, :] * weight
+            sums.append(summed)
+        summed = jnp.concatenate(sums, axis=1)
         head_v[:, chunk] = summed[: head_v.shape[0]]
         mixed = silu(summed).astype(BF16)
         mixed_v[:, chunk] = mixed
@@ -166,31 +165,30 @@
 
 
 def scan_kernel(dims, refs_in, refs_out, scratch):
-    dims, block = dims
-    per_dev, n_replica, slots, _ = dims
+    per_dev = dims[0]
     holder, slot_id, prefix_len, mixed_hbm, head_hbm, z_hbm, dtw_hbm, dtb_hbm, al_hbm, skip_hbm = refs_in[:10]
     out_hbm, state_hbm = refs_out
-    (h_s, s_s, l_s, mixed_v, z_v, dtw_v, dtb_v, al_v, skip_v, parts_v, cache_v, b_tab, c_tab, dt_v, drive_v, gate_v,
+    (h_s, s_s, l_s, mixed_v, z_v, dtw_v, dtb_v, al_v, skip_v, parts_v, cache_v, b_tab, c_tab, dt_v, drive_v,
      a_v, start_tm, final_tm, y_v, out_v, state_v, sems, out_sems) = scratch
-    n_parts, n_pieces = parts_v.shape[0], cache_v.shape[0]
+    n_parts = parts_v.shape[0]
     parts, pieces = refs_in[10 : 10 + n_parts], refs_in[10 + n_parts :]
     head = head_hbm.shape[0]
     rows, channels = z_v.shape
     states = al_v.shape[0]
     rank = dtw_v.shape[0]
-    pairs = [(z_hbm, z_v)] + [(part, parts_v.at[p]) for p, part in enumerate(parts)]
-    pairs += [(dtw_hbm, dtw_v), (dtb_hbm, dtb_v), (al_hbm, al_v), (holder, h_s), (slot_id, s_s), (prefix_len, l_s),
-              (skip_hbm, skip_v), (head_hbm, mixed_v.at[:head]), (mixed_hbm.at[head:], mixed_v.at[head:])]
-    pairs += [(piece, cache_v.at[p]) for p, piece in enumerate(pieces)]
+    pairs = [(part, parts_v.at[p]) for p, part in enumerate(parts)]
+    pairs += [(dtw_hbm, dtw_v), (dtb_hbm, dtb_v), (head_hbm, mixed_v.at[:head]), (mixed_hbm.at[head:], mixed_v.at[head:]),
+              (skip_hbm, skip_v), (al_hbm, al_v), (holder, h_s), (slot_id, s_s), (prefix_len, l_s)]
+    if len(pieces) == 1:
+        pairs.append((pieces[0], cache_v))
+    else:
+        pairs += [(piece, cache_v.at[p]) for p, piece in enumerate(pieces)]
+    pairs.append((z_hbm, z_v))
     copies = [pltpu.make_async_copy(src, dst, sems.at[i]) for i, (src, dst) in enumerate(pairs)]
     for copy in copies:
         copy.start()
 
-    order = one_hot_rows(per_dev, NEW)
-    copies[0].wait()
-    gate_v[...] = silu(jnp.dot(order, z_v[...], preferred_element_type=F32))
-
-    for copy in copies[1 : 1 + n_parts]:
+    for copy in copies[:n_parts]:
         copy.wait()
     projected = parts_v[0].astype(F32)
     for p in range(1, n_parts):
@@ -200,21 +198,28 @@
     for n in range(states):
         b_tab[n] = jnp.broadcast_to(late[:, n : n + 1], (rows, LANES))
         c_tab[n] = jnp.broadcast_to(late[:, states + n : states + n + 1], (rows, LANES))
-    for copy in copies[1 + n_parts :]:
+    for copy in copies[n_parts:-1]:
         copy.wait()
-    dt = softplus(lax.dot_general(dt_low, dtw_v[...], TN, preferred_element_type=F32) + dtb_v[...])
-    dt_v[...] = dt
-    drive_v[...] = dt * mixed_v[...].astype(F32)
-    a_v[...] = -jnp.exp(al_v[...])
+    n_tiles = channels // LANES
+    dt_all = softplus(lax.dot_general(dt_low, dtw_v[...], TN, preferred_element_type=F32) + dtb_v[...])
+    for tile in range(n_tiles):
+        lanes = slice(tile * LANES, (tile + 1) * LANES)
+        dt = dt_all[:, lanes]
+        mixed = mixed_v[:, lanes].astype(F32)
+        dt_v[tile] = dt
+        drive_v[tile] = dt * mixed
+        y_v[tile, :rows, :] = skip_v[:, lanes] * mixed
+    a_v[...] = jnp.exp(al_v[...]) * (-LOG2E)
 
     me = lax.axis_index("replica")
     places, slot_ids, lengths = request_places(dims, (h_s, s_s, l_s), me)
-    state_id, request = split_index(lax.broadcasted_iota(jnp.int32, (per_dev * states, 1), 0), per_dev)
-    starts = [places[r] * block + slot_ids[r] * states for r in range(per_dev)]
-    target = pick_rows(starts, request, per_dev) + state_id
-    live = pick_rows(lengths, request, per_dev) > 0
-    found = [(p * cache_v.shape[1], cache_v[p]) for p in range(n_pieces)]
-    start_tm[...] = fetch_rows(target, live, found)
+    for r in range(per_dev):
+        spot = pl.ds(pl.multiple_of(slot_ids[r] * states, states), states)
+        for tile in range(n_tiles):
+            value = cache_v[places[r], spot, tile * LANES : (tile + 1) * LANES].astype(F32)
+            value = jnp.where(lengths[r] > 0, value, jnp.zeros_like(value))
+            start_tm[tile, pl.ds(r, states, stride=per_dev), :] = value
+    copies[-1].wait()
 
     tiles = 2
     half = states // 2
@@ -229,7 +234,8 @@
         ]
 
     def scan_group(g, carry):
-        lanes = [pl.ds(pl.multiple_of((g * tiles + j) * LANES, LANES), LANES) for j in range(tiles)]
+        group = [g * tiles + j for j in range(tiles)]
+        lanes = [pl.ds(pl.multiple_of(tile * LANES, LANES), LANES) for tile in group]
         for first in range(0, states, half):
             ids = range(first, first + half)
             rates = [[jnp.broadcast_to(a_v[n : n + 1, lane], (per_dev, LANES)) for n in ids] for lane in lanes]
@@ -238,37 +244,38 @@
                 state = list(state)
                 for u in range(UNROLL):
                     now = pl.ds(pl.multiple_of((step * UNROLL + u) * per_dev, per_dev), per_dev)
-                    dt = [dt_v[now, lane] for lane in lanes]
-                    drive = [drive_v[now, lane] for lane in lanes]
+                    dt = [dt_v[tile, now, :] for tile in group]
+                    drive = [drive_v[tile, now, :] for tile in group]
                     sums = [None] * tiles
                     for k, n in enumerate(ids):
                         b, c = b_tab[n, now, :], c_tab[n, now, :]
                         for j in range(tiles):
                             i = j * half + k
-                            state[i] = jnp.exp(dt[j] * rates[j][k]) * state[i] + drive[j] * b
+                            state[i] = jnp.exp2(dt[j] * rates[j][k]) * state[i] + drive[j] * b
                             term = state[i] * c
                             sums[j] = term if sums[j] is None else sums[j] + term
-                    for j, lane in enumerate(lanes):
-                        y_v[now, lane] = sums[j] if first == 0 else y_v[now, lane] + sums[j]
+                    for j, tile in enumerate(group):
+                        y_v[tile, now, :] += sums[j]
                 return tuple(state)
 
-            state = tuple(start_tm[n * per_dev : (n + 1) * per_dev, lane] for lane in lanes for n in ids)
+            state = tuple(start_tm[tile, n * per_dev : (n + 1) * per_dev, :] for tile in group for n in ids)
             state = lax.fori_loop(0, NEW // UNROLL, advance, state)
-            for j, lane in enumerate(lanes):
+            for j, tile in enumerate(group):
                 for k, n in enumerate(ids):
-                    final_tm[n * per_dev : (n + 1) * per_dev, lane] = state[j * half + k]
+                    final_tm[tile, n * per_dev : (n + 1) * per_dev, :] = state[j * half + k]
         return carry
 
     def one_chunk(c, carry):
         lax.fori_loop(c * 2, c * 2 + 2, scan_group, 0)
-        lanes = pl.ds(pl.multiple_of(c * width, width), width)
-        total = y_v[:, lanes] + skip_v[:, lanes] * mixed_v[:, lanes].astype(F32)
-        gated = (total * gate_v[:, lanes]).astype(BF16)
-        back = one_hot_rows(NEW, per_dev)
-        back_s = one_hot_rows(states, per_dev)
-        out_v[:, lanes] = jnp.dot(back, gated, preferred_element_type=F32).astype(BF16)
-        final = jnp.dot(back_s, final_tm[:, lanes].astype(BF16), preferred_element_type=F32)
-        state_v[:, lanes] = final.astype(BF16)
+        for j in range(width // LANES):
+            tile = c * (width // LANES) + j
+            lanes = pl.ds(pl.multiple_of(tile * LANES, LANES), LANES)
+            for r in range(per_dev):
+                here = slice(r * NEW, (r + 1) * NEW)
+                value = y_v[tile, pl.ds(r, NEW, stride=per_dev), :] * silu(z_v[here, lanes].astype(F32))
+                out_v[here, lanes] = value.astype(BF16)
+                final = final_tm[tile, pl.ds(r, states, stride=per_dev), :]
+                state_v[r * states : (r + 1) * states, lanes] = final.astype(BF16)
         for copy in out_copies(c):
             copy.start()
         return carry
@@ -332,8 +339,8 @@
         firsts = (0, block, 2 * block, 4 * block - slots * taps)
         ssm_pieces = [rows_all, near, far, swap(far, "replica", n_replica, 1)]
     else:
-        ssm_pieces = [lax.all_gather(rows_all, "replica", axis=0, tiled=True)]
-        conv_pieces, firsts = ssm_pieces, (0,)
+        ssm_pieces = [lax.all_gather(rows_all, "replica")]
+        conv_pieces, firsts = [ssm_pieces[0].reshape(-1, channels)], (0,)
 
     vmem, dma = pltpu.VMEM, pltpu.SemaphoreType.DMA
     ints = [pltpu.SMEM((requests,), jnp.int32)] * 3
@@ -351,7 +358,7 @@
             vmem((out_cols, channels), BF16),
             vmem((taps, channels), BF16),
             vmem((1, channels), F32),
-            vmem((rows + (taps - 1) * per_dev, channels), F32),
+            vmem((channels // LANES, rows + taps * per_dev, LANES), F32),
             vmem((rows, channels), BF16),
             vmem((head, channels), F32),
             vmem((out_cols, rows), F32),
@@ -382,9 +389,10 @@
         parts = parts + [swap(value, "tensor", n_tensor, mask) for value in reversed(parts)]
         mask //= 2
 
-    blocks = (len(ssm_pieces),) + ssm_pieces[0].shape
+    blocks = (n_replica, block, channels)
+    n_tiles = channels // LANES
     out, state = call(
-        scan_kernel, (dims, block), "dt_scan_gate", 60,
+        scan_kernel, dims, "dt_scan_gate", 60,
         [(holder, True), (slot_id, True), (prefix_len, True), (mixed, False), (mixed_head, False), (z_new, True), (dt_proj_weight, True),
          (dt_bias[None, :], True), (a_log, True), (d_skip[None, :], True)]
         + [(piece, False) for piece in parts + ssm_pieces],
@@ -400,13 +408,12 @@
             vmem(blocks, BF16),
             vmem((states, rows, LANES), F32),
             vmem((states, rows, LANES), F32),
-            vmem((rows, channels), F32),
-            vmem((rows, channels), F32),
-            vmem((rows, channels), F32),
+            vmem((n_tiles, rows, LANES), F32),
+            vmem((n_tiles, rows, LANES), F32),
             vmem((states, channels), F32),
-            vmem((per_dev * states, channels), F32),
-            vmem((per_dev * states, channels), F32),
-            vmem((rows, channels), F32),
+            vmem((n_tiles, per_dev * (states + 1), LANES), F32),
+            vmem((n_tiles, per_dev * (states + 1), LANES), F32),
+            vmem((n_tiles, rows + per_dev, LANES), F32),
             vmem((rows, channels), BF16),
             vmem((per_dev * states, channels), BF16),
             dma((10 + n_tensor + len(ssm_pieces),)),

time: 45.4 us -> 42.7 us (0.941)
  Pallas kernels: 24.7 us -> 22 us
    pallas_call x3, Pallas kernels: 24.7 us -> 22 us  [call(): pl.pallas_call(split_refs(kernel, dims, len(ins), len(outs)), in_specs=[h...]
  transfers between devices with their start and end apart: 7 -> 7, of which waited for: 4 -> 4; matrix products, arithmetic and copies ran while one was open for 0% -> 0% of each run, Pallas kernels for 10% -> 11%
where the time goes in v6:
time: 42.7 us; the launch traced here: 42.4 us
  Pallas kernels  22 us (52%)
  starting transfers between devices  8.65 us (20%)
  waiting for transfers between devices  7.99 us (19%)
  local copies, waits for them, and re-layouts  2.14 us (5%)
  other arithmetic  0.92 us (2%)
  between operations  0.71 us (2%)
    pallas_call x3, Pallas kernels, call(): pl.pallas_call(split_refs(kernel, dims, len(ins), len(outs)), in_specs=[h...  22 us
    ppermute x7, starting transfers between devices, swap(): return lax.ppermute(value, axis, [(i, i ^ mask) for i in range(size)])  8.65 us
    ppermute x7, waiting for transfers between devices, swap(): return lax.ppermute(value, axis, [(i, i ^ mask) for i in range(size)])  7.99 us
    unnamed x17, local copies, waits for them, and re-layouts  2.1 us
    concatenate x1, other arithmetic, shards(): jnp.concatenate([cache_ssm.reshape(slots * states, channels), conv_rows])  0.92 us
  transfers between devices with their start and end apart: 7, of which 4 were waited for; matrix products, arithmetic and copies ran while one was open for 0% of the time, Pallas kernels for 11%

profile of v6, /device:TPU:0, one launch (start us, length us, event | category | flops | bytes accessed | tf_op | source)
XLA Modules:
  0.0 42.4 jit_solution(9744761165601199576)
XLA Ops:
  0.6 0.8 %copy.17 = bf16[2,3,2048]{2,1,0:T(4,128)(2,1)S(1)} copy(bf16[2,3,2048]{2,0,1:T(2,128)(2,1)} %param.24) | data formatting | bytes 49152
  1.4 0.9 %pad_maximum_fusion.refs_7_.refs_14_ = bf16[40,2048]{1,0:T(8,128)(2,1)S(1)} fusion(bf16[8,2048]{1,0:T(8,128)(2,1)S(1)} %reshape.14, bf16[32,2048]{1,0:T(8,128)(2,1)} %bitcast.8), kind=kLoop, calls=%fused_computation | loop fusion | flops 327680 | bytes 327680 | tf_op jit(solution)/shard_map/concatenate | solution.py:331
  2.4 5.1 %collective-permute-start.1 = (bf16[40,2048]{1,0:T(8,128)(2,1)S(1)}, bf16[40,2048]{1,0:T(8,128)(2,1)S(1)}, u32[]{:S(2)}, u32[]{:S(2)}) collective-permute-start(bf16[40,2048]{1,0:T(8,128)(2,1)S(1)} %pad_maximum_fusion.refs_7_.refs_14_), channel_id=1, source_target_pairs={{0,12},{4,8},{8,4},{12,0},{1,13},{5,9},{9,5},{13,1},{2,14},{6,10},... | collective-permute-start | bytes 491528 | tf_op jit(solution)/shard_map/ppermute | solution.py:315
  7.5 0.0 collective-permute-start
  7.5 0.6 %collective-permute-start.2 = (bf16[8,2048]{1,0:T(8,128)(2,1)S(1)}, bf16[8,2048]{1,0:T(8,128)(2,1)S(1)}, u32[]{:S(2)}, u32[]{:S(2)}) collective-permute-start(bf16[8,2048]{1,0:T(8,128)(2,1)S(1)} %reshape.14), channel_id=1, source_target_pairs={{0,8},{4,12},{8,0},{12,4},{1,9},{5,13},{9,1},{13,5},{2,10},{6,14},... | collective-permute-start | bytes 98312 | tf_op jit(solution)/shard_map/ppermute | solution.py:315
  8.1 4.5 %conv_project.1 = (bf16[256,2048]{1,0:T(8,128)(2,1)}, f32[32,2048]{1,0:T(8,128)}, bf16[288,256]{1,0:T(8,128)(2,1)}) custom-call(bf16[256,2048]{1,0:T(8,128)(2,1)} %refs_0_.3, bf16[288,2048]{1,0:T(8,128)(2,1)} %bitcast.6, bf16[4,2048]{1,0:T(4,128)(2,1)} %refs_6_.2, f32[1,2048]{1,0:T(1,128)} %bitcast.9), custom_call_target="tpu_custom_call" | custom-call | tf_op jit(solution)/shard_map/conv_project/pallas_call | solution.py:303
  12.7 2.8 %collective-permute-done.2.refs_10_ = bf16[8,2048]{1,0:T(8,128)(2,1)S(1)} collective-permute-done((bf16[8,2048]{1,0:T(8,128)(2,1)S(1)}, bf16[8,2048]{1,0:T(8,128)(2,1)S(1)}, u32[]{:S(2)}, u32[]{:S(2)}) %collective-permute-start.2) | collective-permute-done | bytes 32800 | tf_op jit(solution)/shard_map/ppermute | solution.py:315
  15.5 0.0 collective-permute-done.1.refs_9_.refs_16_
  15.5 0.5 %collective-permute-done.refs_8_.refs_15_ = bf16[40,2048]{1,0:T(8,128)(2,1)S(1)} collective-permute-done((bf16[40,2048]{1,0:T(8,128)(2,1)S(1)}, bf16[40,2048]{1,0:T(8,128)(2,1)S(1)}, u32[]{:S(2)}, u32[]{:S(2)}) %collective-permute-start) | collective-permute-done | bytes 163872 | tf_op jit(solution)/shard_map/ppermute | solution.py:315
  16.0 0.1 copy-done.7
  16.1 0.1 copy-done.1
  16.2 0.5 %copy-done.2 = bf16[40,2048]{1,0:T(8,128)(2,1)} copy-done((bf16[40,2048]{1,0:T(8,128)(2,1)}, bf16[40,2048]{1,0:T(8,128)(2,1)S(1)}, u32[]{:S(2)}) %copy-start.2) | copy-done | bytes 163864
  16.6 2.8 %history.1 = (bf16[32,2048]{1,0:T(8,128)(2,1)}, bf16[288,256]{1,0:T(8,128)(2,1)}) custom-call(s32[32]{0:T(128)} %refs_0_.5, s32[32]{0:T(128)} %refs_1_.3, s32[32]{0:T(128)} %refs_2_.5, f32[32,2048]{1,0:T(8,128)} %get-tuple-element.10.refs_3_, bf16[288,256]{1,0:T(8,128)(2,1)} %get-tuple-element.11.refs_4_, bf16[288,2048]{1,0:T(8,128)(2,1)} %bitcast.7, ...), custom_call_target="tpu_custom_call" | custom-call | tf_op jit(solution)/shard_map/history/pallas_call | solution.py:303
  19.5 1.6 %collective-permute-start.3 = (bf16[288,256]{1,0:T(8,128)(2,1)}, bf16[288,256]{1,0:T(8,128)(2,1)S(1)}, u32[]{:S(2)}, u32[]{:S(2)}) collective-permute-start(bf16[288,256]{1,0:T(8,128)(2,1)} %get-tuple-element.13.refs_10_), channel_id=1, source_target_pairs={{0,2},{1,3},{2,0},{3,1},{4,6},{5,7},{6,4},{7,5},{8,10},{9,11},{10,... | collective-permute-start | bytes 442376 | tf_op jit(solution)/shard_map/ppermute | solution.py:315
  21.0 1.3 %collective-permute-start.6 = (bf16[40,2048]{1,0:T(8,128)(2,1)}, bf16[40,2048]{1,0:T(8,128)(2,1)S(1)}, u32[]{:S(2)}, u32[]{:S(2)}) collective-permute-start(bf16[40,2048]{1,0:T(8,128)(2,1)} %copy-done.1), channel_id=1, source_target_pairs={{0,4},{4,0},{8,12},{12,8},{1,5},{5,1},{9,13},{13,9},{2,6},{6,2},{1... | collective-permute-start | bytes 491528 | tf_op jit(solution)/shard_map/ppermute | solution.py:315
  22.3 0.0 collective-permute-start.5
  22.4 3.1 %collective-permute-done.3.refs_11_ = bf16[288,256]{1,0:T(8,128)(2,1)S(1)} collective-permute-done((bf16[288,256]{1,0:T(8,128)(2,1)}, bf16[288,256]{1,0:T(8,128)(2,1)S(1)}, u32[]{:S(2)}, u32[]{:S(2)}) %collective-permute-start.3) | collective-permute-done | bytes 147488 | tf_op jit(solution)/shard_map/ppermute | solution.py:315
  25.5 0.0 collective-permute-start.4
  25.5 0.0 collective-permute-done.5.refs_13_
  25.5 1.5 %collective-permute-done.6.refs_17_ = bf16[40,2048]{1,0:T(8,128)(2,1)S(1)} collective-permute-done((bf16[40,2048]{1,0:T(8,128)(2,1)}, bf16[40,2048]{1,0:T(8,128)(2,1)S(1)}, u32[]{:S(2)}, u32[]{:S(2)}) %collective-permute-start.6) | collective-permute-done | bytes 163872 | tf_op jit(solution)/shard_map/ppermute | solution.py:315
  27.0 0.0 collective-permute-done.4.refs_12_
  27.1 0.6 %copy-done.3 = bf16[40,2048]{1,0:T(8,128)(2,1)} copy-done((bf16[40,2048]{1,0:T(8,128)(2,1)}, bf16[40,2048]{1,0:T(8,128)(2,1)S(1)}, u32[]{:S(2)}) %copy-start.3) | copy-done | bytes 163864
  27.7 0.1 copy-done.6
  27.8 14.7 %dt_scan_gate.1 = (bf16[256,2048]{1,0:T(8,128)(2,1)}, bf16[128,2048]{1,0:T(8,128)(2,1)}) custom-call(s32[32]{0:T(128)} %refs_0_.5, s32[32]{0:T(128)} %refs_1_.3, s32[32]{0:T(128)} %refs_2_.5, bf16[256,2048]{1,0:T(8,128)(2,1)} %get-tuple-element.9.refs_3_, bf16[32,2048]{1,0:T(8,128)(2,1)} %get-tuple-element.12.refs_4_, bf16[256,2048]{1,0:T(8,128)(2,1)} %refs_5_.1, ...), custom_call_target="tpu_custom_call" | custom-call | tf_op jit(solution)/shard_map/dt_scan_gate/pallas_call | solution.py:303
  (13 shorter events, 0.1 us)
Async XLA Ops:
  2.4 13.6 %copy-start = (bf16[40,2048]{1,0:T(8,128)(2,1)}, bf16[40,2048]{1,0:T(8,128)(2,1)S(1)}, u32[]{:S(2)}) copy-start(bf16[40,2048]{1,0:T(8,128)(2,1)S(1)} %pad_maximum_fusion.refs_7_.refs_14_) | copy-start | bytes 491524
  2.4 13.1 %collective-permute-start.1 = (bf16[40,2048]{1,0:T(8,128)(2,1)S(1)}, bf16[40,2048]{1,0:T(8,128)(2,1)S(1)}, u32[]{:S(2)}, u32[]{:S(2)}) collective-permute-start(bf16[40,2048]{1,0:T(8,128)(2,1)S(1)} %pad_maximum_fusion.refs_7_.refs_14_), channel_id=1, source_target_pairs={{0,12},{4,8},{8,4},{12,0},{1,13},{5,9},{9,5},{13,1},{2,14},{6,10},... | collective-permute-start | bytes 491528 | tf_op jit(solution)/shard_map/ppermute | solution.py:315
  7.5 8.5 %collective-permute-start = (bf16[40,2048]{1,0:T(8,128)(2,1)S(1)}, bf16[40,2048]{1,0:T(8,128)(2,1)S(1)}, u32[]{:S(2)}, u32[]{:S(2)}) collective-permute-start(bf16[40,2048]{1,0:T(8,128)(2,1)S(1)} %pad_maximum_fusion.refs_7_.refs_14_), channel_id=1, source_target_pairs={{0,4},{4,0},{8,12},{12,8},{1,5},{5,1},{9,13},{13,9},{2,6},{6,2},{1... | collective-permute-start | bytes 491528 | tf_op jit(solution)/shard_map/ppermute | solution.py:315
  7.5 8.0 %collective-permute-start.2 = (bf16[8,2048]{1,0:T(8,128)(2,1)S(1)}, bf16[8,2048]{1,0:T(8,128)(2,1)S(1)}, u32[]{:S(2)}, u32[]{:S(2)}) collective-permute-start(bf16[8,2048]{1,0:T(8,128)(2,1)S(1)} %reshape.14), channel_id=1, source_target_pairs={{0,8},{4,12},{8,0},{12,4},{1,9},{5,13},{9,1},{13,5},{2,10},{6,14},... | collective-permute-start | bytes 98312 | tf_op jit(solution)/shard_map/ppermute | solution.py:315
  15.5 0.6 %copy-start.7 = (bf16[8,2048]{1,0:T(8,128)(2,1)}, bf16[8,2048]{1,0:T(8,128)(2,1)S(1)}, u32[]{:S(2)}) copy-start(bf16[8,2048]{1,0:T(8,128)(2,1)S(1)} %collective-permute-done.2.refs_10_) | copy-start | bytes 98308
  15.5 0.7 %copy-start.1 = (bf16[40,2048]{1,0:T(8,128)(2,1)}, bf16[40,2048]{1,0:T(8,128)(2,1)S(1)}, u32[]{:S(2)}) copy-start(bf16[40,2048]{1,0:T(8,128)(2,1)S(1)} %collective-permute-done.1.refs_9_.refs_16_) | copy-start | bytes 491524
  16.0 0.6 %copy-start.2 = (bf16[40,2048]{1,0:T(8,128)(2,1)}, bf16[40,2048]{1,0:T(8,128)(2,1)S(1)}, u32[]{:S(2)}) copy-start(bf16[40,2048]{1,0:T(8,128)(2,1)S(1)} %collective-permute-done.refs_8_.refs_15_) | copy-start | bytes 491524
  19.5 6.0 %collective-permute-start.3 = (bf16[288,256]{1,0:T(8,128)(2,1)}, bf16[288,256]{1,0:T(8,128)(2,1)S(1)}, u32[]{:S(2)}, u32[]{:S(2)}) collective-permute-start(bf16[288,256]{1,0:T(8,128)(2,1)} %get-tuple-element.13.refs_10_), channel_id=1, source_target_pairs={{0,2},{1,3},{2,0},{3,1},{4,6},{5,7},{6,4},{7,5},{8,10},{9,11},{10,... | collective-permute-start | bytes 442376 | tf_op jit(solution)/shard_map/ppermute | solution.py:315
  21.0 6.0 %collective-permute-start.6 = (bf16[40,2048]{1,0:T(8,128)(2,1)}, bf16[40,2048]{1,0:T(8,128)(2,1)S(1)}, u32[]{:S(2)}, u32[]{:S(2)}) collective-permute-start(bf16[40,2048]{1,0:T(8,128)(2,1)} %copy-done.1), channel_id=1, source_target_pairs={{0,4},{4,0},{8,12},{12,8},{1,5},{5,1},{9,13},{13,9},{2,6},{6,2},{1... | collective-permute-start | bytes 491528 | tf_op jit(solution)/shard_map/ppermute | solution.py:315
  22.3 3.2 %collective-permute-start.5 = (bf16[288,256]{1,0:T(8,128)(2,1)}, bf16[288,256]{1,0:T(8,128)(2,1)S(1)}, u32[]{:S(2)}, u32[]{:S(2)}) collective-permute-start(bf16[288,256]{1,0:T(8,128)(2,1)} %get-tuple-element.13.refs_10_), channel_id=1, source_target_pairs={{0,1},{1,0},{2,3},{3,2},{4,5},{5,4},{6,7},{7,6},{8,9},{9,8},{10,11... | collective-permute-start | bytes 442376 | tf_op jit(solution)/shard_map/ppermute | solution.py:315
  25.5 1.6 %copy-start.4 = (bf16[288,256]{1,0:T(8,128)(2,1)}, bf16[288,256]{1,0:T(8,128)(2,1)S(1)}, u32[]{:S(2)}) copy-start(bf16[288,256]{1,0:T(8,128)(2,1)S(1)} %collective-permute-done.3.refs_11_) | copy-start | bytes 442372
  25.5 1.5 %collective-permute-start.4 = (bf16[288,256]{1,0:T(8,128)(2,1)S(1)}, bf16[288,256]{1,0:T(8,128)(2,1)S(1)}, u32[]{:S(2)}, u32[]{:S(2)}) collective-permute-start(bf16[288,256]{1,0:T(8,128)(2,1)S(1)} %collective-permute-done.3.refs_11_), channel_id=1, source_target_pairs={{0,1},{1,0},{2,3},{3,2},{4,5},{5,4},{6,7},{7,6},{8,9},{9,8},{10,11... | collective-permute-start | bytes 442376 | tf_op jit(solution)/shard_map/ppermute | solution.py:315
  25.5 1.5 %copy-start.5 = (bf16[288,256]{1,0:T(8,128)(2,1)}, bf16[288,256]{1,0:T(8,128)(2,1)S(1)}, u32[]{:S(2)}) copy-start(bf16[288,256]{1,0:T(8,128)(2,1)S(1)} %collective-permute-done.5.refs_13_) | copy-start | bytes 442372
  27.0 0.7 %copy-start.3 = (bf16[40,2048]{1,0:T(8,128)(2,1)}, bf16[40,2048]{1,0:T(8,128)(2,1)S(1)}, u32[]{:S(2)}) copy-start(bf16[40,2048]{1,0:T(8,128)(2,1)S(1)} %collective-permute-done.6.refs_17_) | copy-start | bytes 491524
  27.0 0.7 %copy-start.6 = (bf16[288,256]{1,0:T(8,128)(2,1)}, bf16[288,256]{1,0:T(8,128)(2,1)S(1)}, u32[]{:S(2)}) copy-start(bf16[288,256]{1,0:T(8,128)(2,1)S(1)} %collective-permute-done.4.refs_12_) | copy-start | bytes 442372

commit v7 on v6

--- a/solution.py
+++ b/solution.py
@@ -88,23 +88,23 @@
     outs = []
     for c, chunk in enumerate(chunks):
         copies[2 + 2 * c].wait()
-        sums = []
         for tile in range(c * width // LANES, (c + 1) * width // LANES):
             lanes = slice(tile * LANES, (tile + 1) * LANES)
             for r in range(per_dev):
                 tokens = x_v[r * NEW : (r + 1) * NEW, lanes].astype(F32)
                 joined[tile, pl.ds(lines + r, NEW, stride=per_dev), :] = tokens
-            summed = jnp.broadcast_to(cb_v[:, lanes], (rows, LANES))
-            for k in range(taps):
-                weight = cw_v[k : k + 1, lanes].astype(F32)
-                summed = summed + joined[tile, k * per_dev : k * per_dev + rows, :] * weight
-            sums.append(summed)
-        summed = jnp.concatenate(sums, axis=1)
-        head_v[:, chunk] = summed[: head_v.shape[0]]
-        mixed = silu(summed).astype(BF16)
-        mixed_v[:, chunk] = mixed
+            weight = [cw_v[k : k + 1, lanes].astype(F32) for k in range(taps)]
+            bias = cb_v[:, lanes]
+            for first in range(0, rows, LANES):
+                summed = bias + joined[tile, first : first + LANES, :] * weight[0]
+                for k in range(1, taps):
+                    begin = first + k * per_dev
+                    summed = summed + joined[tile, begin : begin + LANES, :] * weight[k]
+                if first == 0:
+                    head_v[:, lanes] = summed[: head_v.shape[0]]
+                mixed_v[first : first + LANES, lanes] = silu(summed).astype(BF16)
         copies[3 + 2 * c].wait()
-        part = lax.dot_general(wt_v[:, chunk], mixed, NT, preferred_element_type=F32)
+        part = lax.dot_general(wt_v[:, chunk], mixed_v[:, chunk], NT, preferred_element_type=F32)
         if c == 0:
             part_f[...] = part
         else:
@@ -188,27 +188,34 @@
     for copy in copies:
         copy.start()
 
-    for copy in copies[:n_parts]:
+    for copy in copies[: n_parts + 5]:
         copy.wait()
     projected = parts_v[0].astype(F32)
     for p in range(1, n_parts):
         projected = projected + parts_v[p].astype(F32)
     dt_low = projected[:rank].astype(BF16)
     late = projected[rank:].T
-    for n in range(states):
-        b_tab[n] = jnp.broadcast_to(late[:, n : n + 1], (rows, LANES))
-        c_tab[n] = jnp.broadcast_to(late[:, states + n : states + n + 1], (rows, LANES))
-    for copy in copies[n_parts:-1]:
+    n_tiles = channels // LANES
+    wide = min(4, n_tiles)
+    per_chunk = 2 * states * wide // n_tiles
+    for c in range(n_tiles // wide):
+        for n in range(c * per_chunk, (c + 1) * per_chunk):
+            table = b_tab if n < states else c_tab
+            table[n % states] = jnp.broadcast_to(late[:, n : n + 1], (rows, LANES))
+        weights = dtw_v[:, c * wide * LANES : (c + 1) * wide * LANES]
+        raw = lax.dot_general(dt_low, weights, TN, preferred_element_type=F32)
+        for j in range(wide):
+            tile = c * wide + j
+            lanes = slice(tile * LANES, (tile + 1) * LANES)
+            for first in range(0, rows, LANES):
+                here = slice(first, first + LANES)
+                dt = softplus(raw[here, j * LANES : (j + 1) * LANES] + dtb_v[:, lanes])
+                mixed = mixed_v[here, lanes].astype(F32)
+                dt_v[tile, here, :] = dt
+                drive_v[tile, here, :] = dt * mixed
+                y_v[tile, here, :] = skip_v[:, lanes] * mixed
+    for copy in copies[n_parts + 5 : -1]:
         copy.wait()
-    n_tiles = channels // LANES
-    dt_all = softplus(lax.dot_general(dt_low, dtw_v[...], TN, preferred_element_type=F32) + dtb_v[...])
-    for tile in range(n_tiles):
-        lanes = slice(tile * LANES, (tile + 1) * LANES)
-        dt = dt_all[:, lanes]
-        mixed = mixed_v[:, lanes].astype(F32)
-        dt_v[tile] = dt
-        drive_v[tile] = dt * mixed
-        y_v[tile, :rows, :] = skip_v[:, lanes] * mixed
     a_v[...] = jnp.exp(al_v[...]) * (-LOG2E)
 
     me = lax.axis_index("replica")

time: 42.7 us -> 42.9 us (level)
  transfers between devices with their start and end apart: 7 -> 7, of which waited for: 4 -> 4; matrix products, arithmetic and copies ran while one was open for 0% -> 0% of each run, Pallas kernels for 11% -> 10%
where the time goes in v7:
time: 42.9 us; the launch traced here: 42.7 us
  Pallas kernels  22.1 us (52%)
  starting transfers between devices  8.65 us (20%)
  waiting for transfers between devices  8.18 us (19%)
  local copies, waits for them, and re-layouts  2.14 us (5%)
  other arithmetic  0.92 us (2%)
  between operations  0.71 us (2%)
    pallas_call x3, Pallas kernels, call(): pl.pallas_call(split_refs(kernel, dims, len(ins), len(outs)), in_specs=[h...  22.1 us
    ppermute x7, starting transfers between devices, swap(): return lax.ppermute(value, axis, [(i, i ^ mask) for i in range(size)])  8.65 us
    ppermute x7, waiting for transfers between devices, swap(): return lax.ppermute(value, axis, [(i, i ^ mask) for i in range(size)])  8.18 us
    unnamed x17, local copies, waits for them, and re-layouts  2.1 us
    concatenate x1, other arithmetic, shards(): jnp.concatenate([cache_ssm.reshape(slots * states, channels), conv_rows])  0.92 us
  transfers between devices with their start and end apart: 7, of which 4 were waited for; matrix products, arithmetic and copies ran while one was open for 0% of the time, Pallas kernels for 10%

profile of v7, /device:TPU:0, one launch (start us, length us, event | category | flops | bytes accessed | tf_op | source)
XLA Modules:
  0.0 42.7 jit_solution(18358953914235171842)
XLA Ops:
  0.6 0.8 %copy.17 = bf16[2,3,2048]{2,1,0:T(4,128)(2,1)S(1)} copy(bf16[2,3,2048]{2,0,1:T(2,128)(2,1)} %param.24) | data formatting | bytes 49152
  1.4 0.9 %pad_maximum_fusion.refs_7_.refs_14_ = bf16[40,2048]{1,0:T(8,128)(2,1)S(1)} fusion(bf16[8,2048]{1,0:T(8,128)(2,1)S(1)} %reshape.14, bf16[32,2048]{1,0:T(8,128)(2,1)} %bitcast.8), kind=kLoop, calls=%fused_computation | loop fusion | flops 327680 | bytes 327680 | tf_op jit(solution)/shard_map/concatenate | solution.py:338
  2.4 5.1 %collective-permute-start.1 = (bf16[40,2048]{1,0:T(8,128)(2,1)S(1)}, bf16[40,2048]{1,0:T(8,128)(2,1)S(1)}, u32[]{:S(2)}, u32[]{:S(2)}) collective-permute-start(bf16[40,2048]{1,0:T(8,128)(2,1)S(1)} %pad_maximum_fusion.refs_7_.refs_14_), channel_id=1, source_target_pairs={{0,12},{4,8},{8,4},{12,0},{1,13},{5,9},{9,5},{13,1},{2,14},{6,10},... | collective-permute-start | bytes 491528 | tf_op jit(solution)/shard_map/ppermute | solution.py:322
  7.5 0.0 collective-permute-start
  7.5 0.6 %collective-permute-start.2 = (bf16[8,2048]{1,0:T(8,128)(2,1)S(1)}, bf16[8,2048]{1,0:T(8,128)(2,1)S(1)}, u32[]{:S(2)}, u32[]{:S(2)}) collective-permute-start(bf16[8,2048]{1,0:T(8,128)(2,1)S(1)} %reshape.14), channel_id=1, source_target_pairs={{0,8},{4,12},{8,0},{12,4},{1,9},{5,13},{9,1},{13,5},{2,10},{6,14},... | collective-permute-start | bytes 98312 | tf_op jit(solution)/shard_map/ppermute | solution.py:322
  8.1 4.3 %conv_project.1 = (bf16[256,2048]{1,0:T(8,128)(2,1)}, f32[32,2048]{1,0:T(8,128)}, bf16[288,256]{1,0:T(8,128)(2,1)}) custom-call(bf16[256,2048]{1,0:T(8,128)(2,1)} %refs_0_.3, bf16[288,2048]{1,0:T(8,128)(2,1)} %bitcast.6, bf16[4,2048]{1,0:T(4,128)(2,1)} %refs_6_.2, f32[1,2048]{1,0:T(1,128)} %bitcast.9), custom_call_target="tpu_custom_call" | custom-call | tf_op jit(solution)/shard_map/conv_project/pallas_call | solution.py:310
  12.5 3.0 %collective-permute-done.2.refs_10_ = bf16[8,2048]{1,0:T(8,128)(2,1)S(1)} collective-permute-done((bf16[8,2048]{1,0:T(8,128)(2,1)S(1)}, bf16[8,2048]{1,0:T(8,128)(2,1)S(1)}, u32[]{:S(2)}, u32[]{:S(2)}) %collective-permute-start.2) | collective-permute-done | bytes 32800 | tf_op jit(solution)/shard_map/ppermute | solution.py:322
  15.5 0.0 collective-permute-done.1.refs_9_.refs_16_
  15.5 0.5 %collective-permute-done.refs_8_.refs_15_ = bf16[40,2048]{1,0:T(8,128)(2,1)S(1)} collective-permute-done((bf16[40,2048]{1,0:T(8,128)(2,1)S(1)}, bf16[40,2048]{1,0:T(8,128)(2,1)S(1)}, u32[]{:S(2)}, u32[]{:S(2)}) %collective-permute-start) | collective-permute-done | bytes 163872 | tf_op jit(solution)/shard_map/ppermute | solution.py:322
  16.0 0.1 copy-done.7
  16.1 0.1 copy-done.1
  16.2 0.5 %copy-done.2 = bf16[40,2048]{1,0:T(8,128)(2,1)} copy-done((bf16[40,2048]{1,0:T(8,128)(2,1)}, bf16[40,2048]{1,0:T(8,128)(2,1)S(1)}, u32[]{:S(2)}) %copy-start.2) | copy-done | bytes 163864
  16.6 2.8 %history.1 = (bf16[32,2048]{1,0:T(8,128)(2,1)}, bf16[288,256]{1,0:T(8,128)(2,1)}) custom-call(s32[32]{0:T(128)} %refs_0_.5, s32[32]{0:T(128)} %refs_1_.3, s32[32]{0:T(128)} %refs_2_.5, f32[32,2048]{1,0:T(8,128)} %get-tuple-element.10.refs_3_, bf16[288,256]{1,0:T(8,128)(2,1)} %get-tuple-element.11.refs_4_, bf16[288,2048]{1,0:T(8,128)(2,1)} %bitcast.7, ...), custom_call_target="tpu_custom_call" | custom-call | tf_op jit(solution)/shard_map/history/pallas_call | solution.py:310
  19.5 1.6 %collective-permute-start.3 = (bf16[288,256]{1,0:T(8,128)(2,1)}, bf16[288,256]{1,0:T(8,128)(2,1)S(1)}, u32[]{:S(2)}, u32[]{:S(2)}) collective-permute-start(bf16[288,256]{1,0:T(8,128)(2,1)} %get-tuple-element.13.refs_10_), channel_id=1, source_target_pairs={{0,2},{1,3},{2,0},{3,1},{4,6},{5,7},{6,4},{7,5},{8,10},{9,11},{10,... | collective-permute-start | bytes 442376 | tf_op jit(solution)/shard_map/ppermute | solution.py:322
  21.0 1.3 %collective-permute-start.6 = (bf16[40,2048]{1,0:T(8,128)(2,1)}, bf16[40,2048]{1,0:T(8,128)(2,1)S(1)}, u32[]{:S(2)}, u32[]{:S(2)}) collective-permute-start(bf16[40,2048]{1,0:T(8,128)(2,1)} %copy-done.1), channel_id=1, source_target_pairs={{0,4},{4,0},{8,12},{12,8},{1,5},{5,1},{9,13},{13,9},{2,6},{6,2},{1... | collective-permute-start | bytes 491528 | tf_op jit(solution)/shard_map/ppermute | solution.py:322
  22.3 0.0 collective-permute-start.5
  22.4 3.1 %collective-permute-done.3.refs_11_ = bf16[288,256]{1,0:T(8,128)(2,1)S(1)} collective-permute-done((bf16[288,256]{1,0:T(8,128)(2,1)}, bf16[288,256]{1,0:T(8,128)(2,1)S(1)}, u32[]{:S(2)}, u32[]{:S(2)}) %collective-permute-start.3) | collective-permute-done | bytes 147488 | tf_op jit(solution)/shard_map/ppermute | solution.py:322
  25.5 0.0 collective-permute-start.4
  25.5 0.0 collective-permute-done.5.refs_13_
  25.5 1.5 %collective-permute-done.6.refs_17_ = bf16[40,2048]{1,0:T(8,128)(2,1)S(1)} collective-permute-done((bf16[40,2048]{1,0:T(8,128)(2,1)}, bf16[40,2048]{1,0:T(8,128)(2,1)S(1)}, u32[]{:S(2)}, u32[]{:S(2)}) %collective-permute-start.6) | collective-permute-done | bytes 163872 | tf_op jit(solution)/shard_map/ppermute | solution.py:322
  27.0 0.0 collective-permute-done.4.refs_12_
  27.1 0.6 %copy-done.3 = bf16[40,2048]{1,0:T(8,128)(2,1)} copy-done((bf16[40,2048]{1,0:T(8,128)(2,1)}, bf16[40,2048]{1,0:T(8,128)(2,1)S(1)}, u32[]{:S(2)}) %copy-start.3) | copy-done | bytes 163864
  27.7 0.1 copy-done.6
  27.8 14.9 %dt_scan_gate.1 = (bf16[256,2048]{1,0:T(8,128)(2,1)}, bf16[128,2048]{1,0:T(8,128)(2,1)}) custom-call(s32[32]{0:T(128)} %refs_0_.5, s32[32]{0:T(128)} %refs_1_.3, s32[32]{0:T(128)} %refs_2_.5, bf16[256,2048]{1,0:T(8,128)(2,1)} %get-tuple-element.9.refs_3_, bf16[32,2048]{1,0:T(8,128)(2,1)} %get-tuple-element.12.refs_4_, bf16[256,2048]{1,0:T(8,128)(2,1)} %refs_5_.1, ...), custom_call_target="tpu_custom_call" | custom-call | tf_op jit(solution)/shard_map/dt_scan_gate/pallas_call | solution.py:310
  (13 shorter events, 0.1 us)
Async XLA Ops:
  2.4 13.6 %copy-start = (bf16[40,2048]{1,0:T(8,128)(2,1)}, bf16[40,2048]{1,0:T(8,128)(2,1)S(1)}, u32[]{:S(2)}) copy-start(bf16[40,2048]{1,0:T(8,128)(2,1)S(1)} %pad_maximum_fusion.refs_7_.refs_14_) | copy-start | bytes 491524
  2.4 13.1 %collective-permute-start.1 = (bf16[40,2048]{1,0:T(8,128)(2,1)S(1)}, bf16[40,2048]{1,0:T(8,128)(2,1)S(1)}, u32[]{:S(2)}, u32[]{:S(2)}) collective-permute-start(bf16[40,2048]{1,0:T(8,128)(2,1)S(1)} %pad_maximum_fusion.refs_7_.refs_14_), channel_id=1, source_target_pairs={{0,12},{4,8},{8,4},{12,0},{1,13},{5,9},{9,5},{13,1},{2,14},{6,10},... | collective-permute-start | bytes 491528 | tf_op jit(solution)/shard_map/ppermute | solution.py:322
  7.5 8.5 %collective-permute-start = (bf16[40,2048]{1,0:T(8,128)(2,1)S(1)}, bf16[40,2048]{1,0:T(8,128)(2,1)S(1)}, u32[]{:S(2)}, u32[]{:S(2)}) collective-permute-start(bf16[40,2048]{1,0:T(8,128)(2,1)S(1)} %pad_maximum_fusion.refs_7_.refs_14_), channel_id=1, source_target_pairs={{0,4},{4,0},{8,12},{12,8},{1,5},{5,1},{9,13},{13,9},{2,6},{6,2},{1... | collective-permute-start | bytes 491528 | tf_op jit(solution)/shard_map/ppermute | solution.py:322
  7.5 8.0 %collective-permute-start.2 = (bf16[8,2048]{1,0:T(8,128)(2,1)S(1)}, bf16[8,2048]{1,0:T(8,128)(2,1)S(1)}, u32[]{:S(2)}, u32[]{:S(2)}) collective-permute-start(bf16[8,2048]{1,0:T(8,128)(2,1)S(1)} %reshape.14), channel_id=1, source_target_pairs={{0,8},{4,12},{8,0},{12,4},{1,9},{5,13},{9,1},{13,5},{2,10},{6,14},... | collective-permute-start | bytes 98312 | tf_op jit(solution)/shard_map/ppermute | solution.py:322
  15.5 0.6 %copy-start.7 = (bf16[8,2048]{1,0:T(8,128)(2,1)}, bf16[8,2048]{1,0:T(8,128)(2,1)S(1)}, u32[]{:S(2)}) copy-start(bf16[8,2048]{1,0:T(8,128)(2,1)S(1)} %collective-permute-done.2.refs_10_) | copy-start | bytes 98308
  15.5 0.7 %copy-start.1 = (bf16[40,2048]{1,0:T(8,128)(2,1)}, bf16[40,2048]{1,0:T(8,128)(2,1)S(1)}, u32[]{:S(2)}) copy-start(bf16[40,2048]{1,0:T(8,128)(2,1)S(1)} %collective-permute-done.1.refs_9_.refs_16_) | copy-start | bytes 491524
  16.0 0.6 %copy-start.2 = (bf16[40,2048]{1,0:T(8,128)(2,1)}, bf16[40,2048]{1,0:T(8,128)(2,1)S(1)}, u32[]{:S(2)}) copy-start(bf16[40,2048]{1,0:T(8,128)(2,1)S(1)} %collective-permute-done.refs_8_.refs_15_) | copy-start | bytes 491524
  19.5 6.0 %collective-permute-start.3 = (bf16[288,256]{1,0:T(8,128)(2,1)}, bf16[288,256]{1,0:T(8,128)(2,1)S(1)}, u32[]{:S(2)}, u32[]{:S(2)}) collective-permute-start(bf16[288,256]{1,0:T(8,128)(2,1)} %get-tuple-element.13.refs_10_), channel_id=1, source_target_pairs={{0,2},{1,3},{2,0},{3,1},{4,6},{5,7},{6,4},{7,5},{8,10},{9,11},{10,... | collective-permute-start | bytes 442376 | tf_op jit(solution)/shard_map/ppermute | solution.py:322
  21.0 6.0 %collective-permute-start.6 = (bf16[40,2048]{1,0:T(8,128)(2,1)}, bf16[40,2048]{1,0:T(8,128)(2,1)S(1)}, u32[]{:S(2)}, u32[]{:S(2)}) collective-permute-start(bf16[40,2048]{1,0:T(8,128)(2,1)} %copy-done.1), channel_id=1, source_target_pairs={{0,4},{4,0},{8,12},{12,8},{1,5},{5,1},{9,13},{13,9},{2,6},{6,2},{1... | collective-permute-start | bytes 491528 | tf_op jit(solution)/shard_map/ppermute | solution.py:322
  22.3 3.2 %collective-permute-start.5 = (bf16[288,256]{1,0:T(8,128)(2,1)}, bf16[288,256]{1,0:T(8,128)(2,1)S(1)}, u32[]{:S(2)}, u32[]{:S(2)}) collective-permute-start(bf16[288,256]{1,0:T(8,128)(2,1)} %get-tuple-element.13.refs_10_), channel_id=1, source_target_pairs={{0,1},{1,0},{2,3},{3,2},{4,5},{5,4},{6,7},{7,6},{8,9},{9,8},{10,11... | collective-permute-start | bytes 442376 | tf_op jit(solution)/shard_map/ppermute | solution.py:322
  25.5 1.6 %copy-start.4 = (bf16[288,256]{1,0:T(8,128)(2,1)}, bf16[288,256]{1,0:T(8,128)(2,1)S(1)}, u32[]{:S(2)}) copy-start(bf16[288,256]{1,0:T(8,128)(2,1)S(1)} %collective-permute-done.3.refs_11_) | copy-start | bytes 442372
  25.5 1.5 %collective-permute-start.4 = (bf16[288,256]{1,0:T(8,128)(2,1)S(1)}, bf16[288,256]{1,0:T(8,128)(2,1)S(1)}, u32[]{:S(2)}, u32[]{:S(2)}) collective-permute-start(bf16[288,256]{1,0:T(8,128)(2,1)S(1)} %collective-permute-done.3.refs_11_), channel_id=1, source_target_pairs={{0,1},{1,0},{2,3},{3,2},{4,5},{5,4},{6,7},{7,6},{8,9},{9,8},{10,11... | collective-permute-start | bytes 442376 | tf_op jit(solution)/shard_map/ppermute | solution.py:322
  25.5 1.5 %copy-start.5 = (bf16[288,256]{1,0:T(8,128)(2,1)}, bf16[288,256]{1,0:T(8,128)(2,1)S(1)}, u32[]{:S(2)}) copy-start(bf16[288,256]{1,0:T(8,128)(2,1)S(1)} %collective-permute-done.5.refs_13_) | copy-start | bytes 442372
  27.0 0.7 %copy-start.3 = (bf16[40,2048]{1,0:T(8,128)(2,1)}, bf16[40,2048]{1,0:T(8,128)(2,1)S(1)}, u32[]{:S(2)}) copy-start(bf16[40,2048]{1,0:T(8,128)(2,1)S(1)} %collective-permute-done.6.refs_17_) | copy-start | bytes 491524
  27.0 0.7 %copy-start.6 = (bf16[288,256]{1,0:T(8,128)(2,1)}, bf16[288,256]{1,0:T(8,128)(2,1)S(1)}, u32[]{:S(2)}) copy-start(bf16[288,256]{1,0:T(8,128)(2,1)S(1)} %collective-permute-done.4.refs_12_) | copy-start | bytes 442372

commit v8 on v7

--- a/solution.py
+++ b/solution.py
@@ -10,7 +10,7 @@
 NEW = 32
 LANES = 128
 MIB = 1024 * 1024
-UNROLL = 8
+UNROLL = 16
 LOG2E = 1.4426950408889634
 F32, BF16 = jnp.float32, jnp.bfloat16
 NT = (((1,), (1,)), ((), ()))
@@ -122,18 +122,18 @@
 def history_kernel(dims, refs_in, refs_out, scratch):
     dims, block, firsts = dims
     per_dev, n_replica, slots, _ = dims
-    holder, slot_id, prefix_len, head_hbm, part_hbm, wt_hbm, cw_hbm = refs_in[:7]
-    pieces = refs_in[7:]
-    mixed_hbm, fixed_hbm = refs_out
-    h_s, s_s, l_s, head_v, part_v, wt_v, cw_v, mixed_v, sems, out_sems = scratch[:10]
+    holder, slot_id, prefix_len, head_hbm, wt_hbm, cw_hbm = refs_in[:6]
+    pieces = refs_in[6:]
+    mixed_hbm, part_hbm = refs_out
+    h_s, s_s, l_s, head_v, wt_v, cw_v, mixed_v, part_v, sems, out_sems = scratch[:10]
     held = scratch[10:]
     taps = cw_v.shape[0]
     pairs = [(holder, h_s), (slot_id, s_s), (prefix_len, l_s), (cw_hbm, cw_v), (head_hbm, head_v)]
-    pairs += list(zip(pieces, held)) + [(wt_hbm, wt_v), (part_hbm, part_v)]
+    pairs += list(zip(pieces, held)) + [(wt_hbm, wt_v)]
     copies = [pltpu.make_async_copy(src, dst, sems.at[i]) for i, (src, dst) in enumerate(pairs)]
     for copy in copies:
         copy.start()
-    for copy in copies[:-2]:
+    for copy in copies[:-1]:
         copy.wait()
 
     me = lax.axis_index("replica")
@@ -154,11 +154,9 @@
     mixed_v[...] = mixed
     mixed_out = pltpu.make_async_copy(mixed_v, mixed_hbm, out_sems.at[0])
     mixed_out.start()
-    copies[-2].wait()
-    part = lax.dot_general(wt_v[...], mixed, NT, preferred_element_type=F32).astype(BF16)
     copies[-1].wait()
-    part_v[:, : per_dev * taps] = part
-    part_out = pltpu.make_async_copy(part_v, fixed_hbm, out_sems.at[1])
+    part_v[...] = lax.dot_general(wt_v[...], mixed, NT, preferred_element_type=F32).T.astype(BF16)
+    part_out = pltpu.make_async_copy(part_v, part_hbm, out_sems.at[1])
     part_out.start()
     mixed_out.wait()
     part_out.wait()
@@ -168,15 +166,16 @@
     per_dev = dims[0]
     holder, slot_id, prefix_len, mixed_hbm, head_hbm, z_hbm, dtw_hbm, dtb_hbm, al_hbm, skip_hbm = refs_in[:10]
     out_hbm, state_hbm = refs_out
-    (h_s, s_s, l_s, mixed_v, z_v, dtw_v, dtb_v, al_v, skip_v, parts_v, cache_v, b_tab, c_tab, dt_v, drive_v,
+    (h_s, s_s, l_s, mixed_v, z_v, dtw_v, dtb_v, al_v, skip_v, parts_v, fixes_v, proj_v, cache_v, b_tab, c_tab, dt_v, drive_v,
      a_v, start_tm, final_tm, y_v, out_v, state_v, sems, out_sems) = scratch
     n_parts = parts_v.shape[0]
-    parts, pieces = refs_in[10 : 10 + n_parts], refs_in[10 + n_parts :]
+    parts, fixes, pieces = refs_in[10 : 10 + n_parts], refs_in[10 + n_parts : 10 + 2 * n_parts], refs_in[10 + 2 * n_parts :]
     head = head_hbm.shape[0]
     rows, channels = z_v.shape
     states = al_v.shape[0]
     rank = dtw_v.shape[0]
     pairs = [(part, parts_v.at[p]) for p, part in enumerate(parts)]
+    pairs += [(fix, fixes_v.at[p]) for p, fix in enumerate(fixes)]
     pairs += [(dtw_hbm, dtw_v), (dtb_hbm, dtb_v), (head_hbm, mixed_v.at[:head]), (mixed_hbm.at[head:], mixed_v.at[head:]),
               (skip_hbm, skip_v), (al_hbm, al_v), (holder, h_s), (slot_id, s_s), (prefix_len, l_s)]
     if len(pieces) == 1:
@@ -188,11 +187,17 @@
     for copy in copies:
         copy.start()
 
-    for copy in copies[: n_parts + 5]:
+    for copy in copies[: 2 * n_parts + 5]:
         copy.wait()
     projected = parts_v[0].astype(F32)
     for p in range(1, n_parts):
         projected = projected + parts_v[p].astype(F32)
+    fixed = fixes_v[0].astype(F32)
+    for p in range(1, n_parts):
+        fixed = fixed + fixes_v[p].astype(F32)
+    proj_v[...] = projected
+    proj_v[:, :head] = fixed.T
+    projected = proj_v[...]
     dt_low = projected[:rank].astype(BF16)
     late = projected[rank:].T
     n_tiles = channels // LANES
@@ -214,7 +219,7 @@
                 dt_v[tile, here, :] = dt
                 drive_v[tile, here, :] = dt * mixed
                 y_v[tile, here, :] = skip_v[:, lanes] * mixed
-    for copy in copies[n_parts + 5 : -1]:
+    for copy in copies[2 * n_parts + 5 : -1]:
         copy.wait()
     a_v[...] = jnp.exp(al_v[...]) * (-LOG2E)
 
@@ -315,7 +320,7 @@
         scratch_shapes=scratch,
         compiler_params=pltpu.CompilerParams(vmem_limit_bytes=limit * MIB),
         name=name,
-    )(*[value for value, _ in ins])
+    )(*[pltpu.with_memory_space_constraint(value, pltpu.HBM) if fixed else value for value, fixed in ins])
 
 
 def swap(value, axis, size, mask):
@@ -357,7 +362,7 @@
     head = per_dev * taps
     weights = x_proj_weight.T
     mixed, head_sums, part = call(
-        project_kernel, per_dev, "conv_project", 60,
+        project_kernel, per_dev, "conv_project", 40,
         [(x_new, True), (weights, True), (conv_weight, True), (conv_bias[None, :], True)],
         [((rows, channels), BF16), ((head, channels), F32), ((out_cols, rows), BF16)],
         [
@@ -374,19 +379,19 @@
             dma((n_chunks + 2,)),
         ],
     )
-    mixed_head, part = call(
-        history_kernel, (dims, block, firsts), "history", 60,
-        [(holder, True), (slot_id, True), (prefix_len, True), (head_sums, False), (part, False), (weights, True),
+    mixed_head, fix = call(
+        history_kernel, (dims, block, firsts), "history", 40,
+        [(holder, True), (slot_id, True), (prefix_len, True), (head_sums, False), (weights, True),
          (conv_weight, True)]
         + [(piece, False) for piece in conv_pieces],
-        [((head, channels), BF16), ((out_cols, rows), BF16)],
+        [((head, channels), BF16), ((head, out_cols), BF16)],
         ints + [
             vmem((head, channels), F32),
-            vmem((out_cols, rows), BF16),
             vmem((out_cols, channels), BF16),
             vmem((taps, channels), BF16),
             vmem((head, channels), BF16),
-            dma((7 + len(conv_pieces),)),
+            vmem((head, out_cols), BF16),
+            dma((6 + len(conv_pieces),)),
             dma((2,)),
         ] + [vmem(piece.shape, BF16) for piece in conv_pieces],
     )
@@ -395,14 +400,15 @@
     while mask:
         parts = parts + [swap(value, "tensor", n_tensor, mask) for value in reversed(parts)]
         mask //= 2
+    fixes = [fix] + [swap(fix, "tensor", n_tensor, k) for k in range(1, n_tensor)]
 
     blocks = (n_replica, block, channels)
     n_tiles = channels // LANES
     out, state = call(
-        scan_kernel, dims, "dt_scan_gate", 60,
+        scan_kernel, dims, "dt_scan_gate", 40,
         [(holder, True), (slot_id, True), (prefix_len, True), (mixed, False), (mixed_head, False), (z_new, True), (dt_proj_weight, True),
          (dt_bias[None, :], True), (a_log, True), (d_skip[None, :], True)]
-        + [(piece, False) for piece in parts + ssm_pieces],
+        + [(piece, False) for piece in parts + fixes + ssm_pieces],
         [((rows, channels), BF16), ((per_dev * states, channels), BF16)],
         ints + [
             vmem((rows, channels), BF16),
@@ -412,6 +418,8 @@
             vmem((states, channels), F32),
             vmem((1, channels), F32),
             vmem((n_tensor, out_cols, rows), BF16),
+            vmem((n_tensor, head, out_cols), BF16),
+            vmem((out_cols, rows), F32),
             vmem(blocks, BF16),
             vmem((states, rows, LANES), F32),
             vmem((states, rows, LANES), F32),
@@ -423,7 +431,7 @@
             vmem((n_tiles, rows + per_dev, LANES), F32),
             vmem((rows, channels), BF16),
             vmem((per_dev * states, channels), BF16),
-            dma((10 + n_tensor + len(ssm_pieces),)),
+            dma((10 + 2 * n_tensor + len(ssm_pieces),)),
             dma((2, n_chunks)),
         ],
     )

time: 42.9 us -> 44 us (1.026)
  starting transfers between devices: 8.65 us -> 10.6 us
  local copies, waits for them, and re-layouts: 2.14 us -> 0.79 us
  waiting for transfers between devices: 8.18 us -> 9.13 us
  Pallas kernels: 22.1 us -> 21.6 us
    ppermute x7 -> x10, starting transfers between devices: 8.65 us -> 10.6 us  [swap(): return lax.ppermute(value, axis, [(i, i ^ mask) for i in range(size)])]
    unnamed x17 -> x1, local copies, waits for them, and re-layouts: 2.1 us -> 0.76 us
    ppermute x7 -> x10, waiting for transfers between devices: 8.18 us -> 9.13 us  [swap(): return lax.ppermute(value, axis, [(i, i ^ mask) for i in range(size)])]
    pallas_call x3, Pallas kernels: 22.1 us -> 21.6 us  [call(): pl.pallas_call(split_refs(kernel, dims, len(ins), len(outs)), in_specs=[h...]
  transfers between devices with their start and end apart: 7 -> 10, of which waited for: 4 -> 4; matrix products, arithmetic and copies ran while one was open for 0% -> 0% of each run, Pallas kernels for 10% -> 15%
where the time goes in v8:
time: 44 us; the launch traced here: 43.7 us
  Pallas kernels  21.6 us (49%)
  starting transfers between devices  10.6 us (24%)
  waiting for transfers between devices  9.13 us (21%)
  other arithmetic  0.92 us (2%)
  local copies, waits for them, and re-layouts  0.79 us (2%)
  between operations  0.68 us (2%)
    pallas_call x3, Pallas kernels, call(): pl.pallas_call(split_refs(kernel, dims, len(ins), len(outs)), in_specs=[h...  21.6 us
    ppermute x10, starting transfers between devices, swap(): return lax.ppermute(value, axis, [(i, i ^ mask) for i in range(size)])  10.6 us
    ppermute x10, waiting for transfers between devices, swap(): return lax.ppermute(value, axis, [(i, i ^ mask) for i in range(size)])  9.13 us
    concatenate x1, other arithmetic, shards(): jnp.concatenate([cache_ssm.reshape(slots * states, channels), conv_rows])  0.92 us
  transfers between devices with their start and end apart: 10, of which 4 were waited for; matrix products, arithmetic and copies ran while one was open for 0% of the time, Pallas kernels for 15%

profile of v8, /device:TPU:0, one launch (start us, length us, event | category | flops | bytes accessed | tf_op | source)
XLA Modules:
  0.0 43.7 jit_solution(972727744001750967)
XLA Ops:
  0.6 0.8 %copy.17 = bf16[2,3,2048]{2,1,0:T(4,128)(2,1)S(1)} copy(bf16[2,3,2048]{2,0,1:T(2,128)(2,1)} %param.24) | data formatting | bytes 49152
  1.4 0.9 %pad_maximum_fusion.refs_6_.refs_18_ = bf16[40,2048]{1,0:T(8,128)(2,1)S(1)} fusion(bf16[8,2048]{1,0:T(8,128)(2,1)S(1)} %reshape.14, bf16[32,2048]{1,0:T(8,128)(2,1)} %bitcast.8), kind=kLoop, calls=%fused_computation | loop fusion | flops 327680 | bytes 327680 | tf_op jit(solution)/shard_map/concatenate | solution.py:343
  2.4 5.1 %collective-permute-start.1 = (bf16[40,2048]{1,0:T(8,128)(2,1)S(1)}, bf16[40,2048]{1,0:T(8,128)(2,1)S(1)}, u32[]{:S(2)}, u32[]{:S(2)}) collective-permute-start(bf16[40,2048]{1,0:T(8,128)(2,1)S(1)} %pad_maximum_fusion.refs_6_.refs_18_), channel_id=1, source_target_pairs={{0,12},{4,8},{8,4},{12,0},{1,13},{5,9},{9,5},{13,1},{2,14},{6,10},... | collective-permute-start | bytes 491528 | tf_op jit(solution)/shard_map/ppermute | solution.py:327
  7.5 3.9 %conv_project.1 = (bf16[256,2048]{1,0:T(8,128)(2,1)S(1)}, f32[32,2048]{1,0:T(8,128)S(1)}, bf16[288,256]{1,0:T(8,128)(2,1)S(1)}) custom-call(bf16[256,2048]{1,0:T(8,128)(2,1)} %refs_0_.3, bf16[288,2048]{1,0:T(8,128)(2,1)} %bitcast.6, bf16[4,2048]{1,0:T(4,128)(2,1)} %refs_5_.2, f32[1,2048]{1,0:T(1,128)} %bitcast.9), custom_call_target="tpu_custom_call" | custom-call | tf_op jit(solution)/shard_map/conv_project/pallas_call | solution.py:315
  11.4 1.6 %collective-permute-start.3 = (bf16[288,256]{1,0:T(8,128)(2,1)S(1)}, bf16[288,256]{1,0:T(8,128)(2,1)S(1)}, u32[]{:S(2)}, u32[]{:S(2)}) collective-permute-start(bf16[288,256]{1,0:T(8,128)(2,1)S(1)} %get-tuple-element.12.refs_10_), channel_id=1, source_target_pairs={{0,2},{1,3},{2,0},{3,1},{4,6},{5,7},{6,4},{7,5},{8,10},{9,11},{10,... | collective-permute-start | bytes 442376 | tf_op jit(solution)/shard_map/ppermute | solution.py:327
  12.9 0.0 collective-permute-start
  12.9 0.0 collective-permute-start.5
  12.9 0.0 collective-permute-done.1.refs_8_.refs_20_
  12.9 2.0 %collective-permute-start.9 = (bf16[40,2048]{1,0:T(8,128)(2,1)S(1)}, bf16[40,2048]{1,0:T(8,128)(2,1)S(1)}, u32[]{:S(2)}, u32[]{:S(2)}) collective-permute-start(bf16[40,2048]{1,0:T(8,128)(2,1)S(1)} %collective-permute-done.1.refs_8_.refs_20_), channel_id=1, source_target_pairs={{0,4},{4,0},{8,12},{12,8},{1,5},{5,1},{9,13},{13,9},{2,6},{6,2},{1... | collective-permute-start | bytes 491528 | tf_op jit(solution)/shard_map/ppermute | solution.py:327
  15.0 1.8 %collective-permute-done.3.refs_11_ = bf16[288,256]{1,0:T(8,128)(2,1)S(1)} collective-permute-done((bf16[288,256]{1,0:T(8,128)(2,1)S(1)}, bf16[288,256]{1,0:T(8,128)(2,1)S(1)}, u32[]{:S(2)}, u32[]{:S(2)}) %collective-permute-start.3) | collective-permute-done | bytes 147488 | tf_op jit(solution)/shard_map/ppermute | solution.py:327
  16.7 0.0 collective-permute-start.4
  16.7 0.0 collective-permute-start.2
  16.8 5.1 %collective-permute-done.2.refs_9_ = bf16[8,2048]{1,0:T(8,128)(2,1)S(1)} collective-permute-done((bf16[8,2048]{1,0:T(8,128)(2,1)S(1)}, bf16[8,2048]{1,0:T(8,128)(2,1)S(1)}, u32[]{:S(2)}, u32[]{:S(2)}) %collective-permute-start.2) | collective-permute-done | bytes 32800 | tf_op jit(solution)/shard_map/ppermute | solution.py:327
  21.8 0.0 collective-permute-done.refs_7_.refs_19_
  21.8 2.6 %history.1 = (bf16[32,2048]{1,0:T(8,128)(2,1)S(1)}, bf16[32,288]{1,0:T(8,128)(2,1)S(1)}) custom-call(s32[32]{0:T(128)} %refs_0_.5, s32[32]{0:T(128)} %refs_1_.3, s32[32]{0:T(128)} %refs_2_.5, f32[32,2048]{1,0:T(8,128)S(1)} %get-tuple-element.10.refs_3_, bf16[288,2048]{1,0:T(8,128)(2,1)} %bitcast.7, bf16[4,2048]{1,0:T(4,128)(2,1)} %refs_5_.2, ...), custom_call_target="tpu_custom_call" | custom-call | tf_op jit(solution)/shard_map/history/pallas_call | solution.py:315
  24.4 0.4 collective-permute-start.8
  24.8 1.2 %collective-permute-start.7 = (bf16[32,288]{1,0:T(8,128)(2,1)S(1)}, bf16[32,288]{1,0:T(8,128)(2,1)S(1)}, u32[]{:S(2)}, u32[]{:S(2)}) collective-permute-start(bf16[32,288]{1,0:T(8,128)(2,1)S(1)} %get-tuple-element.13.refs_14_), channel_id=1, source_target_pairs={{0,2},{1,3},{2,0},{3,1},{4,6},{5,7},{6,4},{7,5},{8,10},{9,11},{10,... | collective-permute-start | bytes 55304 | tf_op jit(solution)/shard_map/ppermute | solution.py:327
  26.0 0.3 collective-permute-start.6
  26.4 1.6 %collective-permute-done.8.refs_17_ = bf16[32,288]{1,0:T(8,128)(2,1)S(1)} collective-permute-done((bf16[32,288]{1,0:T(8,128)(2,1)S(1)}, bf16[32,288]{1,0:T(8,128)(2,1)S(1)}, u32[]{:S(2)}, u32[]{:S(2)}) %collective-permute-start.8) | collective-permute-done | bytes 18464 | tf_op jit(solution)/shard_map/ppermute | solution.py:327
  28.0 0.6 %collective-permute-done.7.refs_16_ = bf16[32,288]{1,0:T(8,128)(2,1)S(1)} collective-permute-done((bf16[32,288]{1,0:T(8,128)(2,1)S(1)}, bf16[32,288]{1,0:T(8,128)(2,1)S(1)}, u32[]{:S(2)}, u32[]{:S(2)}) %collective-permute-start.7) | collective-permute-done | bytes 18464 | tf_op jit(solution)/shard_map/ppermute | solution.py:327
  28.6 0.0 collective-permute-done.6.refs_15_
  28.6 0.0 collective-permute-done.4.refs_12_
  28.6 0.0 collective-permute-done.9.refs_21_
  28.6 15.1 %dt_scan_gate.1 = (bf16[256,2048]{1,0:T(8,128)(2,1)}, bf16[128,2048]{1,0:T(8,128)(2,1)}) custom-call(s32[32]{0:T(128)} %refs_0_.5, s32[32]{0:T(128)} %refs_1_.3, s32[32]{0:T(128)} %refs_2_.5, bf16[256,2048]{1,0:T(8,128)(2,1)S(1)} %get-tuple-element.9.refs_3_, bf16[32,2048]{1,0:T(8,128)(2,1)S(1)} %get-tuple-element.11.refs_4_, bf16[256,2048]{1,0:T(8,128)(2,1)} %refs_5_.3, ...), custom_call_target="tpu_custom_call" | custom-call | tf_op jit(solution)/shard_map/dt_scan_gate/pallas_call | solution.py:315
  (3 shorter events, 0.0 us)
Async XLA Ops:
  2.4 10.6 %collective-permute-start.1 = (bf16[40,2048]{1,0:T(8,128)(2,1)S(1)}, bf16[40,2048]{1,0:T(8,128)(2,1)S(1)}, u32[]{:S(2)}, u32[]{:S(2)}) collective-permute-start(bf16[40,2048]{1,0:T(8,128)(2,1)S(1)} %pad_maximum_fusion.refs_6_.refs_18_), channel_id=1, source_target_pairs={{0,12},{4,8},{8,4},{12,0},{1,13},{5,9},{9,5},{13,1},{2,14},{6,10},... | collective-permute-start | bytes 491528 | tf_op jit(solution)/shard_map/ppermute | solution.py:327
  11.4 5.4 %collective-permute-start.3 = (bf16[288,256]{1,0:T(8,128)(2,1)S(1)}, bf16[288,256]{1,0:T(8,128)(2,1)S(1)}, u32[]{:S(2)}, u32[]{:S(2)}) collective-permute-start(bf16[288,256]{1,0:T(8,128)(2,1)S(1)} %get-tuple-element.12.refs_10_), channel_id=1, source_target_pairs={{0,2},{1,3},{2,0},{3,1},{4,6},{5,7},{6,4},{7,5},{8,10},{9,11},{10,... | collective-permute-start | bytes 442376 | tf_op jit(solution)/shard_map/ppermute | solution.py:327
  12.9 8.9 %collective-permute-start = (bf16[40,2048]{1,0:T(8,128)(2,1)S(1)}, bf16[40,2048]{1,0:T(8,128)(2,1)S(1)}, u32[]{:S(2)}, u32[]{:S(2)}) collective-permute-start(bf16[40,2048]{1,0:T(8,128)(2,1)S(1)} %pad_maximum_fusion.refs_6_.refs_18_), channel_id=1, source_target_pairs={{0,4},{4,0},{8,12},{12,8},{1,5},{5,1},{9,13},{13,9},{2,6},{6,2},{1... | collective-permute-start | bytes 491528 | tf_op jit(solution)/shard_map/ppermute | solution.py:327
  12.9 13.1 %collective-permute-start.5 = (bf16[288,256]{1,0:T(8,128)(2,1)S(1)}, bf16[288,256]{1,0:T(8,128)(2,1)S(1)}, u32[]{:S(2)}, u32[]{:S(2)}) collective-permute-start(bf16[288,256]{1,0:T(8,128)(2,1)S(1)} %get-tuple-element.12.refs_10_), channel_id=1, source_target_pairs={{0,1},{1,0},{2,3},{3,2},{4,5},{5,4},{6,7},{7,6},{8,9},{9,8},{10,11... | collective-permute-start | bytes 442376 | tf_op jit(solution)/shard_map/ppermute | solution.py:327
  12.9 15.7 %collective-permute-start.9 = (bf16[40,2048]{1,0:T(8,128)(2,1)S(1)}, bf16[40,2048]{1,0:T(8,128)(2,1)S(1)}, u32[]{:S(2)}, u32[]{:S(2)}) collective-permute-start(bf16[40,2048]{1,0:T(8,128)(2,1)S(1)} %collective-permute-done.1.refs_8_.refs_20_), channel_id=1, source_target_pairs={{0,4},{4,0},{8,12},{12,8},{1,5},{5,1},{9,13},{13,9},{2,6},{6,2},{1... | collective-permute-start | bytes 491528 | tf_op jit(solution)/shard_map/ppermute | solution.py:327
  16.7 11.9 %collective-permute-start.4 = (bf16[288,256]{1,0:T(8,128)(2,1)S(1)}, bf16[288,256]{1,0:T(8,128)(2,1)S(1)}, u32[]{:S(2)}, u32[]{:S(2)}) collective-permute-start(bf16[288,256]{1,0:T(8,128)(2,1)S(1)} %collective-permute-done.3.refs_11_), channel_id=1, source_target_pairs={{0,1},{1,0},{2,3},{3,2},{4,5},{5,4},{6,7},{7,6},{8,9},{9,8},{10,11... | collective-permute-start | bytes 442376 | tf_op jit(solution)/shard_map/ppermute | solution.py:327
  16.7 5.1 %collective-permute-start.2 = (bf16[8,2048]{1,0:T(8,128)(2,1)S(1)}, bf16[8,2048]{1,0:T(8,128)(2,1)S(1)}, u32[]{:S(2)}, u32[]{:S(2)}) collective-permute-start(bf16[8,2048]{1,0:T(8,128)(2,1)S(1)} %reshape.14), channel_id=1, source_target_pairs={{0,8},{4,12},{8,0},{12,4},{1,9},{5,13},{9,1},{13,5},{2,10},{6,14},... | collective-permute-start | bytes 98312 | tf_op jit(solution)/shard_map/ppermute | solution.py:327
  24.4 3.6 %collective-permute-start.8 = (bf16[32,288]{1,0:T(8,128)(2,1)S(1)}, bf16[32,288]{1,0:T(8,128)(2,1)S(1)}, u32[]{:S(2)}, u32[]{:S(2)}) collective-permute-start(bf16[32,288]{1,0:T(8,128)(2,1)S(1)} %get-tuple-element.13.refs_14_), channel_id=1, source_target_pairs={{0,3},{1,2},{2,1},{3,0},{4,7},{5,6},{6,5},{7,4},{8,11},{9,10},{10,... | collective-permute-start | bytes 55304 | tf_op jit(solution)/shard_map/ppermute | solution.py:327
  24.8 3.8 %collective-permute-start.7 = (bf16[32,288]{1,0:T(8,128)(2,1)S(1)}, bf16[32,288]{1,0:T(8,128)(2,1)S(1)}, u32[]{:S(2)}, u32[]{:S(2)}) collective-permute-start(bf16[32,288]{1,0:T(8,128)(2,1)S(1)} %get-tuple-element.13.refs_14_), channel_id=1, source_target_pairs={{0,2},{1,3},{2,0},{3,1},{4,6},{5,7},{6,4},{7,5},{8,10},{9,11},{10,... | collective-permute-start | bytes 55304 | tf_op jit(solution)/shard_map/ppermute | solution.py:327
  26.0 2.6 %collective-permute-start.6 = (bf16[32,288]{1,0:T(8,128)(2,1)S(1)}, bf16[32,288]{1,0:T(8,128)(2,1)S(1)}, u32[]{:S(2)}, u32[]{:S(2)}) collective-permute-start(bf16[32,288]{1,0:T(8,128)(2,1)S(1)} %get-tuple-element.13.refs_14_), channel_id=1, source_target_pairs={{0,1},{1,0},{2,3},{3,2},{4,5},{5,4},{6,7},{7,6},{8,9},{9,8},{10,11... | collective-permute-start | bytes 55304 | tf_op jit(solution)/shard_map/ppermute | solution.py:327

commit v9 on v8

--- a/solution.py
+++ b/solution.py
@@ -10,7 +10,7 @@
 NEW = 32
 LANES = 128
 MIB = 1024 * 1024
-UNROLL = 16
+UNROLL = 8
 LOG2E = 1.4426950408889634
 F32, BF16 = jnp.float32, jnp.bfloat16
 NT = (((1,), (1,)), ((), ()))
@@ -67,7 +67,7 @@
 
 def project_kernel(dims, refs_in, refs_out, scratch):
     per_dev = dims
-    x_hbm, wt_hbm, cw_hbm, cb_hbm = refs_in
+    x_hbm, wt_hbm, cw_hbm, cb_hbm = refs_in[:4]
     mixed_hbm, head_hbm, part_hbm = refs_out
     x_v, wt_v, cw_v, cb_v, joined, mixed_v, head_v, part_f, part_v, sems, out_sems = scratch
     rows, channels = x_v.shape
@@ -349,10 +349,11 @@
         conv_two = swap(conv_rows, "replica", n_replica, 2)
         conv_pieces = [rows_all, near, far, conv_two]
         firsts = (0, block, 2 * block, 4 * block - slots * taps)
+        first_pieces = [conv_two]
         ssm_pieces = [rows_all, near, far, swap(far, "replica", n_replica, 1)]
     else:
         ssm_pieces = [lax.all_gather(rows_all, "replica")]
-        conv_pieces, firsts = [ssm_pieces[0].reshape(-1, channels)], (0,)
+        conv_pieces, firsts, first_pieces = [ssm_pieces[0].reshape(-1, channels)], (0,), []
 
     vmem, dma = pltpu.VMEM, pltpu.SemaphoreType.DMA
     ints = [pltpu.SMEM((requests,), jnp.int32)] * 3
@@ -363,7 +364,8 @@
     weights = x_proj_weight.T
     mixed, head_sums, part = call(
         project_kernel, per_dev, "conv_project", 40,
-        [(x_new, True), (weights, True), (conv_weight, True), (conv_bias[None, :], True)],
+        [(x_new, True), (weights, True), (conv_weight, True), (conv_bias[None, :], True)]
+        + [(piece, False) for piece in first_pieces],
         [((rows, channels), BF16), ((head, channels), F32), ((out_cols, rows), BF16)],
         [
             vmem((rows, channels), BF16),
@@ -381,8 +383,8 @@
     )
     mixed_head, fix = call(
         history_kernel, (dims, block, firsts), "history", 40,
-        [(holder, True), (slot_id, True), (prefix_len, True), (head_sums, False), (weights, True),
-         (conv_weight, True)]
+        [(holder, False), (slot_id, False), (prefix_len, False), (head_sums, False), (weights, False),
+         (conv_weight, False)]
         + [(piece, False) for piece in conv_pieces],
         [((head, channels), BF16), ((head, out_cols), BF16)],
         ints + [
@@ -406,8 +408,8 @@
     n_tiles = channels // LANES
     out, state = call(
         scan_kernel, dims, "dt_scan_gate", 40,
-        [(holder, True), (slot_id, True), (prefix_len, True), (mixed, False), (mixed_head, False), (z_new, True), (dt_proj_weight, True),
-         (dt_bias[None, :], True), (a_log, True), (d_skip[None, :], True)]
+        [(holder, False), (slot_id, False), (prefix_len, False), (mixed, False), (mixed_head, False), (z_new, False), (dt_proj_weight, False),
+         (dt_bias[None, :], False), (a_log, False), (d_skip[None, :], False)]
         + [(piece, False) for piece in parts + fixes + ssm_pieces],
         [((rows, channels), BF16), ((per_dev * states, channels), BF16)],
         ints + [

time: 44 us -> 42 us (0.955)
  waiting for transfers between devices: 9.13 us -> 4.55 us
  starting transfers between devices: 10.6 us -> 12.7 us
    ppermute x10, waiting for transfers between devices: 9.13 us -> 4.55 us  [swap(): return lax.ppermute(value, axis, [(i, i ^ mask) for i in range(size)])]
    ppermute x10, starting transfers between devices: 10.6 us -> 12.7 us  [swap(): return lax.ppermute(value, axis, [(i, i ^ mask) for i in range(size)])]
  transfers between devices with their start and end apart: 10 -> 10, of which waited for: 4 -> 3; matrix products, arithmetic and copies ran while one was open for 0% -> 2% of each run, Pallas kernels for 15% -> 15%
where the time goes in v9:
time: 42 us; the launch traced here: 41.8 us
  Pallas kernels  22 us (52%)
  starting transfers between devices  12.7 us (30%)
  waiting for transfers between devices  4.55 us (11%)
  other arithmetic  0.91 us (2%)
  local copies, waits for them, and re-layouts  0.85 us (2%)
  between operations  0.82 us (2%)
    pallas_call x3, Pallas kernels, call(): pl.pallas_call(split_refs(kernel, dims, len(ins), len(outs)), in_specs=[h...  22 us
    ppermute x10, starting transfers between devices, swap(): return lax.ppermute(value, axis, [(i, i ^ mask) for i in range(size)])  12.7 us
    ppermute x10, waiting for transfers between devices, swap(): return lax.ppermute(value, axis, [(i, i ^ mask) for i in range(size)])  4.55 us
    concatenate x1, other arithmetic, shards(): jnp.concatenate([cache_ssm.reshape(slots * states, channels), conv_rows])  0.91 us
  transfers between devices with their start and end apart: 10, of which 3 were waited for; matrix products, arithmetic and copies ran while one was open for 2% of the time, Pallas kernels for 15%

profile of v9, /device:TPU:0, one launch (start us, length us, event | category | flops | bytes accessed | tf_op | source)
XLA Modules:
  0.0 41.8 jit_solution(5368904589908019142)
XLA Ops:
  0.6 0.8 %copy.17 = bf16[2,3,2048]{2,1,0:T(4,128)(2,1)S(1)} copy(bf16[2,3,2048]{2,0,1:T(2,128)(2,1)} %param.24) | data formatting | bytes 49152
  1.4 4.1 %collective-permute-start = (bf16[8,2048]{1,0:T(8,128)(2,1)S(1)}, bf16[8,2048]{1,0:T(8,128)(2,1)S(1)}, u32[]{:S(2)}, u32[]{:S(2)}) collective-permute-start(bf16[8,2048]{1,0:T(8,128)(2,1)S(1)} %reshape.13), channel_id=1, source_target_pairs={{0,8},{4,12},{8,0},{12,4},{1,9},{5,13},{9,1},{13,5},{2,10},{6,14},... | collective-permute-start | bytes 98312 | tf_op jit(solution)/shard_map/ppermute | solution.py:327
  5.5 0.9 %pad_maximum_fusion.refs_6_.refs_18_ = bf16[40,2048]{1,0:T(8,128)(2,1)S(1)} fusion(bf16[8,2048]{1,0:T(8,128)(2,1)S(1)} %reshape.13, bf16[32,2048]{1,0:T(8,128)(2,1)} %bitcast.10), kind=kLoop, calls=%fused_computation | loop fusion | flops 327680 | bytes 327680 | tf_op jit(solution)/shard_map/concatenate | solution.py:343
  6.5 0.0 copy-start
  6.5 0.0 copy-start.4
  6.5 0.0 copy-start.7
  6.5 0.0 copy-start.8
  6.5 0.0 copy-start.9
  6.5 1.4 %collective-permute-start.2 = (bf16[40,2048]{1,0:T(8,128)(2,1)S(1)}, bf16[40,2048]{1,0:T(8,128)(2,1)S(1)}, u32[]{:S(2)}, u32[]{:S(2)}) collective-permute-start(bf16[40,2048]{1,0:T(8,128)(2,1)S(1)} %pad_maximum_fusion.refs_6_.refs_18_), channel_id=1, source_target_pairs={{0,12},{4,8},{8,4},{12,0},{1,13},{5,9},{9,5},{13,1},{2,14},{6,10},... | collective-permute-start | bytes 491528 | tf_op jit(solution)/shard_map/ppermute | solution.py:327
  7.9 4.0 %conv_project.1 = (bf16[256,2048]{1,0:T(8,128)(2,1)S(1)}, f32[32,2048]{1,0:T(8,128)S(1)}, bf16[288,256]{1,0:T(8,128)(2,1)S(1)}) custom-call(bf16[256,2048]{1,0:T(8,128)(2,1)} %refs_0_.3, bf16[288,2048]{1,0:T(8,128)(2,1)} %bitcast.6, bf16[4,2048]{1,0:T(4,128)(2,1)} %refs_5_.2, f32[1,2048]{1,0:T(1,128)} %bitcast.11, ...), custom_call_target="tpu_custom_call" | custom-call | tf_op jit(solution)/shard_map/conv_project/pallas_call | solution.py:315
  12.0 0.0 copy-start.1
  12.0 0.0 copy-start.3
  12.0 0.0 copy-start.5
  12.0 1.6 %collective-permute-start.3 = (bf16[288,256]{1,0:T(8,128)(2,1)S(1)}, bf16[288,256]{1,0:T(8,128)(2,1)S(1)}, u32[]{:S(2)}, u32[]{:S(2)}) collective-permute-start(bf16[288,256]{1,0:T(8,128)(2,1)S(1)} %get-tuple-element.12.refs_10_), channel_id=1, source_target_pairs={{0,2},{1,3},{2,0},{3,1},{4,6},{5,7},{6,4},{7,5},{8,10},{9,11},{10,... | collective-permute-start | bytes 442376 | tf_op jit(solution)/shard_map/ppermute | solution.py:327
  13.6 1.3 %collective-permute-start.1 = (bf16[40,2048]{1,0:T(8,128)(2,1)S(1)}, bf16[40,2048]{1,0:T(8,128)(2,1)S(1)}, u32[]{:S(2)}, u32[]{:S(2)}) collective-permute-start(bf16[40,2048]{1,0:T(8,128)(2,1)S(1)} %pad_maximum_fusion.refs_6_.refs_18_), channel_id=1, source_target_pairs={{0,4},{4,0},{8,12},{12,8},{1,5},{5,1},{9,13},{13,9},{2,6},{6,2},{1... | collective-permute-start | bytes 491528 | tf_op jit(solution)/shard_map/ppermute | solution.py:327
  15.0 2.3 %collective-permute-start.9 = (bf16[40,2048]{1,0:T(8,128)(2,1)S(1)}, bf16[40,2048]{1,0:T(8,128)(2,1)S(1)}, u32[]{:S(2)}, u32[]{:S(2)}) collective-permute-start(bf16[40,2048]{1,0:T(8,128)(2,1)S(1)} %collective-permute-done.2.refs_8_.refs_20_), channel_id=1, source_target_pairs={{0,4},{4,0},{8,12},{12,8},{1,5},{5,1},{9,13},{13,9},{2,6},{6,2},{1... | collective-permute-start | bytes 491528 | tf_op jit(solution)/shard_map/ppermute | solution.py:327
  17.3 2.5 %collective-permute-done.1.refs_7_.refs_19_ = bf16[40,2048]{1,0:T(8,128)(2,1)S(1)} collective-permute-done((bf16[40,2048]{1,0:T(8,128)(2,1)S(1)}, bf16[40,2048]{1,0:T(8,128)(2,1)S(1)}, u32[]{:S(2)}, u32[]{:S(2)}) %collective-permute-start.1) | collective-permute-done | bytes 163872 | tf_op jit(solution)/shard_map/ppermute | solution.py:327
  19.9 2.1 %history.1 = (bf16[32,2048]{1,0:T(8,128)(2,1)S(1)}, bf16[32,288]{1,0:T(8,128)(2,1)S(1)}) custom-call(s32[32]{0:T(128)S(1)} %copy-done.7, s32[32]{0:T(128)S(1)} %copy-done.8, s32[32]{0:T(128)S(1)} %copy-done.9, f32[32,2048]{1,0:T(8,128)S(1)} %get-tuple-element.10.refs_3_, bf16[288,2048]{1,0:T(8,128)(2,1)S(1)} %bitcast.7, bf16[4,2048]{1,0:T(4,128)(2,1)S(1)} %copy-done.4, ...), custom_call_target="tpu_custom_call" | custom-call | tf_op jit(solution)/shard_map/history/pallas_call | solution.py:315
  22.0 0.1 collective-permute-start.8
  22.1 0.2 collective-permute-start.7
  22.3 1.6 %collective-permute-start.6 = (bf16[32,288]{1,0:T(8,128)(2,1)S(1)}, bf16[32,288]{1,0:T(8,128)(2,1)S(1)}, u32[]{:S(2)}, u32[]{:S(2)}) collective-permute-start(bf16[32,288]{1,0:T(8,128)(2,1)S(1)} %get-tuple-element.13.refs_14_), channel_id=1, source_target_pairs={{0,1},{1,0},{2,3},{3,2},{4,5},{5,4},{6,7},{7,6},{8,9},{9,8},{10,11... | collective-permute-start | bytes 55304 | tf_op jit(solution)/shard_map/ppermute | solution.py:327
  23.9 1.4 %collective-permute-done.8.refs_17_ = bf16[32,288]{1,0:T(8,128)(2,1)S(1)} collective-permute-done((bf16[32,288]{1,0:T(8,128)(2,1)S(1)}, bf16[32,288]{1,0:T(8,128)(2,1)S(1)}, u32[]{:S(2)}, u32[]{:S(2)}) %collective-permute-start.8) | collective-permute-done | bytes 18464 | tf_op jit(solution)/shard_map/ppermute | solution.py:327
  25.3 0.7 %collective-permute-done.7.refs_16_ = bf16[32,288]{1,0:T(8,128)(2,1)S(1)} collective-permute-done((bf16[32,288]{1,0:T(8,128)(2,1)S(1)}, bf16[32,288]{1,0:T(8,128)(2,1)S(1)}, u32[]{:S(2)}, u32[]{:S(2)}) %collective-permute-start.7) | collective-permute-done | bytes 18464 | tf_op jit(solution)/shard_map/ppermute | solution.py:327
  26.0 15.8 %dt_scan_gate.1 = (bf16[256,2048]{1,0:T(8,128)(2,1)}, bf16[128,2048]{1,0:T(8,128)(2,1)}) custom-call(s32[32]{0:T(128)S(1)} %copy-done.7, s32[32]{0:T(128)S(1)} %copy-done.8, s32[32]{0:T(128)S(1)} %copy-done.9, bf16[256,2048]{1,0:T(8,128)(2,1)S(1)} %get-tuple-element.9.refs_3_, bf16[32,2048]{1,0:T(8,128)(2,1)S(1)} %get-tuple-element.11.refs_4_, ...), custom_call_target="tpu_custom_call" | custom-call | tf_op jit(solution)/shard_map/dt_scan_gate/pallas_call | solution.py:315
  (23 shorter events, 0.1 us)
Async XLA Ops:
  1.4 6.5 %collective-permute-start = (bf16[8,2048]{1,0:T(8,128)(2,1)S(1)}, bf16[8,2048]{1,0:T(8,128)(2,1)S(1)}, u32[]{:S(2)}, u32[]{:S(2)}) collective-permute-start(bf16[8,2048]{1,0:T(8,128)(2,1)S(1)} %reshape.13), channel_id=1, source_target_pairs={{0,8},{4,12},{8,0},{12,4},{1,9},{5,13},{9,1},{13,5},{2,10},{6,14},... | collective-permute-start | bytes 98312 | tf_op jit(solution)/shard_map/ppermute | solution.py:327
  6.5 13.4 %copy-start = (bf16[2048,288]{0,1:T(8,128)(2,1)S(1)}, bf16[2048,288]{0,1:T(8,128)(2,1)}, u32[]{:S(2)}) copy-start(bf16[2048,288]{0,1:T(8,128)(2,1)} %param.18) | copy-start | bytes 3538948
  6.5 13.4 %copy-start.4 = (bf16[4,2048]{1,0:T(4,128)(2,1)S(1)}, bf16[4,2048]{1,0:T(4,128)(2,1)}, u32[]{:S(2)}) copy-start(bf16[4,2048]{1,0:T(4,128)(2,1)} %refs_5_.2) | copy-start | bytes 49156
  6.5 13.4 %copy-start.7 = (s32[32]{0:T(128)S(1)}, s32[32]{0:T(128)}, u32[]{:S(2)}) copy-start(s32[32]{0:T(128)} %refs_0_.5) | copy-start | bytes 388
  6.5 13.4 %copy-start.8 = (s32[32]{0:T(128)S(1)}, s32[32]{0:T(128)}, u32[]{:S(2)}) copy-start(s32[32]{0:T(128)} %refs_1_.3) | copy-start | bytes 388
  6.5 13.3 %copy-start.9 = (s32[32]{0:T(128)S(1)}, s32[32]{0:T(128)}, u32[]{:S(2)}) copy-start(s32[32]{0:T(128)} %refs_2_.5) | copy-start | bytes 388
  6.5 8.5 %collective-permute-start.2 = (bf16[40,2048]{1,0:T(8,128)(2,1)S(1)}, bf16[40,2048]{1,0:T(8,128)(2,1)S(1)}, u32[]{:S(2)}, u32[]{:S(2)}) collective-permute-start(bf16[40,2048]{1,0:T(8,128)(2,1)S(1)} %pad_maximum_fusion.refs_6_.refs_18_), channel_id=1, source_target_pairs={{0,12},{4,8},{8,4},{12,0},{1,13},{5,9},{9,5},{13,1},{2,14},{6,10},... | collective-permute-start | bytes 491528 | tf_op jit(solution)/shard_map/ppermute | solution.py:327
  7.9 18.1 %copy-start.2 = (bf16[256,2048]{1,0:T(8,128)(2,1)S(1)}, bf16[256,2048]{1,0:T(8,128)(2,1)}, u32[]{:S(2)}) copy-start(bf16[256,2048]{1,0:T(8,128)(2,1)} %refs_6_.1) | copy-start | bytes 3145732
  12.0 14.0 %copy-start.1 = (bf16[256,2048]{1,0:T(8,128)(2,1)S(1)}, bf16[256,2048]{1,0:T(8,128)(2,1)}, u32[]{:S(2)}) copy-start(bf16[256,2048]{1,0:T(8,128)(2,1)} %refs_5_.3) | copy-start | bytes 3145732
  12.0 14.0 %copy-start.3 = (f32[16,2048]{1,0:T(8,128)S(1)}, f32[16,2048]{1,0:T(8,128)}, u32[]{:S(2)}) copy-start(f32[16,2048]{1,0:T(8,128)} %refs_8_.1) | copy-start | bytes 393220
  12.0 14.0 %copy-start.5 = (f32[2048]{0:T(1024)S(1)}, f32[2048]{0:T(1024)}, u32[]{:S(2)}) copy-start(f32[2048]{0:T(1024)} %param.20) | copy-start | bytes 24580
  12.0 14.0 %copy-start.6 = (f32[2048]{0:T(1024)S(1)}, f32[2048]{0:T(1024)}, u32[]{:S(2)}) copy-start(f32[2048]{0:T(1024)} %param.22) | copy-start | bytes 24580
  12.0 5.3 %collective-permute-start.3 = (bf16[288,256]{1,0:T(8,128)(2,1)S(1)}, bf16[288,256]{1,0:T(8,128)(2,1)S(1)}, u32[]{:S(2)}, u32[]{:S(2)}) collective-permute-start(bf16[288,256]{1,0:T(8,128)(2,1)S(1)} %get-tuple-element.12.refs_10_), channel_id=1, source_target_pairs={{0,2},{1,3},{2,0},{3,1},{4,6},{5,7},{6,4},{7,5},{8,10},{9,11},{10,... | collective-permute-start | bytes 442376 | tf_op jit(solution)/shard_map/ppermute | solution.py:327
  13.6 6.2 %collective-permute-start.1 = (bf16[40,2048]{1,0:T(8,128)(2,1)S(1)}, bf16[40,2048]{1,0:T(8,128)(2,1)S(1)}, u32[]{:S(2)}, u32[]{:S(2)}) collective-permute-start(bf16[40,2048]{1,0:T(8,128)(2,1)S(1)} %pad_maximum_fusion.refs_6_.refs_18_), channel_id=1, source_target_pairs={{0,4},{4,0},{8,12},{12,8},{1,5},{5,1},{9,13},{13,9},{2,6},{6,2},{1... | collective-permute-start | bytes 491528 | tf_op jit(solution)/shard_map/ppermute | solution.py:327
  15.0 7.3 %collective-permute-start.5 = (bf16[288,256]{1,0:T(8,128)(2,1)S(1)}, bf16[288,256]{1,0:T(8,128)(2,1)S(1)}, u32[]{:S(2)}, u32[]{:S(2)}) collective-permute-start(bf16[288,256]{1,0:T(8,128)(2,1)S(1)} %get-tuple-element.12.refs_10_), channel_id=1, source_target_pairs={{0,1},{1,0},{2,3},{3,2},{4,5},{5,4},{6,7},{7,6},{8,9},{9,8},{10,11... | collective-permute-start | bytes 442376 | tf_op jit(solution)/shard_map/ppermute | solution.py:327
  15.0 11.0 %collective-permute-start.9 = (bf16[40,2048]{1,0:T(8,128)(2,1)S(1)}, bf16[40,2048]{1,0:T(8,128)(2,1)S(1)}, u32[]{:S(2)}, u32[]{:S(2)}) collective-permute-start(bf16[40,2048]{1,0:T(8,128)(2,1)S(1)} %collective-permute-done.2.refs_8_.refs_20_), channel_id=1, source_target_pairs={{0,4},{4,0},{8,12},{12,8},{1,5},{5,1},{9,13},{13,9},{2,6},{6,2},{1... | collective-permute-start | bytes 491528 | tf_op jit(solution)/shard_map/ppermute | solution.py:327
  17.3 8.7 %collective-permute-start.4 = (bf16[288,256]{1,0:T(8,128)(2,1)S(1)}, bf16[288,256]{1,0:T(8,128)(2,1)S(1)}, u32[]{:S(2)}, u32[]{:S(2)}) collective-permute-start(bf16[288,256]{1,0:T(8,128)(2,1)S(1)} %collective-permute-done.3.refs_11_), channel_id=1, source_target_pairs={{0,1},{1,0},{2,3},{3,2},{4,5},{5,4},{6,7},{7,6},{8,9},{9,8},{10,11... | collective-permute-start | bytes 442376 | tf_op jit(solution)/shard_map/ppermute | solution.py:327
  22.0 3.3 %collective-permute-start.8 = (bf16[32,288]{1,0:T(8,128)(2,1)S(1)}, bf16[32,288]{1,0:T(8,128)(2,1)S(1)}, u32[]{:S(2)}, u32[]{:S(2)}) collective-permute-start(bf16[32,288]{1,0:T(8,128)(2,1)S(1)} %get-tuple-element.13.refs_14_), channel_id=1, source_target_pairs={{0,3},{1,2},{2,1},{3,0},{4,7},{5,6},{6,5},{7,4},{8,11},{9,10},{10,... | collective-permute-start | bytes 55304 | tf_op jit(solution)/shard_map/ppermute | solution.py:327
  22.1 3.9 %collective-permute-start.7 = (bf16[32,288]{1,0:T(8,128)(2,1)S(1)}, bf16[32,288]{1,0:T(8,128)(2,1)S(1)}, u32[]{:S(2)}, u32[]{:S(2)}) collective-permute-start(bf16[32,288]{1,0:T(8,128)(2,1)S(1)} %get-tuple-element.13.refs_14_), channel_id=1, source_target_pairs={{0,2},{1,3},{2,0},{3,1},{4,6},{5,7},{6,4},{7,5},{8,10},{9,11},{10,... | collective-permute-start | bytes 55304 | tf_op jit(solution)/shard_map/ppermute | solution.py:327
  22.3 3.7 %collective-permute-start.6 = (bf16[32,288]{1,0:T(8,128)(2,1)S(1)}, bf16[32,288]{1,0:T(8,128)(2,1)S(1)}, u32[]{:S(2)}, u32[]{:S(2)}) collective-permute-start(bf16[32,288]{1,0:T(8,128)(2,1)S(1)} %get-tuple-element.13.refs_14_), channel_id=1, source_target_pairs={{0,1},{1,0},{2,3},{3,2},{4,5},{5,4},{6,7},{7,6},{8,9},{9,8},{10,11... | collective-permute-start | bytes 55304 | tf_op jit(solution)/shard_map/ppermute | solution.py:327

commit v10 on v7

--- a/solution.py
+++ b/solution.py
@@ -122,77 +122,46 @@
 def history_kernel(dims, refs_in, refs_out, scratch):
     dims, block, firsts = dims
     per_dev, n_replica, slots, _ = dims
-    holder, slot_id, prefix_len, head_hbm, part_hbm, wt_hbm, cw_hbm = refs_in[:7]
+    holder, slot_id, prefix_len, head_ref, part_ref, wt_ref, cw_ref = refs_in[:7]
     pieces = refs_in[7:]
-    mixed_hbm, fixed_hbm = refs_out
-    h_s, s_s, l_s, head_v, part_v, wt_v, cw_v, mixed_v, sems, out_sems = scratch[:10]
-    held = scratch[10:]
-    taps = cw_v.shape[0]
-    pairs = [(holder, h_s), (slot_id, s_s), (prefix_len, l_s), (cw_hbm, cw_v), (head_hbm, head_v)]
-    pairs += list(zip(pieces, held)) + [(wt_hbm, wt_v), (part_hbm, part_v)]
-    copies = [pltpu.make_async_copy(src, dst, sems.at[i]) for i, (src, dst) in enumerate(pairs)]
-    for copy in copies:
-        copy.start()
-    for copy in copies[:-2]:
-        copy.wait()
-
+    mixed_ref, fixed_ref = refs_out
+    taps = cw_ref.shape[0]
     me = lax.axis_index("replica")
-    places, slot_ids, lengths = request_places(dims, (h_s, s_s, l_s), me)
+    places, slot_ids, lengths = request_places(dims, (holder, slot_id, prefix_len), me)
     tap, request = split_index(lax.broadcasted_iota(jnp.int32, (per_dev * taps, 1), 0), per_dev)
     starts = [places[r] * block + (block - slots * taps) + slot_ids[r] * taps for r in range(per_dev)]
     target = pick_rows(starts, request, per_dev) + tap
     live = (tap < taps - 1) & (taps - 1 - tap <= pick_rows(lengths, request, per_dev))
-    history = fetch_rows(target, live, [(first, ref[...]) for first, ref in zip(firsts, held)])
-    for t in range(taps - 1):
-        now = slice(t * per_dev, (t + 1) * per_dev)
-        summed = head_v[now]
+    history = fetch_rows(target, live, [(first, ref[...]) for first, ref in zip(firsts, pieces)])
+    sums = []
+    for t in range(taps):
+        summed = head_ref[t * per_dev : (t + 1) * per_dev]
         for k in range(taps - 1 - t):
-            weight = cw_v[k : k + 1].astype(F32)
+            weight = cw_ref[k : k + 1].astype(F32)
             summed = summed + history[(t + k) * per_dev : (t + k + 1) * per_dev] * weight
-        head_v[now] = summed
-    mixed = silu(head_v[...]).astype(BF16)
-    mixed_v[...] = mixed
-    mixed_out = pltpu.make_async_copy(mixed_v, mixed_hbm, out_sems.at[0])
-    mixed_out.start()
-    copies[-2].wait()
-    part = lax.dot_general(wt_v[...], mixed, NT, preferred_element_type=F32).astype(BF16)
-    copies[-1].wait()
-    part_v[:, : per_dev * taps] = part
-    part_out = pltpu.make_async_copy(part_v, fixed_hbm, out_sems.at[1])
-    part_out.start()
-    mixed_out.wait()
-    part_out.wait()
+        sums.append(summed)
+    mixed = silu(jnp.concatenate(sums, axis=0)).astype(BF16)
+    mixed_ref[...] = mixed
+    part = lax.dot_general(wt_ref[...], mixed, NT, preferred_element_type=F32)
+    fixed_ref[...] = part_ref[...]
+    fixed_ref[:, : per_dev * taps] = part.astype(BF16)
 
 
 def scan_kernel(dims, refs_in, refs_out, scratch):
-    per_dev = dims[0]
-    holder, slot_id, prefix_len, mixed_hbm, head_hbm, z_hbm, dtw_hbm, dtb_hbm, al_hbm, skip_hbm = refs_in[:10]
+    per_dev, n_replica, _, _ = dims
+    holder, slot_id, prefix_len, mixed_ref, head_ref, z_ref, dtw_ref, dtb_ref, al_ref, skip_ref = refs_in[:10]
     out_hbm, state_hbm = refs_out
-    (h_s, s_s, l_s, mixed_v, z_v, dtw_v, dtb_v, al_v, skip_v, parts_v, cache_v, b_tab, c_tab, dt_v, drive_v,
-     a_v, start_tm, final_tm, y_v, out_v, state_v, sems, out_sems) = scratch
-    n_parts = parts_v.shape[0]
-    parts, pieces = refs_in[10 : 10 + n_parts], refs_in[10 + n_parts :]
-    head = head_hbm.shape[0]
-    rows, channels = z_v.shape
-    states = al_v.shape[0]
-    rank = dtw_v.shape[0]
-    pairs = [(part, parts_v.at[p]) for p, part in enumerate(parts)]
-    pairs += [(dtw_hbm, dtw_v), (dtb_hbm, dtb_v), (head_hbm, mixed_v.at[:head]), (mixed_hbm.at[head:], mixed_v.at[head:]),
-              (skip_hbm, skip_v), (al_hbm, al_v), (holder, h_s), (slot_id, s_s), (prefix_len, l_s)]
-    if len(pieces) == 1:
-        pairs.append((pieces[0], cache_v))
-    else:
-        pairs += [(piece, cache_v.at[p]) for p, piece in enumerate(pieces)]
-    pairs.append((z_hbm, z_v))
-    copies = [pltpu.make_async_copy(src, dst, sems.at[i]) for i, (src, dst) in enumerate(pairs)]
-    for copy in copies:
-        copy.start()
-
-    for copy in copies[: n_parts + 5]:
-        copy.wait()
-    projected = parts_v[0].astype(F32)
-    for p in range(1, n_parts):
-        projected = projected + parts_v[p].astype(F32)
+    b_tab, c_tab, dt_v, drive_v, a_v, start_tm, final_tm, y_v, out_v, state_v, out_sems = scratch
+    n_pieces = sum(1 for ref in refs_in[10:] if ref.shape[-1] == z_ref.shape[1])
+    parts, pieces = refs_in[10:-n_pieces], refs_in[-n_pieces:]
+    rows, channels = z_ref.shape
+    states = al_ref.shape[0]
+    rank = dtw_ref.shape[0]
+    head = head_ref.shape[0]
+
+    projected = parts[0][...].astype(F32)
+    for part in parts[1:]:
+        projected = projected + part[...].astype(F32)
     dt_low = projected[:rank].astype(BF16)
     late = projected[rank:].T
     n_tiles = channels // LANES
@@ -202,31 +171,38 @@
         for n in range(c * per_chunk, (c + 1) * per_chunk):
             table = b_tab if n < states else c_tab
             table[n % states] = jnp.broadcast_to(late[:, n : n + 1], (rows, LANES))
-        weights = dtw_v[:, c * wide * LANES : (c + 1) * wide * LANES]
+        weights = dtw_ref[:, c * wide * LANES : (c + 1) * wide * LANES]
         raw = lax.dot_general(dt_low, weights, TN, preferred_element_type=F32)
         for j in range(wide):
             tile = c * wide + j
             lanes = slice(tile * LANES, (tile + 1) * LANES)
             for first in range(0, rows, LANES):
                 here = slice(first, first + LANES)
-                dt = softplus(raw[here, j * LANES : (j + 1) * LANES] + dtb_v[:, lanes])
-                mixed = mixed_v[here, lanes].astype(F32)
+                dt = softplus(raw[here, j * LANES : (j + 1) * LANES] + dtb_ref[:, lanes])
+                mixed = mixed_ref[here, lanes]
+                if first == 0:
+                    mixed = jnp.concatenate([head_ref[:, lanes], mixed[head:]], axis=0)
+                mixed = mixed.astype(F32)
                 dt_v[tile, here, :] = dt
                 drive_v[tile, here, :] = dt * mixed
-                y_v[tile, here, :] = skip_v[:, lanes] * mixed
-    for copy in copies[n_parts + 5 : -1]:
-        copy.wait()
-    a_v[...] = jnp.exp(al_v[...]) * (-LOG2E)
+                y_v[tile, here, :] = skip_ref[:, lanes] * mixed
+    a_v[...] = jnp.exp(al_ref[...]) * (-LOG2E)
 
     me = lax.axis_index("replica")
-    places, slot_ids, lengths = request_places(dims, (h_s, s_s, l_s), me)
+    places, slot_ids, lengths = request_places(dims, (holder, slot_id, prefix_len), me)
     for r in range(per_dev):
         spot = pl.ds(pl.multiple_of(slot_ids[r] * states, states), states)
         for tile in range(n_tiles):
-            value = cache_v[places[r], spot, tile * LANES : (tile + 1) * LANES].astype(F32)
+            lanes = slice(tile * LANES, (tile + 1) * LANES)
+            if n_pieces == 1:
+                value = pieces[0][places[r], spot, lanes]
+            else:
+                value = pieces[0][spot, lanes]
+                for p in range(1, n_pieces):
+                    value = jnp.where(places[r] == p, pieces[p][spot, lanes], value)
+            value = value.astype(F32)
             value = jnp.where(lengths[r] > 0, value, jnp.zeros_like(value))
             start_tm[tile, pl.ds(r, states, stride=per_dev), :] = value
-    copies[-1].wait()
 
     tiles = 2
     half = states // 2
@@ -279,7 +255,7 @@
             lanes = pl.ds(pl.multiple_of(tile * LANES, LANES), LANES)
             for r in range(per_dev):
                 here = slice(r * NEW, (r + 1) * NEW)
-                value = y_v[tile, pl.ds(r, NEW, stride=per_dev), :] * silu(z_v[here, lanes].astype(F32))
+                value = y_v[tile, pl.ds(r, NEW, stride=per_dev), :] * silu(z_ref[here, lanes].astype(F32))
                 out_v[here, lanes] = value.astype(BF16)
                 final = final_tm[tile, pl.ds(r, states, stride=per_dev), :]
                 state_v[r * states : (r + 1) * states, lanes] = final.astype(BF16)
@@ -305,17 +281,19 @@
 
 
 def call(kernel, dims, name, limit, ins, outs, scratch):
-    hbm = pl.BlockSpec(memory_space=pltpu.HBM)
-    anywhere = pl.BlockSpec(memory_space=pl.ANY)
+    spaces = {"hbm": pltpu.HBM, "any": pl.ANY, "vmem": pltpu.VMEM, "smem": pltpu.SMEM}
+    values = [
+        pltpu.with_memory_space_constraint(value, pltpu.HBM) if place == "hbm" else value for value, place in ins
+    ]
     return pl.pallas_call(
         split_refs(kernel, dims, len(ins), len(outs)),
-        in_specs=[hbm if fixed else anywhere for _, fixed in ins],
-        out_specs=[anywhere] * len(outs),
-        out_shape=[jax.ShapeDtypeStruct(*out) for out in outs],
+        in_specs=[pl.BlockSpec(memory_space=spaces[place]) for _, place in ins],
+        out_specs=[pl.BlockSpec(memory_space=spaces[place]) for _, _, place in outs],
+        out_shape=[jax.ShapeDtypeStruct(shape, dtype) for shape, dtype, _ in outs],
         scratch_shapes=scratch,
         compiler_params=pltpu.CompilerParams(vmem_limit_bytes=limit * MIB),
         name=name,
-    )(*[value for value, _ in ins])
+    )(*values)
 
 
 def swap(value, axis, size, mask):
@@ -350,16 +328,16 @@
         conv_pieces, firsts = [ssm_pieces[0].reshape(-1, channels)], (0,)
 
     vmem, dma = pltpu.VMEM, pltpu.SemaphoreType.DMA
-    ints = [pltpu.SMEM((requests,), jnp.int32)] * 3
     n_chunks = channels // min(512, channels)
     dims = (per_dev, n_replica, slots, relative)
-
     head = per_dev * taps
     weights = x_proj_weight.T
+    requests = [(holder, "smem"), (slot_id, "smem"), (prefix_len, "smem")]
+
     mixed, head_sums, part = call(
-        project_kernel, per_dev, "conv_project", 60,
-        [(x_new, True), (weights, True), (conv_weight, True), (conv_bias[None, :], True)],
-        [((rows, channels), BF16), ((head, channels), F32), ((out_cols, rows), BF16)],
+        project_kernel, per_dev, "conv_project", 40,
+        [(x_new, "hbm"), (weights, "hbm"), (conv_weight, "hbm"), (conv_bias[None, :], "hbm")],
+        [((rows, channels), BF16, "any"), ((head, channels), F32, "any"), ((out_cols, rows), BF16, "any")],
         [
             vmem((rows, channels), BF16),
             vmem((out_cols, channels), BF16),
@@ -375,20 +353,11 @@
         ],
     )
     mixed_head, part = call(
-        history_kernel, (dims, block, firsts), "history", 60,
-        [(holder, True), (slot_id, True), (prefix_len, True), (head_sums, False), (part, False), (weights, True),
-         (conv_weight, True)]
-        + [(piece, False) for piece in conv_pieces],
-        [((head, channels), BF16), ((out_cols, rows), BF16)],
-        ints + [
-            vmem((head, channels), F32),
-            vmem((out_cols, rows), BF16),
-            vmem((out_cols, channels), BF16),
-            vmem((taps, channels), BF16),
-            vmem((head, channels), BF16),
-            dma((7 + len(conv_pieces),)),
-            dma((2,)),
-        ] + [vmem(piece.shape, BF16) for piece in conv_pieces],
+        history_kernel, (dims, block, firsts), "history", 20,
+        requests
+        + [(value, "vmem") for value in [head_sums, part, weights, conv_weight] + conv_pieces],
+        [((head, channels), BF16, "vmem"), ((out_cols, rows), BF16, "vmem")],
+        [],
     )
     parts = [part]
     mask = n_tensor // 2
@@ -396,23 +365,13 @@
         parts = parts + [swap(value, "tensor", n_tensor, mask) for value in reversed(parts)]
         mask //= 2
 
-    blocks = (n_replica, block, channels)
     n_tiles = channels // LANES
+    operands = [mixed, mixed_head, z_new, dt_proj_weight, dt_bias[None, :], a_log, d_skip[None, :]]
     out, state = call(
-        scan_kernel, dims, "dt_scan_gate", 60,
-        [(holder, True), (slot_id, True), (prefix_len, True), (mixed, False), (mixed_head, False), (z_new, True), (dt_proj_weight, True),
-         (dt_bias[None, :], True), (a_log, True), (d_skip[None, :], True)]
-        + [(piece, False) for piece in parts + ssm_pieces],
-        [((rows, channels), BF16), ((per_dev * states, channels), BF16)],
-        ints + [
-            vmem((rows, channels), BF16),
-            vmem((rows, channels), BF16),
-            vmem((rank, channels), BF16),
-            vmem((1, channels), F32),
-            vmem((states, channels), F32),
-            vmem((1, channels), F32),
-            vmem((n_tensor, out_cols, rows), BF16),
-            vmem(blocks, BF16),
+        scan_kernel, dims, "dt_scan_gate", 40,
+        requests + [(value, "vmem") for value in operands + parts + ssm_pieces],
+        [((rows, channels), BF16, "any"), ((per_dev * states, channels), BF16, "any")],
+        [
             vmem((states, rows, LANES), F32),
             vmem((states, rows, LANES), F32),
             vmem((n_tiles, rows, LANES), F32),
@@ -423,7 +382,6 @@
             vmem((n_tiles, rows + per_dev, LANES), F32),
             vmem((rows, channels), BF16),
             vmem((per_dev * states, channels), BF16),
-            dma((10 + n_tensor + len(ssm_pieces),)),
             dma((2, n_chunks)),
         ],
     )

time: 42.9 us -> 38.6 us (0.90)
  Pallas kernels: 22.1 us -> 18.8 us
  local copies, waits for them, and re-layouts: 2.14 us -> 0.85 us
    pallas_call x3, Pallas kernels: 22.1 us -> 18.8 us  [call(): pl.pallas_call(split_refs(kernel, dims, len(ins), len(outs)), in_specs=[p...]
    unnamed x17 -> x21, local copies, waits for them, and re-layouts: 2.1 us -> 0.82 us
where the time goes in v10:
time: 38.6 us; the launch traced here: 38.4 us
  Pallas kernels  18.8 us (49%)
  starting transfers between devices  8.65 us (22%)
  waiting for transfers between devices  8.37 us (22%)
  other arithmetic  0.92 us (2%)
  local copies, waits for them, and re-layouts  0.85 us (2%)
  between operations  0.79 us (2%)
    pallas_call x3, Pallas kernels, call(): pl.pallas_call(split_refs(kernel, dims, len(ins), len(outs)), in_specs=[p...  18.8 us
    ppermute x7, starting transfers between devices, swap(): return lax.ppermute(value, axis, [(i, i ^ mask) for i in range(size)])  8.65 us
    ppermute x7, waiting for transfers between devices, swap(): return lax.ppermute(value, axis, [(i, i ^ mask) for i in range(size)])  8.37 us
    concatenate x1, other arithmetic, shards(): jnp.concatenate([cache_ssm.reshape(slots * states, channels), conv_rows])  0.92 us
    unnamed x21, local copies, waits for them, and re-layouts  0.82 us
  transfers between devices with their start and end apart: 7, of which 4 were waited for; matrix products, arithmetic and copies ran while one was open for 0% of the time, Pallas kernels for 10%

profile of v10, /device:TPU:0, one launch (start us, length us, event | category | flops | bytes accessed | tf_op | source)
XLA Modules:
  0.0 38.4 jit_solution(14319288689957135600)
XLA Ops:
  0.6 0.8 %copy.17 = bf16[2,3,2048]{2,1,0:T(4,128)(2,1)S(1)} copy(bf16[2,3,2048]{2,0,1:T(2,128)(2,1)} %param.24) | data formatting | bytes 49152
  1.4 0.9 %pad_maximum_fusion.refs_7_.refs_14_ = bf16[40,2048]{1,0:T(8,128)(2,1)S(1)} fusion(bf16[8,2048]{1,0:T(8,128)(2,1)S(1)} %reshape.14, bf16[32,2048]{1,0:T(8,128)(2,1)} %bitcast.10), kind=kLoop, calls=%fused_computation | loop fusion | flops 327680 | bytes 327680 | tf_op jit(solution)/shard_map/concatenate | solution.py:316
  2.4 0.0 copy-start
  2.4 0.0 copy-start.4
  2.4 0.0 copy-start.7
  2.4 0.0 copy-start.8
  2.4 0.0 copy-start.9
  2.4 5.1 %collective-permute-start.1 = (bf16[40,2048]{1,0:T(8,128)(2,1)S(1)}, bf16[40,2048]{1,0:T(8,128)(2,1)S(1)}, u32[]{:S(2)}, u32[]{:S(2)}) collective-permute-start(bf16[40,2048]{1,0:T(8,128)(2,1)S(1)} %pad_maximum_fusion.refs_7_.refs_14_), channel_id=1, source_target_pairs={{0,12},{4,8},{8,4},{12,0},{1,13},{5,9},{9,5},{13,1},{2,14},{6,10},... | collective-permute-start | bytes 491528 | tf_op jit(solution)/shard_map/ppermute | solution.py:300
  7.5 0.0 collective-permute-start
  7.5 0.6 %collective-permute-start.2 = (bf16[8,2048]{1,0:T(8,128)(2,1)S(1)}, bf16[8,2048]{1,0:T(8,128)(2,1)S(1)}, u32[]{:S(2)}, u32[]{:S(2)}) collective-permute-start(bf16[8,2048]{1,0:T(8,128)(2,1)S(1)} %reshape.14), channel_id=1, source_target_pairs={{0,8},{4,12},{8,0},{12,4},{1,9},{5,13},{9,1},{13,5},{2,10},{6,14},... | collective-permute-start | bytes 98312 | tf_op jit(solution)/shard_map/ppermute | solution.py:300
  8.2 3.9 %conv_project.1 = (bf16[256,2048]{1,0:T(8,128)(2,1)S(1)}, f32[32,2048]{1,0:T(8,128)S(1)}, bf16[288,256]{1,0:T(8,128)(2,1)S(1)}) custom-call(bf16[256,2048]{1,0:T(8,128)(2,1)} %refs_0_.3, bf16[288,2048]{1,0:T(8,128)(2,1)} %bitcast.6, bf16[4,2048]{1,0:T(4,128)(2,1)} %refs_6_.2, f32[1,2048]{1,0:T(1,128)} %bitcast.11), custom_call_target="tpu_custom_call" | custom-call | tf_op jit(solution)/shard_map/conv_project/pallas_call | solution.py:288
  12.1 0.0 copy-start.1
  12.1 0.0 copy-start.2
  12.1 0.0 copy-start.5
  12.2 0.0 copy-start.6
  12.2 3.4 %collective-permute-done.2.refs_10_ = bf16[8,2048]{1,0:T(8,128)(2,1)S(1)} collective-permute-done((bf16[8,2048]{1,0:T(8,128)(2,1)S(1)}, bf16[8,2048]{1,0:T(8,128)(2,1)S(1)}, u32[]{:S(2)}, u32[]{:S(2)}) %collective-permute-start.2) | collective-permute-done | bytes 32800 | tf_op jit(solution)/shard_map/ppermute | solution.py:300
  15.6 0.5 %collective-permute-done.refs_8_.refs_15_ = bf16[40,2048]{1,0:T(8,128)(2,1)S(1)} collective-permute-done((bf16[40,2048]{1,0:T(8,128)(2,1)S(1)}, bf16[40,2048]{1,0:T(8,128)(2,1)S(1)}, u32[]{:S(2)}, u32[]{:S(2)}) %collective-permute-start) | collective-permute-done | bytes 163872 | tf_op jit(solution)/shard_map/ppermute | solution.py:300
  16.1 1.3 %history.1 = (bf16[32,2048]{1,0:T(8,128)(2,1)S(1)}, bf16[288,256]{1,0:T(8,128)(2,1)S(1)}) custom-call(s32[32]{0:T(128)S(1)} %copy-done.7, s32[32]{0:T(128)S(1)} %copy-done.8, s32[32]{0:T(128)S(1)} %copy-done.9, f32[32,2048]{1,0:T(8,128)S(1)} %get-tuple-element.10.refs_3_, bf16[288,256]{1,0:T(8,128)(2,1)S(1)} %get-tuple-element.11.refs_4_, ...), custom_call_target="tpu_custom_call" | custom-call | tf_op jit(solution)/shard_map/history/pallas_call | solution.py:288
  17.4 1.6 %collective-permute-start.3 = (bf16[288,256]{1,0:T(8,128)(2,1)S(1)}, bf16[288,256]{1,0:T(8,128)(2,1)S(1)}, u32[]{:S(2)}, u32[]{:S(2)}) collective-permute-start(bf16[288,256]{1,0:T(8,128)(2,1)S(1)} %get-tuple-element.13.refs_10_), channel_id=1, source_target_pairs={{0,2},{1,3},{2,0},{3,1},{4,6},{5,7},{6,4},{7,5},{8,10},{9,11},{10,... | collective-permute-start | bytes 442376 | tf_op jit(solution)/shard_map/ppermute | solution.py:300
  19.0 1.3 %collective-permute-start.6 = (bf16[40,2048]{1,0:T(8,128)(2,1)S(1)}, bf16[40,2048]{1,0:T(8,128)(2,1)S(1)}, u32[]{:S(2)}, u32[]{:S(2)}) collective-permute-start(bf16[40,2048]{1,0:T(8,128)(2,1)S(1)} %collective-permute-done.1.refs_9_.refs_16_), channel_id=1, source_target_pairs={{0,4},{4,0},{8,12},{12,8},{1,5},{5,1},{9,13},{13,9},{2,6},{6,2},{1... | collective-permute-start | bytes 491528 | tf_op jit(solution)/shard_map/ppermute | solution.py:300
  20.3 0.0 collective-permute-start.5
  20.3 2.9 %collective-permute-done.3.refs_11_ = bf16[288,256]{1,0:T(8,128)(2,1)S(1)} collective-permute-done((bf16[288,256]{1,0:T(8,128)(2,1)S(1)}, bf16[288,256]{1,0:T(8,128)(2,1)S(1)}, u32[]{:S(2)}, u32[]{:S(2)}) %collective-permute-start.3) | collective-permute-done | bytes 147488 | tf_op jit(solution)/shard_map/ppermute | solution.py:300
  23.2 1.6 %collective-permute-done.6.refs_17_ = bf16[40,2048]{1,0:T(8,128)(2,1)S(1)} collective-permute-done((bf16[40,2048]{1,0:T(8,128)(2,1)S(1)}, bf16[40,2048]{1,0:T(8,128)(2,1)S(1)}, u32[]{:S(2)}, u32[]{:S(2)}) %collective-permute-start.6) | collective-permute-done | bytes 163872 | tf_op jit(solution)/shard_map/ppermute | solution.py:300
  24.8 13.6 %dt_scan_gate.1 = (bf16[256,2048]{1,0:T(8,128)(2,1)}, bf16[128,2048]{1,0:T(8,128)(2,1)}) custom-call(s32[32]{0:T(128)S(1)} %copy-done.7, s32[32]{0:T(128)S(1)} %copy-done.8, s32[32]{0:T(128)S(1)} %copy-done.9, bf16[256,2048]{1,0:T(8,128)(2,1)S(1)} %get-tuple-element.9.refs_3_, bf16[32,2048]{1,0:T(8,128)(2,1)S(1)} %get-tuple-element.12.refs_4_, ...), custom_call_target="tpu_custom_call" | custom-call | tf_op jit(solution)/shard_map/dt_scan_gate/pallas_call | solution.py:288
  (17 shorter events, 0.1 us)
Async XLA Ops:
  2.4 13.7 %copy-start = (bf16[2048,288]{0,1:T(8,128)(2,1)S(1)}, bf16[2048,288]{0,1:T(8,128)(2,1)}, u32[]{:S(2)}) copy-start(bf16[2048,288]{0,1:T(8,128)(2,1)} %param.18) | copy-start | bytes 3538948
  2.4 13.7 %copy-start.4 = (bf16[4,2048]{1,0:T(4,128)(2,1)S(1)}, bf16[4,2048]{1,0:T(4,128)(2,1)}, u32[]{:S(2)}) copy-start(bf16[4,2048]{1,0:T(4,128)(2,1)} %refs_6_.2) | copy-start | bytes 49156
  2.4 13.7 %copy-start.7 = (s32[32]{0:T(128)S(1)}, s32[32]{0:T(128)}, u32[]{:S(2)}) copy-start(s32[32]{0:T(128)} %refs_0_.5) | copy-start | bytes 388
  2.4 13.7 %copy-start.8 = (s32[32]{0:T(128)S(1)}, s32[32]{0:T(128)}, u32[]{:S(2)}) copy-start(s32[32]{0:T(128)} %refs_1_.3) | copy-start | bytes 388
  2.4 13.7 %copy-start.9 = (s32[32]{0:T(128)S(1)}, s32[32]{0:T(128)}, u32[]{:S(2)}) copy-start(s32[32]{0:T(128)} %refs_2_.5) | copy-start | bytes 388
  2.4 13.1 %collective-permute-start.1 = (bf16[40,2048]{1,0:T(8,128)(2,1)S(1)}, bf16[40,2048]{1,0:T(8,128)(2,1)S(1)}, u32[]{:S(2)}, u32[]{:S(2)}) collective-permute-start(bf16[40,2048]{1,0:T(8,128)(2,1)S(1)} %pad_maximum_fusion.refs_7_.refs_14_), channel_id=1, source_target_pairs={{0,12},{4,8},{8,4},{12,0},{1,13},{5,9},{9,5},{13,1},{2,14},{6,10},... | collective-permute-start | bytes 491528 | tf_op jit(solution)/shard_map/ppermute | solution.py:300
  7.5 8.5 %collective-permute-start = (bf16[40,2048]{1,0:T(8,128)(2,1)S(1)}, bf16[40,2048]{1,0:T(8,128)(2,1)S(1)}, u32[]{:S(2)}, u32[]{:S(2)}) collective-permute-start(bf16[40,2048]{1,0:T(8,128)(2,1)S(1)} %pad_maximum_fusion.refs_7_.refs_14_), channel_id=1, source_target_pairs={{0,4},{4,0},{8,12},{12,8},{1,5},{5,1},{9,13},{13,9},{2,6},{6,2},{1... | collective-permute-start | bytes 491528 | tf_op jit(solution)/shard_map/ppermute | solution.py:300
  7.5 8.0 %collective-permute-start.2 = (bf16[8,2048]{1,0:T(8,128)(2,1)S(1)}, bf16[8,2048]{1,0:T(8,128)(2,1)S(1)}, u32[]{:S(2)}, u32[]{:S(2)}) collective-permute-start(bf16[8,2048]{1,0:T(8,128)(2,1)S(1)} %reshape.14), channel_id=1, source_target_pairs={{0,8},{4,12},{8,0},{12,4},{1,9},{5,13},{9,1},{13,5},{2,10},{6,14},... | collective-permute-start | bytes 98312 | tf_op jit(solution)/shard_map/ppermute | solution.py:300
  8.2 16.6 %copy-start.3 = (f32[16,2048]{1,0:T(8,128)S(1)}, f32[16,2048]{1,0:T(8,128)}, u32[]{:S(2)}) copy-start(f32[16,2048]{1,0:T(8,128)} %refs_8_.1) | copy-start | bytes 393220
  12.1 12.7 %copy-start.1 = (bf16[256,2048]{1,0:T(8,128)(2,1)S(1)}, bf16[256,2048]{1,0:T(8,128)(2,1)}, u32[]{:S(2)}) copy-start(bf16[256,2048]{1,0:T(8,128)(2,1)} %refs_5_.1) | copy-start | bytes 3145732
  12.1 12.7 %copy-start.2 = (bf16[256,2048]{1,0:T(8,128)(2,1)S(1)}, bf16[256,2048]{1,0:T(8,128)(2,1)}, u32[]{:S(2)}) copy-start(bf16[256,2048]{1,0:T(8,128)(2,1)} %refs_6_.3) | copy-start | bytes 3145732
  12.1 12.7 %copy-start.5 = (f32[2048]{0:T(1024)S(1)}, f32[2048]{0:T(1024)}, u32[]{:S(2)}) copy-start(f32[2048]{0:T(1024)} %param.20) | copy-start | bytes 24580
  12.2 12.7 %copy-start.6 = (f32[2048]{0:T(1024)S(1)}, f32[2048]{0:T(1024)}, u32[]{:S(2)}) copy-start(f32[2048]{0:T(1024)} %param.22) | copy-start | bytes 24580
  17.4 5.8 %collective-permute-start.3 = (bf16[288,256]{1,0:T(8,128)(2,1)S(1)}, bf16[288,256]{1,0:T(8,128)(2,1)S(1)}, u32[]{:S(2)}, u32[]{:S(2)}) collective-permute-start(bf16[288,256]{1,0:T(8,128)(2,1)S(1)} %get-tuple-element.13.refs_10_), channel_id=1, source_target_pairs={{0,2},{1,3},{2,0},{3,1},{4,6},{5,7},{6,4},{7,5},{8,10},{9,11},{10,... | collective-permute-start | bytes 442376 | tf_op jit(solution)/shard_map/ppermute | solution.py:300
  19.0 5.8 %collective-permute-start.6 = (bf16[40,2048]{1,0:T(8,128)(2,1)S(1)}, bf16[40,2048]{1,0:T(8,128)(2,1)S(1)}, u32[]{:S(2)}, u32[]{:S(2)}) collective-permute-start(bf16[40,2048]{1,0:T(8,128)(2,1)S(1)} %collective-permute-done.1.refs_9_.refs_16_), channel_id=1, source_target_pairs={{0,4},{4,0},{8,12},{12,8},{1,5},{5,1},{9,13},{13,9},{2,6},{6,2},{1... | collective-permute-start | bytes 491528 | tf_op jit(solution)/shard_map/ppermute | solution.py:300
  20.3 2.9 %collective-permute-start.5 = (bf16[288,256]{1,0:T(8,128)(2,1)S(1)}, bf16[288,256]{1,0:T(8,128)(2,1)S(1)}, u32[]{:S(2)}, u32[]{:S(2)}) collective-permute-start(bf16[288,256]{1,0:T(8,128)(2,1)S(1)} %get-tuple-element.13.refs_10_), channel_id=1, source_target_pairs={{0,1},{1,0},{2,3},{3,2},{4,5},{5,4},{6,7},{7,6},{8,9},{9,8},{10,11... | collective-permute-start | bytes 442376 | tf_op jit(solution)/shard_map/ppermute | solution.py:300
  23.2 1.6 %collective-permute-start.4 = (bf16[288,256]{1,0:T(8,128)(2,1)S(1)}, bf16[288,256]{1,0:T(8,128)(2,1)S(1)}, u32[]{:S(2)}, u32[]{:S(2)}) collective-permute-start(bf16[288,256]{1,0:T(8,128)(2,1)S(1)} %collective-permute-done.3.refs_11_), channel_id=1, source_target_pairs={{0,1},{1,0},{2,3},{3,2},{4,5},{5,4},{6,7},{7,6},{8,9},{9,8},{10,11... | collective-permute-start | bytes 442376 | tf_op jit(solution)/shard_map/ppermute | solution.py:300

commit v11 on v10

--- a/solution.py
+++ b/solution.py
@@ -14,7 +14,6 @@
 LOG2E = 1.4426950408889634
 F32, BF16 = jnp.float32, jnp.bfloat16
 NT = (((1,), (1,)), ((), ()))
-TN = (((0,), (0,)), ((), ()))
 
 
 def silu(v):
@@ -23,9 +22,8 @@
 
 
 def softplus(v):
-    u = jnp.exp(-jnp.abs(v))
-    small = u * (1.0 - u * (0.5 - u * (1.0 / 3.0)))
-    return jnp.maximum(v, 0.0) + jnp.where(u < 0.004, small, jnp.log(1.0 + u))
+    u = jnp.exp2(jnp.abs(v) * -LOG2E)
+    return jnp.maximum(v, 0.0) + jnp.where(u < 2.0**-10, u - 0.5 * (u * u), jnp.log(1.0 + u))
 
 
 def split_index(value, inner):
@@ -63,6 +61,27 @@
         part = jnp.dot(select, value, preferred_element_type=F32)
         total = part if total is None else total + part
     return total
+
+
+def pack_kernel(dims, refs_in, refs_out, scratch):
+    slots, taps = dims
+    ssm_hbm, conv_hbm = refs_in
+    block_ref, conv_ref = refs_out
+    conv_v, sems = scratch
+    states = pltpu.make_async_copy(ssm_hbm, block_ref.at[: ssm_hbm.shape[0]], sems.at[0])
+    inputs = pltpu.make_async_copy(conv_hbm, conv_v, sems.at[1])
+    states.start()
+    inputs.start()
+    inputs.wait()
+    lines = []
+    for slot in range(slots):
+        for tap in range(taps):
+            line = conv_v[min(tap, taps - 2)].astype(F32)[slot : slot + 1]
+            lines.append(line if tap < taps - 1 else jnp.zeros_like(line))
+    rows = jnp.concatenate(lines, axis=0).astype(BF16)
+    conv_ref[...] = rows
+    block_ref[ssm_hbm.shape[0] :, :] = rows
+    states.wait()
 
 
 def project_kernel(dims, refs_in, refs_out, scratch):
@@ -149,9 +168,13 @@
 
 def scan_kernel(dims, refs_in, refs_out, scratch):
     per_dev, n_replica, _, _ = dims
-    holder, slot_id, prefix_len, mixed_ref, head_ref, z_ref, dtw_ref, dtb_ref, al_ref, skip_ref = refs_in[:10]
+    mixed_ref, head_ref, z_ref, dtw_ref, dtb_ref, al_ref, skip_ref = refs_in[3:10]
     out_hbm, state_hbm = refs_out
-    b_tab, c_tab, dt_v, drive_v, a_v, start_tm, final_tm, y_v, out_v, state_v, out_sems = scratch
+    b_tab, c_tab, dt_v, drive_v, a_v, start_tm, final_tm, y_v, out_v, state_v, out_sems, int_sems = scratch[:12]
+    ints = scratch[12:]
+    int_copies = [pltpu.make_async_copy(refs_in[i], ints[i], int_sems.at[i]) for i in range(len(ints))]
+    for copy in int_copies:
+        copy.start()
     n_pieces = sum(1 for ref in refs_in[10:] if ref.shape[-1] == z_ref.shape[1])
     parts, pieces = refs_in[10:-n_pieces], refs_in[-n_pieces:]
     rows, channels = z_ref.shape
@@ -162,8 +185,9 @@
     projected = parts[0][...].astype(F32)
     for part in parts[1:]:
         projected = projected + part[...].astype(F32)
-    dt_low = projected[:rank].astype(BF16)
-    late = projected[rank:].T
+    projected = projected.T
+    dt_low = projected[:, :rank].astype(BF16)
+    late = projected[:, rank:]
     n_tiles = channels // LANES
     wide = min(4, n_tiles)
     per_chunk = 2 * states * wide // n_tiles
@@ -172,7 +196,7 @@
             table = b_tab if n < states else c_tab
             table[n % states] = jnp.broadcast_to(late[:, n : n + 1], (rows, LANES))
         weights = dtw_ref[:, c * wide * LANES : (c + 1) * wide * LANES]
-        raw = lax.dot_general(dt_low, weights, TN, preferred_element_type=F32)
+        raw = jnp.dot(dt_low, weights, preferred_element_type=F32)
         for j in range(wide):
             tile = c * wide + j
             lanes = slice(tile * LANES, (tile + 1) * LANES)
@@ -189,7 +213,9 @@
     a_v[...] = jnp.exp(al_ref[...]) * (-LOG2E)
 
     me = lax.axis_index("replica")
-    places, slot_ids, lengths = request_places(dims, (holder, slot_id, prefix_len), me)
+    for copy in int_copies:
+        copy.wait()
+    places, slot_ids, lengths = request_places(dims, ints, me)
     for r in range(per_dev):
         spot = pl.ds(pl.multiple_of(slot_ids[r] * states, states), states)
         for tile in range(n_tiles):
@@ -312,8 +338,14 @@
     out_cols = x_proj_weight.shape[1]
     requests = holder.shape[0]
 
-    conv_rows = jnp.pad(cache_conv, ((0, 0), (0, 1), (0, 0))).reshape(slots * taps, channels)
-    rows_all = jnp.concatenate([cache_ssm.reshape(slots * states, channels), conv_rows])
+    vmem, dma = pltpu.VMEM, pltpu.SemaphoreType.DMA
+    ssm_rows = slots * states
+    rows_all, conv_rows = call(
+        pack_kernel, (slots, taps), "pack", 20,
+        [(cache_ssm.reshape(ssm_rows, channels), "hbm"), (cache_conv.transpose(1, 0, 2), "hbm")],
+        [((ssm_rows + slots * taps, channels), BF16, "vmem"), ((slots * taps, channels), BF16, "vmem")],
+        [vmem((taps - 1, slots, channels), BF16), dma((2,))],
+    )
     block = rows_all.shape[0]
     relative = n_replica == 4
     if relative:
@@ -327,7 +359,6 @@
         ssm_pieces = [lax.all_gather(rows_all, "replica")]
         conv_pieces, firsts = [ssm_pieces[0].reshape(-1, channels)], (0,)
 
-    vmem, dma = pltpu.VMEM, pltpu.SemaphoreType.DMA
     n_chunks = channels // min(512, channels)
     dims = (per_dev, n_replica, slots, relative)
     head = per_dev * taps
@@ -369,7 +400,7 @@
     operands = [mixed, mixed_head, z_new, dt_proj_weight, dt_bias[None, :], a_log, d_skip[None, :]]
     out, state = call(
         scan_kernel, dims, "dt_scan_gate", 40,
-        requests + [(value, "vmem") for value in operands + parts + ssm_pieces],
+        [(value, "any") for value, _ in requests] + [(value, "vmem") for value in operands + parts + ssm_pieces],
         [((rows, channels), BF16, "any"), ((per_dev * states, channels), BF16, "any")],
         [
             vmem((states, rows, LANES), F32),
@@ -383,7 +414,8 @@
             vmem((rows, channels), BF16),
             vmem((per_dev * states, channels), BF16),
             dma((2, n_chunks)),
-        ],
+            dma((3,)),
+        ] + [pltpu.SMEM(holder.shape, jnp.int32)] * 3,
     )
     return out, state.reshape(per_dev, states, channels)
 

time: 38.6 us -> 37.2 us (0.964)
  other arithmetic: 0.92 us -> 0 us
  local copies, waits for them, and re-layouts: 0.85 us -> 0.05 us
  Pallas kernels: 18.8 us -> 19.2 us
    concatenate x1 -> x0, other arithmetic: 0.92 us -> none  [shards(): jnp.concatenate([cache_ssm.reshape(slots * states, channels), conv_rows])]
    unnamed x21 -> x20, local copies, waits for them, and re-layouts: 0.82 us -> 0.05 us
    pallas_call x3 -> x4, Pallas kernels: 18.8 us -> 19.2 us  [call(): pl.pallas_call(split_refs(kernel, dims, len(ins), len(outs)), in_specs=[p...]
  transfers between devices with their start and end apart: 7 -> 7, of which waited for: 4 -> 4; matrix products, arithmetic and copies ran while one was open for 0% -> 0% of each run, Pallas kernels for 10% -> 11%
where the time goes in v11:
time: 37.2 us; the launch traced here: 37.1 us
  Pallas kernels  19.2 us (52%)
  starting transfers between devices  8.65 us (23%)
  waiting for transfers between devices  8.35 us (22%)
  between operations  0.78 us (2%)
    pallas_call x4, Pallas kernels, call(): pl.pallas_call(split_refs(kernel, dims, len(ins), len(outs)), in_specs=[p...  19.2 us
    ppermute x7, starting transfers between devices, swap(): return lax.ppermute(value, axis, [(i, i ^ mask) for i in range(size)])  8.65 us
    ppermute x7, waiting for transfers between devices, swap(): return lax.ppermute(value, axis, [(i, i ^ mask) for i in range(size)])  8.35 us
  transfers between devices with their start and end apart: 7, of which 4 were waited for; matrix products, arithmetic and copies ran while one was open for 0% of the time, Pallas kernels for 11%

profile of v11, /device:TPU:0, one launch (start us, length us, event | category | flops | bytes accessed | tf_op | source)
XLA Modules:
  0.0 37.1 jit_solution(3993168246219473545)
XLA Ops:
  0.6 0.0 copy-start
  0.6 0.0 copy-start.4
  0.7 1.0 %pack.1 = (bf16[40,2048]{1,0:T(8,128)(2,1)S(1)}, bf16[8,2048]{1,0:T(8,128)(2,1)S(1)}) custom-call(bf16[32,2048]{1,0:T(8,128)(2,1)} %bitcast.11, bf16[3,2,2048]{2,1,0:T(2,128)(2,1)} %bitcast.12), custom_call_target="tpu_custom_call" | custom-call | tf_op jit(solution)/shard_map/pack/pallas_call | solution.py:314
  1.7 5.1 %collective-permute-start.1 = (bf16[40,2048]{1,0:T(8,128)(2,1)S(1)}, bf16[40,2048]{1,0:T(8,128)(2,1)S(1)}, u32[]{:S(2)}, u32[]{:S(2)}) collective-permute-start(bf16[40,2048]{1,0:T(8,128)(2,1)S(1)} %get-tuple-element.14.refs_7_.refs_14_), channel_id=1, source_target_pairs={{0,12},{4,8},{8,4},{12,0},{1,13},{5,9},{9,5},{13,1},{2,14},{6,10},... | collective-permute-start | bytes 491528 | tf_op jit(solution)/shard_map/ppermute | solution.py:326
  6.8 0.0 collective-permute-start
  6.8 0.6 %collective-permute-start.2 = (bf16[8,2048]{1,0:T(8,128)(2,1)S(1)}, bf16[8,2048]{1,0:T(8,128)(2,1)S(1)}, u32[]{:S(2)}, u32[]{:S(2)}) collective-permute-start(bf16[8,2048]{1,0:T(8,128)(2,1)S(1)} %get-tuple-element.15), channel_id=1, source_target_pairs={{0,8},{4,12},{8,0},{12,4},{1,9},{5,13},{9,1},{13,5},{2,10},{6,14},... | collective-permute-start | bytes 98312 | tf_op jit(solution)/shard_map/ppermute | solution.py:326
  7.5 3.9 %conv_project.1 = (bf16[256,2048]{1,0:T(8,128)(2,1)S(1)}, f32[32,2048]{1,0:T(8,128)S(1)}, bf16[288,256]{1,0:T(8,128)(2,1)S(1)}) custom-call(bf16[256,2048]{1,0:T(8,128)(2,1)} %refs_0_.3, bf16[288,2048]{1,0:T(8,128)(2,1)} %bitcast.7, bf16[4,2048]{1,0:T(4,128)(2,1)} %refs_6_.2, f32[1,2048]{1,0:T(1,128)} %bitcast.13), custom_call_target="tpu_custom_call" | custom-call | tf_op jit(solution)/shard_map/conv_project/pallas_call | solution.py:314
  11.4 0.0 copy-start.1
  11.4 0.0 copy-start.2
  11.4 0.0 copy-start.5
  11.4 0.0 copy-start.6
  11.5 3.4 %collective-permute-done.2.refs_10_ = bf16[8,2048]{1,0:T(8,128)(2,1)S(1)} collective-permute-done((bf16[8,2048]{1,0:T(8,128)(2,1)S(1)}, bf16[8,2048]{1,0:T(8,128)(2,1)S(1)}, u32[]{:S(2)}, u32[]{:S(2)}) %collective-permute-start.2) | collective-permute-done | bytes 32800 | tf_op jit(solution)/shard_map/ppermute | solution.py:326
  14.8 0.0 collective-permute-done.1.refs_9_.refs_16_
  14.8 0.5 %collective-permute-done.refs_8_.refs_15_ = bf16[40,2048]{1,0:T(8,128)(2,1)S(1)} collective-permute-done((bf16[40,2048]{1,0:T(8,128)(2,1)S(1)}, bf16[40,2048]{1,0:T(8,128)(2,1)S(1)}, u32[]{:S(2)}, u32[]{:S(2)}) %collective-permute-start) | collective-permute-done | bytes 163872 | tf_op jit(solution)/shard_map/ppermute | solution.py:326
  15.4 1.3 %history.1 = (bf16[32,2048]{1,0:T(8,128)(2,1)S(1)}, bf16[288,256]{1,0:T(8,128)(2,1)S(1)}) custom-call(s32[32]{0:T(128)S(1)} %copy-done.7, s32[32]{0:T(128)S(1)} %copy-done.8, s32[32]{0:T(128)S(1)} %copy-done.9, f32[32,2048]{1,0:T(8,128)S(1)} %get-tuple-element.12.refs_3_, bf16[288,256]{1,0:T(8,128)(2,1)S(1)} %get-tuple-element.13.refs_4_, ...), custom_call_target="tpu_custom_call" | custom-call | tf_op jit(solution)/shard_map/history/pallas_call | solution.py:314
  16.7 1.6 %collective-permute-start.3 = (bf16[288,256]{1,0:T(8,128)(2,1)S(1)}, bf16[288,256]{1,0:T(8,128)(2,1)S(1)}, u32[]{:S(2)}, u32[]{:S(2)}) collective-permute-start(bf16[288,256]{1,0:T(8,128)(2,1)S(1)} %get-tuple-element.17.refs_10_), channel_id=1, source_target_pairs={{0,2},{1,3},{2,0},{3,1},{4,6},{5,7},{6,4},{7,5},{8,10},{9,11},{10,... | collective-permute-start | bytes 442376 | tf_op jit(solution)/shard_map/ppermute | solution.py:326
  18.2 1.3 %collective-permute-start.6 = (bf16[40,2048]{1,0:T(8,128)(2,1)S(1)}, bf16[40,2048]{1,0:T(8,128)(2,1)S(1)}, u32[]{:S(2)}, u32[]{:S(2)}) collective-permute-start(bf16[40,2048]{1,0:T(8,128)(2,1)S(1)} %collective-permute-done.1.refs_9_.refs_16_), channel_id=1, source_target_pairs={{0,4},{4,0},{8,12},{12,8},{1,5},{5,1},{9,13},{13,9},{2,6},{6,2},{1... | collective-permute-start | bytes 491528 | tf_op jit(solution)/shard_map/ppermute | solution.py:326
  19.6 0.0 collective-permute-start.5
  19.6 2.9 %collective-permute-done.3.refs_11_ = bf16[288,256]{1,0:T(8,128)(2,1)S(1)} collective-permute-done((bf16[288,256]{1,0:T(8,128)(2,1)S(1)}, bf16[288,256]{1,0:T(8,128)(2,1)S(1)}, u32[]{:S(2)}, u32[]{:S(2)}) %collective-permute-start.3) | collective-permute-done | bytes 147488 | tf_op jit(solution)/shard_map/ppermute | solution.py:326
  22.5 0.0 collective-permute-start.4
  22.5 0.0 collective-permute-done.5.refs_13_
  22.5 1.5 %collective-permute-done.6.refs_17_ = bf16[40,2048]{1,0:T(8,128)(2,1)S(1)} collective-permute-done((bf16[40,2048]{1,0:T(8,128)(2,1)S(1)}, bf16[40,2048]{1,0:T(8,128)(2,1)S(1)}, u32[]{:S(2)}, u32[]{:S(2)}) %collective-permute-start.6) | collective-permute-done | bytes 163872 | tf_op jit(solution)/shard_map/ppermute | solution.py:326
  24.1 0.0 collective-permute-done.4.refs_12_
  24.1 13.0 %dt_scan_gate.1 = (bf16[256,2048]{1,0:T(8,128)(2,1)}, bf16[128,2048]{1,0:T(8,128)(2,1)}) custom-call(s32[32]{0:T(128)S(1)} %copy-done.7, s32[32]{0:T(128)S(1)} %copy-done.8, s32[32]{0:T(128)S(1)} %copy-done.9, bf16[256,2048]{1,0:T(8,128)(2,1)S(1)} %get-tuple-element.11.refs_3_, bf16[32,2048]{1,0:T(8,128)(2,1)S(1)} %get-tuple-element.16.refs_4_, ...), custom_call_target="tpu_custom_call" | custom-call | tf_op jit(solution)/shard_map/dt_scan_gate/pallas_call | solution.py:314
  (14 shorter events, 0.0 us)
Async XLA Ops:
  0.6 14.7 %copy-start = (bf16[2048,288]{0,1:T(8,128)(2,1)S(1)}, bf16[2048,288]{0,1:T(8,128)(2,1)}, u32[]{:S(2)}) copy-start(bf16[2048,288]{0,1:T(8,128)(2,1)} %param.18) | copy-start | bytes 3538948
  0.6 14.7 %copy-start.4 = (bf16[4,2048]{1,0:T(4,128)(2,1)S(1)}, bf16[4,2048]{1,0:T(4,128)(2,1)}, u32[]{:S(2)}) copy-start(bf16[4,2048]{1,0:T(4,128)(2,1)} %refs_6_.2) | copy-start | bytes 49156
  0.7 14.7 %copy-start.7 = (s32[32]{0:T(128)S(1)}, s32[32]{0:T(128)}, u32[]{:S(2)}) copy-start(s32[32]{0:T(128)} %refs_0_.5) | copy-start | bytes 388
  0.7 14.7 %copy-start.8 = (s32[32]{0:T(128)S(1)}, s32[32]{0:T(128)}, u32[]{:S(2)}) copy-start(s32[32]{0:T(128)} %refs_1_.3) | copy-start | bytes 388
  0.7 14.7 %copy-start.9 = (s32[32]{0:T(128)S(1)}, s32[32]{0:T(128)}, u32[]{:S(2)}) copy-start(s32[32]{0:T(128)} %refs_2_.5) | copy-start | bytes 388
  1.7 13.1 %collective-permute-start.1 = (bf16[40,2048]{1,0:T(8,128)(2,1)S(1)}, bf16[40,2048]{1,0:T(8,128)(2,1)S(1)}, u32[]{:S(2)}, u32[]{:S(2)}) collective-permute-start(bf16[40,2048]{1,0:T(8,128)(2,1)S(1)} %get-tuple-element.14.refs_7_.refs_14_), channel_id=1, source_target_pairs={{0,12},{4,8},{8,4},{12,0},{1,13},{5,9},{9,5},{13,1},{2,14},{6,10},... | collective-permute-start | bytes 491528 | tf_op jit(solution)/shard_map/ppermute | solution.py:326
  6.8 8.5 %collective-permute-start = (bf16[40,2048]{1,0:T(8,128)(2,1)S(1)}, bf16[40,2048]{1,0:T(8,128)(2,1)S(1)}, u32[]{:S(2)}, u32[]{:S(2)}) collective-permute-start(bf16[40,2048]{1,0:T(8,128)(2,1)S(1)} %get-tuple-element.14.refs_7_.refs_14_), channel_id=1, source_target_pairs={{0,4},{4,0},{8,12},{12,8},{1,5},{5,1},{9,13},{13,9},{2,6},{6,2},{1... | collective-permute-start | bytes 491528 | tf_op jit(solution)/shard_map/ppermute | solution.py:326
  6.8 8.0 %collective-permute-start.2 = (bf16[8,2048]{1,0:T(8,128)(2,1)S(1)}, bf16[8,2048]{1,0:T(8,128)(2,1)S(1)}, u32[]{:S(2)}, u32[]{:S(2)}) collective-permute-start(bf16[8,2048]{1,0:T(8,128)(2,1)S(1)} %get-tuple-element.15), channel_id=1, source_target_pairs={{0,8},{4,12},{8,0},{12,4},{1,9},{5,13},{9,1},{13,5},{2,10},{6,14},... | collective-permute-start | bytes 98312 | tf_op jit(solution)/shard_map/ppermute | solution.py:326
  7.5 16.6 %copy-start.3 = (f32[16,2048]{1,0:T(8,128)S(1)}, f32[16,2048]{1,0:T(8,128)}, u32[]{:S(2)}) copy-start(f32[16,2048]{1,0:T(8,128)} %refs_8_.1) | copy-start | bytes 393220
  11.4 12.7 %copy-start.1 = (bf16[256,2048]{1,0:T(8,128)(2,1)S(1)}, bf16[256,2048]{1,0:T(8,128)(2,1)}, u32[]{:S(2)}) copy-start(bf16[256,2048]{1,0:T(8,128)(2,1)} %refs_5_.1) | copy-start | bytes 3145732
  11.4 12.7 %copy-start.2 = (bf16[256,2048]{1,0:T(8,128)(2,1)S(1)}, bf16[256,2048]{1,0:T(8,128)(2,1)}, u32[]{:S(2)}) copy-start(bf16[256,2048]{1,0:T(8,128)(2,1)} %refs_6_.3) | copy-start | bytes 3145732
  11.4 12.7 %copy-start.5 = (f32[2048]{0:T(1024)S(1)}, f32[2048]{0:T(1024)}, u32[]{:S(2)}) copy-start(f32[2048]{0:T(1024)} %param.20) | copy-start | bytes 24580
  11.4 12.7 %copy-start.6 = (f32[2048]{0:T(1024)S(1)}, f32[2048]{0:T(1024)}, u32[]{:S(2)}) copy-start(f32[2048]{0:T(1024)} %param.22) | copy-start | bytes 24580
  16.7 5.8 %collective-permute-start.3 = (bf16[288,256]{1,0:T(8,128)(2,1)S(1)}, bf16[288,256]{1,0:T(8,128)(2,1)S(1)}, u32[]{:S(2)}, u32[]{:S(2)}) collective-permute-start(bf16[288,256]{1,0:T(8,128)(2,1)S(1)} %get-tuple-element.17.refs_10_), channel_id=1, source_target_pairs={{0,2},{1,3},{2,0},{3,1},{4,6},{5,7},{6,4},{7,5},{8,10},{9,11},{10,... | collective-permute-start | bytes 442376 | tf_op jit(solution)/shard_map/ppermute | solution.py:326
  18.2 5.8 %collective-permute-start.6 = (bf16[40,2048]{1,0:T(8,128)(2,1)S(1)}, bf16[40,2048]{1,0:T(8,128)(2,1)S(1)}, u32[]{:S(2)}, u32[]{:S(2)}) collective-permute-start(bf16[40,2048]{1,0:T(8,128)(2,1)S(1)} %collective-permute-done.1.refs_9_.refs_16_), channel_id=1, source_target_pairs={{0,4},{4,0},{8,12},{12,8},{1,5},{5,1},{9,13},{13,9},{2,6},{6,2},{1... | collective-permute-start | bytes 491528 | tf_op jit(solution)/shard_map/ppermute | solution.py:326
  19.6 2.9 %collective-permute-start.5 = (bf16[288,256]{1,0:T(8,128)(2,1)S(1)}, bf16[288,256]{1,0:T(8,128)(2,1)S(1)}, u32[]{:S(2)}, u32[]{:S(2)}) collective-permute-start(bf16[288,256]{1,0:T(8,128)(2,1)S(1)} %get-tuple-element.17.refs_10_), channel_id=1, source_target_pairs={{0,1},{1,0},{2,3},{3,2},{4,5},{5,4},{6,7},{7,6},{8,9},{9,8},{10,11... | collective-permute-start | bytes 442376 | tf_op jit(solution)/shard_map/ppermute | solution.py:326
  22.5 1.5 %collective-permute-start.4 = (bf16[288,256]{1,0:T(8,128)(2,1)S(1)}, bf16[288,256]{1,0:T(8,128)(2,1)S(1)}, u32[]{:S(2)}, u32[]{:S(2)}) collective-permute-start(bf16[288,256]{1,0:T(8,128)(2,1)S(1)} %collective-permute-done.3.refs_11_), channel_id=1, source_target_pairs={{0,1},{1,0},{2,3},{3,2},{4,5},{5,4},{6,7},{7,6},{8,9},{9,8},{10,11... | collective-permute-start | bytes 442376 | tf_op jit(solution)/shard_map/ppermute | solution.py:326

commit v12 on v11

--- a/solution.py
+++ b/solution.py
@@ -10,7 +10,7 @@
 NEW = 32
 LANES = 128
 MIB = 1024 * 1024
-UNROLL = 8
+UNROLL = 32
 LOG2E = 1.4426950408889634
 F32, BF16 = jnp.float32, jnp.bfloat16
 NT = (((1,), (1,)), ((), ()))
@@ -232,17 +232,28 @@
 
     tiles = 2
     half = states // 2
-    width = 2 * tiles * LANES
-    n_chunks = channels // width
-
-    def out_copies(c):
-        lanes = pl.ds(pl.multiple_of(c * width, width), width)
+    width = tiles * LANES
+    n_groups = n_tiles // tiles
+
+    def out_copies(g):
+        lanes = pl.ds(pl.multiple_of(g * width, width), width)
         return [
-            pltpu.make_async_copy(src.at[:, lanes], dst.at[:, lanes], out_sems.at[i, c])
+            pltpu.make_async_copy(src.at[:, lanes], dst.at[:, lanes], out_sems.at[i, g])
             for i, (src, dst) in enumerate(((out_v, out_hbm), (state_v, state_hbm)))
         ]
 
-    def scan_group(g, carry):
+    def finish(g):
+        for j in range(tiles):
+            tile = g * tiles + j
+            lanes = pl.ds(pl.multiple_of(tile * LANES, LANES), LANES)
+            for r in range(per_dev):
+                here = slice(r * NEW, (r + 1) * NEW)
+                value = y_v[tile, pl.ds(r, NEW, stride=per_dev), :] * silu(z_ref[here, lanes].astype(F32))
+                out_v[here, lanes] = value.astype(BF16)
+                final = final_tm[tile, pl.ds(r, states, stride=per_dev), :]
+                state_v[r * states : (r + 1) * states, lanes] = final.astype(BF16)
+
+    def scan_group(g):
         group = [g * tiles + j for j in range(tiles)]
         lanes = [pl.ds(pl.multiple_of(tile * LANES, LANES), LANES) for tile in group]
         for first in range(0, states, half):
@@ -268,35 +279,38 @@
                 return tuple(state)
 
             state = tuple(start_tm[tile, n * per_dev : (n + 1) * per_dev, :] for tile in group for n in ids)
-            state = lax.fori_loop(0, NEW // UNROLL, advance, state)
+            if NEW == UNROLL:
+                state = advance(0, state)
+            else:
+                state = lax.fori_loop(0, NEW // UNROLL, advance, state)
             for j, tile in enumerate(group):
                 for k, n in enumerate(ids):
                     final_tm[tile, n * per_dev : (n + 1) * per_dev, :] = state[j * half + k]
+
+    def one_group(g, carry):
+        before = jnp.maximum(g - 1, 0)
+        finish(before)
+        scan_group(g)
+
+        @pl.when(g > 0)
+        def _():
+            for copy in out_copies(before):
+                copy.start()
+
         return carry
 
-    def one_chunk(c, carry):
-        lax.fori_loop(c * 2, c * 2 + 2, scan_group, 0)
-        for j in range(width // LANES):
-            tile = c * (width // LANES) + j
-            lanes = pl.ds(pl.multiple_of(tile * LANES, LANES), LANES)
-            for r in range(per_dev):
-                here = slice(r * NEW, (r + 1) * NEW)
-                value = y_v[tile, pl.ds(r, NEW, stride=per_dev), :] * silu(z_ref[here, lanes].astype(F32))
-                out_v[here, lanes] = value.astype(BF16)
-                final = final_tm[tile, pl.ds(r, states, stride=per_dev), :]
-                state_v[r * states : (r + 1) * states, lanes] = final.astype(BF16)
-        for copy in out_copies(c):
-            copy.start()
-        return carry
-
-    lax.fori_loop(0, n_chunks, one_chunk, 0)
-
-    def last_wait(c, carry):
-        for copy in out_copies(c):
+    final_tm[:tiles] = jnp.zeros((tiles,) + final_tm.shape[1:], F32)
+    lax.fori_loop(0, n_groups, one_group, 0)
+    finish(n_groups - 1)
+    for copy in out_copies(n_groups - 1):
+        copy.start()
+
+    def last_wait(g, carry):
+        for copy in out_copies(g):
             copy.wait()
         return carry
 
-    lax.fori_loop(0, n_chunks, last_wait, 0)
+    lax.fori_loop(0, n_groups, last_wait, 0)
 
 
 def split_refs(kernel, dims, n_in, n_out):
@@ -413,7 +427,7 @@
             vmem((n_tiles, rows + per_dev, LANES), F32),
             vmem((rows, channels), BF16),
             vmem((per_dev * states, channels), BF16),
-            dma((2, n_chunks)),
+            dma((2, n_tiles // 2)),
             dma((3,)),
         ] + [pltpu.SMEM(holder.shape, jnp.int32)] * 3,
     )

time: 37.2 us -> 36.7 us (0.987)
  Pallas kernels: 19.2 us -> 18.7 us
    pallas_call x4, Pallas kernels: 19.2 us -> 18.7 us  [call(): pl.pallas_call(split_refs(kernel, dims, len(ins), len(outs)), in_specs=[p...]
where the time goes in v12:
time: 36.7 us; the launch traced here: 36.5 us
  Pallas kernels  18.7 us (51%)
  starting transfers between devices  8.65 us (24%)
  waiting for transfers between devices  8.35 us (23%)
  between operations  0.78 us (2%)
    pallas_call x4, Pallas kernels, call(): pl.pallas_call(split_refs(kernel, dims, len(ins), len(outs)), in_specs=[p...  18.7 us
    ppermute x7, starting transfers between devices, swap(): return lax.ppermute(value, axis, [(i, i ^ mask) for i in range(size)])  8.65 us
    ppermute x7, waiting for transfers between devices, swap(): return lax.ppermute(value, axis, [(i, i ^ mask) for i in range(size)])  8.35 us
  transfers between devices with their start and end apart: 7, of which 4 were waited for; matrix products, arithmetic and copies ran while one was open for 0% of the time, Pallas kernels for 11%

profile of v12, /device:TPU:0, one launch (start us, length us, event | category | flops | bytes accessed | tf_op | source)
XLA Modules:
  0.0 36.5 jit_solution(2397367918418096027)
XLA Ops:
  0.6 0.0 copy-start
  0.6 0.0 copy-start.4
  0.7 1.0 %pack.1 = (bf16[40,2048]{1,0:T(8,128)(2,1)S(1)}, bf16[8,2048]{1,0:T(8,128)(2,1)S(1)}) custom-call(bf16[32,2048]{1,0:T(8,128)(2,1)} %bitcast.11, bf16[3,2,2048]{2,1,0:T(2,128)(2,1)} %bitcast.12), custom_call_target="tpu_custom_call" | custom-call | tf_op jit(solution)/shard_map/pack/pallas_call | solution.py:328
  1.7 5.1 %collective-permute-start.1 = (bf16[40,2048]{1,0:T(8,128)(2,1)S(1)}, bf16[40,2048]{1,0:T(8,128)(2,1)S(1)}, u32[]{:S(2)}, u32[]{:S(2)}) collective-permute-start(bf16[40,2048]{1,0:T(8,128)(2,1)S(1)} %get-tuple-element.14.refs_7_.refs_14_), channel_id=1, source_target_pairs={{0,12},{4,8},{8,4},{12,0},{1,13},{5,9},{9,5},{13,1},{2,14},{6,10},... | collective-permute-start | bytes 491528 | tf_op jit(solution)/shard_map/ppermute | solution.py:340
  6.8 0.0 collective-permute-start
  6.8 0.6 %collective-permute-start.2 = (bf16[8,2048]{1,0:T(8,128)(2,1)S(1)}, bf16[8,2048]{1,0:T(8,128)(2,1)S(1)}, u32[]{:S(2)}, u32[]{:S(2)}) collective-permute-start(bf16[8,2048]{1,0:T(8,128)(2,1)S(1)} %get-tuple-element.15), channel_id=1, source_target_pairs={{0,8},{4,12},{8,0},{12,4},{1,9},{5,13},{9,1},{13,5},{2,10},{6,14},... | collective-permute-start | bytes 98312 | tf_op jit(solution)/shard_map/ppermute | solution.py:340
  7.5 3.9 %conv_project.1 = (bf16[256,2048]{1,0:T(8,128)(2,1)S(1)}, f32[32,2048]{1,0:T(8,128)S(1)}, bf16[288,256]{1,0:T(8,128)(2,1)S(1)}) custom-call(bf16[256,2048]{1,0:T(8,128)(2,1)} %refs_0_.3, bf16[288,2048]{1,0:T(8,128)(2,1)} %bitcast.7, bf16[4,2048]{1,0:T(4,128)(2,1)} %refs_6_.2, f32[1,2048]{1,0:T(1,128)} %bitcast.13), custom_call_target="tpu_custom_call" | custom-call | tf_op jit(solution)/shard_map/conv_project/pallas_call | solution.py:328
  11.4 0.0 copy-start.1
  11.4 0.0 copy-start.2
  11.4 0.0 copy-start.5
  11.4 0.0 copy-start.6
  11.5 3.4 %collective-permute-done.2.refs_10_ = bf16[8,2048]{1,0:T(8,128)(2,1)S(1)} collective-permute-done((bf16[8,2048]{1,0:T(8,128)(2,1)S(1)}, bf16[8,2048]{1,0:T(8,128)(2,1)S(1)}, u32[]{:S(2)}, u32[]{:S(2)}) %collective-permute-start.2) | collective-permute-done | bytes 32800 | tf_op jit(solution)/shard_map/ppermute | solution.py:340
  14.8 0.0 collective-permute-done.1.refs_9_.refs_16_
  14.8 0.5 %collective-permute-done.refs_8_.refs_15_ = bf16[40,2048]{1,0:T(8,128)(2,1)S(1)} collective-permute-done((bf16[40,2048]{1,0:T(8,128)(2,1)S(1)}, bf16[40,2048]{1,0:T(8,128)(2,1)S(1)}, u32[]{:S(2)}, u32[]{:S(2)}) %collective-permute-start) | collective-permute-done | bytes 163872 | tf_op jit(solution)/shard_map/ppermute | solution.py:340
  15.4 1.3 %history.1 = (bf16[32,2048]{1,0:T(8,128)(2,1)S(1)}, bf16[288,256]{1,0:T(8,128)(2,1)S(1)}) custom-call(s32[32]{0:T(128)S(1)} %copy-done.7, s32[32]{0:T(128)S(1)} %copy-done.8, s32[32]{0:T(128)S(1)} %copy-done.9, f32[32,2048]{1,0:T(8,128)S(1)} %get-tuple-element.12.refs_3_, bf16[288,256]{1,0:T(8,128)(2,1)S(1)} %get-tuple-element.13.refs_4_, ...), custom_call_target="tpu_custom_call" | custom-call | tf_op jit(solution)/shard_map/history/pallas_call | solution.py:328
  16.7 1.6 %collective-permute-start.3 = (bf16[288,256]{1,0:T(8,128)(2,1)S(1)}, bf16[288,256]{1,0:T(8,128)(2,1)S(1)}, u32[]{:S(2)}, u32[]{:S(2)}) collective-permute-start(bf16[288,256]{1,0:T(8,128)(2,1)S(1)} %get-tuple-element.17.refs_10_), channel_id=1, source_target_pairs={{0,2},{1,3},{2,0},{3,1},{4,6},{5,7},{6,4},{7,5},{8,10},{9,11},{10,... | collective-permute-start | bytes 442376 | tf_op jit(solution)/shard_map/ppermute | solution.py:340
  18.2 1.3 %collective-permute-start.6 = (bf16[40,2048]{1,0:T(8,128)(2,1)S(1)}, bf16[40,2048]{1,0:T(8,128)(2,1)S(1)}, u32[]{:S(2)}, u32[]{:S(2)}) collective-permute-start(bf16[40,2048]{1,0:T(8,128)(2,1)S(1)} %collective-permute-done.1.refs_9_.refs_16_), channel_id=1, source_target_pairs={{0,4},{4,0},{8,12},{12,8},{1,5},{5,1},{9,13},{13,9},{2,6},{6,2},{1... | collective-permute-start | bytes 491528 | tf_op jit(solution)/shard_map/ppermute | solution.py:340
  19.6 0.0 collective-permute-start.5
  19.6 2.9 %collective-permute-done.3.refs_11_ = bf16[288,256]{1,0:T(8,128)(2,1)S(1)} collective-permute-done((bf16[288,256]{1,0:T(8,128)(2,1)S(1)}, bf16[288,256]{1,0:T(8,128)(2,1)S(1)}, u32[]{:S(2)}, u32[]{:S(2)}) %collective-permute-start.3) | collective-permute-done | bytes 147488 | tf_op jit(solution)/shard_map/ppermute | solution.py:340
  22.5 0.0 collective-permute-start.4
  22.5 0.0 collective-permute-done.5.refs_13_
  22.5 1.5 %collective-permute-done.6.refs_17_ = bf16[40,2048]{1,0:T(8,128)(2,1)S(1)} collective-permute-done((bf16[40,2048]{1,0:T(8,128)(2,1)S(1)}, bf16[40,2048]{1,0:T(8,128)(2,1)S(1)}, u32[]{:S(2)}, u32[]{:S(2)}) %collective-permute-start.6) | collective-permute-done | bytes 163872 | tf_op jit(solution)/shard_map/ppermute | solution.py:340
  24.1 0.0 collective-permute-done.4.refs_12_
  24.1 12.4 %dt_scan_gate.1 = (bf16[256,2048]{1,0:T(8,128)(2,1)}, bf16[128,2048]{1,0:T(8,128)(2,1)}) custom-call(s32[32]{0:T(128)S(1)} %copy-done.7, s32[32]{0:T(128)S(1)} %copy-done.8, s32[32]{0:T(128)S(1)} %copy-done.9, bf16[256,2048]{1,0:T(8,128)(2,1)S(1)} %get-tuple-element.11.refs_3_, bf16[32,2048]{1,0:T(8,128)(2,1)S(1)} %get-tuple-element.16.refs_4_, ...), custom_call_target="tpu_custom_call" | custom-call | tf_op jit(solution)/shard_map/dt_scan_gate/pallas_call | solution.py:328
  (14 shorter events, 0.0 us)
Async XLA Ops:
  0.6 14.7 %copy-start = (bf16[2048,288]{0,1:T(8,128)(2,1)S(1)}, bf16[2048,288]{0,1:T(8,128)(2,1)}, u32[]{:S(2)}) copy-start(bf16[2048,288]{0,1:T(8,128)(2,1)} %param.18) | copy-start | bytes 3538948
  0.6 14.7 %copy-start.4 = (bf16[4,2048]{1,0:T(4,128)(2,1)S(1)}, bf16[4,2048]{1,0:T(4,128)(2,1)}, u32[]{:S(2)}) copy-start(bf16[4,2048]{1,0:T(4,128)(2,1)} %refs_6_.2) | copy-start | bytes 49156
  0.7 14.7 %copy-start.7 = (s32[32]{0:T(128)S(1)}, s32[32]{0:T(128)}, u32[]{:S(2)}) copy-start(s32[32]{0:T(128)} %refs_0_.5) | copy-start | bytes 388
  0.7 14.7 %copy-start.8 = (s32[32]{0:T(128)S(1)}, s32[32]{0:T(128)}, u32[]{:S(2)}) copy-start(s32[32]{0:T(128)} %refs_1_.3) | copy-start | bytes 388
  0.7 14.7 %copy-start.9 = (s32[32]{0:T(128)S(1)}, s32[32]{0:T(128)}, u32[]{:S(2)}) copy-start(s32[32]{0:T(128)} %refs_2_.5) | copy-start | bytes 388
  1.7 13.1 %collective-permute-start.1 = (bf16[40,2048]{1,0:T(8,128)(2,1)S(1)}, bf16[40,2048]{1,0:T(8,128)(2,1)S(1)}, u32[]{:S(2)}, u32[]{:S(2)}) collective-permute-start(bf16[40,2048]{1,0:T(8,128)(2,1)S(1)} %get-tuple-element.14.refs_7_.refs_14_), channel_id=1, source_target_pairs={{0,12},{4,8},{8,4},{12,0},{1,13},{5,9},{9,5},{13,1},{2,14},{6,10},... | collective-permute-start | bytes 491528 | tf_op jit(solution)/shard_map/ppermute | solution.py:340
  6.8 8.5 %collective-permute-start = (bf16[40,2048]{1,0:T(8,128)(2,1)S(1)}, bf16[40,2048]{1,0:T(8,128)(2,1)S(1)}, u32[]{:S(2)}, u32[]{:S(2)}) collective-permute-start(bf16[40,2048]{1,0:T(8,128)(2,1)S(1)} %get-tuple-element.14.refs_7_.refs_14_), channel_id=1, source_target_pairs={{0,4},{4,0},{8,12},{12,8},{1,5},{5,1},{9,13},{13,9},{2,6},{6,2},{1... | collective-permute-start | bytes 491528 | tf_op jit(solution)/shard_map/ppermute | solution.py:340
  6.8 8.0 %collective-permute-start.2 = (bf16[8,2048]{1,0:T(8,128)(2,1)S(1)}, bf16[8,2048]{1,0:T(8,128)(2,1)S(1)}, u32[]{:S(2)}, u32[]{:S(2)}) collective-permute-start(bf16[8,2048]{1,0:T(8,128)(2,1)S(1)} %get-tuple-element.15), channel_id=1, source_target_pairs={{0,8},{4,12},{8,0},{12,4},{1,9},{5,13},{9,1},{13,5},{2,10},{6,14},... | collective-permute-start | bytes 98312 | tf_op jit(solution)/shard_map/ppermute | solution.py:340
  7.5 16.6 %copy-start.3 = (f32[16,2048]{1,0:T(8,128)S(1)}, f32[16,2048]{1,0:T(8,128)}, u32[]{:S(2)}) copy-start(f32[16,2048]{1,0:T(8,128)} %refs_8_.1) | copy-start | bytes 393220
  11.4 12.7 %copy-start.1 = (bf16[256,2048]{1,0:T(8,128)(2,1)S(1)}, bf16[256,2048]{1,0:T(8,128)(2,1)}, u32[]{:S(2)}) copy-start(bf16[256,2048]{1,0:T(8,128)(2,1)} %refs_5_.1) | copy-start | bytes 3145732
  11.4 12.7 %copy-start.2 = (bf16[256,2048]{1,0:T(8,128)(2,1)S(1)}, bf16[256,2048]{1,0:T(8,128)(2,1)}, u32[]{:S(2)}) copy-start(bf16[256,2048]{1,0:T(8,128)(2,1)} %refs_6_.3) | copy-start | bytes 3145732
  11.4 12.7 %copy-start.5 = (f32[2048]{0:T(1024)S(1)}, f32[2048]{0:T(1024)}, u32[]{:S(2)}) copy-start(f32[2048]{0:T(1024)} %param.20) | copy-start | bytes 24580
  11.4 12.7 %copy-start.6 = (f32[2048]{0:T(1024)S(1)}, f32[2048]{0:T(1024)}, u32[]{:S(2)}) copy-start(f32[2048]{0:T(1024)} %param.22) | copy-start | bytes 24580
  16.7 5.8 %collective-permute-start.3 = (bf16[288,256]{1,0:T(8,128)(2,1)S(1)}, bf16[288,256]{1,0:T(8,128)(2,1)S(1)}, u32[]{:S(2)}, u32[]{:S(2)}) collective-permute-start(bf16[288,256]{1,0:T(8,128)(2,1)S(1)} %get-tuple-element.17.refs_10_), channel_id=1, source_target_pairs={{0,2},{1,3},{2,0},{3,1},{4,6},{5,7},{6,4},{7,5},{8,10},{9,11},{10,... | collective-permute-start | bytes 442376 | tf_op jit(solution)/shard_map/ppermute | solution.py:340
  18.2 5.8 %collective-permute-start.6 = (bf16[40,2048]{1,0:T(8,128)(2,1)S(1)}, bf16[40,2048]{1,0:T(8,128)(2,1)S(1)}, u32[]{:S(2)}, u32[]{:S(2)}) collective-permute-start(bf16[40,2048]{1,0:T(8,128)(2,1)S(1)} %collective-permute-done.1.refs_9_.refs_16_), channel_id=1, source_target_pairs={{0,4},{4,0},{8,12},{12,8},{1,5},{5,1},{9,13},{13,9},{2,6},{6,2},{1... | collective-permute-start | bytes 491528 | tf_op jit(solution)/shard_map/ppermute | solution.py:340
  19.6 2.9 %collective-permute-start.5 = (bf16[288,256]{1,0:T(8,128)(2,1)S(1)}, bf16[288,256]{1,0:T(8,128)(2,1)S(1)}, u32[]{:S(2)}, u32[]{:S(2)}) collective-permute-start(bf16[288,256]{1,0:T(8,128)(2,1)S(1)} %get-tuple-element.17.refs_10_), channel_id=1, source_target_pairs={{0,1},{1,0},{2,3},{3,2},{4,5},{5,4},{6,7},{7,6},{8,9},{9,8},{10,11... | collective-permute-start | bytes 442376 | tf_op jit(solution)/shard_map/ppermute | solution.py:340
  22.5 1.5 %collective-permute-start.4 = (bf16[288,256]{1,0:T(8,128)(2,1)S(1)}, bf16[288,256]{1,0:T(8,128)(2,1)S(1)}, u32[]{:S(2)}, u32[]{:S(2)}) collective-permute-start(bf16[288,256]{1,0:T(8,128)(2,1)S(1)} %collective-permute-done.3.refs_11_), channel_id=1, source_target_pairs={{0,1},{1,0},{2,3},{3,2},{4,5},{5,4},{6,7},{7,6},{8,9},{9,8},{10,11... | collective-permute-start | bytes 442376 | tf_op jit(solution)/shard_map/ppermute | solution.py:340

commit v13 on v12

--- a/solution.py
+++ b/solution.py
@@ -141,9 +141,9 @@
 def history_kernel(dims, refs_in, refs_out, scratch):
     dims, block, firsts = dims
     per_dev, n_replica, slots, _ = dims
-    holder, slot_id, prefix_len, head_ref, part_ref, wt_ref, cw_ref = refs_in[:7]
-    pieces = refs_in[7:]
-    mixed_ref, fixed_ref = refs_out
+    holder, slot_id, prefix_len, head_ref, wt_ref, cw_ref = refs_in[:6]
+    pieces = refs_in[6:]
+    mixed_ref, part_ref = refs_out
     taps = cw_ref.shape[0]
     me = lax.axis_index("replica")
     places, slot_ids, lengths = request_places(dims, (holder, slot_id, prefix_len), me)
@@ -162,8 +162,15 @@
     mixed = silu(jnp.concatenate(sums, axis=0)).astype(BF16)
     mixed_ref[...] = mixed
     part = lax.dot_general(wt_ref[...], mixed, NT, preferred_element_type=F32)
-    fixed_ref[...] = part_ref[...]
-    fixed_ref[:, : per_dev * taps] = part.astype(BF16)
+    part_ref[...] = part.T.astype(BF16)
+
+
+def merge_kernel(dims, refs_in, refs_out, scratch):
+    part_ref, across_ref, head_ref, head_across_ref = refs_in
+    (sum_ref,) = refs_out
+    head = head_ref[...].astype(F32) + head_across_ref[...].astype(F32)
+    sum_ref[...] = (part_ref[...].astype(F32) + across_ref[...].astype(F32)).astype(BF16)
+    sum_ref[:, : head_ref.shape[0]] = head.T.astype(BF16)
 
 
 def scan_kernel(dims, refs_in, refs_out, scratch):
@@ -397,18 +404,21 @@
             dma((n_chunks + 2,)),
         ],
     )
-    mixed_head, part = call(
+    mixed_head, part_head = call(
         history_kernel, (dims, block, firsts), "history", 20,
-        requests
-        + [(value, "vmem") for value in [head_sums, part, weights, conv_weight] + conv_pieces],
-        [((head, channels), BF16, "vmem"), ((out_cols, rows), BF16, "vmem")],
+        requests + [(value, "vmem") for value in [head_sums, weights, conv_weight] + conv_pieces],
+        [((head, channels), BF16, "vmem"), ((head, out_cols), BF16, "vmem")],
         [],
     )
-    parts = [part]
     mask = n_tensor // 2
-    while mask:
-        parts = parts + [swap(value, "tensor", n_tensor, mask) for value in reversed(parts)]
-        mask //= 2
+    pairs = [part, swap(part, "tensor", n_tensor, mask), part_head, swap(part_head, "tensor", n_tensor, mask)]
+    (merged,) = call(
+        merge_kernel, None, "merge", 20,
+        [(value, "vmem") for value in pairs],
+        [((out_cols, rows), BF16, "vmem")],
+        [],
+    )
+    parts = [merged] + [swap(merged, "tensor", n_tensor, k) for k in range(1, mask)]
 
     n_tiles = channels // LANES
     operands = [mixed, mixed_head, z_new, dt_proj_weight, dt_bias[None, :], a_log, d_skip[None, :]]

time: 36.7 us -> 37.2 us (1.014)
  starting transfers between devices: 8.65 us -> 10.1 us
  waiting for transfers between devices: 8.35 us -> 7.15 us
    ppermute x7, starting transfers between devices: 8.65 us -> 10.1 us  [swap(): return lax.ppermute(value, axis, [(i, i ^ mask) for i in range(size)])]
    ppermute x7, waiting for transfers between devices: 8.35 us -> 7.15 us  [swap(): return lax.ppermute(value, axis, [(i, i ^ mask) for i in range(size)])]
    pallas_call x4 -> x5, Pallas kernels: 18.7 us -> 18.8 us  [call(): pl.pallas_call(split_refs(kernel, dims, len(ins), len(outs)), in_specs=[p...]
  transfers between devices with their start and end apart: 7 -> 7, of which waited for: 4 -> 3; matrix products, arithmetic and copies ran while one was open for 0% -> 0% of each run, Pallas kernels for 11% -> 15%
where the time goes in v13:
time: 37.2 us; the launch traced here: 36.9 us
  Pallas kernels  18.8 us (51%)
  starting transfers between devices  10.1 us (27%)
  waiting for transfers between devices  7.15 us (19%)
  between operations  0.8 us (2%)
    pallas_call x5, Pallas kernels, call(): pl.pallas_call(split_refs(kernel, dims, len(ins), len(outs)), in_specs=[p...  18.8 us
    ppermute x7, starting transfers between devices, swap(): return lax.ppermute(value, axis, [(i, i ^ mask) for i in range(size)])  10.1 us
    ppermute x7, waiting for transfers between devices, swap(): return lax.ppermute(value, axis, [(i, i ^ mask) for i in range(size)])  7.15 us
  transfers between devices with their start and end apart: 7, of which 3 were waited for; matrix products, arithmetic and copies ran while one was open for 0% of the time, Pallas kernels for 15%

profile of v13, /device:TPU:0, one launch (start us, length us, event | category | flops | bytes accessed | tf_op | source)
XLA Modules:
  0.0 36.9 jit_solution(17393655273224164031)
XLA Ops:
  0.6 0.0 copy-start
  0.6 0.0 copy-start.4
  0.7 1.0 %pack.1 = (bf16[40,2048]{1,0:T(8,128)(2,1)S(1)}, bf16[8,2048]{1,0:T(8,128)(2,1)S(1)}) custom-call(bf16[32,2048]{1,0:T(8,128)(2,1)} %bitcast.11, bf16[3,2,2048]{2,1,0:T(2,128)(2,1)} %bitcast.12), custom_call_target="tpu_custom_call" | custom-call | tf_op jit(solution)/shard_map/pack/pallas_call | solution.py:335
  1.7 5.1 %collective-permute-start.1 = (bf16[40,2048]{1,0:T(8,128)(2,1)S(1)}, bf16[40,2048]{1,0:T(8,128)(2,1)S(1)}, u32[]{:S(2)}, u32[]{:S(2)}) collective-permute-start(bf16[40,2048]{1,0:T(8,128)(2,1)S(1)} %get-tuple-element.13.refs_6_.refs_12_), channel_id=1, source_target_pairs={{0,12},{4,8},{8,4},{12,0},{1,13},{5,9},{9,5},{13,1},{2,14},{6,10},... | collective-permute-start | bytes 491528 | tf_op jit(solution)/shard_map/ppermute | solution.py:347
  6.8 0.0 collective-permute-start
  6.8 3.9 %conv_project.1 = (bf16[256,2048]{1,0:T(8,128)(2,1)S(1)}, f32[32,2048]{1,0:T(8,128)S(1)}, bf16[288,256]{1,0:T(8,128)(2,1)S(1)}) custom-call(bf16[256,2048]{1,0:T(8,128)(2,1)} %refs_0_.3, bf16[288,2048]{1,0:T(8,128)(2,1)} %bitcast.7, bf16[4,2048]{1,0:T(4,128)(2,1)} %refs_5_.2, f32[1,2048]{1,0:T(1,128)} %bitcast.13), custom_call_target="tpu_custom_call" | custom-call | tf_op jit(solution)/shard_map/conv_project/pallas_call | solution.py:335
  10.7 1.6 %collective-permute-start.3 = (bf16[288,256]{1,0:T(8,128)(2,1)S(1)}, bf16[288,256]{1,0:T(8,128)(2,1)S(1)}, u32[]{:S(2)}, u32[]{:S(2)}) collective-permute-start(bf16[288,256]{1,0:T(8,128)(2,1)S(1)} %get-tuple-element.16.refs_0_), channel_id=1, source_target_pairs={{0,2},{1,3},{2,0},{3,1},{4,6},{5,7},{6,4},{7,5},{8,10},{9,11},{10,... | collective-permute-start | bytes 442376 | tf_op jit(solution)/shard_map/ppermute | solution.py:347
  12.3 0.8 %collective-permute-start.2 = (bf16[8,2048]{1,0:T(8,128)(2,1)S(1)}, bf16[8,2048]{1,0:T(8,128)(2,1)S(1)}, u32[]{:S(2)}, u32[]{:S(2)}) collective-permute-start(bf16[8,2048]{1,0:T(8,128)(2,1)S(1)} %get-tuple-element.14), channel_id=1, source_target_pairs={{0,8},{4,12},{8,0},{12,4},{1,9},{5,13},{9,1},{13,5},{2,10},{6,14},... | collective-permute-start | bytes 98312 | tf_op jit(solution)/shard_map/ppermute | solution.py:347
  13.1 4.0 %collective-permute-done.2.refs_9_ = bf16[8,2048]{1,0:T(8,128)(2,1)S(1)} collective-permute-done((bf16[8,2048]{1,0:T(8,128)(2,1)S(1)}, bf16[8,2048]{1,0:T(8,128)(2,1)S(1)}, u32[]{:S(2)}, u32[]{:S(2)}) %collective-permute-start.2) | collective-permute-done | bytes 32800 | tf_op jit(solution)/shard_map/ppermute | solution.py:347
  17.1 0.0 collective-permute-done.1.refs_8_.refs_14_
  17.2 0.0 copy-start.1
  17.2 0.0 copy-start.2
  17.2 0.0 copy-start.3
  17.2 0.0 copy-start.5
  17.2 0.0 copy-start.6
  17.2 1.4 %history.1 = (bf16[32,2048]{1,0:T(8,128)(2,1)S(1)}, bf16[32,288]{1,0:T(8,128)(2,1)S(1)}) custom-call(s32[32]{0:T(128)S(1)} %copy-done.7, s32[32]{0:T(128)S(1)} %copy-done.8, s32[32]{0:T(128)S(1)} %copy-done.9, f32[32,2048]{1,0:T(8,128)S(1)} %get-tuple-element.12.refs_3_, bf16[288,2048]{1,0:T(8,128)(2,1)S(1)} %bitcast.8, bf16[4,2048]{1,0:T(4,128)(2,1)S(1)} %copy-done.4, ...), custom_call_target="tpu_custom_call" | custom-call | tf_op jit(solution)/shard_map/history/pallas_call | solution.py:335
  18.6 0.6 %collective-permute-start.4 = (bf16[32,288]{1,0:T(8,128)(2,1)S(1)}, bf16[32,288]{1,0:T(8,128)(2,1)S(1)}, u32[]{:S(2)}, u32[]{:S(2)}) collective-permute-start(bf16[32,288]{1,0:T(8,128)(2,1)S(1)} %get-tuple-element.17.refs_2_), channel_id=1, source_target_pairs={{0,2},{1,3},{2,0},{3,1},{4,6},{5,7},{6,4},{7,5},{8,10},{9,11},{10,... | collective-permute-start | bytes 55304 | tf_op jit(solution)/shard_map/ppermute | solution.py:347
  19.2 2.0 %collective-permute-start.6 = (bf16[40,2048]{1,0:T(8,128)(2,1)S(1)}, bf16[40,2048]{1,0:T(8,128)(2,1)S(1)}, u32[]{:S(2)}, u32[]{:S(2)}) collective-permute-start(bf16[40,2048]{1,0:T(8,128)(2,1)S(1)} %collective-permute-done.1.refs_8_.refs_14_), channel_id=1, source_target_pairs={{0,4},{4,0},{8,12},{12,8},{1,5},{5,1},{9,13},{13,9},{2,6},{6,2},{1... | collective-permute-start | bytes 491528 | tf_op jit(solution)/shard_map/ppermute | solution.py:347
  21.2 0.0 collective-permute-done.3.refs_1_
  21.2 1.3 %collective-permute-done.4.refs_3_ = bf16[32,288]{1,0:T(8,128)(2,1)S(1)} collective-permute-done((bf16[32,288]{1,0:T(8,128)(2,1)S(1)}, bf16[32,288]{1,0:T(8,128)(2,1)S(1)}, u32[]{:S(2)}, u32[]{:S(2)}) %collective-permute-start.4) | collective-permute-done | bytes 18464 | tf_op jit(solution)/shard_map/ppermute | solution.py:347
  22.5 0.1 merge.1.refs_10_
  22.6 0.1 collective-permute-start.5
  22.7 1.8 %collective-permute-done.6.refs_15_ = bf16[40,2048]{1,0:T(8,128)(2,1)S(1)} collective-permute-done((bf16[40,2048]{1,0:T(8,128)(2,1)S(1)}, bf16[40,2048]{1,0:T(8,128)(2,1)S(1)}, u32[]{:S(2)}, u32[]{:S(2)}) %collective-permute-start.6) | collective-permute-done | bytes 163872 | tf_op jit(solution)/shard_map/ppermute | solution.py:347
  24.6 12.4 %dt_scan_gate.1 = (bf16[256,2048]{1,0:T(8,128)(2,1)}, bf16[128,2048]{1,0:T(8,128)(2,1)}) custom-call(s32[32]{0:T(128)S(1)} %copy-done.7, s32[32]{0:T(128)S(1)} %copy-done.8, s32[32]{0:T(128)S(1)} %copy-done.9, bf16[256,2048]{1,0:T(8,128)(2,1)S(1)} %get-tuple-element.11.refs_3_, bf16[32,2048]{1,0:T(8,128)(2,1)S(1)} %get-tuple-element.15.refs_4_, ...), custom_call_target="tpu_custom_call" | custom-call | tf_op jit(solution)/shard_map/dt_scan_gate/pallas_call | solution.py:335
  (15 shorter events, 0.0 us)
Async XLA Ops:
  0.6 16.5 %copy-start = (bf16[2048,288]{0,1:T(8,128)(2,1)S(1)}, bf16[2048,288]{0,1:T(8,128)(2,1)}, u32[]{:S(2)}) copy-start(bf16[2048,288]{0,1:T(8,128)(2,1)} %param.18) | copy-start | bytes 3538948
  0.6 16.5 %copy-start.4 = (bf16[4,2048]{1,0:T(4,128)(2,1)S(1)}, bf16[4,2048]{1,0:T(4,128)(2,1)}, u32[]{:S(2)}) copy-start(bf16[4,2048]{1,0:T(4,128)(2,1)} %refs_5_.2) | copy-start | bytes 49156
  0.7 16.5 %copy-start.7 = (s32[32]{0:T(128)S(1)}, s32[32]{0:T(128)}, u32[]{:S(2)}) copy-start(s32[32]{0:T(128)} %refs_0_.5) | copy-start | bytes 388
  0.7 16.5 %copy-start.8 = (s32[32]{0:T(128)S(1)}, s32[32]{0:T(128)}, u32[]{:S(2)}) copy-start(s32[32]{0:T(128)} %refs_1_.3) | copy-start | bytes 388
  0.7 16.5 %copy-start.9 = (s32[32]{0:T(128)S(1)}, s32[32]{0:T(128)}, u32[]{:S(2)}) copy-start(s32[32]{0:T(128)} %refs_2_.5) | copy-start | bytes 388
  1.7 15.4 %collective-permute-start.1 = (bf16[40,2048]{1,0:T(8,128)(2,1)S(1)}, bf16[40,2048]{1,0:T(8,128)(2,1)S(1)}, u32[]{:S(2)}, u32[]{:S(2)}) collective-permute-start(bf16[40,2048]{1,0:T(8,128)(2,1)S(1)} %get-tuple-element.13.refs_6_.refs_12_), channel_id=1, source_target_pairs={{0,12},{4,8},{8,4},{12,0},{1,13},{5,9},{9,5},{13,1},{2,14},{6,10},... | collective-permute-start | bytes 491528 | tf_op jit(solution)/shard_map/ppermute | solution.py:347
  6.8 10.3 %collective-permute-start = (bf16[40,2048]{1,0:T(8,128)(2,1)S(1)}, bf16[40,2048]{1,0:T(8,128)(2,1)S(1)}, u32[]{:S(2)}, u32[]{:S(2)}) collective-permute-start(bf16[40,2048]{1,0:T(8,128)(2,1)S(1)} %get-tuple-element.13.refs_6_.refs_12_), channel_id=1, source_target_pairs={{0,4},{4,0},{8,12},{12,8},{1,5},{5,1},{9,13},{13,9},{2,6},{6,2},{1... | collective-permute-start | bytes 491528 | tf_op jit(solution)/shard_map/ppermute | solution.py:347
  10.7 10.5 %collective-permute-start.3 = (bf16[288,256]{1,0:T(8,128)(2,1)S(1)}, bf16[288,256]{1,0:T(8,128)(2,1)S(1)}, u32[]{:S(2)}, u32[]{:S(2)}) collective-permute-start(bf16[288,256]{1,0:T(8,128)(2,1)S(1)} %get-tuple-element.16.refs_0_), channel_id=1, source_target_pairs={{0,2},{1,3},{2,0},{3,1},{4,6},{5,7},{6,4},{7,5},{8,10},{9,11},{10,... | collective-permute-start | bytes 442376 | tf_op jit(solution)/shard_map/ppermute | solution.py:347
  12.3 4.8 %collective-permute-start.2 = (bf16[8,2048]{1,0:T(8,128)(2,1)S(1)}, bf16[8,2048]{1,0:T(8,128)(2,1)S(1)}, u32[]{:S(2)}, u32[]{:S(2)}) collective-permute-start(bf16[8,2048]{1,0:T(8,128)(2,1)S(1)} %get-tuple-element.14), channel_id=1, source_target_pairs={{0,8},{4,12},{8,0},{12,4},{1,9},{5,13},{9,1},{13,5},{2,10},{6,14},... | collective-permute-start | bytes 98312 | tf_op jit(solution)/shard_map/ppermute | solution.py:347
  17.2 7.4 %copy-start.1 = (bf16[256,2048]{1,0:T(8,128)(2,1)S(1)}, bf16[256,2048]{1,0:T(8,128)(2,1)}, u32[]{:S(2)}) copy-start(bf16[256,2048]{1,0:T(8,128)(2,1)} %refs_5_.3) | copy-start | bytes 3145732
  17.2 7.4 %copy-start.2 = (bf16[256,2048]{1,0:T(8,128)(2,1)S(1)}, bf16[256,2048]{1,0:T(8,128)(2,1)}, u32[]{:S(2)}) copy-start(bf16[256,2048]{1,0:T(8,128)(2,1)} %refs_6_.1) | copy-start | bytes 3145732
  17.2 7.4 %copy-start.3 = (f32[16,2048]{1,0:T(8,128)S(1)}, f32[16,2048]{1,0:T(8,128)}, u32[]{:S(2)}) copy-start(f32[16,2048]{1,0:T(8,128)} %refs_8_.1) | copy-start | bytes 393220
  17.2 7.4 %copy-start.5 = (f32[2048]{0:T(1024)S(1)}, f32[2048]{0:T(1024)}, u32[]{:S(2)}) copy-start(f32[2048]{0:T(1024)} %param.20) | copy-start | bytes 24580
  17.2 7.4 %copy-start.6 = (f32[2048]{0:T(1024)S(1)}, f32[2048]{0:T(1024)}, u32[]{:S(2)}) copy-start(f32[2048]{0:T(1024)} %param.22) | copy-start | bytes 24580
  18.6 3.9 %collective-permute-start.4 = (bf16[32,288]{1,0:T(8,128)(2,1)S(1)}, bf16[32,288]{1,0:T(8,128)(2,1)S(1)}, u32[]{:S(2)}, u32[]{:S(2)}) collective-permute-start(bf16[32,288]{1,0:T(8,128)(2,1)S(1)} %get-tuple-element.17.refs_2_), channel_id=1, source_target_pairs={{0,2},{1,3},{2,0},{3,1},{4,6},{5,7},{6,4},{7,5},{8,10},{9,11},{10,... | collective-permute-start | bytes 55304 | tf_op jit(solution)/shard_map/ppermute | solution.py:347
  19.2 5.3 %collective-permute-start.6 = (bf16[40,2048]{1,0:T(8,128)(2,1)S(1)}, bf16[40,2048]{1,0:T(8,128)(2,1)S(1)}, u32[]{:S(2)}, u32[]{:S(2)}) collective-permute-start(bf16[40,2048]{1,0:T(8,128)(2,1)S(1)} %collective-permute-done.1.refs_8_.refs_14_), channel_id=1, source_target_pairs={{0,4},{4,0},{8,12},{12,8},{1,5},{5,1},{9,13},{13,9},{2,6},{6,2},{1... | collective-permute-start | bytes 491528 | tf_op jit(solution)/shard_map/ppermute | solution.py:347
  22.6 1.9 %collective-permute-start.5 = (bf16[288,256]{1,0:T(8,128)(2,1)S(1)}, bf16[288,256]{1,0:T(8,128)(2,1)S(1)}, u32[]{:S(2)}, u32[]{:S(2)}) collective-permute-start(bf16[288,256]{1,0:T(8,128)(2,1)S(1)} %merge.1.refs_10_), channel_id=1, source_target_pairs={{0,1},{1,0},{2,3},{3,2},{4,5},{5,4},{6,7},{7,6},{8,9},{9,8},{10,11... | collective-permute-start | bytes 442376 | tf_op jit(solution)/shard_map/ppermute | solution.py:347

commit v14 on v12

--- a/solution.py
+++ b/solution.py
@@ -185,16 +185,26 @@
     projected = parts[0][...].astype(F32)
     for part in parts[1:]:
         projected = projected + part[...].astype(F32)
-    projected = projected.T
+    c_part = projected[rank + states :]
+    c_high = c_part.astype(BF16).astype(F32)
+    shape = (2 * states, states * LANES)
+    term = lax.broadcasted_iota(jnp.int32, shape, 0) & (states - 1)
+    lane_group, _ = split_index(lax.broadcasted_iota(jnp.int32, shape, 1), LANES)
+    spread = jnp.where(term == lane_group, 1.0, 0.0).astype(BF16)
+    c_terms = jnp.concatenate([c_high, c_part - c_high], axis=0).T.astype(BF16)
+    projected = projected[: rank + states].T
     dt_low = projected[:, :rank].astype(BF16)
     late = projected[:, rank:]
     n_tiles = channels // LANES
     wide = min(4, n_tiles)
-    per_chunk = 2 * states * wide // n_tiles
+    per_chunk = states * wide // n_tiles
     for c in range(n_tiles // wide):
         for n in range(c * per_chunk, (c + 1) * per_chunk):
-            table = b_tab if n < states else c_tab
-            table[n % states] = jnp.broadcast_to(late[:, n : n + 1], (rows, LANES))
+            b_tab[n] = jnp.broadcast_to(late[:, n : n + 1], (rows, LANES))
+        lanes = slice(c * per_chunk * LANES, (c + 1) * per_chunk * LANES)
+        repeated = jnp.dot(c_terms, spread[:, lanes], preferred_element_type=F32)
+        for n in range(per_chunk):
+            c_tab[c * per_chunk + n] = repeated[:, n * LANES : (n + 1) * LANES]
         weights = dtw_ref[:, c * wide * LANES : (c + 1) * wide * LANES]
         raw = jnp.dot(dt_low, weights, preferred_element_type=F32)
         for j in range(wide):

time: 36.7 us -> 36.3 us (0.989)
  Pallas kernels: 18.7 us -> 18.3 us
    pallas_call x4, Pallas kernels: 18.7 us -> 18.3 us  [call(): pl.pallas_call(split_refs(kernel, dims, len(ins), len(outs)), in_specs=[p...]
where the time goes in v14:
time: 36.3 us; the launch traced here: 36.1 us
  Pallas kernels  18.3 us (50%)
  starting transfers between devices  8.65 us (24%)
  waiting for transfers between devices  8.35 us (23%)
  between operations  0.78 us (2%)
    pallas_call x4, Pallas kernels, call(): pl.pallas_call(split_refs(kernel, dims, len(ins), len(outs)), in_specs=[p...  18.3 us
    ppermute x7, starting transfers between devices, swap(): return lax.ppermute(value, axis, [(i, i ^ mask) for i in range(size)])  8.65 us
    ppermute x7, waiting for transfers between devices, swap(): return lax.ppermute(value, axis, [(i, i ^ mask) for i in range(size)])  8.35 us
  transfers between devices with their start and end apart: 7, of which 4 were waited for; matrix products, arithmetic and copies ran while one was open for 0% of the time, Pallas kernels for 11%

profile of v14, /device:TPU:0, one launch (start us, length us, event | category | flops | bytes accessed | tf_op | source)
XLA Modules:
  0.0 36.1 jit_solution(3164734047420001606)
XLA Ops:
  0.6 0.0 copy-start
  0.6 0.0 copy-start.4
  0.7 1.0 %pack.1 = (bf16[40,2048]{1,0:T(8,128)(2,1)S(1)}, bf16[8,2048]{1,0:T(8,128)(2,1)S(1)}) custom-call(bf16[32,2048]{1,0:T(8,128)(2,1)} %bitcast.11, bf16[3,2,2048]{2,1,0:T(2,128)(2,1)} %bitcast.12), custom_call_target="tpu_custom_call" | custom-call | tf_op jit(solution)/shard_map/pack/pallas_call | solution.py:338
  1.7 5.1 %collective-permute-start.1 = (bf16[40,2048]{1,0:T(8,128)(2,1)S(1)}, bf16[40,2048]{1,0:T(8,128)(2,1)S(1)}, u32[]{:S(2)}, u32[]{:S(2)}) collective-permute-start(bf16[40,2048]{1,0:T(8,128)(2,1)S(1)} %get-tuple-element.14.refs_7_.refs_14_), channel_id=1, source_target_pairs={{0,12},{4,8},{8,4},{12,0},{1,13},{5,9},{9,5},{13,1},{2,14},{6,10},... | collective-permute-start | bytes 491528 | tf_op jit(solution)/shard_map/ppermute | solution.py:350
  6.8 0.0 collective-permute-start
  6.8 0.6 %collective-permute-start.2 = (bf16[8,2048]{1,0:T(8,128)(2,1)S(1)}, bf16[8,2048]{1,0:T(8,128)(2,1)S(1)}, u32[]{:S(2)}, u32[]{:S(2)}) collective-permute-start(bf16[8,2048]{1,0:T(8,128)(2,1)S(1)} %get-tuple-element.15), channel_id=1, source_target_pairs={{0,8},{4,12},{8,0},{12,4},{1,9},{5,13},{9,1},{13,5},{2,10},{6,14},... | collective-permute-start | bytes 98312 | tf_op jit(solution)/shard_map/ppermute | solution.py:350
  7.5 3.9 %conv_project.1 = (bf16[256,2048]{1,0:T(8,128)(2,1)S(1)}, f32[32,2048]{1,0:T(8,128)S(1)}, bf16[288,256]{1,0:T(8,128)(2,1)S(1)}) custom-call(bf16[256,2048]{1,0:T(8,128)(2,1)} %refs_0_.3, bf16[288,2048]{1,0:T(8,128)(2,1)} %bitcast.7, bf16[4,2048]{1,0:T(4,128)(2,1)} %refs_6_.2, f32[1,2048]{1,0:T(1,128)} %bitcast.13), custom_call_target="tpu_custom_call" | custom-call | tf_op jit(solution)/shard_map/conv_project/pallas_call | solution.py:338
  11.4 0.0 copy-start.1
  11.4 0.0 copy-start.2
  11.4 0.0 copy-start.5
  11.4 0.0 copy-start.6
  11.5 3.4 %collective-permute-done.2.refs_10_ = bf16[8,2048]{1,0:T(8,128)(2,1)S(1)} collective-permute-done((bf16[8,2048]{1,0:T(8,128)(2,1)S(1)}, bf16[8,2048]{1,0:T(8,128)(2,1)S(1)}, u32[]{:S(2)}, u32[]{:S(2)}) %collective-permute-start.2) | collective-permute-done | bytes 32800 | tf_op jit(solution)/shard_map/ppermute | solution.py:350
  14.8 0.0 collective-permute-done.1.refs_9_.refs_16_
  14.8 0.5 %collective-permute-done.refs_8_.refs_15_ = bf16[40,2048]{1,0:T(8,128)(2,1)S(1)} collective-permute-done((bf16[40,2048]{1,0:T(8,128)(2,1)S(1)}, bf16[40,2048]{1,0:T(8,128)(2,1)S(1)}, u32[]{:S(2)}, u32[]{:S(2)}) %collective-permute-start) | collective-permute-done | bytes 163872 | tf_op jit(solution)/shard_map/ppermute | solution.py:350
  15.4 1.3 %history.1 = (bf16[32,2048]{1,0:T(8,128)(2,1)S(1)}, bf16[288,256]{1,0:T(8,128)(2,1)S(1)}) custom-call(s32[32]{0:T(128)S(1)} %copy-done.7, s32[32]{0:T(128)S(1)} %copy-done.8, s32[32]{0:T(128)S(1)} %copy-done.9, f32[32,2048]{1,0:T(8,128)S(1)} %get-tuple-element.12.refs_3_, bf16[288,256]{1,0:T(8,128)(2,1)S(1)} %get-tuple-element.13.refs_4_, ...), custom_call_target="tpu_custom_call" | custom-call | tf_op jit(solution)/shard_map/history/pallas_call | solution.py:338
  16.7 1.6 %collective-permute-start.3 = (bf16[288,256]{1,0:T(8,128)(2,1)S(1)}, bf16[288,256]{1,0:T(8,128)(2,1)S(1)}, u32[]{:S(2)}, u32[]{:S(2)}) collective-permute-start(bf16[288,256]{1,0:T(8,128)(2,1)S(1)} %get-tuple-element.17.refs_10_), channel_id=1, source_target_pairs={{0,2},{1,3},{2,0},{3,1},{4,6},{5,7},{6,4},{7,5},{8,10},{9,11},{10,... | collective-permute-start | bytes 442376 | tf_op jit(solution)/shard_map/ppermute | solution.py:350
  18.2 1.3 %collective-permute-start.6 = (bf16[40,2048]{1,0:T(8,128)(2,1)S(1)}, bf16[40,2048]{1,0:T(8,128)(2,1)S(1)}, u32[]{:S(2)}, u32[]{:S(2)}) collective-permute-start(bf16[40,2048]{1,0:T(8,128)(2,1)S(1)} %collective-permute-done.1.refs_9_.refs_16_), channel_id=1, source_target_pairs={{0,4},{4,0},{8,12},{12,8},{1,5},{5,1},{9,13},{13,9},{2,6},{6,2},{1... | collective-permute-start | bytes 491528 | tf_op jit(solution)/shard_map/ppermute | solution.py:350
  19.6 0.0 collective-permute-start.5
  19.6 2.9 %collective-permute-done.3.refs_11_ = bf16[288,256]{1,0:T(8,128)(2,1)S(1)} collective-permute-done((bf16[288,256]{1,0:T(8,128)(2,1)S(1)}, bf16[288,256]{1,0:T(8,128)(2,1)S(1)}, u32[]{:S(2)}, u32[]{:S(2)}) %collective-permute-start.3) | collective-permute-done | bytes 147488 | tf_op jit(solution)/shard_map/ppermute | solution.py:350
  22.5 0.0 collective-permute-start.4
  22.5 0.0 collective-permute-done.5.refs_13_
  22.5 1.5 %collective-permute-done.6.refs_17_ = bf16[40,2048]{1,0:T(8,128)(2,1)S(1)} collective-permute-done((bf16[40,2048]{1,0:T(8,128)(2,1)S(1)}, bf16[40,2048]{1,0:T(8,128)(2,1)S(1)}, u32[]{:S(2)}, u32[]{:S(2)}) %collective-permute-start.6) | collective-permute-done | bytes 163872 | tf_op jit(solution)/shard_map/ppermute | solution.py:350
  24.1 0.0 collective-permute-done.4.refs_12_
  24.1 12.0 %dt_scan_gate.1 = (bf16[256,2048]{1,0:T(8,128)(2,1)}, bf16[128,2048]{1,0:T(8,128)(2,1)}) custom-call(s32[32]{0:T(128)S(1)} %copy-done.7, s32[32]{0:T(128)S(1)} %copy-done.8, s32[32]{0:T(128)S(1)} %copy-done.9, bf16[256,2048]{1,0:T(8,128)(2,1)S(1)} %get-tuple-element.11.refs_3_, bf16[32,2048]{1,0:T(8,128)(2,1)S(1)} %get-tuple-element.16.refs_4_, ...), custom_call_target="tpu_custom_call" | custom-call | tf_op jit(solution)/shard_map/dt_scan_gate/pallas_call | solution.py:338
  (14 shorter events, 0.0 us)
Async XLA Ops:
  0.6 14.7 %copy-start = (bf16[2048,288]{0,1:T(8,128)(2,1)S(1)}, bf16[2048,288]{0,1:T(8,128)(2,1)}, u32[]{:S(2)}) copy-start(bf16[2048,288]{0,1:T(8,128)(2,1)} %param.18) | copy-start | bytes 3538948
  0.6 14.7 %copy-start.4 = (bf16[4,2048]{1,0:T(4,128)(2,1)S(1)}, bf16[4,2048]{1,0:T(4,128)(2,1)}, u32[]{:S(2)}) copy-start(bf16[4,2048]{1,0:T(4,128)(2,1)} %refs_6_.2) | copy-start | bytes 49156
  0.7 14.7 %copy-start.7 = (s32[32]{0:T(128)S(1)}, s32[32]{0:T(128)}, u32[]{:S(2)}) copy-start(s32[32]{0:T(128)} %refs_0_.5) | copy-start | bytes 388
  0.7 14.7 %copy-start.8 = (s32[32]{0:T(128)S(1)}, s32[32]{0:T(128)}, u32[]{:S(2)}) copy-start(s32[32]{0:T(128)} %refs_1_.3) | copy-start | bytes 388
  0.7 14.7 %copy-start.9 = (s32[32]{0:T(128)S(1)}, s32[32]{0:T(128)}, u32[]{:S(2)}) copy-start(s32[32]{0:T(128)} %refs_2_.5) | copy-start | bytes 388
  1.7 13.1 %collective-permute-start.1 = (bf16[40,2048]{1,0:T(8,128)(2,1)S(1)}, bf16[40,2048]{1,0:T(8,128)(2,1)S(1)}, u32[]{:S(2)}, u32[]{:S(2)}) collective-permute-start(bf16[40,2048]{1,0:T(8,128)(2,1)S(1)} %get-tuple-element.14.refs_7_.refs_14_), channel_id=1, source_target_pairs={{0,12},{4,8},{8,4},{12,0},{1,13},{5,9},{9,5},{13,1},{2,14},{6,10},... | collective-permute-start | bytes 491528 | tf_op jit(solution)/shard_map/ppermute | solution.py:350
  6.8 8.5 %collective-permute-start = (bf16[40,2048]{1,0:T(8,128)(2,1)S(1)}, bf16[40,2048]{1,0:T(8,128)(2,1)S(1)}, u32[]{:S(2)}, u32[]{:S(2)}) collective-permute-start(bf16[40,2048]{1,0:T(8,128)(2,1)S(1)} %get-tuple-element.14.refs_7_.refs_14_), channel_id=1, source_target_pairs={{0,4},{4,0},{8,12},{12,8},{1,5},{5,1},{9,13},{13,9},{2,6},{6,2},{1... | collective-permute-start | bytes 491528 | tf_op jit(solution)/shard_map/ppermute | solution.py:350
  6.8 8.0 %collective-permute-start.2 = (bf16[8,2048]{1,0:T(8,128)(2,1)S(1)}, bf16[8,2048]{1,0:T(8,128)(2,1)S(1)}, u32[]{:S(2)}, u32[]{:S(2)}) collective-permute-start(bf16[8,2048]{1,0:T(8,128)(2,1)S(1)} %get-tuple-element.15), channel_id=1, source_target_pairs={{0,8},{4,12},{8,0},{12,4},{1,9},{5,13},{9,1},{13,5},{2,10},{6,14},... | collective-permute-start | bytes 98312 | tf_op jit(solution)/shard_map/ppermute | solution.py:350
  7.5 16.6 %copy-start.3 = (f32[16,2048]{1,0:T(8,128)S(1)}, f32[16,2048]{1,0:T(8,128)}, u32[]{:S(2)}) copy-start(f32[16,2048]{1,0:T(8,128)} %refs_8_.1) | copy-start | bytes 393220
  11.4 12.7 %copy-start.1 = (bf16[256,2048]{1,0:T(8,128)(2,1)S(1)}, bf16[256,2048]{1,0:T(8,128)(2,1)}, u32[]{:S(2)}) copy-start(bf16[256,2048]{1,0:T(8,128)(2,1)} %refs_5_.1) | copy-start | bytes 3145732
  11.4 12.7 %copy-start.2 = (bf16[256,2048]{1,0:T(8,128)(2,1)S(1)}, bf16[256,2048]{1,0:T(8,128)(2,1)}, u32[]{:S(2)}) copy-start(bf16[256,2048]{1,0:T(8,128)(2,1)} %refs_6_.3) | copy-start | bytes 3145732
  11.4 12.7 %copy-start.5 = (f32[2048]{0:T(1024)S(1)}, f32[2048]{0:T(1024)}, u32[]{:S(2)}) copy-start(f32[2048]{0:T(1024)} %param.20) | copy-start | bytes 24580
  11.4 12.7 %copy-start.6 = (f32[2048]{0:T(1024)S(1)}, f32[2048]{0:T(1024)}, u32[]{:S(2)}) copy-start(f32[2048]{0:T(1024)} %param.22) | copy-start | bytes 24580
  16.7 5.8 %collective-permute-start.3 = (bf16[288,256]{1,0:T(8,128)(2,1)S(1)}, bf16[288,256]{1,0:T(8,128)(2,1)S(1)}, u32[]{:S(2)}, u32[]{:S(2)}) collective-permute-start(bf16[288,256]{1,0:T(8,128)(2,1)S(1)} %get-tuple-element.17.refs_10_), channel_id=1, source_target_pairs={{0,2},{1,3},{2,0},{3,1},{4,6},{5,7},{6,4},{7,5},{8,10},{9,11},{10,... | collective-permute-start | bytes 442376 | tf_op jit(solution)/shard_map/ppermute | solution.py:350
  18.2 5.8 %collective-permute-start.6 = (bf16[40,2048]{1,0:T(8,128)(2,1)S(1)}, bf16[40,2048]{1,0:T(8,128)(2,1)S(1)}, u32[]{:S(2)}, u32[]{:S(2)}) collective-permute-start(bf16[40,2048]{1,0:T(8,128)(2,1)S(1)} %collective-permute-done.1.refs_9_.refs_16_), channel_id=1, source_target_pairs={{0,4},{4,0},{8,12},{12,8},{1,5},{5,1},{9,13},{13,9},{2,6},{6,2},{1... | collective-permute-start | bytes 491528 | tf_op jit(solution)/shard_map/ppermute | solution.py:350
  19.6 2.9 %collective-permute-start.5 = (bf16[288,256]{1,0:T(8,128)(2,1)S(1)}, bf16[288,256]{1,0:T(8,128)(2,1)S(1)}, u32[]{:S(2)}, u32[]{:S(2)}) collective-permute-start(bf16[288,256]{1,0:T(8,128)(2,1)S(1)} %get-tuple-element.17.refs_10_), channel_id=1, source_target_pairs={{0,1},{1,0},{2,3},{3,2},{4,5},{5,4},{6,7},{7,6},{8,9},{9,8},{10,11... | collective-permute-start | bytes 442376 | tf_op jit(solution)/shard_map/ppermute | solution.py:350
  22.5 1.5 %collective-permute-start.4 = (bf16[288,256]{1,0:T(8,128)(2,1)S(1)}, bf16[288,256]{1,0:T(8,128)(2,1)S(1)}, u32[]{:S(2)}, u32[]{:S(2)}) collective-permute-start(bf16[288,256]{1,0:T(8,128)(2,1)S(1)} %collective-permute-done.3.refs_11_), channel_id=1, source_target_pairs={{0,1},{1,0},{2,3},{3,2},{4,5},{5,4},{6,7},{7,6},{8,9},{9,8},{10,11... | collective-permute-start | bytes 442376 | tf_op jit(solution)/shard_map/ppermute | solution.py:350

commit v15 on v14

--- a/solution.py
+++ b/solution.py
@@ -185,26 +185,25 @@
     projected = parts[0][...].astype(F32)
     for part in parts[1:]:
         projected = projected + part[...].astype(F32)
-    c_part = projected[rank + states :]
-    c_high = c_part.astype(BF16).astype(F32)
+    late = projected[rank:]
+    high = late.astype(BF16).astype(F32)
+    low = late - high
     shape = (2 * states, states * LANES)
     term = lax.broadcasted_iota(jnp.int32, shape, 0) & (states - 1)
     lane_group, _ = split_index(lax.broadcasted_iota(jnp.int32, shape, 1), LANES)
     spread = jnp.where(term == lane_group, 1.0, 0.0).astype(BF16)
-    c_terms = jnp.concatenate([c_high, c_part - c_high], axis=0).T.astype(BF16)
-    projected = projected[: rank + states].T
-    dt_low = projected[:, :rank].astype(BF16)
-    late = projected[:, rank:]
+    b_terms = jnp.concatenate([high[:states], low[:states]], axis=0).T.astype(BF16)
+    c_terms = jnp.concatenate([high[states:], low[states:]], axis=0).T.astype(BF16)
+    dt_low = projected[:rank].T.astype(BF16)
     n_tiles = channels // LANES
     wide = min(4, n_tiles)
     per_chunk = states * wide // n_tiles
     for c in range(n_tiles // wide):
-        for n in range(c * per_chunk, (c + 1) * per_chunk):
-            b_tab[n] = jnp.broadcast_to(late[:, n : n + 1], (rows, LANES))
         lanes = slice(c * per_chunk * LANES, (c + 1) * per_chunk * LANES)
-        repeated = jnp.dot(c_terms, spread[:, lanes], preferred_element_type=F32)
-        for n in range(per_chunk):
-            c_tab[c * per_chunk + n] = repeated[:, n * LANES : (n + 1) * LANES]
+        for table, terms in ((b_tab, b_terms), (c_tab, c_terms)):
+            repeated = jnp.dot(terms, spread[:, lanes], preferred_element_type=F32)
+            for n in range(per_chunk):
+                table[c * per_chunk + n] = repeated[:, n * LANES : (n + 1) * LANES]
         weights = dtw_ref[:, c * wide * LANES : (c + 1) * wide * LANES]
         raw = jnp.dot(dt_low, weights, preferred_element_type=F32)
         for j in range(wide):

time: 36.3 us -> 36.3 us (level)
  no operation moved by 1% of the time
where the time goes in v15:
time: 36.3 us; the launch traced here: 36.2 us
  Pallas kernels  18.3 us (50%)
  starting transfers between devices  8.65 us (24%)
  waiting for transfers between devices  8.35 us (23%)
  between operations  0.78 us (2%)
    pallas_call x4, Pallas kernels, call(): pl.pallas_call(split_refs(kernel, dims, len(ins), len(outs)), in_specs=[p...  18.3 us
    ppermute x7, starting transfers between devices, swap(): return lax.ppermute(value, axis, [(i, i ^ mask) for i in range(size)])  8.65 us
    ppermute x7, waiting for transfers between devices, swap(): return lax.ppermute(value, axis, [(i, i ^ mask) for i in range(size)])  8.35 us
  transfers between devices with their start and end apart: 7, of which 4 were waited for; matrix products, arithmetic and copies ran while one was open for 0% of the time, Pallas kernels for 11%

profile of v15, /device:TPU:0, one launch (start us, length us, event | category | flops | bytes accessed | tf_op | source)
XLA Modules:
  0.0 36.2 jit_solution(11419599719716006628)
XLA Ops:
  0.6 0.0 copy-start
  0.6 0.0 copy-start.4
  0.7 1.0 %pack.1 = (bf16[40,2048]{1,0:T(8,128)(2,1)S(1)}, bf16[8,2048]{1,0:T(8,128)(2,1)S(1)}) custom-call(bf16[32,2048]{1,0:T(8,128)(2,1)} %bitcast.11, bf16[3,2,2048]{2,1,0:T(2,128)(2,1)} %bitcast.12), custom_call_target="tpu_custom_call" | custom-call | tf_op jit(solution)/shard_map/pack/pallas_call | solution.py:337
  1.7 5.1 %collective-permute-start.1 = (bf16[40,2048]{1,0:T(8,128)(2,1)S(1)}, bf16[40,2048]{1,0:T(8,128)(2,1)S(1)}, u32[]{:S(2)}, u32[]{:S(2)}) collective-permute-start(bf16[40,2048]{1,0:T(8,128)(2,1)S(1)} %get-tuple-element.14.refs_7_.refs_14_), channel_id=1, source_target_pairs={{0,12},{4,8},{8,4},{12,0},{1,13},{5,9},{9,5},{13,1},{2,14},{6,10},... | collective-permute-start | bytes 491528 | tf_op jit(solution)/shard_map/ppermute | solution.py:349
  6.8 0.0 collective-permute-start
  6.8 0.6 %collective-permute-start.2 = (bf16[8,2048]{1,0:T(8,128)(2,1)S(1)}, bf16[8,2048]{1,0:T(8,128)(2,1)S(1)}, u32[]{:S(2)}, u32[]{:S(2)}) collective-permute-start(bf16[8,2048]{1,0:T(8,128)(2,1)S(1)} %get-tuple-element.15), channel_id=1, source_target_pairs={{0,8},{4,12},{8,0},{12,4},{1,9},{5,13},{9,1},{13,5},{2,10},{6,14},... | collective-permute-start | bytes 98312 | tf_op jit(solution)/shard_map/ppermute | solution.py:349
  7.5 3.9 %conv_project.1 = (bf16[256,2048]{1,0:T(8,128)(2,1)S(1)}, f32[32,2048]{1,0:T(8,128)S(1)}, bf16[288,256]{1,0:T(8,128)(2,1)S(1)}) custom-call(bf16[256,2048]{1,0:T(8,128)(2,1)} %refs_0_.3, bf16[288,2048]{1,0:T(8,128)(2,1)} %bitcast.7, bf16[4,2048]{1,0:T(4,128)(2,1)} %refs_6_.2, f32[1,2048]{1,0:T(1,128)} %bitcast.13), custom_call_target="tpu_custom_call" | custom-call | tf_op jit(solution)/shard_map/conv_project/pallas_call | solution.py:337
  11.4 0.0 copy-start.1
  11.4 0.0 copy-start.2
  11.4 0.0 copy-start.5
  11.4 0.0 copy-start.6
  11.5 3.4 %collective-permute-done.2.refs_10_ = bf16[8,2048]{1,0:T(8,128)(2,1)S(1)} collective-permute-done((bf16[8,2048]{1,0:T(8,128)(2,1)S(1)}, bf16[8,2048]{1,0:T(8,128)(2,1)S(1)}, u32[]{:S(2)}, u32[]{:S(2)}) %collective-permute-start.2) | collective-permute-done | bytes 32800 | tf_op jit(solution)/shard_map/ppermute | solution.py:349
  14.8 0.0 collective-permute-done.1.refs_9_.refs_16_
  14.8 0.5 %collective-permute-done.refs_8_.refs_15_ = bf16[40,2048]{1,0:T(8,128)(2,1)S(1)} collective-permute-done((bf16[40,2048]{1,0:T(8,128)(2,1)S(1)}, bf16[40,2048]{1,0:T(8,128)(2,1)S(1)}, u32[]{:S(2)}, u32[]{:S(2)}) %collective-permute-start) | collective-permute-done | bytes 163872 | tf_op jit(solution)/shard_map/ppermute | solution.py:349
  15.4 1.3 %history.1 = (bf16[32,2048]{1,0:T(8,128)(2,1)S(1)}, bf16[288,256]{1,0:T(8,128)(2,1)S(1)}) custom-call(s32[32]{0:T(128)S(1)} %copy-done.7, s32[32]{0:T(128)S(1)} %copy-done.8, s32[32]{0:T(128)S(1)} %copy-done.9, f32[32,2048]{1,0:T(8,128)S(1)} %get-tuple-element.12.refs_3_, bf16[288,256]{1,0:T(8,128)(2,1)S(1)} %get-tuple-element.13.refs_4_, ...), custom_call_target="tpu_custom_call" | custom-call | tf_op jit(solution)/shard_map/history/pallas_call | solution.py:337
  16.7 1.6 %collective-permute-start.3 = (bf16[288,256]{1,0:T(8,128)(2,1)S(1)}, bf16[288,256]{1,0:T(8,128)(2,1)S(1)}, u32[]{:S(2)}, u32[]{:S(2)}) collective-permute-start(bf16[288,256]{1,0:T(8,128)(2,1)S(1)} %get-tuple-element.17.refs_10_), channel_id=1, source_target_pairs={{0,2},{1,3},{2,0},{3,1},{4,6},{5,7},{6,4},{7,5},{8,10},{9,11},{10,... | collective-permute-start | bytes 442376 | tf_op jit(solution)/shard_map/ppermute | solution.py:349
  18.2 1.3 %collective-permute-start.6 = (bf16[40,2048]{1,0:T(8,128)(2,1)S(1)}, bf16[40,2048]{1,0:T(8,128)(2,1)S(1)}, u32[]{:S(2)}, u32[]{:S(2)}) collective-permute-start(bf16[40,2048]{1,0:T(8,128)(2,1)S(1)} %collective-permute-done.1.refs_9_.refs_16_), channel_id=1, source_target_pairs={{0,4},{4,0},{8,12},{12,8},{1,5},{5,1},{9,13},{13,9},{2,6},{6,2},{1... | collective-permute-start | bytes 491528 | tf_op jit(solution)/shard_map/ppermute | solution.py:349
  19.6 0.0 collective-permute-start.5
  19.6 2.9 %collective-permute-done.3.refs_11_ = bf16[288,256]{1,0:T(8,128)(2,1)S(1)} collective-permute-done((bf16[288,256]{1,0:T(8,128)(2,1)S(1)}, bf16[288,256]{1,0:T(8,128)(2,1)S(1)}, u32[]{:S(2)}, u32[]{:S(2)}) %collective-permute-start.3) | collective-permute-done | bytes 147488 | tf_op jit(solution)/shard_map/ppermute | solution.py:349
  22.5 0.0 collective-permute-start.4
  22.5 0.0 collective-permute-done.5.refs_13_
  22.5 1.5 %collective-permute-done.6.refs_17_ = bf16[40,2048]{1,0:T(8,128)(2,1)S(1)} collective-permute-done((bf16[40,2048]{1,0:T(8,128)(2,1)S(1)}, bf16[40,2048]{1,0:T(8,128)(2,1)S(1)}, u32[]{:S(2)}, u32[]{:S(2)}) %collective-permute-start.6) | collective-permute-done | bytes 163872 | tf_op jit(solution)/shard_map/ppermute | solution.py:349
  24.1 0.0 collective-permute-done.4.refs_12_
  24.1 12.0 %dt_scan_gate.1 = (bf16[256,2048]{1,0:T(8,128)(2,1)}, bf16[128,2048]{1,0:T(8,128)(2,1)}) custom-call(s32[32]{0:T(128)S(1)} %copy-done.7, s32[32]{0:T(128)S(1)} %copy-done.8, s32[32]{0:T(128)S(1)} %copy-done.9, bf16[256,2048]{1,0:T(8,128)(2,1)S(1)} %get-tuple-element.11.refs_3_, bf16[32,2048]{1,0:T(8,128)(2,1)S(1)} %get-tuple-element.16.refs_4_, ...), custom_call_target="tpu_custom_call" | custom-call | tf_op jit(solution)/shard_map/dt_scan_gate/pallas_call | solution.py:337
  (14 shorter events, 0.0 us)
Async XLA Ops:
  0.6 14.7 %copy-start = (bf16[2048,288]{0,1:T(8,128)(2,1)S(1)}, bf16[2048,288]{0,1:T(8,128)(2,1)}, u32[]{:S(2)}) copy-start(bf16[2048,288]{0,1:T(8,128)(2,1)} %param.18) | copy-start | bytes 3538948
  0.6 14.7 %copy-start.4 = (bf16[4,2048]{1,0:T(4,128)(2,1)S(1)}, bf16[4,2048]{1,0:T(4,128)(2,1)}, u32[]{:S(2)}) copy-start(bf16[4,2048]{1,0:T(4,128)(2,1)} %refs_6_.2) | copy-start | bytes 49156
  0.7 14.7 %copy-start.7 = (s32[32]{0:T(128)S(1)}, s32[32]{0:T(128)}, u32[]{:S(2)}) copy-start(s32[32]{0:T(128)} %refs_0_.5) | copy-start | bytes 388
  0.7 14.7 %copy-start.8 = (s32[32]{0:T(128)S(1)}, s32[32]{0:T(128)}, u32[]{:S(2)}) copy-start(s32[32]{0:T(128)} %refs_1_.3) | copy-start | bytes 388
  0.7 14.7 %copy-start.9 = (s32[32]{0:T(128)S(1)}, s32[32]{0:T(128)}, u32[]{:S(2)}) copy-start(s32[32]{0:T(128)} %refs_2_.5) | copy-start | bytes 388
  1.7 13.1 %collective-permute-start.1 = (bf16[40,2048]{1,0:T(8,128)(2,1)S(1)}, bf16[40,2048]{1,0:T(8,128)(2,1)S(1)}, u32[]{:S(2)}, u32[]{:S(2)}) collective-permute-start(bf16[40,2048]{1,0:T(8,128)(2,1)S(1)} %get-tuple-element.14.refs_7_.refs_14_), channel_id=1, source_target_pairs={{0,12},{4,8},{8,4},{12,0},{1,13},{5,9},{9,5},{13,1},{2,14},{6,10},... | collective-permute-start | bytes 491528 | tf_op jit(solution)/shard_map/ppermute | solution.py:349
  6.8 8.5 %collective-permute-start = (bf16[40,2048]{1,0:T(8,128)(2,1)S(1)}, bf16[40,2048]{1,0:T(8,128)(2,1)S(1)}, u32[]{:S(2)}, u32[]{:S(2)}) collective-permute-start(bf16[40,2048]{1,0:T(8,128)(2,1)S(1)} %get-tuple-element.14.refs_7_.refs_14_), channel_id=1, source_target_pairs={{0,4},{4,0},{8,12},{12,8},{1,5},{5,1},{9,13},{13,9},{2,6},{6,2},{1... | collective-permute-start | bytes 491528 | tf_op jit(solution)/shard_map/ppermute | solution.py:349
  6.8 8.0 %collective-permute-start.2 = (bf16[8,2048]{1,0:T(8,128)(2,1)S(1)}, bf16[8,2048]{1,0:T(8,128)(2,1)S(1)}, u32[]{:S(2)}, u32[]{:S(2)}) collective-permute-start(bf16[8,2048]{1,0:T(8,128)(2,1)S(1)} %get-tuple-element.15), channel_id=1, source_target_pairs={{0,8},{4,12},{8,0},{12,4},{1,9},{5,13},{9,1},{13,5},{2,10},{6,14},... | collective-permute-start | bytes 98312 | tf_op jit(solution)/shard_map/ppermute | solution.py:349
  7.5 16.6 %copy-start.3 = (f32[16,2048]{1,0:T(8,128)S(1)}, f32[16,2048]{1,0:T(8,128)}, u32[]{:S(2)}) copy-start(f32[16,2048]{1,0:T(8,128)} %refs_8_.1) | copy-start | bytes 393220
  11.4 12.7 %copy-start.1 = (bf16[256,2048]{1,0:T(8,128)(2,1)S(1)}, bf16[256,2048]{1,0:T(8,128)(2,1)}, u32[]{:S(2)}) copy-start(bf16[256,2048]{1,0:T(8,128)(2,1)} %refs_5_.1) | copy-start | bytes 3145732
  11.4 12.7 %copy-start.2 = (bf16[256,2048]{1,0:T(8,128)(2,1)S(1)}, bf16[256,2048]{1,0:T(8,128)(2,1)}, u32[]{:S(2)}) copy-start(bf16[256,2048]{1,0:T(8,128)(2,1)} %refs_6_.3) | copy-start | bytes 3145732
  11.4 12.7 %copy-start.5 = (f32[2048]{0:T(1024)S(1)}, f32[2048]{0:T(1024)}, u32[]{:S(2)}) copy-start(f32[2048]{0:T(1024)} %param.20) | copy-start | bytes 24580
  11.4 12.7 %copy-start.6 = (f32[2048]{0:T(1024)S(1)}, f32[2048]{0:T(1024)}, u32[]{:S(2)}) copy-start(f32[2048]{0:T(1024)} %param.22) | copy-start | bytes 24580
  16.7 5.8 %collective-permute-start.3 = (bf16[288,256]{1,0:T(8,128)(2,1)S(1)}, bf16[288,256]{1,0:T(8,128)(2,1)S(1)}, u32[]{:S(2)}, u32[]{:S(2)}) collective-permute-start(bf16[288,256]{1,0:T(8,128)(2,1)S(1)} %get-tuple-element.17.refs_10_), channel_id=1, source_target_pairs={{0,2},{1,3},{2,0},{3,1},{4,6},{5,7},{6,4},{7,5},{8,10},{9,11},{10,... | collective-permute-start | bytes 442376 | tf_op jit(solution)/shard_map/ppermute | solution.py:349
  18.2 5.8 %collective-permute-start.6 = (bf16[40,2048]{1,0:T(8,128)(2,1)S(1)}, bf16[40,2048]{1,0:T(8,128)(2,1)S(1)}, u32[]{:S(2)}, u32[]{:S(2)}) collective-permute-start(bf16[40,2048]{1,0:T(8,128)(2,1)S(1)} %collective-permute-done.1.refs_9_.refs_16_), channel_id=1, source_target_pairs={{0,4},{4,0},{8,12},{12,8},{1,5},{5,1},{9,13},{13,9},{2,6},{6,2},{1... | collective-permute-start | bytes 491528 | tf_op jit(solution)/shard_map/ppermute | solution.py:349
  19.6 2.9 %collective-permute-start.5 = (bf16[288,256]{1,0:T(8,128)(2,1)S(1)}, bf16[288,256]{1,0:T(8,128)(2,1)S(1)}, u32[]{:S(2)}, u32[]{:S(2)}) collective-permute-start(bf16[288,256]{1,0:T(8,128)(2,1)S(1)} %get-tuple-element.17.refs_10_), channel_id=1, source_target_pairs={{0,1},{1,0},{2,3},{3,2},{4,5},{5,4},{6,7},{7,6},{8,9},{9,8},{10,11... | collective-permute-start | bytes 442376 | tf_op jit(solution)/shard_map/ppermute | solution.py:349
  22.5 1.5 %collective-permute-start.4 = (bf16[288,256]{1,0:T(8,128)(2,1)S(1)}, bf16[288,256]{1,0:T(8,128)(2,1)S(1)}, u32[]{:S(2)}, u32[]{:S(2)}) collective-permute-start(bf16[288,256]{1,0:T(8,128)(2,1)S(1)} %collective-permute-done.3.refs_11_), channel_id=1, source_target_pairs={{0,1},{1,0},{2,3},{3,2},{4,5},{5,4},{6,7},{7,6},{8,9},{9,8},{10,11... | collective-permute-start | bytes 442376 | tf_op jit(solution)/shard_map/ppermute | solution.py:349

commit v16 on v14

--- a/solution.py
+++ b/solution.py
@@ -166,19 +166,32 @@
     fixed_ref[:, : per_dev * taps] = part.astype(BF16)
 
 
+def prepare_kernel(dims, refs_in, refs_out, scratch):
+    mixed_ref, head_ref, z_ref, al_ref, skip_ref = refs_in
+    gate_ref, skipped_ref, rate_ref = refs_out
+    rows, channels = z_ref.shape
+    head = head_ref.shape[0]
+    gate_ref[...] = silu(z_ref[...].astype(F32))
+    rate_ref[...] = jnp.exp(al_ref[...]) * (-LOG2E)
+    for tile in range(channels // LANES):
+        lanes = slice(tile * LANES, (tile + 1) * LANES)
+        skipped_ref[tile, :head, :] = skip_ref[:, lanes] * head_ref[:, lanes].astype(F32)
+        skipped_ref[tile, head:, :] = skip_ref[:, lanes] * mixed_ref[head:, lanes].astype(F32)
+
+
 def scan_kernel(dims, refs_in, refs_out, scratch):
     per_dev, n_replica, _, _ = dims
-    mixed_ref, head_ref, z_ref, dtw_ref, dtb_ref, al_ref, skip_ref = refs_in[3:10]
+    mixed_ref, head_ref, dtw_ref, dtb_ref, gate_ref, skipped_ref, rate_ref = refs_in[3:10]
     out_hbm, state_hbm = refs_out
-    b_tab, c_tab, dt_v, drive_v, a_v, start_tm, final_tm, y_v, out_v, state_v, out_sems, int_sems = scratch[:12]
-    ints = scratch[12:]
+    b_tab, c_tab, dt_v, drive_v, start_tm, final_tm, y_v, out_v, state_v, out_sems, int_sems = scratch[:11]
+    ints = scratch[11:]
     int_copies = [pltpu.make_async_copy(refs_in[i], ints[i], int_sems.at[i]) for i in range(len(ints))]
     for copy in int_copies:
         copy.start()
-    n_pieces = sum(1 for ref in refs_in[10:] if ref.shape[-1] == z_ref.shape[1])
+    n_pieces = sum(1 for ref in refs_in[10:] if ref.shape[-1] == gate_ref.shape[1])
     parts, pieces = refs_in[10:-n_pieces], refs_in[-n_pieces:]
-    rows, channels = z_ref.shape
-    states = al_ref.shape[0]
+    rows, channels = gate_ref.shape
+    states = rate_ref.shape[0]
     rank = dtw_ref.shape[0]
     head = head_ref.shape[0]
 
@@ -219,8 +232,6 @@
                 mixed = mixed.astype(F32)
                 dt_v[tile, here, :] = dt
                 drive_v[tile, here, :] = dt * mixed
-                y_v[tile, here, :] = skip_ref[:, lanes] * mixed
-    a_v[...] = jnp.exp(al_ref[...]) * (-LOG2E)
 
     me = lax.axis_index("replica")
     for copy in int_copies:
@@ -258,7 +269,7 @@
             lanes = pl.ds(pl.multiple_of(tile * LANES, LANES), LANES)
             for r in range(per_dev):
                 here = slice(r * NEW, (r + 1) * NEW)
-                value = y_v[tile, pl.ds(r, NEW, stride=per_dev), :] * silu(z_ref[here, lanes].astype(F32))
+                value = y_v[tile, pl.ds(r, NEW, stride=per_dev), :] * gate_ref[here, lanes]
                 out_v[here, lanes] = value.astype(BF16)
                 final = final_tm[tile, pl.ds(r, states, stride=per_dev), :]
                 state_v[r * states : (r + 1) * states, lanes] = final.astype(BF16)
@@ -268,7 +279,7 @@
         lanes = [pl.ds(pl.multiple_of(tile * LANES, LANES), LANES) for tile in group]
         for first in range(0, states, half):
             ids = range(first, first + half)
-            rates = [[jnp.broadcast_to(a_v[n : n + 1, lane], (per_dev, LANES)) for n in ids] for lane in lanes]
+            rates = [[jnp.broadcast_to(rate_ref[n : n + 1, lane], (per_dev, LANES)) for n in ids] for lane in lanes]
 
             def advance(step, state):
                 state = list(state)
@@ -285,7 +296,8 @@
                             term = state[i] * c
                             sums[j] = term if sums[j] is None else sums[j] + term
                     for j, tile in enumerate(group):
-                        y_v[tile, now, :] += sums[j]
+                        before = skipped_ref[tile, now, :] if first == 0 else y_v[tile, now, :]
+                        y_v[tile, now, :] = before + sums[j]
                 return tuple(state)
 
             state = tuple(start_tm[tile, n * per_dev : (n + 1) * per_dev, :] for tile in group for n in ids)
@@ -310,6 +322,7 @@
         return carry
 
     final_tm[:tiles] = jnp.zeros((tiles,) + final_tm.shape[1:], F32)
+    y_v[:tiles] = jnp.zeros((tiles,) + y_v.shape[1:], F32)
     lax.fori_loop(0, n_groups, one_group, 0)
     finish(n_groups - 1)
     for copy in out_copies(n_groups - 1):
@@ -421,7 +434,13 @@
         mask //= 2
 
     n_tiles = channels // LANES
-    operands = [mixed, mixed_head, z_new, dt_proj_weight, dt_bias[None, :], a_log, d_skip[None, :]]
+    prepared = call(
+        prepare_kernel, None, "prepare", 40,
+        [(value, "vmem") for value in (mixed, mixed_head, z_new, a_log, d_skip[None, :])],
+        [((rows, channels), F32, "vmem"), ((n_tiles, rows, LANES), F32, "vmem"), ((states, channels), F32, "vmem")],
+        [],
+    )
+    operands = [mixed, mixed_head, dt_proj_weight, dt_bias[None, :], *prepared]
     out, state = call(
         scan_kernel, dims, "dt_scan_gate", 40,
         [(value, "any") for value, _ in requests] + [(value, "vmem") for value in operands + parts + ssm_pieces],
@@ -431,7 +450,6 @@
             vmem((states, rows, LANES), F32),
             vmem((n_tiles, rows, LANES), F32),
             vmem((n_tiles, rows, LANES), F32),
-            vmem((states, channels), F32),
             vmem((n_tiles, per_dev * (states + 1), LANES), F32),
             vmem((n_tiles, per_dev * (states + 1), LANES), F32),
             vmem((n_tiles, rows + per_dev, LANES), F32),

time: 36.3 us -> 35.9 us (0.989)
  waiting for transfers between devices: 8.35 us -> 7.75 us
    ppermute x7, waiting for transfers between devices: 8.35 us -> 7.75 us  [swap(): return lax.ppermute(value, axis, [(i, i ^ mask) for i in range(size)])]
    pallas_call x4 -> x5, Pallas kernels: 18.3 us -> 18.5 us  [call(): pl.pallas_call(split_refs(kernel, dims, len(ins), len(outs)), in_specs=[p...]
  transfers between devices with their start and end apart: 7 -> 7, of which waited for: 4 -> 4; matrix products, arithmetic and copies ran while one was open for 0% -> 0% of each run, Pallas kernels for 11% -> 13%
where the time goes in v16:
time: 35.9 us; the launch traced here: 35.7 us
  Pallas kernels  18.5 us (52%)
  starting transfers between devices  8.67 us (24%)
  waiting for transfers between devices  7.75 us (22%)
  between operations  0.77 us (2%)
    pallas_call x5, Pallas kernels, call(): pl.pallas_call(split_refs(kernel, dims, len(ins), len(outs)), in_specs=[p...  18.5 us
    ppermute x7, starting transfers between devices, swap(): return lax.ppermute(value, axis, [(i, i ^ mask) for i in range(size)])  8.67 us
    ppermute x7, waiting for transfers between devices, swap(): return lax.ppermute(value, axis, [(i, i ^ mask) for i in range(size)])  7.75 us
  transfers between devices with their start and end apart: 7, of which 4 were waited for; matrix products, arithmetic and copies ran while one was open for 0% of the time, Pallas kernels for 13%

profile of v16, /device:TPU:0, one launch (start us, length us, event | category | flops | bytes accessed | tf_op | source)
XLA Modules:
  0.0 35.7 jit_solution(13273831660462093712)
XLA Ops:
  0.6 0.0 copy-start.4
  0.6 0.0 copy-start
  0.7 1.0 %pack.1 = (bf16[40,2048]{1,0:T(8,128)(2,1)S(1)}, bf16[8,2048]{1,0:T(8,128)(2,1)S(1)}) custom-call(bf16[32,2048]{1,0:T(8,128)(2,1)} %bitcast.11, bf16[3,2,2048]{2,1,0:T(2,128)(2,1)} %bitcast.12), custom_call_target="tpu_custom_call" | custom-call | tf_op jit(solution)/shard_map/pack/pallas_call | solution.py:351
  1.7 5.1 %collective-permute-start.1 = (bf16[40,2048]{1,0:T(8,128)(2,1)S(1)}, bf16[40,2048]{1,0:T(8,128)(2,1)S(1)}, u32[]{:S(2)}, u32[]{:S(2)}) collective-permute-start(bf16[40,2048]{1,0:T(8,128)(2,1)S(1)} %get-tuple-element.17.refs_7_.refs_14_), channel_id=1, source_target_pairs={{0,12},{4,8},{8,4},{12,0},{1,13},{5,9},{9,5},{13,1},{2,14},{6,10},... | collective-permute-start | bytes 491528 | tf_op jit(solution)/shard_map/ppermute | solution.py:363
  6.8 0.0 collective-permute-start
  6.8 0.6 %collective-permute-start.2 = (bf16[8,2048]{1,0:T(8,128)(2,1)S(1)}, bf16[8,2048]{1,0:T(8,128)(2,1)S(1)}, u32[]{:S(2)}, u32[]{:S(2)}) collective-permute-start(bf16[8,2048]{1,0:T(8,128)(2,1)S(1)} %get-tuple-element.18), channel_id=1, source_target_pairs={{0,8},{4,12},{8,0},{12,4},{1,9},{5,13},{9,1},{13,5},{2,10},{6,14},... | collective-permute-start | bytes 98312 | tf_op jit(solution)/shard_map/ppermute | solution.py:363
  7.5 4.0 %conv_project.1 = (bf16[256,2048]{1,0:T(8,128)(2,1)S(1)}, f32[32,2048]{1,0:T(8,128)S(1)}, bf16[288,256]{1,0:T(8,128)(2,1)S(1)}) custom-call(bf16[256,2048]{1,0:T(8,128)(2,1)} %refs_0_.3, bf16[288,2048]{1,0:T(8,128)(2,1)} %bitcast.7, bf16[4,2048]{1,0:T(4,128)(2,1)} %refs_6_.1, f32[1,2048]{1,0:T(1,128)} %bitcast.13), custom_call_target="tpu_custom_call" | custom-call | tf_op jit(solution)/shard_map/conv_project/pallas_call | solution.py:351
  11.5 3.3 %collective-permute-done.2.refs_10_ = bf16[8,2048]{1,0:T(8,128)(2,1)S(1)} collective-permute-done((bf16[8,2048]{1,0:T(8,128)(2,1)S(1)}, bf16[8,2048]{1,0:T(8,128)(2,1)S(1)}, u32[]{:S(2)}, u32[]{:S(2)}) %collective-permute-start.2) | collective-permute-done | bytes 32800 | tf_op jit(solution)/shard_map/ppermute | solution.py:363
  14.8 0.0 collective-permute-done.1.refs_9_.refs_16_
  14.8 0.5 %collective-permute-done.refs_8_.refs_15_ = bf16[40,2048]{1,0:T(8,128)(2,1)S(1)} collective-permute-done((bf16[40,2048]{1,0:T(8,128)(2,1)S(1)}, bf16[40,2048]{1,0:T(8,128)(2,1)S(1)}, u32[]{:S(2)}, u32[]{:S(2)}) %collective-permute-start) | collective-permute-done | bytes 163872 | tf_op jit(solution)/shard_map/ppermute | solution.py:363
  15.4 0.0 copy-start.1
  15.4 0.0 copy-start.6
  15.4 1.3 %history.1 = (bf16[32,2048]{1,0:T(8,128)(2,1)S(1)}, bf16[288,256]{1,0:T(8,128)(2,1)S(1)}) custom-call(s32[32]{0:T(128)S(1)} %copy-done.7, s32[32]{0:T(128)S(1)} %copy-done.8, s32[32]{0:T(128)S(1)} %copy-done.9, f32[32,2048]{1,0:T(8,128)S(1)} %get-tuple-element.15.refs_3_, bf16[288,256]{1,0:T(8,128)(2,1)S(1)} %get-tuple-element.16.refs_4_, ...), custom_call_target="tpu_custom_call" | custom-call | tf_op jit(solution)/shard_map/history/pallas_call | solution.py:351
  16.7 1.6 %collective-permute-start.3 = (bf16[288,256]{1,0:T(8,128)(2,1)S(1)}, bf16[288,256]{1,0:T(8,128)(2,1)S(1)}, u32[]{:S(2)}, u32[]{:S(2)}) collective-permute-start(bf16[288,256]{1,0:T(8,128)(2,1)S(1)} %get-tuple-element.23.refs_10_), channel_id=1, source_target_pairs={{0,2},{1,3},{2,0},{3,1},{4,6},{5,7},{6,4},{7,5},{8,10},{9,11},{10,... | collective-permute-start | bytes 442376 | tf_op jit(solution)/shard_map/ppermute | solution.py:363
  18.3 1.3 %collective-permute-start.6 = (bf16[40,2048]{1,0:T(8,128)(2,1)S(1)}, bf16[40,2048]{1,0:T(8,128)(2,1)S(1)}, u32[]{:S(2)}, u32[]{:S(2)}) collective-permute-start(bf16[40,2048]{1,0:T(8,128)(2,1)S(1)} %collective-permute-done.1.refs_9_.refs_16_), channel_id=1, source_target_pairs={{0,4},{4,0},{8,12},{12,8},{1,5},{5,1},{9,13},{13,9},{2,6},{6,2},{1... | collective-permute-start | bytes 491528 | tf_op jit(solution)/shard_map/ppermute | solution.py:363
  19.6 0.0 collective-permute-start.5
  19.6 2.9 %collective-permute-done.3.refs_11_ = bf16[288,256]{1,0:T(8,128)(2,1)S(1)} collective-permute-done((bf16[288,256]{1,0:T(8,128)(2,1)S(1)}, bf16[288,256]{1,0:T(8,128)(2,1)S(1)}, u32[]{:S(2)}, u32[]{:S(2)}) %collective-permute-start.3) | collective-permute-done | bytes 147488 | tf_op jit(solution)/shard_map/ppermute | solution.py:363
  22.6 0.0 collective-permute-start.4
  22.6 0.0 copy-done.3
  22.6 0.5 %prepare.1 = (f32[256,2048]{1,0:T(8,128)S(1)}, f32[16,256,128]{2,1,0:T(8,128)S(1)}, f32[16,2048]{1,0:T(8,128)S(1)}) custom-call(bf16[256,2048]{1,0:T(8,128)(2,1)S(1)} %get-tuple-element.14.refs_0_.refs_3_, bf16[32,2048]{1,0:T(8,128)(2,1)S(1)} %get-tuple-element.19.refs_1_.refs_4_, bf16[256,2048]{1,0:T(8,128)(2,1)S(1)} %copy-done.2, ...), custom_call_target="tpu_custom_call" | custom-call | tf_op jit(solution)/shard_map/prepare/pallas_call | solution.py:351
  23.1 0.0 collective-permute-done.5.refs_13_
  23.1 1.0 %collective-permute-done.6.refs_17_ = bf16[40,2048]{1,0:T(8,128)(2,1)S(1)} collective-permute-done((bf16[40,2048]{1,0:T(8,128)(2,1)S(1)}, bf16[40,2048]{1,0:T(8,128)(2,1)S(1)}, u32[]{:S(2)}, u32[]{:S(2)}) %collective-permute-start.6) | collective-permute-done | bytes 163872 | tf_op jit(solution)/shard_map/ppermute | solution.py:363
  24.1 0.0 collective-permute-done.4.refs_12_
  24.1 11.6 %dt_scan_gate.1 = (bf16[256,2048]{1,0:T(8,128)(2,1)}, bf16[128,2048]{1,0:T(8,128)(2,1)}) custom-call(s32[32]{0:T(128)S(1)} %copy-done.7, s32[32]{0:T(128)S(1)} %copy-done.8, s32[32]{0:T(128)S(1)} %copy-done.9, bf16[256,2048]{1,0:T(8,128)(2,1)S(1)} %get-tuple-element.14.refs_0_.refs_3_, bf16[32,2048]{1,0:T(8,128)(2,1)S(1)} %get-tuple-element.19.refs_1_.refs_4_, ...), custom_call_target="tpu_custom_call" | custom-call | tf_op jit(solution)/shard_map/dt_scan_gate/pallas_call | solution.py:351
  (15 shorter events, 0.0 us)
Async XLA Ops:
  0.6 14.7 %copy-start.4 = (bf16[4,2048]{1,0:T(4,128)(2,1)S(1)}, bf16[4,2048]{1,0:T(4,128)(2,1)}, u32[]{:S(2)}) copy-start(bf16[4,2048]{1,0:T(4,128)(2,1)} %refs_6_.1) | copy-start | bytes 49156
  0.6 14.7 %copy-start = (bf16[2048,288]{0,1:T(8,128)(2,1)S(1)}, bf16[2048,288]{0,1:T(8,128)(2,1)}, u32[]{:S(2)}) copy-start(bf16[2048,288]{0,1:T(8,128)(2,1)} %param.18) | copy-start | bytes 3538948
  0.7 14.7 %copy-start.9 = (s32[32]{0:T(128)S(1)}, s32[32]{0:T(128)}, u32[]{:S(2)}) copy-start(s32[32]{0:T(128)} %refs_2_.7) | copy-start | bytes 388
  0.7 14.7 %copy-start.8 = (s32[32]{0:T(128)S(1)}, s32[32]{0:T(128)}, u32[]{:S(2)}) copy-start(s32[32]{0:T(128)} %refs_1_.3) | copy-start | bytes 388
  0.7 14.7 %copy-start.7 = (s32[32]{0:T(128)S(1)}, s32[32]{0:T(128)}, u32[]{:S(2)}) copy-start(s32[32]{0:T(128)} %refs_0_.5) | copy-start | bytes 388
  1.7 13.1 %collective-permute-start.1 = (bf16[40,2048]{1,0:T(8,128)(2,1)S(1)}, bf16[40,2048]{1,0:T(8,128)(2,1)S(1)}, u32[]{:S(2)}, u32[]{:S(2)}) collective-permute-start(bf16[40,2048]{1,0:T(8,128)(2,1)S(1)} %get-tuple-element.17.refs_7_.refs_14_), channel_id=1, source_target_pairs={{0,12},{4,8},{8,4},{12,0},{1,13},{5,9},{9,5},{13,1},{2,14},{6,10},... | collective-permute-start | bytes 491528 | tf_op jit(solution)/shard_map/ppermute | solution.py:363
  6.8 8.5 %collective-permute-start = (bf16[40,2048]{1,0:T(8,128)(2,1)S(1)}, bf16[40,2048]{1,0:T(8,128)(2,1)S(1)}, u32[]{:S(2)}, u32[]{:S(2)}) collective-permute-start(bf16[40,2048]{1,0:T(8,128)(2,1)S(1)} %get-tuple-element.17.refs_7_.refs_14_), channel_id=1, source_target_pairs={{0,4},{4,0},{8,12},{12,8},{1,5},{5,1},{9,13},{13,9},{2,6},{6,2},{1... | collective-permute-start | bytes 491528 | tf_op jit(solution)/shard_map/ppermute | solution.py:363
  6.8 8.0 %collective-permute-start.2 = (bf16[8,2048]{1,0:T(8,128)(2,1)S(1)}, bf16[8,2048]{1,0:T(8,128)(2,1)S(1)}, u32[]{:S(2)}, u32[]{:S(2)}) collective-permute-start(bf16[8,2048]{1,0:T(8,128)(2,1)S(1)} %get-tuple-element.18), channel_id=1, source_target_pairs={{0,8},{4,12},{8,0},{12,4},{1,9},{5,13},{9,1},{13,5},{2,10},{6,14},... | collective-permute-start | bytes 98312 | tf_op jit(solution)/shard_map/ppermute | solution.py:363
  7.5 15.1 %copy-start.2 = (bf16[256,2048]{1,0:T(8,128)(2,1)S(1)}, bf16[256,2048]{1,0:T(8,128)(2,1)}, u32[]{:S(2)}) copy-start(bf16[256,2048]{1,0:T(8,128)(2,1)} %refs_2_.6) | copy-start | bytes 3145732
  7.5 15.1 %copy-start.3 = (f32[16,2048]{1,0:T(8,128)S(1)}, f32[16,2048]{1,0:T(8,128)}, u32[]{:S(2)}) copy-start(f32[16,2048]{1,0:T(8,128)} %refs_3_.1) | copy-start | bytes 393220
  7.5 15.1 %copy-start.5 = (f32[2048]{0:T(1024)S(1)}, f32[2048]{0:T(1024)}, u32[]{:S(2)}) copy-start(f32[2048]{0:T(1024)} %param.22) | copy-start | bytes 24580
  15.4 8.7 %copy-start.1 = (bf16[256,2048]{1,0:T(8,128)(2,1)S(1)}, bf16[256,2048]{1,0:T(8,128)(2,1)}, u32[]{:S(2)}) copy-start(bf16[256,2048]{1,0:T(8,128)(2,1)} %refs_5_.1) | copy-start | bytes 3145732
  15.4 8.7 %copy-start.6 = (f32[2048]{0:T(1024)S(1)}, f32[2048]{0:T(1024)}, u32[]{:S(2)}) copy-start(f32[2048]{0:T(1024)} %param.20) | copy-start | bytes 24580
  16.7 5.8 %collective-permute-start.3 = (bf16[288,256]{1,0:T(8,128)(2,1)S(1)}, bf16[288,256]{1,0:T(8,128)(2,1)S(1)}, u32[]{:S(2)}, u32[]{:S(2)}) collective-permute-start(bf16[288,256]{1,0:T(8,128)(2,1)S(1)} %get-tuple-element.23.refs_10_), channel_id=1, source_target_pairs={{0,2},{1,3},{2,0},{3,1},{4,6},{5,7},{6,4},{7,5},{8,10},{9,11},{10,... | collective-permute-start | bytes 442376 | tf_op jit(solution)/shard_map/ppermute | solution.py:363
  18.3 5.8 %collective-permute-start.6 = (bf16[40,2048]{1,0:T(8,128)(2,1)S(1)}, bf16[40,2048]{1,0:T(8,128)(2,1)S(1)}, u32[]{:S(2)}, u32[]{:S(2)}) collective-permute-start(bf16[40,2048]{1,0:T(8,128)(2,1)S(1)} %collective-permute-done.1.refs_9_.refs_16_), channel_id=1, source_target_pairs={{0,4},{4,0},{8,12},{12,8},{1,5},{5,1},{9,13},{13,9},{2,6},{6,2},{1... | collective-permute-start | bytes 491528 | tf_op jit(solution)/shard_map/ppermute | solution.py:363
  19.6 3.5 %collective-permute-start.5 = (bf16[288,256]{1,0:T(8,128)(2,1)S(1)}, bf16[288,256]{1,0:T(8,128)(2,1)S(1)}, u32[]{:S(2)}, u32[]{:S(2)}) collective-permute-start(bf16[288,256]{1,0:T(8,128)(2,1)S(1)} %get-tuple-element.23.refs_10_), channel_id=1, source_target_pairs={{0,1},{1,0},{2,3},{3,2},{4,5},{5,4},{6,7},{7,6},{8,9},{9,8},{10,11... | collective-permute-start | bytes 442376 | tf_op jit(solution)/shard_map/ppermute | solution.py:363
  22.6 1.5 %collective-permute-start.4 = (bf16[288,256]{1,0:T(8,128)(2,1)S(1)}, bf16[288,256]{1,0:T(8,128)(2,1)S(1)}, u32[]{:S(2)}, u32[]{:S(2)}) collective-permute-start(bf16[288,256]{1,0:T(8,128)(2,1)S(1)} %collective-permute-done.3.refs_11_), channel_id=1, source_target_pairs={{0,1},{1,0},{2,3},{3,2},{4,5},{5,4},{6,7},{7,6},{8,9},{9,8},{10,11... | collective-permute-start | bytes 442376 | tf_op jit(solution)/shard_map/ppermute | solution.py:363

commit v17 on v16

--- a/solution.py
+++ b/solution.py
@@ -10,7 +10,6 @@
 NEW = 32
 LANES = 128
 MIB = 1024 * 1024
-UNROLL = 32
 LOG2E = 1.4426950408889634
 F32, BF16 = jnp.float32, jnp.bfloat16
 NT = (((1,), (1,)), ((), ()))
@@ -183,8 +182,8 @@
     per_dev, n_replica, _, _ = dims
     mixed_ref, head_ref, dtw_ref, dtb_ref, gate_ref, skipped_ref, rate_ref = refs_in[3:10]
     out_hbm, state_hbm = refs_out
-    b_tab, c_tab, dt_v, drive_v, start_tm, final_tm, y_v, out_v, state_v, out_sems, int_sems = scratch[:11]
-    ints = scratch[11:]
+    b_tab, c_tab, low_v, start_tm, out_v, state_v, out_sems, int_sems = scratch[:8]
+    even, odd, ints = scratch[8:12], scratch[12:16], scratch[16:]
     int_copies = [pltpu.make_async_copy(refs_in[i], ints[i], int_sems.at[i]) for i in range(len(ints))]
     for copy in int_copies:
         copy.start()
@@ -209,29 +208,41 @@
     dt_low = projected[:, :rank].astype(BF16)
     late = projected[:, rank:]
     n_tiles = channels // LANES
-    wide = min(4, n_tiles)
-    per_chunk = states * wide // n_tiles
-    for c in range(n_tiles // wide):
-        for n in range(c * per_chunk, (c + 1) * per_chunk):
-            b_tab[n] = jnp.broadcast_to(late[:, n : n + 1], (rows, LANES))
-        lanes = slice(c * per_chunk * LANES, (c + 1) * per_chunk * LANES)
-        repeated = jnp.dot(c_terms, spread[:, lanes], preferred_element_type=F32)
-        for n in range(per_chunk):
-            c_tab[c * per_chunk + n] = repeated[:, n * LANES : (n + 1) * LANES]
-        weights = dtw_ref[:, c * wide * LANES : (c + 1) * wide * LANES]
-        raw = jnp.dot(dt_low, weights, preferred_element_type=F32)
-        for j in range(wide):
-            tile = c * wide + j
-            lanes = slice(tile * LANES, (tile + 1) * LANES)
+    tiles = 2
+    half = states // 2
+    width = tiles * LANES
+    n_groups = n_tiles // tiles
+    low_v[...] = dt_low
+
+    def group_lanes(g):
+        return pl.ds(pl.multiple_of(g * width, width), width)
+
+    def tile_lanes(g, j):
+        return pl.ds(pl.multiple_of((g * tiles + j) * LANES, LANES), LANES)
+
+    def steps(g, held):
+        dt_v, drive_v = held[:2]
+        raw = jnp.dot(low_v[...], dtw_ref[:, group_lanes(g)], preferred_element_type=F32)
+        for j in range(tiles):
+            lanes = tile_lanes(g, j)
+            bias = dtb_ref[:, lanes]
             for first in range(0, rows, LANES):
                 here = slice(first, first + LANES)
-                dt = softplus(raw[here, j * LANES : (j + 1) * LANES] + dtb_ref[:, lanes])
+                dt = softplus(raw[here, j * LANES : (j + 1) * LANES] + bias)
                 mixed = mixed_ref[here, lanes]
                 if first == 0:
                     mixed = jnp.concatenate([head_ref[:, lanes], mixed[head:]], axis=0)
-                mixed = mixed.astype(F32)
-                dt_v[tile, here, :] = dt
-                drive_v[tile, here, :] = dt * mixed
+                dt_v[j, here, :] = dt
+                drive_v[j, here, :] = dt * mixed.astype(F32)
+
+    wide = 4
+    for c in range(0, states, wide):
+        for n in range(c, c + wide):
+            b_tab[n] = jnp.broadcast_to(late[:, n : n + 1], (rows, LANES))
+        repeated = jnp.dot(c_terms, spread[:, c * LANES : (c + wide) * LANES], preferred_element_type=F32)
+        for n in range(wide):
+            c_tab[c + n] = repeated[:, n * LANES : (n + 1) * LANES]
+    steps(0, even)
 
     me = lax.axis_index("replica")
     for copy in int_copies:
@@ -251,80 +262,72 @@
             value = jnp.where(lengths[r] > 0, value, jnp.zeros_like(value))
             start_tm[tile, pl.ds(r, states, stride=per_dev), :] = value
 
-    tiles = 2
-    half = states // 2
-    width = tiles * LANES
-    n_groups = n_tiles // tiles
-
     def out_copies(g):
-        lanes = pl.ds(pl.multiple_of(g * width, width), width)
+        lanes = group_lanes(g)
         return [
             pltpu.make_async_copy(src.at[:, lanes], dst.at[:, lanes], out_sems.at[i, g])
             for i, (src, dst) in enumerate(((out_v, out_hbm), (state_v, state_hbm)))
         ]
 
-    def finish(g):
+    def finish(g, held):
+        y_v, final_tm = held[2:]
         for j in range(tiles):
-            tile = g * tiles + j
-            lanes = pl.ds(pl.multiple_of(tile * LANES, LANES), LANES)
+            lanes = tile_lanes(g, j)
             for r in range(per_dev):
                 here = slice(r * NEW, (r + 1) * NEW)
-                value = y_v[tile, pl.ds(r, NEW, stride=per_dev), :] * gate_ref[here, lanes]
+                value = y_v[j, pl.ds(r, NEW, stride=per_dev), :] * gate_ref[here, lanes]
                 out_v[here, lanes] = value.astype(BF16)
-                final = final_tm[tile, pl.ds(r, states, stride=per_dev), :]
+                final = final_tm[j, pl.ds(r, states, stride=per_dev), :]
                 state_v[r * states : (r + 1) * states, lanes] = final.astype(BF16)
 
-    def scan_group(g):
-        group = [g * tiles + j for j in range(tiles)]
-        lanes = [pl.ds(pl.multiple_of(tile * LANES, LANES), LANES) for tile in group]
+    def scan(g, held):
+        dt_v, drive_v, y_v, final_tm = held
         for first in range(0, states, half):
             ids = range(first, first + half)
-            rates = [[jnp.broadcast_to(rate_ref[n : n + 1, lane], (per_dev, LANES)) for n in ids] for lane in lanes]
-
-            def advance(step, state):
-                state = list(state)
-                for u in range(UNROLL):
-                    now = pl.ds(pl.multiple_of((step * UNROLL + u) * per_dev, per_dev), per_dev)
-                    dt = [dt_v[tile, now, :] for tile in group]
-                    drive = [drive_v[tile, now, :] for tile in group]
-                    sums = [None] * tiles
-                    for k, n in enumerate(ids):
-                        b, c = b_tab[n, now, :], c_tab[n, now, :]
-                        for j in range(tiles):
-                            i = j * half + k
-                            state[i] = jnp.exp2(dt[j] * rates[j][k]) * state[i] + drive[j] * b
-                            term = state[i] * c
-                            sums[j] = term if sums[j] is None else sums[j] + term
-                    for j, tile in enumerate(group):
-                        before = skipped_ref[tile, now, :] if first == 0 else y_v[tile, now, :]
-                        y_v[tile, now, :] = before + sums[j]
-                return tuple(state)
-
-            state = tuple(start_tm[tile, n * per_dev : (n + 1) * per_dev, :] for tile in group for n in ids)
-            if NEW == UNROLL:
-                state = advance(0, state)
-            else:
-                state = lax.fori_loop(0, NEW // UNROLL, advance, state)
-            for j, tile in enumerate(group):
-                for k, n in enumerate(ids):
-                    final_tm[tile, n * per_dev : (n + 1) * per_dev, :] = state[j * half + k]
-
-    def one_group(g, carry):
+            rates, state = {}, {}
+            for j in range(tiles):
+                for n in ids:
+                    rates[j, n] = jnp.broadcast_to(rate_ref[n : n + 1, tile_lanes(g, j)], (per_dev, LANES))
+                    state[j, n] = start_tm[g * tiles + j, n * per_dev : (n + 1) * per_dev, :]
+            for t in range(NEW):
+                now = slice(t * per_dev, (t + 1) * per_dev)
+                dt = [dt_v[j, now, :] for j in range(tiles)]
+                drive = [drive_v[j, now, :] for j in range(tiles)]
+                sums = [skipped_ref[g * tiles + j, now, :] if first == 0 else y_v[j, now, :] for j in range(tiles)]
+                for n in ids:
+                    b, c = b_tab[n, now, :], c_tab[n, now, :]
+                    for j in range(tiles):
+                        state[j, n] = jnp.exp2(dt[j] * rates[j, n]) * state[j, n] + drive[j] * b
+                        sums[j] = sums[j] + state[j, n] * c
+                for j in range(tiles):
+                    y_v[j, now, :] = sums[j]
+            for j in range(tiles):
+                for n in ids:
+                    final_tm[j, n * per_dev : (n + 1) * per_dev, :] = state[j, n]
+
+    def two_groups(i, carry):
+        g = 2 * i
         before = jnp.maximum(g - 1, 0)
-        finish(before)
-        scan_group(g)
-
-        @pl.when(g > 0)
+        finish(before, odd)
+        scan(g, even)
+        steps(g + 1, odd)
+        finish(g, even)
+        scan(g + 1, odd)
+        steps(jnp.minimum(g + 2, n_groups - 1), even)
+        for copy in out_copies(g):
+            copy.start()
+
+        @pl.when(i > 0)
         def _():
             for copy in out_copies(before):
                 copy.start()
 
         return carry
 
-    final_tm[:tiles] = jnp.zeros((tiles,) + final_tm.shape[1:], F32)
-    y_v[:tiles] = jnp.zeros((tiles,) + y_v.shape[1:], F32)
-    lax.fori_loop(0, n_groups, one_group, 0)
-    finish(n_groups - 1)
+    for ref in odd[2:]:
+        ref[...] = jnp.zeros(ref.shape, F32)
+    lax.fori_loop(0, n_groups // 2, two_groups, 0)
+    finish(n_groups - 1, odd)
     for copy in out_copies(n_groups - 1):
         copy.start()
 
@@ -448,16 +451,20 @@
         [
             vmem((states, rows, LANES), F32),
             vmem((states, rows, LANES), F32),
-            vmem((n_tiles, rows, LANES), F32),
-            vmem((n_tiles, rows, LANES), F32),
+            vmem((rows, rank), BF16),
             vmem((n_tiles, per_dev * (states + 1), LANES), F32),
-            vmem((n_tiles, per_dev * (states + 1), LANES), F32),
-            vmem((n_tiles, rows + per_dev, LANES), F32),
             vmem((rows, channels), BF16),
             vmem((per_dev * states, channels), BF16),
             dma((2, n_tiles // 2)),
             dma((3,)),
-        ] + [pltpu.SMEM(holder.shape, jnp.int32)] * 3,
+        ]
+        + [
+            vmem((2, rows, LANES), F32),
+            vmem((2, rows, LANES), F32),
+            vmem((2, rows + per_dev, LANES), F32),
+            vmem((2, per_dev * (states + 1), LANES), F32),
+        ] * 2
+        + [pltpu.SMEM(holder.shape, jnp.int32)] * 3,
     )
     return out, state.reshape(per_dev, states, channels)
 

time: 35.9 us -> 37.1 us (1.033)
  Pallas kernels: 18.5 us -> 19.8 us
    pallas_call x5, Pallas kernels: 18.5 us -> 19.8 us  [call(): pl.pallas_call(split_refs(kernel, dims, len(ins), len(outs)), in_specs=[p...]
  transfers between devices with their start and end apart: 7 -> 7, of which waited for: 4 -> 4; matrix products, arithmetic and copies ran while one was open for 0% -> 0% of each run, Pallas kernels for 13% -> 12%
where the time goes in v17:
time: 37.1 us; the launch traced here: 37 us
  Pallas kernels  19.8 us (53%)
  starting transfers between devices  8.67 us (23%)
  waiting for transfers between devices  7.75 us (21%)
  between operations  0.77 us (2%)
    pallas_call x5, Pallas kernels, call(): pl.pallas_call(split_refs(kernel, dims, len(ins), len(outs)), in_specs=[p...  19.8 us
    ppermute x7, starting transfers between devices, swap(): return lax.ppermute(value, axis, [(i, i ^ mask) for i in range(size)])  8.67 us
    ppermute x7, waiting for transfers between devices, swap(): return lax.ppermute(value, axis, [(i, i ^ mask) for i in range(size)])  7.75 us
  transfers between devices with their start and end apart: 7, of which 4 were waited for; matrix products, arithmetic and copies ran while one was open for 0% of the time, Pallas kernels for 12%

profile of v17, /device:TPU:0, one launch (start us, length us, event | category | flops | bytes accessed | tf_op | source)
XLA Modules:
  0.0 37.0 jit_solution(18313300153245052614)
XLA Ops:
  0.6 0.0 copy-start.4
  0.6 0.0 copy-start
  0.7 1.0 %pack.1 = (bf16[40,2048]{1,0:T(8,128)(2,1)S(1)}, bf16[8,2048]{1,0:T(8,128)(2,1)S(1)}) custom-call(bf16[32,2048]{1,0:T(8,128)(2,1)} %bitcast.11, bf16[3,2,2048]{2,1,0:T(2,128)(2,1)} %bitcast.12), custom_call_target="tpu_custom_call" | custom-call | tf_op jit(solution)/shard_map/pack/pallas_call | solution.py:354
  1.7 5.1 %collective-permute-start.1 = (bf16[40,2048]{1,0:T(8,128)(2,1)S(1)}, bf16[40,2048]{1,0:T(8,128)(2,1)S(1)}, u32[]{:S(2)}, u32[]{:S(2)}) collective-permute-start(bf16[40,2048]{1,0:T(8,128)(2,1)S(1)} %get-tuple-element.17.refs_7_.refs_14_), channel_id=1, source_target_pairs={{0,12},{4,8},{8,4},{12,0},{1,13},{5,9},{9,5},{13,1},{2,14},{6,10},... | collective-permute-start | bytes 491528 | tf_op jit(solution)/shard_map/ppermute | solution.py:366
  6.8 0.0 collective-permute-start
  6.8 0.6 %collective-permute-start.2 = (bf16[8,2048]{1,0:T(8,128)(2,1)S(1)}, bf16[8,2048]{1,0:T(8,128)(2,1)S(1)}, u32[]{:S(2)}, u32[]{:S(2)}) collective-permute-start(bf16[8,2048]{1,0:T(8,128)(2,1)S(1)} %get-tuple-element.18), channel_id=1, source_target_pairs={{0,8},{4,12},{8,0},{12,4},{1,9},{5,13},{9,1},{13,5},{2,10},{6,14},... | collective-permute-start | bytes 98312 | tf_op jit(solution)/shard_map/ppermute | solution.py:366
  7.5 4.0 %conv_project.1 = (bf16[256,2048]{1,0:T(8,128)(2,1)S(1)}, f32[32,2048]{1,0:T(8,128)S(1)}, bf16[288,256]{1,0:T(8,128)(2,1)S(1)}) custom-call(bf16[256,2048]{1,0:T(8,128)(2,1)} %refs_0_.3, bf16[288,2048]{1,0:T(8,128)(2,1)} %bitcast.7, bf16[4,2048]{1,0:T(4,128)(2,1)} %refs_6_.1, f32[1,2048]{1,0:T(1,128)} %bitcast.13), custom_call_target="tpu_custom_call" | custom-call | tf_op jit(solution)/shard_map/conv_project/pallas_call | solution.py:354
  11.5 3.3 %collective-permute-done.2.refs_10_ = bf16[8,2048]{1,0:T(8,128)(2,1)S(1)} collective-permute-done((bf16[8,2048]{1,0:T(8,128)(2,1)S(1)}, bf16[8,2048]{1,0:T(8,128)(2,1)S(1)}, u32[]{:S(2)}, u32[]{:S(2)}) %collective-permute-start.2) | collective-permute-done | bytes 32800 | tf_op jit(solution)/shard_map/ppermute | solution.py:366
  14.8 0.0 collective-permute-done.1.refs_9_.refs_16_
  14.8 0.5 %collective-permute-done.refs_8_.refs_15_ = bf16[40,2048]{1,0:T(8,128)(2,1)S(1)} collective-permute-done((bf16[40,2048]{1,0:T(8,128)(2,1)S(1)}, bf16[40,2048]{1,0:T(8,128)(2,1)S(1)}, u32[]{:S(2)}, u32[]{:S(2)}) %collective-permute-start) | collective-permute-done | bytes 163872 | tf_op jit(solution)/shard_map/ppermute | solution.py:366
  15.3 0.0 copy-done
  15.4 0.0 copy-start.1
  15.4 0.0 copy-start.6
  15.4 1.3 %history.1 = (bf16[32,2048]{1,0:T(8,128)(2,1)S(1)}, bf16[288,256]{1,0:T(8,128)(2,1)S(1)}) custom-call(s32[32]{0:T(128)S(1)} %copy-done.7, s32[32]{0:T(128)S(1)} %copy-done.8, s32[32]{0:T(128)S(1)} %copy-done.9, f32[32,2048]{1,0:T(8,128)S(1)} %get-tuple-element.15.refs_3_, bf16[288,256]{1,0:T(8,128)(2,1)S(1)} %get-tuple-element.16.refs_4_, ...), custom_call_target="tpu_custom_call" | custom-call | tf_op jit(solution)/shard_map/history/pallas_call | solution.py:354
  16.7 1.6 %collective-permute-start.3 = (bf16[288,256]{1,0:T(8,128)(2,1)S(1)}, bf16[288,256]{1,0:T(8,128)(2,1)S(1)}, u32[]{:S(2)}, u32[]{:S(2)}) collective-permute-start(bf16[288,256]{1,0:T(8,128)(2,1)S(1)} %get-tuple-element.23.refs_10_), channel_id=1, source_target_pairs={{0,2},{1,3},{2,0},{3,1},{4,6},{5,7},{6,4},{7,5},{8,10},{9,11},{10,... | collective-permute-start | bytes 442376 | tf_op jit(solution)/shard_map/ppermute | solution.py:366
  18.3 1.3 %collective-permute-start.6 = (bf16[40,2048]{1,0:T(8,128)(2,1)S(1)}, bf16[40,2048]{1,0:T(8,128)(2,1)S(1)}, u32[]{:S(2)}, u32[]{:S(2)}) collective-permute-start(bf16[40,2048]{1,0:T(8,128)(2,1)S(1)} %collective-permute-done.1.refs_9_.refs_16_), channel_id=1, source_target_pairs={{0,4},{4,0},{8,12},{12,8},{1,5},{5,1},{9,13},{13,9},{2,6},{6,2},{1... | collective-permute-start | bytes 491528 | tf_op jit(solution)/shard_map/ppermute | solution.py:366
  19.6 0.0 collective-permute-start.5
  19.6 2.9 %collective-permute-done.3.refs_11_ = bf16[288,256]{1,0:T(8,128)(2,1)S(1)} collective-permute-done((bf16[288,256]{1,0:T(8,128)(2,1)S(1)}, bf16[288,256]{1,0:T(8,128)(2,1)S(1)}, u32[]{:S(2)}, u32[]{:S(2)}) %collective-permute-start.3) | collective-permute-done | bytes 147488 | tf_op jit(solution)/shard_map/ppermute | solution.py:366
  22.6 0.0 collective-permute-start.4
  22.6 0.5 %prepare.1 = (f32[256,2048]{1,0:T(8,128)S(1)}, f32[16,256,128]{2,1,0:T(8,128)S(1)}, f32[16,2048]{1,0:T(8,128)S(1)}) custom-call(bf16[256,2048]{1,0:T(8,128)(2,1)S(1)} %get-tuple-element.14.refs_0_.refs_3_, bf16[32,2048]{1,0:T(8,128)(2,1)S(1)} %get-tuple-element.19.refs_1_.refs_4_, bf16[256,2048]{1,0:T(8,128)(2,1)S(1)} %copy-done.2, ...), custom_call_target="tpu_custom_call" | custom-call | tf_op jit(solution)/shard_map/prepare/pallas_call | solution.py:354
  23.1 0.0 collective-permute-done.5.refs_13_
  23.1 1.0 %collective-permute-done.6.refs_17_ = bf16[40,2048]{1,0:T(8,128)(2,1)S(1)} collective-permute-done((bf16[40,2048]{1,0:T(8,128)(2,1)S(1)}, bf16[40,2048]{1,0:T(8,128)(2,1)S(1)}, u32[]{:S(2)}, u32[]{:S(2)}) %collective-permute-start.6) | collective-permute-done | bytes 163872 | tf_op jit(solution)/shard_map/ppermute | solution.py:366
  24.1 0.0 collective-permute-done.4.refs_12_
  24.1 12.9 %dt_scan_gate.1 = (bf16[256,2048]{1,0:T(8,128)(2,1)}, bf16[128,2048]{1,0:T(8,128)(2,1)}) custom-call(s32[32]{0:T(128)S(1)} %copy-done.7, s32[32]{0:T(128)S(1)} %copy-done.8, s32[32]{0:T(128)S(1)} %copy-done.9, bf16[256,2048]{1,0:T(8,128)(2,1)S(1)} %get-tuple-element.14.refs_0_.refs_3_, bf16[32,2048]{1,0:T(8,128)(2,1)S(1)} %get-tuple-element.19.refs_1_.refs_4_, ...), custom_call_target="tpu_custom_call" | custom-call | tf_op jit(solution)/shard_map/dt_scan_gate/pallas_call | solution.py:354
  (15 shorter events, 0.0 us)
Async XLA Ops:
  0.6 14.7 %copy-start.4 = (bf16[4,2048]{1,0:T(4,128)(2,1)S(1)}, bf16[4,2048]{1,0:T(4,128)(2,1)}, u32[]{:S(2)}) copy-start(bf16[4,2048]{1,0:T(4,128)(2,1)} %refs_6_.1) | copy-start | bytes 49156
  0.6 14.7 %copy-start = (bf16[2048,288]{0,1:T(8,128)(2,1)S(1)}, bf16[2048,288]{0,1:T(8,128)(2,1)}, u32[]{:S(2)}) copy-start(bf16[2048,288]{0,1:T(8,128)(2,1)} %param.18) | copy-start | bytes 3538948
  0.7 14.7 %copy-start.9 = (s32[32]{0:T(128)S(1)}, s32[32]{0:T(128)}, u32[]{:S(2)}) copy-start(s32[32]{0:T(128)} %refs_2_.7) | copy-start | bytes 388
  0.7 14.7 %copy-start.8 = (s32[32]{0:T(128)S(1)}, s32[32]{0:T(128)}, u32[]{:S(2)}) copy-start(s32[32]{0:T(128)} %refs_1_.3) | copy-start | bytes 388
  0.7 14.7 %copy-start.7 = (s32[32]{0:T(128)S(1)}, s32[32]{0:T(128)}, u32[]{:S(2)}) copy-start(s32[32]{0:T(128)} %refs_0_.5) | copy-start | bytes 388
  1.7 13.1 %collective-permute-start.1 = (bf16[40,2048]{1,0:T(8,128)(2,1)S(1)}, bf16[40,2048]{1,0:T(8,128)(2,1)S(1)}, u32[]{:S(2)}, u32[]{:S(2)}) collective-permute-start(bf16[40,2048]{1,0:T(8,128)(2,1)S(1)} %get-tuple-element.17.refs_7_.refs_14_), channel_id=1, source_target_pairs={{0,12},{4,8},{8,4},{12,0},{1,13},{5,9},{9,5},{13,1},{2,14},{6,10},... | collective-permute-start | bytes 491528 | tf_op jit(solution)/shard_map/ppermute | solution.py:366
  6.8 8.5 %collective-permute-start = (bf16[40,2048]{1,0:T(8,128)(2,1)S(1)}, bf16[40,2048]{1,0:T(8,128)(2,1)S(1)}, u32[]{:S(2)}, u32[]{:S(2)}) collective-permute-start(bf16[40,2048]{1,0:T(8,128)(2,1)S(1)} %get-tuple-element.17.refs_7_.refs_14_), channel_id=1, source_target_pairs={{0,4},{4,0},{8,12},{12,8},{1,5},{5,1},{9,13},{13,9},{2,6},{6,2},{1... | collective-permute-start | bytes 491528 | tf_op jit(solution)/shard_map/ppermute | solution.py:366
  6.8 8.0 %collective-permute-start.2 = (bf16[8,2048]{1,0:T(8,128)(2,1)S(1)}, bf16[8,2048]{1,0:T(8,128)(2,1)S(1)}, u32[]{:S(2)}, u32[]{:S(2)}) collective-permute-start(bf16[8,2048]{1,0:T(8,128)(2,1)S(1)} %get-tuple-element.18), channel_id=1, source_target_pairs={{0,8},{4,12},{8,0},{12,4},{1,9},{5,13},{9,1},{13,5},{2,10},{6,14},... | collective-permute-start | bytes 98312 | tf_op jit(solution)/shard_map/ppermute | solution.py:366
  7.5 15.1 %copy-start.2 = (bf16[256,2048]{1,0:T(8,128)(2,1)S(1)}, bf16[256,2048]{1,0:T(8,128)(2,1)}, u32[]{:S(2)}) copy-start(bf16[256,2048]{1,0:T(8,128)(2,1)} %refs_2_.6) | copy-start | bytes 3145732
  7.5 15.1 %copy-start.3 = (f32[16,2048]{1,0:T(8,128)S(1)}, f32[16,2048]{1,0:T(8,128)}, u32[]{:S(2)}) copy-start(f32[16,2048]{1,0:T(8,128)} %refs_3_.1) | copy-start | bytes 393220
  7.5 15.1 %copy-start.5 = (f32[2048]{0:T(1024)S(1)}, f32[2048]{0:T(1024)}, u32[]{:S(2)}) copy-start(f32[2048]{0:T(1024)} %param.22) | copy-start | bytes 24580
  15.4 8.7 %copy-start.1 = (bf16[256,2048]{1,0:T(8,128)(2,1)S(1)}, bf16[256,2048]{1,0:T(8,128)(2,1)}, u32[]{:S(2)}) copy-start(bf16[256,2048]{1,0:T(8,128)(2,1)} %refs_5_.1) | copy-start | bytes 3145732
  15.4 8.7 %copy-start.6 = (f32[2048]{0:T(1024)S(1)}, f32[2048]{0:T(1024)}, u32[]{:S(2)}) copy-start(f32[2048]{0:T(1024)} %param.20) | copy-start | bytes 24580
  16.7 5.8 %collective-permute-start.3 = (bf16[288,256]{1,0:T(8,128)(2,1)S(1)}, bf16[288,256]{1,0:T(8,128)(2,1)S(1)}, u32[]{:S(2)}, u32[]{:S(2)}) collective-permute-start(bf16[288,256]{1,0:T(8,128)(2,1)S(1)} %get-tuple-element.23.refs_10_), channel_id=1, source_target_pairs={{0,2},{1,3},{2,0},{3,1},{4,6},{5,7},{6,4},{7,5},{8,10},{9,11},{10,... | collective-permute-start | bytes 442376 | tf_op jit(solution)/shard_map/ppermute | solution.py:366
  18.3 5.8 %collective-permute-start.6 = (bf16[40,2048]{1,0:T(8,128)(2,1)S(1)}, bf16[40,2048]{1,0:T(8,128)(2,1)S(1)}, u32[]{:S(2)}, u32[]{:S(2)}) collective-permute-start(bf16[40,2048]{1,0:T(8,128)(2,1)S(1)} %collective-permute-done.1.refs_9_.refs_16_), channel_id=1, source_target_pairs={{0,4},{4,0},{8,12},{12,8},{1,5},{5,1},{9,13},{13,9},{2,6},{6,2},{1... | collective-permute-start | bytes 491528 | tf_op jit(solution)/shard_map/ppermute | solution.py:366
  19.6 3.5 %collective-permute-start.5 = (bf16[288,256]{1,0:T(8,128)(2,1)S(1)}, bf16[288,256]{1,0:T(8,128)(2,1)S(1)}, u32[]{:S(2)}, u32[]{:S(2)}) collective-permute-start(bf16[288,256]{1,0:T(8,128)(2,1)S(1)} %get-tuple-element.23.refs_10_), channel_id=1, source_target_pairs={{0,1},{1,0},{2,3},{3,2},{4,5},{5,4},{6,7},{7,6},{8,9},{9,8},{10,11... | collective-permute-start | bytes 442376 | tf_op jit(solution)/shard_map/ppermute | solution.py:366
  22.6 1.5 %collective-permute-start.4 = (bf16[288,256]{1,0:T(8,128)(2,1)S(1)}, bf16[288,256]{1,0:T(8,128)(2,1)S(1)}, u32[]{:S(2)}, u32[]{:S(2)}) collective-permute-start(bf16[288,256]{1,0:T(8,128)(2,1)S(1)} %collective-permute-done.3.refs_11_), channel_id=1, source_target_pairs={{0,1},{1,0},{2,3},{3,2},{4,5},{5,4},{6,7},{7,6},{8,9},{9,8},{10,11... | collective-permute-start | bytes 442376 | tf_op jit(solution)/shard_map/ppermute | solution.py:366

commit v18 on v16

--- a/solution.py
+++ b/solution.py
@@ -252,7 +252,7 @@
             start_tm[tile, pl.ds(r, states, stride=per_dev), :] = value
 
     tiles = 2
-    half = states // 2
+    half = states // 4
     width = tiles * LANES
     n_groups = n_tiles // tiles
 

time: 35.9 us -> 36.1 us (level)
  no operation moved by 1% of the time
where the time goes in v18:
time: 36.1 us; the launch traced here: 35.9 us
  Pallas kernels  18.7 us (52%)
  starting transfers between devices  8.67 us (24%)
  waiting for transfers between devices  7.75 us (21%)
  between operations  0.77 us (2%)
    pallas_call x5, Pallas kernels, call(): pl.pallas_call(split_refs(kernel, dims, len(ins), len(outs)), in_specs=[p...  18.7 us
    ppermute x7, starting transfers between devices, swap(): return lax.ppermute(value, axis, [(i, i ^ mask) for i in range(size)])  8.67 us
    ppermute x7, waiting for transfers between devices, swap(): return lax.ppermute(value, axis, [(i, i ^ mask) for i in range(size)])  7.75 us
  transfers between devices with their start and end apart: 7, of which 4 were waited for; matrix products, arithmetic and copies ran while one was open for 0% of the time, Pallas kernels for 13%

profile of v18, /device:TPU:0, one launch (start us, length us, event | category | flops | bytes accessed | tf_op | source)
XLA Modules:
  0.0 35.9 jit_solution(11145999432359451049)
XLA Ops:
  0.6 0.0 copy-start.4
  0.6 0.0 copy-start
  0.7 1.0 %pack.1 = (bf16[40,2048]{1,0:T(8,128)(2,1)S(1)}, bf16[8,2048]{1,0:T(8,128)(2,1)S(1)}) custom-call(bf16[32,2048]{1,0:T(8,128)(2,1)} %bitcast.11, bf16[3,2,2048]{2,1,0:T(2,128)(2,1)} %bitcast.12), custom_call_target="tpu_custom_call" | custom-call | tf_op jit(solution)/shard_map/pack/pallas_call | solution.py:351
  1.7 5.1 %collective-permute-start.1 = (bf16[40,2048]{1,0:T(8,128)(2,1)S(1)}, bf16[40,2048]{1,0:T(8,128)(2,1)S(1)}, u32[]{:S(2)}, u32[]{:S(2)}) collective-permute-start(bf16[40,2048]{1,0:T(8,128)(2,1)S(1)} %get-tuple-element.17.refs_7_.refs_14_), channel_id=1, source_target_pairs={{0,12},{4,8},{8,4},{12,0},{1,13},{5,9},{9,5},{13,1},{2,14},{6,10},... | collective-permute-start | bytes 491528 | tf_op jit(solution)/shard_map/ppermute | solution.py:363
  6.8 0.0 collective-permute-start
  6.8 0.6 %collective-permute-start.2 = (bf16[8,2048]{1,0:T(8,128)(2,1)S(1)}, bf16[8,2048]{1,0:T(8,128)(2,1)S(1)}, u32[]{:S(2)}, u32[]{:S(2)}) collective-permute-start(bf16[8,2048]{1,0:T(8,128)(2,1)S(1)} %get-tuple-element.18), channel_id=1, source_target_pairs={{0,8},{4,12},{8,0},{12,4},{1,9},{5,13},{9,1},{13,5},{2,10},{6,14},... | collective-permute-start | bytes 98312 | tf_op jit(solution)/shard_map/ppermute | solution.py:363
  7.5 4.0 %conv_project.1 = (bf16[256,2048]{1,0:T(8,128)(2,1)S(1)}, f32[32,2048]{1,0:T(8,128)S(1)}, bf16[288,256]{1,0:T(8,128)(2,1)S(1)}) custom-call(bf16[256,2048]{1,0:T(8,128)(2,1)} %refs_0_.3, bf16[288,2048]{1,0:T(8,128)(2,1)} %bitcast.7, bf16[4,2048]{1,0:T(4,128)(2,1)} %refs_6_.1, f32[1,2048]{1,0:T(1,128)} %bitcast.13), custom_call_target="tpu_custom_call" | custom-call | tf_op jit(solution)/shard_map/conv_project/pallas_call | solution.py:351
  11.5 3.3 %collective-permute-done.2.refs_10_ = bf16[8,2048]{1,0:T(8,128)(2,1)S(1)} collective-permute-done((bf16[8,2048]{1,0:T(8,128)(2,1)S(1)}, bf16[8,2048]{1,0:T(8,128)(2,1)S(1)}, u32[]{:S(2)}, u32[]{:S(2)}) %collective-permute-start.2) | collective-permute-done | bytes 32800 | tf_op jit(solution)/shard_map/ppermute | solution.py:363
  14.8 0.0 collective-permute-done.1.refs_9_.refs_16_
  14.8 0.5 %collective-permute-done.refs_8_.refs_15_ = bf16[40,2048]{1,0:T(8,128)(2,1)S(1)} collective-permute-done((bf16[40,2048]{1,0:T(8,128)(2,1)S(1)}, bf16[40,2048]{1,0:T(8,128)(2,1)S(1)}, u32[]{:S(2)}, u32[]{:S(2)}) %collective-permute-start) | collective-permute-done | bytes 163872 | tf_op jit(solution)/shard_map/ppermute | solution.py:363
  15.4 0.0 copy-start.1
  15.4 0.0 copy-start.6
  15.4 1.3 %history.1 = (bf16[32,2048]{1,0:T(8,128)(2,1)S(1)}, bf16[288,256]{1,0:T(8,128)(2,1)S(1)}) custom-call(s32[32]{0:T(128)S(1)} %copy-done.7, s32[32]{0:T(128)S(1)} %copy-done.8, s32[32]{0:T(128)S(1)} %copy-done.9, f32[32,2048]{1,0:T(8,128)S(1)} %get-tuple-element.15.refs_3_, bf16[288,256]{1,0:T(8,128)(2,1)S(1)} %get-tuple-element.16.refs_4_, ...), custom_call_target="tpu_custom_call" | custom-call | tf_op jit(solution)/shard_map/history/pallas_call | solution.py:351
  16.7 1.6 %collective-permute-start.3 = (bf16[288,256]{1,0:T(8,128)(2,1)S(1)}, bf16[288,256]{1,0:T(8,128)(2,1)S(1)}, u32[]{:S(2)}, u32[]{:S(2)}) collective-permute-start(bf16[288,256]{1,0:T(8,128)(2,1)S(1)} %get-tuple-element.23.refs_10_), channel_id=1, source_target_pairs={{0,2},{1,3},{2,0},{3,1},{4,6},{5,7},{6,4},{7,5},{8,10},{9,11},{10,... | collective-permute-start | bytes 442376 | tf_op jit(solution)/shard_map/ppermute | solution.py:363
  18.3 1.3 %collective-permute-start.6 = (bf16[40,2048]{1,0:T(8,128)(2,1)S(1)}, bf16[40,2048]{1,0:T(8,128)(2,1)S(1)}, u32[]{:S(2)}, u32[]{:S(2)}) collective-permute-start(bf16[40,2048]{1,0:T(8,128)(2,1)S(1)} %collective-permute-done.1.refs_9_.refs_16_), channel_id=1, source_target_pairs={{0,4},{4,0},{8,12},{12,8},{1,5},{5,1},{9,13},{13,9},{2,6},{6,2},{1... | collective-permute-start | bytes 491528 | tf_op jit(solution)/shard_map/ppermute | solution.py:363
  19.6 0.0 collective-permute-start.5
  19.6 2.9 %collective-permute-done.3.refs_11_ = bf16[288,256]{1,0:T(8,128)(2,1)S(1)} collective-permute-done((bf16[288,256]{1,0:T(8,128)(2,1)S(1)}, bf16[288,256]{1,0:T(8,128)(2,1)S(1)}, u32[]{:S(2)}, u32[]{:S(2)}) %collective-permute-start.3) | collective-permute-done | bytes 147488 | tf_op jit(solution)/shard_map/ppermute | solution.py:363
  22.6 0.0 collective-permute-start.4
  22.6 0.0 copy-done.3
  22.6 0.5 %prepare.1 = (f32[256,2048]{1,0:T(8,128)S(1)}, f32[16,256,128]{2,1,0:T(8,128)S(1)}, f32[16,2048]{1,0:T(8,128)S(1)}) custom-call(bf16[256,2048]{1,0:T(8,128)(2,1)S(1)} %get-tuple-element.14.refs_0_.refs_3_, bf16[32,2048]{1,0:T(8,128)(2,1)S(1)} %get-tuple-element.19.refs_1_.refs_4_, bf16[256,2048]{1,0:T(8,128)(2,1)S(1)} %copy-done.2, ...), custom_call_target="tpu_custom_call" | custom-call | tf_op jit(solution)/shard_map/prepare/pallas_call | solution.py:351
  23.1 0.0 collective-permute-done.5.refs_13_
  23.1 1.0 %collective-permute-done.6.refs_17_ = bf16[40,2048]{1,0:T(8,128)(2,1)S(1)} collective-permute-done((bf16[40,2048]{1,0:T(8,128)(2,1)S(1)}, bf16[40,2048]{1,0:T(8,128)(2,1)S(1)}, u32[]{:S(2)}, u32[]{:S(2)}) %collective-permute-start.6) | collective-permute-done | bytes 163872 | tf_op jit(solution)/shard_map/ppermute | solution.py:363
  24.1 0.0 collective-permute-done.4.refs_12_
  24.1 11.8 %dt_scan_gate.1 = (bf16[256,2048]{1,0:T(8,128)(2,1)}, bf16[128,2048]{1,0:T(8,128)(2,1)}) custom-call(s32[32]{0:T(128)S(1)} %copy-done.7, s32[32]{0:T(128)S(1)} %copy-done.8, s32[32]{0:T(128)S(1)} %copy-done.9, bf16[256,2048]{1,0:T(8,128)(2,1)S(1)} %get-tuple-element.14.refs_0_.refs_3_, bf16[32,2048]{1,0:T(8,128)(2,1)S(1)} %get-tuple-element.19.refs_1_.refs_4_, ...), custom_call_target="tpu_custom_call" | custom-call | tf_op jit(solution)/shard_map/dt_scan_gate/pallas_call | solution.py:351
  (15 shorter events, 0.0 us)
Async XLA Ops:
  0.6 14.7 %copy-start.4 = (bf16[4,2048]{1,0:T(4,128)(2,1)S(1)}, bf16[4,2048]{1,0:T(4,128)(2,1)}, u32[]{:S(2)}) copy-start(bf16[4,2048]{1,0:T(4,128)(2,1)} %refs_6_.1) | copy-start | bytes 49156
  0.6 14.7 %copy-start = (bf16[2048,288]{0,1:T(8,128)(2,1)S(1)}, bf16[2048,288]{0,1:T(8,128)(2,1)}, u32[]{:S(2)}) copy-start(bf16[2048,288]{0,1:T(8,128)(2,1)} %param.18) | copy-start | bytes 3538948
  0.7 14.7 %copy-start.9 = (s32[32]{0:T(128)S(1)}, s32[32]{0:T(128)}, u32[]{:S(2)}) copy-start(s32[32]{0:T(128)} %refs_2_.7) | copy-start | bytes 388
  0.7 14.7 %copy-start.8 = (s32[32]{0:T(128)S(1)}, s32[32]{0:T(128)}, u32[]{:S(2)}) copy-start(s32[32]{0:T(128)} %refs_1_.3) | copy-start | bytes 388
  0.7 14.7 %copy-start.7 = (s32[32]{0:T(128)S(1)}, s32[32]{0:T(128)}, u32[]{:S(2)}) copy-start(s32[32]{0:T(128)} %refs_0_.5) | copy-start | bytes 388
  1.7 13.1 %collective-permute-start.1 = (bf16[40,2048]{1,0:T(8,128)(2,1)S(1)}, bf16[40,2048]{1,0:T(8,128)(2,1)S(1)}, u32[]{:S(2)}, u32[]{:S(2)}) collective-permute-start(bf16[40,2048]{1,0:T(8,128)(2,1)S(1)} %get-tuple-element.17.refs_7_.refs_14_), channel_id=1, source_target_pairs={{0,12},{4,8},{8,4},{12,0},{1,13},{5,9},{9,5},{13,1},{2,14},{6,10},... | collective-permute-start | bytes 491528 | tf_op jit(solution)/shard_map/ppermute | solution.py:363
  6.8 8.5 %collective-permute-start = (bf16[40,2048]{1,0:T(8,128)(2,1)S(1)}, bf16[40,2048]{1,0:T(8,128)(2,1)S(1)}, u32[]{:S(2)}, u32[]{:S(2)}) collective-permute-start(bf16[40,2048]{1,0:T(8,128)(2,1)S(1)} %get-tuple-element.17.refs_7_.refs_14_), channel_id=1, source_target_pairs={{0,4},{4,0},{8,12},{12,8},{1,5},{5,1},{9,13},{13,9},{2,6},{6,2},{1... | collective-permute-start | bytes 491528 | tf_op jit(solution)/shard_map/ppermute | solution.py:363
  6.8 8.0 %collective-permute-start.2 = (bf16[8,2048]{1,0:T(8,128)(2,1)S(1)}, bf16[8,2048]{1,0:T(8,128)(2,1)S(1)}, u32[]{:S(2)}, u32[]{:S(2)}) collective-permute-start(bf16[8,2048]{1,0:T(8,128)(2,1)S(1)} %get-tuple-element.18), channel_id=1, source_target_pairs={{0,8},{4,12},{8,0},{12,4},{1,9},{5,13},{9,1},{13,5},{2,10},{6,14},... | collective-permute-start | bytes 98312 | tf_op jit(solution)/shard_map/ppermute | solution.py:363
  7.5 15.1 %copy-start.2 = (bf16[256,2048]{1,0:T(8,128)(2,1)S(1)}, bf16[256,2048]{1,0:T(8,128)(2,1)}, u32[]{:S(2)}) copy-start(bf16[256,2048]{1,0:T(8,128)(2,1)} %refs_2_.6) | copy-start | bytes 3145732
  7.5 15.1 %copy-start.3 = (f32[16,2048]{1,0:T(8,128)S(1)}, f32[16,2048]{1,0:T(8,128)}, u32[]{:S(2)}) copy-start(f32[16,2048]{1,0:T(8,128)} %refs_3_.1) | copy-start | bytes 393220
  7.5 15.1 %copy-start.5 = (f32[2048]{0:T(1024)S(1)}, f32[2048]{0:T(1024)}, u32[]{:S(2)}) copy-start(f32[2048]{0:T(1024)} %param.22) | copy-start | bytes 24580
  15.4 8.7 %copy-start.1 = (bf16[256,2048]{1,0:T(8,128)(2,1)S(1)}, bf16[256,2048]{1,0:T(8,128)(2,1)}, u32[]{:S(2)}) copy-start(bf16[256,2048]{1,0:T(8,128)(2,1)} %refs_5_.1) | copy-start | bytes 3145732
  15.4 8.7 %copy-start.6 = (f32[2048]{0:T(1024)S(1)}, f32[2048]{0:T(1024)}, u32[]{:S(2)}) copy-start(f32[2048]{0:T(1024)} %param.20) | copy-start | bytes 24580
  16.7 5.8 %collective-permute-start.3 = (bf16[288,256]{1,0:T(8,128)(2,1)S(1)}, bf16[288,256]{1,0:T(8,128)(2,1)S(1)}, u32[]{:S(2)}, u32[]{:S(2)}) collective-permute-start(bf16[288,256]{1,0:T(8,128)(2,1)S(1)} %get-tuple-element.23.refs_10_), channel_id=1, source_target_pairs={{0,2},{1,3},{2,0},{3,1},{4,6},{5,7},{6,4},{7,5},{8,10},{9,11},{10,... | collective-permute-start | bytes 442376 | tf_op jit(solution)/shard_map/ppermute | solution.py:363
  18.3 5.8 %collective-permute-start.6 = (bf16[40,2048]{1,0:T(8,128)(2,1)S(1)}, bf16[40,2048]{1,0:T(8,128)(2,1)S(1)}, u32[]{:S(2)}, u32[]{:S(2)}) collective-permute-start(bf16[40,2048]{1,0:T(8,128)(2,1)S(1)} %collective-permute-done.1.refs_9_.refs_16_), channel_id=1, source_target_pairs={{0,4},{4,0},{8,12},{12,8},{1,5},{5,1},{9,13},{13,9},{2,6},{6,2},{1... | collective-permute-start | bytes 491528 | tf_op jit(solution)/shard_map/ppermute | solution.py:363
  19.6 3.5 %collective-permute-start.5 = (bf16[288,256]{1,0:T(8,128)(2,1)S(1)}, bf16[288,256]{1,0:T(8,128)(2,1)S(1)}, u32[]{:S(2)}, u32[]{:S(2)}) collective-permute-start(bf16[288,256]{1,0:T(8,128)(2,1)S(1)} %get-tuple-element.23.refs_10_), channel_id=1, source_target_pairs={{0,1},{1,0},{2,3},{3,2},{4,5},{5,4},{6,7},{7,6},{8,9},{9,8},{10,11... | collective-permute-start | bytes 442376 | tf_op jit(solution)/shard_map/ppermute | solution.py:363
  22.6 1.5 %collective-permute-start.4 = (bf16[288,256]{1,0:T(8,128)(2,1)S(1)}, bf16[288,256]{1,0:T(8,128)(2,1)S(1)}, u32[]{:S(2)}, u32[]{:S(2)}) collective-permute-start(bf16[288,256]{1,0:T(8,128)(2,1)S(1)} %collective-permute-done.3.refs_11_), channel_id=1, source_target_pairs={{0,1},{1,0},{2,3},{3,2},{4,5},{5,4},{6,7},{7,6},{8,9},{9,8},{10,11... | collective-permute-start | bytes 442376 | tf_op jit(solution)/shard_map/ppermute | solution.py:363

commit v19 on v18

--- a/solution.py
+++ b/solution.py
@@ -195,6 +195,10 @@
     rank = dtw_ref.shape[0]
     head = head_ref.shape[0]
 
+    me = lax.axis_index("replica")
+    for copy in int_copies:
+        copy.wait()
+    places, slot_ids, lengths = request_places(dims, ints, me)
     projected = parts[0][...].astype(F32)
     for part in parts[1:]:
         projected = projected + part[...].astype(F32)
@@ -212,6 +216,19 @@
     wide = min(4, n_tiles)
     per_chunk = states * wide // n_tiles
     for c in range(n_tiles // wide):
+        for r in range(c * per_dev * wide // n_tiles, (c + 1) * per_dev * wide // n_tiles):
+            spot = pl.ds(pl.multiple_of(slot_ids[r] * states, states), states)
+            for tile in range(n_tiles):
+                lanes = slice(tile * LANES, (tile + 1) * LANES)
+                if n_pieces == 1:
+                    value = pieces[0][places[r], spot, lanes]
+                else:
+                    value = pieces[0][spot, lanes]
+                    for p in range(1, n_pieces):
+                        value = jnp.where(places[r] == p, pieces[p][spot, lanes], value)
+                value = value.astype(F32)
+                value = jnp.where(lengths[r] > 0, value, jnp.zeros_like(value))
+                start_tm[tile, pl.ds(r, states, stride=per_dev), :] = value
         for n in range(c * per_chunk, (c + 1) * per_chunk):
             b_tab[n] = jnp.broadcast_to(late[:, n : n + 1], (rows, LANES))
         lanes = slice(c * per_chunk * LANES, (c + 1) * per_chunk * LANES)
@@ -233,24 +250,6 @@
                 dt_v[tile, here, :] = dt
                 drive_v[tile, here, :] = dt * mixed
 
-    me = lax.axis_index("replica")
-    for copy in int_copies:
-        copy.wait()
-    places, slot_ids, lengths = request_places(dims, ints, me)
-    for r in range(per_dev):
-        spot = pl.ds(pl.multiple_of(slot_ids[r] * states, states), states)
-        for tile in range(n_tiles):
-            lanes = slice(tile * LANES, (tile + 1) * LANES)
-            if n_pieces == 1:
-                value = pieces[0][places[r], spot, lanes]
-            else:
-                value = pieces[0][spot, lanes]
-                for p in range(1, n_pieces):
-                    value = jnp.where(places[r] == p, pieces[p][spot, lanes], value)
-            value = value.astype(F32)
-            value = jnp.where(lengths[r] > 0, value, jnp.zeros_like(value))
-            start_tm[tile, pl.ds(r, states, stride=per_dev), :] = value
-
     tiles = 2
     half = states // 4
     width = tiles * LANES

time: 36.1 us -> 36.6 us (1.014)
  Pallas kernels: 18.7 us -> 19.2 us
    pallas_call x5, Pallas kernels: 18.7 us -> 19.2 us  [call(): pl.pallas_call(split_refs(kernel, dims, len(ins), len(outs)), in_specs=[p...]
  transfers between devices with their start and end apart: 7 -> 7, of which waited for: 4 -> 4; matrix products, arithmetic and copies ran while one was open for 0% -> 0% of each run, Pallas kernels for 13% -> 12%
where the time goes in v19:
time: 36.6 us; the launch traced here: 36.4 us
  Pallas kernels  19.2 us (52%)
  starting transfers between devices  8.67 us (24%)
  waiting for transfers between devices  7.75 us (21%)
  between operations  0.77 us (2%)
    pallas_call x5, Pallas kernels, call(): pl.pallas_call(split_refs(kernel, dims, len(ins), len(outs)), in_specs=[p...  19.2 us
    ppermute x7, starting transfers between devices, swap(): return lax.ppermute(value, axis, [(i, i ^ mask) for i in range(size)])  8.67 us
    ppermute x7, waiting for transfers between devices, swap(): return lax.ppermute(value, axis, [(i, i ^ mask) for i in range(size)])  7.75 us
  transfers between devices with their start and end apart: 7, of which 4 were waited for; matrix products, arithmetic and copies ran while one was open for 0% of the time, Pallas kernels for 12%

profile of v19, /device:TPU:0, one launch (start us, length us, event | category | flops | bytes accessed | tf_op | source)
XLA Modules:
  0.0 36.4 jit_solution(356646839040482166)
XLA Ops:
  0.6 0.0 copy-start.4
  0.6 0.0 copy-start
  0.7 1.0 %pack.1 = (bf16[40,2048]{1,0:T(8,128)(2,1)S(1)}, bf16[8,2048]{1,0:T(8,128)(2,1)S(1)}) custom-call(bf16[32,2048]{1,0:T(8,128)(2,1)} %bitcast.11, bf16[3,2,2048]{2,1,0:T(2,128)(2,1)} %bitcast.12), custom_call_target="tpu_custom_call" | custom-call | tf_op jit(solution)/shard_map/pack/pallas_call | solution.py:350
  1.7 5.1 %collective-permute-start.1 = (bf16[40,2048]{1,0:T(8,128)(2,1)S(1)}, bf16[40,2048]{1,0:T(8,128)(2,1)S(1)}, u32[]{:S(2)}, u32[]{:S(2)}) collective-permute-start(bf16[40,2048]{1,0:T(8,128)(2,1)S(1)} %get-tuple-element.17.refs_7_.refs_14_), channel_id=1, source_target_pairs={{0,12},{4,8},{8,4},{12,0},{1,13},{5,9},{9,5},{13,1},{2,14},{6,10},... | collective-permute-start | bytes 491528 | tf_op jit(solution)/shard_map/ppermute | solution.py:362
  6.8 0.0 collective-permute-start
  6.8 0.6 %collective-permute-start.2 = (bf16[8,2048]{1,0:T(8,128)(2,1)S(1)}, bf16[8,2048]{1,0:T(8,128)(2,1)S(1)}, u32[]{:S(2)}, u32[]{:S(2)}) collective-permute-start(bf16[8,2048]{1,0:T(8,128)(2,1)S(1)} %get-tuple-element.18), channel_id=1, source_target_pairs={{0,8},{4,12},{8,0},{12,4},{1,9},{5,13},{9,1},{13,5},{2,10},{6,14},... | collective-permute-start | bytes 98312 | tf_op jit(solution)/shard_map/ppermute | solution.py:362
  7.5 4.0 %conv_project.1 = (bf16[256,2048]{1,0:T(8,128)(2,1)S(1)}, f32[32,2048]{1,0:T(8,128)S(1)}, bf16[288,256]{1,0:T(8,128)(2,1)S(1)}) custom-call(bf16[256,2048]{1,0:T(8,128)(2,1)} %refs_0_.3, bf16[288,2048]{1,0:T(8,128)(2,1)} %bitcast.7, bf16[4,2048]{1,0:T(4,128)(2,1)} %refs_6_.1, f32[1,2048]{1,0:T(1,128)} %bitcast.13), custom_call_target="tpu_custom_call" | custom-call | tf_op jit(solution)/shard_map/conv_project/pallas_call | solution.py:350
  11.5 3.3 %collective-permute-done.2.refs_10_ = bf16[8,2048]{1,0:T(8,128)(2,1)S(1)} collective-permute-done((bf16[8,2048]{1,0:T(8,128)(2,1)S(1)}, bf16[8,2048]{1,0:T(8,128)(2,1)S(1)}, u32[]{:S(2)}, u32[]{:S(2)}) %collective-permute-start.2) | collective-permute-done | bytes 32800 | tf_op jit(solution)/shard_map/ppermute | solution.py:362
  14.8 0.0 collective-permute-done.1.refs_9_.refs_16_
  14.8 0.5 %collective-permute-done.refs_8_.refs_15_ = bf16[40,2048]{1,0:T(8,128)(2,1)S(1)} collective-permute-done((bf16[40,2048]{1,0:T(8,128)(2,1)S(1)}, bf16[40,2048]{1,0:T(8,128)(2,1)S(1)}, u32[]{:S(2)}, u32[]{:S(2)}) %collective-permute-start) | collective-permute-done | bytes 163872 | tf_op jit(solution)/shard_map/ppermute | solution.py:362
  15.3 0.0 copy-done
  15.4 0.0 copy-start.1
  15.4 0.0 copy-start.6
  15.4 1.3 %history.1 = (bf16[32,2048]{1,0:T(8,128)(2,1)S(1)}, bf16[288,256]{1,0:T(8,128)(2,1)S(1)}) custom-call(s32[32]{0:T(128)S(1)} %copy-done.7, s32[32]{0:T(128)S(1)} %copy-done.8, s32[32]{0:T(128)S(1)} %copy-done.9, f32[32,2048]{1,0:T(8,128)S(1)} %get-tuple-element.15.refs_3_, bf16[288,256]{1,0:T(8,128)(2,1)S(1)} %get-tuple-element.16.refs_4_, ...), custom_call_target="tpu_custom_call" | custom-call | tf_op jit(solution)/shard_map/history/pallas_call | solution.py:350
  16.7 1.6 %collective-permute-start.3 = (bf16[288,256]{1,0:T(8,128)(2,1)S(1)}, bf16[288,256]{1,0:T(8,128)(2,1)S(1)}, u32[]{:S(2)}, u32[]{:S(2)}) collective-permute-start(bf16[288,256]{1,0:T(8,128)(2,1)S(1)} %get-tuple-element.23.refs_10_), channel_id=1, source_target_pairs={{0,2},{1,3},{2,0},{3,1},{4,6},{5,7},{6,4},{7,5},{8,10},{9,11},{10,... | collective-permute-start | bytes 442376 | tf_op jit(solution)/shard_map/ppermute | solution.py:362
  18.3 1.3 %collective-permute-start.6 = (bf16[40,2048]{1,0:T(8,128)(2,1)S(1)}, bf16[40,2048]{1,0:T(8,128)(2,1)S(1)}, u32[]{:S(2)}, u32[]{:S(2)}) collective-permute-start(bf16[40,2048]{1,0:T(8,128)(2,1)S(1)} %collective-permute-done.1.refs_9_.refs_16_), channel_id=1, source_target_pairs={{0,4},{4,0},{8,12},{12,8},{1,5},{5,1},{9,13},{13,9},{2,6},{6,2},{1... | collective-permute-start | bytes 491528 | tf_op jit(solution)/shard_map/ppermute | solution.py:362
  19.6 0.0 collective-permute-start.5
  19.6 2.9 %collective-permute-done.3.refs_11_ = bf16[288,256]{1,0:T(8,128)(2,1)S(1)} collective-permute-done((bf16[288,256]{1,0:T(8,128)(2,1)S(1)}, bf16[288,256]{1,0:T(8,128)(2,1)S(1)}, u32[]{:S(2)}, u32[]{:S(2)}) %collective-permute-start.3) | collective-permute-done | bytes 147488 | tf_op jit(solution)/shard_map/ppermute | solution.py:362
  22.6 0.0 collective-permute-start.4
  22.6 0.5 %prepare.1 = (f32[256,2048]{1,0:T(8,128)S(1)}, f32[16,256,128]{2,1,0:T(8,128)S(1)}, f32[16,2048]{1,0:T(8,128)S(1)}) custom-call(bf16[256,2048]{1,0:T(8,128)(2,1)S(1)} %get-tuple-element.14.refs_0_.refs_3_, bf16[32,2048]{1,0:T(8,128)(2,1)S(1)} %get-tuple-element.19.refs_1_.refs_4_, bf16[256,2048]{1,0:T(8,128)(2,1)S(1)} %copy-done.2, ...), custom_call_target="tpu_custom_call" | custom-call | tf_op jit(solution)/shard_map/prepare/pallas_call | solution.py:350
  23.1 0.0 collective-permute-done.5.refs_13_
  23.1 1.0 %collective-permute-done.6.refs_17_ = bf16[40,2048]{1,0:T(8,128)(2,1)S(1)} collective-permute-done((bf16[40,2048]{1,0:T(8,128)(2,1)S(1)}, bf16[40,2048]{1,0:T(8,128)(2,1)S(1)}, u32[]{:S(2)}, u32[]{:S(2)}) %collective-permute-start.6) | collective-permute-done | bytes 163872 | tf_op jit(solution)/shard_map/ppermute | solution.py:362
  24.1 0.0 collective-permute-done.4.refs_12_
  24.1 12.3 %dt_scan_gate.1 = (bf16[256,2048]{1,0:T(8,128)(2,1)}, bf16[128,2048]{1,0:T(8,128)(2,1)}) custom-call(s32[32]{0:T(128)S(1)} %copy-done.7, s32[32]{0:T(128)S(1)} %copy-done.8, s32[32]{0:T(128)S(1)} %copy-done.9, bf16[256,2048]{1,0:T(8,128)(2,1)S(1)} %get-tuple-element.14.refs_0_.refs_3_, bf16[32,2048]{1,0:T(8,128)(2,1)S(1)} %get-tuple-element.19.refs_1_.refs_4_, ...), custom_call_target="tpu_custom_call" | custom-call | tf_op jit(solution)/shard_map/dt_scan_gate/pallas_call | solution.py:350
  (15 shorter events, 0.0 us)
Async XLA Ops:
  0.6 14.7 %copy-start.4 = (bf16[4,2048]{1,0:T(4,128)(2,1)S(1)}, bf16[4,2048]{1,0:T(4,128)(2,1)}, u32[]{:S(2)}) copy-start(bf16[4,2048]{1,0:T(4,128)(2,1)} %refs_6_.1) | copy-start | bytes 49156
  0.6 14.7 %copy-start = (bf16[2048,288]{0,1:T(8,128)(2,1)S(1)}, bf16[2048,288]{0,1:T(8,128)(2,1)}, u32[]{:S(2)}) copy-start(bf16[2048,288]{0,1:T(8,128)(2,1)} %param.18) | copy-start | bytes 3538948
  0.7 14.7 %copy-start.9 = (s32[32]{0:T(128)S(1)}, s32[32]{0:T(128)}, u32[]{:S(2)}) copy-start(s32[32]{0:T(128)} %refs_2_.7) | copy-start | bytes 388
  0.7 14.7 %copy-start.8 = (s32[32]{0:T(128)S(1)}, s32[32]{0:T(128)}, u32[]{:S(2)}) copy-start(s32[32]{0:T(128)} %refs_1_.3) | copy-start | bytes 388
  0.7 14.7 %copy-start.7 = (s32[32]{0:T(128)S(1)}, s32[32]{0:T(128)}, u32[]{:S(2)}) copy-start(s32[32]{0:T(128)} %refs_0_.5) | copy-start | bytes 388
  1.7 13.1 %collective-permute-start.1 = (bf16[40,2048]{1,0:T(8,128)(2,1)S(1)}, bf16[40,2048]{1,0:T(8,128)(2,1)S(1)}, u32[]{:S(2)}, u32[]{:S(2)}) collective-permute-start(bf16[40,2048]{1,0:T(8,128)(2,1)S(1)} %get-tuple-element.17.refs_7_.refs_14_), channel_id=1, source_target_pairs={{0,12},{4,8},{8,4},{12,0},{1,13},{5,9},{9,5},{13,1},{2,14},{6,10},... | collective-permute-start | bytes 491528 | tf_op jit(solution)/shard_map/ppermute | solution.py:362
  6.8 8.5 %collective-permute-start = (bf16[40,2048]{1,0:T(8,128)(2,1)S(1)}, bf16[40,2048]{1,0:T(8,128)(2,1)S(1)}, u32[]{:S(2)}, u32[]{:S(2)}) collective-permute-start(bf16[40,2048]{1,0:T(8,128)(2,1)S(1)} %get-tuple-element.17.refs_7_.refs_14_), channel_id=1, source_target_pairs={{0,4},{4,0},{8,12},{12,8},{1,5},{5,1},{9,13},{13,9},{2,6},{6,2},{1... | collective-permute-start | bytes 491528 | tf_op jit(solution)/shard_map/ppermute | solution.py:362
  6.8 8.0 %collective-permute-start.2 = (bf16[8,2048]{1,0:T(8,128)(2,1)S(1)}, bf16[8,2048]{1,0:T(8,128)(2,1)S(1)}, u32[]{:S(2)}, u32[]{:S(2)}) collective-permute-start(bf16[8,2048]{1,0:T(8,128)(2,1)S(1)} %get-tuple-element.18), channel_id=1, source_target_pairs={{0,8},{4,12},{8,0},{12,4},{1,9},{5,13},{9,1},{13,5},{2,10},{6,14},... | collective-permute-start | bytes 98312 | tf_op jit(solution)/shard_map/ppermute | solution.py:362
  7.5 15.1 %copy-start.2 = (bf16[256,2048]{1,0:T(8,128)(2,1)S(1)}, bf16[256,2048]{1,0:T(8,128)(2,1)}, u32[]{:S(2)}) copy-start(bf16[256,2048]{1,0:T(8,128)(2,1)} %refs_2_.6) | copy-start | bytes 3145732
  7.5 15.1 %copy-start.3 = (f32[16,2048]{1,0:T(8,128)S(1)}, f32[16,2048]{1,0:T(8,128)}, u32[]{:S(2)}) copy-start(f32[16,2048]{1,0:T(8,128)} %refs_3_.1) | copy-start | bytes 393220
  7.5 15.1 %copy-start.5 = (f32[2048]{0:T(1024)S(1)}, f32[2048]{0:T(1024)}, u32[]{:S(2)}) copy-start(f32[2048]{0:T(1024)} %param.22) | copy-start | bytes 24580
  15.4 8.7 %copy-start.1 = (bf16[256,2048]{1,0:T(8,128)(2,1)S(1)}, bf16[256,2048]{1,0:T(8,128)(2,1)}, u32[]{:S(2)}) copy-start(bf16[256,2048]{1,0:T(8,128)(2,1)} %refs_5_.1) | copy-start | bytes 3145732
  15.4 8.7 %copy-start.6 = (f32[2048]{0:T(1024)S(1)}, f32[2048]{0:T(1024)}, u32[]{:S(2)}) copy-start(f32[2048]{0:T(1024)} %param.20) | copy-start | bytes 24580
  16.7 5.8 %collective-permute-start.3 = (bf16[288,256]{1,0:T(8,128)(2,1)S(1)}, bf16[288,256]{1,0:T(8,128)(2,1)S(1)}, u32[]{:S(2)}, u32[]{:S(2)}) collective-permute-start(bf16[288,256]{1,0:T(8,128)(2,1)S(1)} %get-tuple-element.23.refs_10_), channel_id=1, source_target_pairs={{0,2},{1,3},{2,0},{3,1},{4,6},{5,7},{6,4},{7,5},{8,10},{9,11},{10,... | collective-permute-start | bytes 442376 | tf_op jit(solution)/shard_map/ppermute | solution.py:362
  18.3 5.8 %collective-permute-start.6 = (bf16[40,2048]{1,0:T(8,128)(2,1)S(1)}, bf16[40,2048]{1,0:T(8,128)(2,1)S(1)}, u32[]{:S(2)}, u32[]{:S(2)}) collective-permute-start(bf16[40,2048]{1,0:T(8,128)(2,1)S(1)} %collective-permute-done.1.refs_9_.refs_16_), channel_id=1, source_target_pairs={{0,4},{4,0},{8,12},{12,8},{1,5},{5,1},{9,13},{13,9},{2,6},{6,2},{1... | collective-permute-start | bytes 491528 | tf_op jit(solution)/shard_map/ppermute | solution.py:362
  19.6 3.5 %collective-permute-start.5 = (bf16[288,256]{1,0:T(8,128)(2,1)S(1)}, bf16[288,256]{1,0:T(8,128)(2,1)S(1)}, u32[]{:S(2)}, u32[]{:S(2)}) collective-permute-start(bf16[288,256]{1,0:T(8,128)(2,1)S(1)} %get-tuple-element.23.refs_10_), channel_id=1, source_target_pairs={{0,1},{1,0},{2,3},{3,2},{4,5},{5,4},{6,7},{7,6},{8,9},{9,8},{10,11... | collective-permute-start | bytes 442376 | tf_op jit(solution)/shard_map/ppermute | solution.py:362
  22.6 1.5 %collective-permute-start.4 = (bf16[288,256]{1,0:T(8,128)(2,1)S(1)}, bf16[288,256]{1,0:T(8,128)(2,1)S(1)}, u32[]{:S(2)}, u32[]{:S(2)}) collective-permute-start(bf16[288,256]{1,0:T(8,128)(2,1)S(1)} %collective-permute-done.3.refs_11_), channel_id=1, source_target_pairs={{0,1},{1,0},{2,3},{3,2},{4,5},{5,4},{6,7},{7,6},{8,9},{9,8},{10,11... | collective-permute-start | bytes 442376 | tf_op jit(solution)/shard_map/ppermute | solution.py:362

commit v20 on v18

--- a/solution.py
+++ b/solution.py
@@ -85,9 +85,10 @@
 
 
 def project_kernel(dims, refs_in, refs_out, scratch):
-    per_dev = dims
-    x_hbm, wt_hbm, cw_hbm, cb_hbm = refs_in
-    mixed_hbm, head_hbm, part_hbm = refs_out
+    dims, block = dims
+    per_dev, _, slots, _ = dims
+    x_hbm, wt_hbm, cw_hbm, cb_hbm = refs_in[:4]
+    mixed_hbm, head_hbm, part_hbm, target_ref = refs_out
     x_v, wt_v, cw_v, cb_v, joined, mixed_v, head_v, part_f, part_v, sems, out_sems = scratch
     rows, channels = x_v.shape
     taps = cw_v.shape[0]
@@ -100,6 +101,13 @@
     copies = [pltpu.make_async_copy(src, dst, sems.at[i]) for i, (src, dst) in enumerate(pairs)]
     for copy in copies:
         copy.start()
+
+    me = lax.axis_index("replica")
+    places, slot_ids, lengths = request_places(dims, refs_in[4:], me)
+    tap, request = split_index(lax.broadcasted_iota(jnp.int32, target_ref.shape, 0), per_dev)
+    starts = [places[r] * block + (block - slots * taps) + slot_ids[r] * taps for r in range(per_dev)]
+    live = (tap < taps - 1) & (taps - 1 - tap <= pick_rows(lengths, request, per_dev))
+    target_ref[...] = jnp.where(live, pick_rows(starts, request, per_dev) + tap, -1)
 
     joined[:, :lines, :] = jnp.zeros((channels // LANES, lines, LANES), F32)
     copies[0].wait()
@@ -139,19 +147,13 @@
 
 
 def history_kernel(dims, refs_in, refs_out, scratch):
-    dims, block, firsts = dims
-    per_dev, n_replica, slots, _ = dims
-    holder, slot_id, prefix_len, head_ref, part_ref, wt_ref, cw_ref = refs_in[:7]
-    pieces = refs_in[7:]
+    per_dev, firsts = dims
+    target_ref, head_ref, part_ref, wt_ref, cw_ref = refs_in[:5]
+    pieces = refs_in[5:]
     mixed_ref, fixed_ref = refs_out
     taps = cw_ref.shape[0]
-    me = lax.axis_index("replica")
-    places, slot_ids, lengths = request_places(dims, (holder, slot_id, prefix_len), me)
-    tap, request = split_index(lax.broadcasted_iota(jnp.int32, (per_dev * taps, 1), 0), per_dev)
-    starts = [places[r] * block + (block - slots * taps) + slot_ids[r] * taps for r in range(per_dev)]
-    target = pick_rows(starts, request, per_dev) + tap
-    live = (tap < taps - 1) & (taps - 1 - tap <= pick_rows(lengths, request, per_dev))
-    history = fetch_rows(target, live, [(first, ref[...]) for first, ref in zip(firsts, pieces)])
+    target = target_ref[:, :1]
+    history = fetch_rows(target, target >= 0, [(first, ref[...]) for first, ref in zip(firsts, pieces)])
     sums = []
     for t in range(taps):
         summed = head_ref[t * per_dev : (t + 1) * per_dev]
@@ -209,7 +211,7 @@
     dt_low = projected[:, :rank].astype(BF16)
     late = projected[:, rank:]
     n_tiles = channels // LANES
-    wide = min(4, n_tiles)
+    wide = min(2, n_tiles)
     per_chunk = states * wide // n_tiles
     for c in range(n_tiles // wide):
         for n in range(c * per_chunk, (c + 1) * per_chunk):
@@ -402,10 +404,11 @@
     weights = x_proj_weight.T
     requests = [(holder, "smem"), (slot_id, "smem"), (prefix_len, "smem")]
 
-    mixed, head_sums, part = call(
-        project_kernel, per_dev, "conv_project", 40,
-        [(x_new, "hbm"), (weights, "hbm"), (conv_weight, "hbm"), (conv_bias[None, :], "hbm")],
-        [((rows, channels), BF16, "any"), ((head, channels), F32, "any"), ((out_cols, rows), BF16, "any")],
+    mixed, head_sums, part, target = call(
+        project_kernel, (dims, block), "conv_project", 40,
+        [(x_new, "hbm"), (weights, "hbm"), (conv_weight, "hbm"), (conv_bias[None, :], "hbm")] + requests,
+        [((rows, channels), BF16, "any"), ((head, channels), F32, "any"), ((out_cols, rows), BF16, "any"),
+         ((head, LANES), jnp.int32, "vmem")],
         [
             vmem((rows, channels), BF16),
             vmem((out_cols, channels), BF16),
@@ -421,9 +424,8 @@
         ],
     )
     mixed_head, part = call(
-        history_kernel, (dims, block, firsts), "history", 20,
-        requests
-        + [(value, "vmem") for value in [head_sums, part, weights, conv_weight] + conv_pieces],
+        history_kernel, (per_dev, firsts), "history", 20,
+        [(value, "vmem") for value in [target, head_sums, part, weights, conv_weight] + conv_pieces],
         [((head, channels), BF16, "vmem"), ((out_cols, rows), BF16, "vmem")],
         [],
     )

time: 36.1 us -> 35.4 us (0.981)
  waiting for transfers between devices: 7.75 us -> 5.32 us
  local copies, waits for them, and re-layouts: 0.05 us -> 2 us
    ppermute x7, waiting for transfers between devices: 7.75 us -> 5.32 us  [swap(): return lax.ppermute(value, axis, [(i, i ^ mask) for i in range(size)])]
    unnamed x20 -> x22, local copies, waits for them, and re-layouts: 0.05 us -> 2 us
  transfers between devices with their start and end apart: 7 -> 7, of which waited for: 4 -> 4; matrix products, arithmetic and copies ran while one was open for 0% -> 0% of each run, Pallas kernels for 13% -> 14%
where the time goes in v20:
time: 35.4 us; the launch traced here: 35.2 us
  Pallas kernels  18.5 us (52%)
  starting transfers between devices  8.67 us (24%)
  waiting for transfers between devices  5.32 us (15%)
  local copies, waits for them, and re-layouts  2 us (6%)
  between operations  0.74 us (2%)
    pallas_call x5, Pallas kernels, call(): pl.pallas_call(split_refs(kernel, dims, len(ins), len(outs)), in_specs=[p...  18.5 us
    ppermute x7, starting transfers between devices, swap(): return lax.ppermute(value, axis, [(i, i ^ mask) for i in range(size)])  8.67 us
    ppermute x7, waiting for transfers between devices, swap(): return lax.ppermute(value, axis, [(i, i ^ mask) for i in range(size)])  5.32 us
    unnamed x22, local copies, waits for them, and re-layouts  2 us
  transfers between devices with their start and end apart: 7, of which 4 were waited for; matrix products, arithmetic and copies ran while one was open for 0% of the time, Pallas kernels for 14%

profile of v20, /device:TPU:0, one launch (start us, length us, event | category | flops | bytes accessed | tf_op | source)
XLA Modules:
  0.0 35.2 jit_solution(13751246912901659740)
XLA Ops:
  0.6 0.0 copy-start.4
  0.6 0.0 copy-start
  0.7 1.0 %pack.1 = (bf16[40,2048]{1,0:T(8,128)(2,1)S(1)}, bf16[8,2048]{1,0:T(8,128)(2,1)S(1)}) custom-call(bf16[32,2048]{1,0:T(8,128)(2,1)} %bitcast.11, bf16[3,2,2048]{2,1,0:T(2,128)(2,1)} %bitcast.12), custom_call_target="tpu_custom_call" | custom-call | tf_op jit(solution)/shard_map/pack/pallas_call | solution.py:353
  1.7 5.1 %collective-permute-start.1 = (bf16[40,2048]{1,0:T(8,128)(2,1)S(1)}, bf16[40,2048]{1,0:T(8,128)(2,1)S(1)}, u32[]{:S(2)}, u32[]{:S(2)}) collective-permute-start(bf16[40,2048]{1,0:T(8,128)(2,1)S(1)} %get-tuple-element.19.refs_5_.refs_14_), channel_id=1, source_target_pairs={{0,12},{4,8},{8,4},{12,0},{1,13},{5,9},{9,5},{13,1},{2,14},{6,10},... | collective-permute-start | bytes 491528 | tf_op jit(solution)/shard_map/ppermute | solution.py:365
  6.8 0.0 collective-permute-start
  6.8 0.6 %collective-permute-start.2 = (bf16[8,2048]{1,0:T(8,128)(2,1)S(1)}, bf16[8,2048]{1,0:T(8,128)(2,1)S(1)}, u32[]{:S(2)}, u32[]{:S(2)}) collective-permute-start(bf16[8,2048]{1,0:T(8,128)(2,1)S(1)} %get-tuple-element.20), channel_id=1, source_target_pairs={{0,8},{4,12},{8,0},{12,4},{1,9},{5,13},{9,1},{13,5},{2,10},{6,14},... | collective-permute-start | bytes 98312 | tf_op jit(solution)/shard_map/ppermute | solution.py:365
  7.4 0.7 %copy-done.7 = s32[32]{0:T(128)S(1)} copy-done((s32[32]{0:T(128)S(1)}, s32[32]{0:T(128)}, u32[]{:S(2)}) %copy-start.7) | copy-done | bytes 152
  8.1 0.7 %copy-done.8 = s32[32]{0:T(128)S(1)} copy-done((s32[32]{0:T(128)S(1)}, s32[32]{0:T(128)}, u32[]{:S(2)}) %copy-start.8) | copy-done | bytes 152
  8.8 0.7 %copy-done.9 = s32[32]{0:T(128)S(1)} copy-done((s32[32]{0:T(128)S(1)}, s32[32]{0:T(128)}, u32[]{:S(2)}) %copy-start.9) | copy-done | bytes 152
  9.4 4.5 %conv_project.1 = (bf16[256,2048]{1,0:T(8,128)(2,1)S(1)}, f32[32,2048]{1,0:T(8,128)S(1)}, bf16[288,256]{1,0:T(8,128)(2,1)S(1)}, s32[32,128]{1,0:T(8,128)S(1)}) custom-call(bf16[256,2048]{1,0:T(8,128)(2,1)} %refs_0_.2, bf16[288,2048]{1,0:T(8,128)(2,1)} %bitcast.7, bf16[4,2048]{1,0:T(4,128)(2,1)} %refs_4_.3, f32[1,2048]{1,0:T(1,128)} %bitcast.13, ...), custom_call_target="tpu_custom_call" | custom-call | tf_op jit(solution)/shard_map/conv_project/pallas_call | solution.py:353
  13.9 0.9 %collective-permute-done.2.refs_8_ = bf16[8,2048]{1,0:T(8,128)(2,1)S(1)} collective-permute-done((bf16[8,2048]{1,0:T(8,128)(2,1)S(1)}, bf16[8,2048]{1,0:T(8,128)(2,1)S(1)}, u32[]{:S(2)}, u32[]{:S(2)}) %collective-permute-start.2) | collective-permute-done | bytes 32800 | tf_op jit(solution)/shard_map/ppermute | solution.py:365
  14.8 0.0 collective-permute-done.1.refs_7_.refs_16_
  14.8 0.5 %collective-permute-done.refs_6_.refs_15_ = bf16[40,2048]{1,0:T(8,128)(2,1)S(1)} collective-permute-done((bf16[40,2048]{1,0:T(8,128)(2,1)S(1)}, bf16[40,2048]{1,0:T(8,128)(2,1)S(1)}, u32[]{:S(2)}, u32[]{:S(2)}) %collective-permute-start) | collective-permute-done | bytes 163872 | tf_op jit(solution)/shard_map/ppermute | solution.py:365
  15.3 0.0 copy-start.10
  15.3 0.8 %history.1 = (bf16[32,2048]{1,0:T(8,128)(2,1)S(1)}, bf16[288,256]{1,0:T(8,128)(2,1)S(1)}) custom-call(s32[32,128]{1,0:T(8,128)S(1)} %get-tuple-element.16.refs_0_, f32[32,2048]{1,0:T(8,128)S(1)} %get-tuple-element.17.refs_1_, bf16[288,256]{1,0:T(8,128)(2,1)S(1)} %get-tuple-element.18.refs_2_, bf16[288,2048]{1,0:T(8,128)(2,1)S(1)} %bitcast.8, ...), custom_call_target="tpu_custom_call" | custom-call | tf_op jit(solution)/shard_map/history/pallas_call | solution.py:353
  16.1 1.6 %collective-permute-start.3 = (bf16[288,256]{1,0:T(8,128)(2,1)S(1)}, bf16[288,256]{1,0:T(8,128)(2,1)S(1)}, u32[]{:S(2)}, u32[]{:S(2)}) collective-permute-start(bf16[288,256]{1,0:T(8,128)(2,1)S(1)} %get-tuple-element.25.refs_10_), channel_id=1, source_target_pairs={{0,2},{1,3},{2,0},{3,1},{4,6},{5,7},{6,4},{7,5},{8,10},{9,11},{10,... | collective-permute-start | bytes 442376 | tf_op jit(solution)/shard_map/ppermute | solution.py:365
  17.7 1.3 %collective-permute-start.6 = (bf16[40,2048]{1,0:T(8,128)(2,1)S(1)}, bf16[40,2048]{1,0:T(8,128)(2,1)S(1)}, u32[]{:S(2)}, u32[]{:S(2)}) collective-permute-start(bf16[40,2048]{1,0:T(8,128)(2,1)S(1)} %collective-permute-done.1.refs_7_.refs_16_), channel_id=1, source_target_pairs={{0,4},{4,0},{8,12},{12,8},{1,5},{5,1},{9,13},{13,9},{2,6},{6,2},{1... | collective-permute-start | bytes 491528 | tf_op jit(solution)/shard_map/ppermute | solution.py:365
  19.1 0.0 collective-permute-start.5
  19.1 2.9 %collective-permute-done.3.refs_11_ = bf16[288,256]{1,0:T(8,128)(2,1)S(1)} collective-permute-done((bf16[288,256]{1,0:T(8,128)(2,1)S(1)}, bf16[288,256]{1,0:T(8,128)(2,1)S(1)}, u32[]{:S(2)}, u32[]{:S(2)}) %collective-permute-start.3) | collective-permute-done | bytes 147488 | tf_op jit(solution)/shard_map/ppermute | solution.py:365
  22.0 0.0 collective-permute-start.4
  22.0 0.5 %prepare.1 = (f32[256,2048]{1,0:T(8,128)S(1)}, f32[16,256,128]{2,1,0:T(8,128)S(1)}, f32[16,2048]{1,0:T(8,128)S(1)}) custom-call(bf16[256,2048]{1,0:T(8,128)(2,1)S(1)} %get-tuple-element.15.refs_0_.refs_3_, bf16[32,2048]{1,0:T(8,128)(2,1)S(1)} %get-tuple-element.21.refs_1_.refs_4_, bf16[256,2048]{1,0:T(8,128)(2,1)S(1)} %copy-done.2, ...), custom_call_target="tpu_custom_call" | custom-call | tf_op jit(solution)/shard_map/prepare/pallas_call | solution.py:353
  22.5 0.0 collective-permute-done.5.refs_13_
  22.5 1.0 %collective-permute-done.6.refs_17_ = bf16[40,2048]{1,0:T(8,128)(2,1)S(1)} collective-permute-done((bf16[40,2048]{1,0:T(8,128)(2,1)S(1)}, bf16[40,2048]{1,0:T(8,128)(2,1)S(1)}, u32[]{:S(2)}, u32[]{:S(2)}) %collective-permute-start.6) | collective-permute-done | bytes 163872 | tf_op jit(solution)/shard_map/ppermute | solution.py:365
  23.5 11.7 %dt_scan_gate.1 = (bf16[256,2048]{1,0:T(8,128)(2,1)}, bf16[128,2048]{1,0:T(8,128)(2,1)}) custom-call(s32[32]{0:T(128)S(1)} %copy-done.7, s32[32]{0:T(128)S(1)} %copy-done.8, s32[32]{0:T(128)S(1)} %copy-done.10, bf16[256,2048]{1,0:T(8,128)(2,1)S(1)} %get-tuple-element.15.refs_0_.refs_3_, bf16[32,2048]{1,0:T(8,128)(2,1)S(1)} %get-tuple-element.21.refs_1_.refs_4_, ...), custom_call_target="tpu_custom_call" | custom-call | tf_op jit(solution)/shard_map/dt_scan_gate/pallas_call | solution.py:353
  (17 shorter events, 0.0 us)
Async XLA Ops:
  0.6 14.7 %copy-start.4 = (bf16[4,2048]{1,0:T(4,128)(2,1)S(1)}, bf16[4,2048]{1,0:T(4,128)(2,1)}, u32[]{:S(2)}) copy-start(bf16[4,2048]{1,0:T(4,128)(2,1)} %refs_4_.3) | copy-start | bytes 49156
  0.6 14.7 %copy-start = (bf16[2048,288]{0,1:T(8,128)(2,1)S(1)}, bf16[2048,288]{0,1:T(8,128)(2,1)}, u32[]{:S(2)}) copy-start(bf16[2048,288]{0,1:T(8,128)(2,1)} %param.18) | copy-start | bytes 3538948
  1.7 13.1 %collective-permute-start.1 = (bf16[40,2048]{1,0:T(8,128)(2,1)S(1)}, bf16[40,2048]{1,0:T(8,128)(2,1)S(1)}, u32[]{:S(2)}, u32[]{:S(2)}) collective-permute-start(bf16[40,2048]{1,0:T(8,128)(2,1)S(1)} %get-tuple-element.19.refs_5_.refs_14_), channel_id=1, source_target_pairs={{0,12},{4,8},{8,4},{12,0},{1,13},{5,9},{9,5},{13,1},{2,14},{6,10},... | collective-permute-start | bytes 491528 | tf_op jit(solution)/shard_map/ppermute | solution.py:365
  6.8 8.5 %collective-permute-start = (bf16[40,2048]{1,0:T(8,128)(2,1)S(1)}, bf16[40,2048]{1,0:T(8,128)(2,1)S(1)}, u32[]{:S(2)}, u32[]{:S(2)}) collective-permute-start(bf16[40,2048]{1,0:T(8,128)(2,1)S(1)} %get-tuple-element.19.refs_5_.refs_14_), channel_id=1, source_target_pairs={{0,4},{4,0},{8,12},{12,8},{1,5},{5,1},{9,13},{13,9},{2,6},{6,2},{1... | collective-permute-start | bytes 491528 | tf_op jit(solution)/shard_map/ppermute | solution.py:365
  6.8 8.0 %collective-permute-start.2 = (bf16[8,2048]{1,0:T(8,128)(2,1)S(1)}, bf16[8,2048]{1,0:T(8,128)(2,1)S(1)}, u32[]{:S(2)}, u32[]{:S(2)}) collective-permute-start(bf16[8,2048]{1,0:T(8,128)(2,1)S(1)} %get-tuple-element.20), channel_id=1, source_target_pairs={{0,8},{4,12},{8,0},{12,4},{1,9},{5,13},{9,1},{13,5},{2,10},{6,14},... | collective-permute-start | bytes 98312 | tf_op jit(solution)/shard_map/ppermute | solution.py:365
  7.4 0.7 %copy-start.7 = (s32[32]{0:T(128)S(1)}, s32[32]{0:T(128)}, u32[]{:S(2)}) copy-start(s32[32]{0:T(128)} %refs_0_.3) | copy-start | bytes 388
  8.1 0.7 %copy-start.8 = (s32[32]{0:T(128)S(1)}, s32[32]{0:T(128)}, u32[]{:S(2)}) copy-start(s32[32]{0:T(128)} %refs_1_.1) | copy-start | bytes 388
  8.7 0.7 %copy-start.9 = (s32[32]{0:T(128)S(1)}, s32[32]{0:T(128)}, u32[]{:S(2)}) copy-start(s32[32]{0:T(128)} %refs_2_.5) | copy-start | bytes 388
  9.4 12.6 %copy-start.2 = (bf16[256,2048]{1,0:T(8,128)(2,1)S(1)}, bf16[256,2048]{1,0:T(8,128)(2,1)}, u32[]{:S(2)}) copy-start(bf16[256,2048]{1,0:T(8,128)(2,1)} %refs_2_.4) | copy-start | bytes 3145732
  9.4 12.6 %copy-start.3 = (f32[16,2048]{1,0:T(8,128)S(1)}, f32[16,2048]{1,0:T(8,128)}, u32[]{:S(2)}) copy-start(f32[16,2048]{1,0:T(8,128)} %refs_3_.1) | copy-start | bytes 393220
  9.4 12.6 %copy-start.5 = (f32[2048]{0:T(1024)S(1)}, f32[2048]{0:T(1024)}, u32[]{:S(2)}) copy-start(f32[2048]{0:T(1024)} %param.22) | copy-start | bytes 24580
  15.3 8.2 %copy-start.1 = (bf16[256,2048]{1,0:T(8,128)(2,1)S(1)}, bf16[256,2048]{1,0:T(8,128)(2,1)}, u32[]{:S(2)}) copy-start(bf16[256,2048]{1,0:T(8,128)(2,1)} %refs_5_.3) | copy-start | bytes 3145732
  15.3 8.2 %copy-start.6 = (f32[2048]{0:T(1024)S(1)}, f32[2048]{0:T(1024)}, u32[]{:S(2)}) copy-start(f32[2048]{0:T(1024)} %param.20) | copy-start | bytes 24580
  15.3 8.2 %copy-start.10 = (s32[32]{0:T(128)S(1)}, s32[32]{0:T(128)}, u32[]{:S(2)}) copy-start(s32[32]{0:T(128)} %refs_2_.5) | copy-start | bytes 388
  16.1 5.8 %collective-permute-start.3 = (bf16[288,256]{1,0:T(8,128)(2,1)S(1)}, bf16[288,256]{1,0:T(8,128)(2,1)S(1)}, u32[]{:S(2)}, u32[]{:S(2)}) collective-permute-start(bf16[288,256]{1,0:T(8,128)(2,1)S(1)} %get-tuple-element.25.refs_10_), channel_id=1, source_target_pairs={{0,2},{1,3},{2,0},{3,1},{4,6},{5,7},{6,4},{7,5},{8,10},{9,11},{10,... | collective-permute-start | bytes 442376 | tf_op jit(solution)/shard_map/ppermute | solution.py:365
  17.7 5.8 %collective-permute-start.6 = (bf16[40,2048]{1,0:T(8,128)(2,1)S(1)}, bf16[40,2048]{1,0:T(8,128)(2,1)S(1)}, u32[]{:S(2)}, u32[]{:S(2)}) collective-permute-start(bf16[40,2048]{1,0:T(8,128)(2,1)S(1)} %collective-permute-done.1.refs_7_.refs_16_), channel_id=1, source_target_pairs={{0,4},{4,0},{8,12},{12,8},{1,5},{5,1},{9,13},{13,9},{2,6},{6,2},{1... | collective-permute-start | bytes 491528 | tf_op jit(solution)/shard_map/ppermute | solution.py:365
  19.1 3.5 %collective-permute-start.5 = (bf16[288,256]{1,0:T(8,128)(2,1)S(1)}, bf16[288,256]{1,0:T(8,128)(2,1)S(1)}, u32[]{:S(2)}, u32[]{:S(2)}) collective-permute-start(bf16[288,256]{1,0:T(8,128)(2,1)S(1)} %get-tuple-element.25.refs_10_), channel_id=1, source_target_pairs={{0,1},{1,0},{2,3},{3,2},{4,5},{5,4},{6,7},{7,6},{8,9},{9,8},{10,11... | collective-permute-start | bytes 442376 | tf_op jit(solution)/shard_map/ppermute | solution.py:365
  22.0 1.5 %collective-permute-start.4 = (bf16[288,256]{1,0:T(8,128)(2,1)S(1)}, bf16[288,256]{1,0:T(8,128)(2,1)S(1)}, u32[]{:S(2)}, u32[]{:S(2)}) collective-permute-start(bf16[288,256]{1,0:T(8,128)(2,1)S(1)} %collective-permute-done.3.refs_11_), channel_id=1, source_target_pairs={{0,1},{1,0},{2,3},{3,2},{4,5},{5,4},{6,7},{7,6},{8,9},{9,8},{10,11... | collective-permute-start | bytes 442376 | tf_op jit(solution)/shard_map/ppermute | solution.py:365

commit v21 on v20

--- a/solution.py
+++ b/solution.py
@@ -89,7 +89,9 @@
     per_dev, _, slots, _ = dims
     x_hbm, wt_hbm, cw_hbm, cb_hbm = refs_in[:4]
     mixed_hbm, head_hbm, part_hbm, target_ref = refs_out
-    x_v, wt_v, cw_v, cb_v, joined, mixed_v, head_v, part_f, part_v, sems, out_sems = scratch
+    x_v, wt_v, cw_v, cb_v, joined, mixed_v, head_v, part_f, part_v, sems, out_sems, int_sems = scratch[:12]
+    ints = scratch[12:]
+    int_copies = [pltpu.make_async_copy(refs_in[4 + i], ints[i], int_sems.at[i]) for i in range(len(ints))]
     rows, channels = x_v.shape
     taps = cw_v.shape[0]
     lines = (taps - 1) * per_dev
@@ -99,15 +101,8 @@
     for chunk in chunks:
         pairs += [(x_hbm.at[:, chunk], x_v.at[:, chunk]), (wt_hbm.at[:, chunk], wt_v.at[:, chunk])]
     copies = [pltpu.make_async_copy(src, dst, sems.at[i]) for i, (src, dst) in enumerate(pairs)]
-    for copy in copies:
+    for copy in copies + int_copies:
         copy.start()
-
-    me = lax.axis_index("replica")
-    places, slot_ids, lengths = request_places(dims, refs_in[4:], me)
-    tap, request = split_index(lax.broadcasted_iota(jnp.int32, target_ref.shape, 0), per_dev)
-    starts = [places[r] * block + (block - slots * taps) + slot_ids[r] * taps for r in range(per_dev)]
-    live = (tap < taps - 1) & (taps - 1 - tap <= pick_rows(lengths, request, per_dev))
-    target_ref[...] = jnp.where(live, pick_rows(starts, request, per_dev) + tap, -1)
 
     joined[:, :lines, :] = jnp.zeros((channels // LANES, lines, LANES), F32)
     copies[0].wait()
@@ -138,6 +133,14 @@
             part_f[...] += part
         outs.append(pltpu.make_async_copy(mixed_v.at[:, chunk], mixed_hbm.at[:, chunk], out_sems.at[c]))
         outs[-1].start()
+    for copy in int_copies:
+        copy.wait()
+    me = lax.axis_index("replica")
+    places, slot_ids, lengths = request_places(dims, ints, me)
+    tap, request = split_index(lax.broadcasted_iota(jnp.int32, target_ref.shape, 0), per_dev)
+    starts = [places[r] * block + (block - slots * taps) + slot_ids[r] * taps for r in range(per_dev)]
+    live = (tap < taps - 1) & (taps - 1 - tap <= pick_rows(lengths, request, per_dev))
+    target_ref[...] = jnp.where(live, pick_rows(starts, request, per_dev) + tap, -1)
     part_v[...] = part_f[...].astype(BF16)
     for src, dst in ((part_v, part_hbm), (head_v, head_hbm)):
         outs.append(pltpu.make_async_copy(src, dst, out_sems.at[len(outs)]))
@@ -406,7 +409,8 @@
 
     mixed, head_sums, part, target = call(
         project_kernel, (dims, block), "conv_project", 40,
-        [(x_new, "hbm"), (weights, "hbm"), (conv_weight, "hbm"), (conv_bias[None, :], "hbm")] + requests,
+        [(x_new, "hbm"), (weights, "hbm"), (conv_weight, "hbm"), (conv_bias[None, :], "hbm")]
+        + [(value, "hbm") for value, _ in requests],
         [((rows, channels), BF16, "any"), ((head, channels), F32, "any"), ((out_cols, rows), BF16, "any"),
          ((head, LANES), jnp.int32, "vmem")],
         [
@@ -421,7 +425,8 @@
             vmem((out_cols, rows), BF16),
             dma((2 + 2 * n_chunks,)),
             dma((n_chunks + 2,)),
-        ],
+            dma((3,)),
+        ] + [pltpu.SMEM(holder.shape, jnp.int32)] * 3,
     )
     mixed_head, part = call(
         history_kernel, (per_dev, firsts), "history", 20,

time: 35.4 us -> 35.4 us (level)
  waiting for transfers between devices: 5.32 us -> 7.68 us
  local copies, waits for them, and re-layouts: 2 us -> 0.05 us
  Pallas kernels: 18.5 us -> 18.1 us
    ppermute x7, waiting for transfers between devices: 5.32 us -> 7.68 us  [swap(): return lax.ppermute(value, axis, [(i, i ^ mask) for i in range(size)])]
    unnamed x22 -> x20, local copies, waits for them, and re-layouts: 2 us -> 0.05 us
    pallas_call x5, Pallas kernels: 18.5 us -> 18.1 us  [call(): pl.pallas_call(split_refs(kernel, dims, len(ins), len(outs)), in_specs=[p...]
  transfers between devices with their start and end apart: 7 -> 7, of which waited for: 4 -> 4; matrix products, arithmetic and copies ran while one was open for 0% -> 0% of each run, Pallas kernels for 14% -> 13%
where the time goes in v21:
time: 35.4 us; the launch traced here: 35.3 us
  Pallas kernels  18.1 us (51%)
  starting transfers between devices  8.66 us (24%)
  waiting for transfers between devices  7.68 us (22%)
  between operations  0.76 us (2%)
    pallas_call x5, Pallas kernels, call(): pl.pallas_call(split_refs(kernel, dims, len(ins), len(outs)), in_specs=[p...  18.1 us
    ppermute x7, starting transfers between devices, swap(): return lax.ppermute(value, axis, [(i, i ^ mask) for i in range(size)])  8.66 us
    ppermute x7, waiting for transfers between devices, swap(): return lax.ppermute(value, axis, [(i, i ^ mask) for i in range(size)])  7.68 us
  transfers between devices with their start and end apart: 7, of which 4 were waited for; matrix products, arithmetic and copies ran while one was open for 0% of the time, Pallas kernels for 13%

profile of v21, /device:TPU:0, one launch (start us, length us, event | category | flops | bytes accessed | tf_op | source)
XLA Modules:
  0.0 35.3 jit_solution(14907374397967583502)
XLA Ops:
  0.6 0.0 copy-start.4
  0.6 0.0 copy-start
  0.7 1.0 %pack.1 = (bf16[40,2048]{1,0:T(8,128)(2,1)S(1)}, bf16[8,2048]{1,0:T(8,128)(2,1)S(1)}) custom-call(bf16[32,2048]{1,0:T(8,128)(2,1)} %bitcast.11, bf16[3,2,2048]{2,1,0:T(2,128)(2,1)} %bitcast.12), custom_call_target="tpu_custom_call" | custom-call | tf_op jit(solution)/shard_map/pack/pallas_call | solution.py:356
  1.7 5.1 %collective-permute-start.1 = (bf16[40,2048]{1,0:T(8,128)(2,1)S(1)}, bf16[40,2048]{1,0:T(8,128)(2,1)S(1)}, u32[]{:S(2)}, u32[]{:S(2)}) collective-permute-start(bf16[40,2048]{1,0:T(8,128)(2,1)S(1)} %get-tuple-element.19.refs_5_.refs_14_), channel_id=1, source_target_pairs={{0,12},{4,8},{8,4},{12,0},{1,13},{5,9},{9,5},{13,1},{2,14},{6,10},... | collective-permute-start | bytes 491528 | tf_op jit(solution)/shard_map/ppermute | solution.py:368
  6.8 0.0 collective-permute-start
  6.8 0.6 %collective-permute-start.2 = (bf16[8,2048]{1,0:T(8,128)(2,1)S(1)}, bf16[8,2048]{1,0:T(8,128)(2,1)S(1)}, u32[]{:S(2)}, u32[]{:S(2)}) collective-permute-start(bf16[8,2048]{1,0:T(8,128)(2,1)S(1)} %get-tuple-element.20), channel_id=1, source_target_pairs={{0,8},{4,12},{8,0},{12,4},{1,9},{5,13},{9,1},{13,5},{2,10},{6,14},... | collective-permute-start | bytes 98312 | tf_op jit(solution)/shard_map/ppermute | solution.py:368
  7.4 4.1 %conv_project.1 = (bf16[256,2048]{1,0:T(8,128)(2,1)S(1)}, f32[32,2048]{1,0:T(8,128)S(1)}, bf16[288,256]{1,0:T(8,128)(2,1)S(1)}, s32[32,128]{1,0:T(8,128)S(1)}) custom-call(bf16[256,2048]{1,0:T(8,128)(2,1)} %refs_0_.2, bf16[288,2048]{1,0:T(8,128)(2,1)} %bitcast.7, bf16[4,2048]{1,0:T(4,128)(2,1)} %refs_4_.3, f32[1,2048]{1,0:T(1,128)} %bitcast.13, s32[32]{0:T(128)} %refs_0_.3, ...), custom_call_target="tpu_custom_call" | custom-call | tf_op jit(solution)/shard_map/conv_project/pallas_call | solution.py:356
  11.6 3.2 %collective-permute-done.2.refs_8_ = bf16[8,2048]{1,0:T(8,128)(2,1)S(1)} collective-permute-done((bf16[8,2048]{1,0:T(8,128)(2,1)S(1)}, bf16[8,2048]{1,0:T(8,128)(2,1)S(1)}, u32[]{:S(2)}, u32[]{:S(2)}) %collective-permute-start.2) | collective-permute-done | bytes 32800 | tf_op jit(solution)/shard_map/ppermute | solution.py:368
  14.8 0.0 collective-permute-done.1.refs_7_.refs_16_
  14.8 0.5 %collective-permute-done.refs_6_.refs_15_ = bf16[40,2048]{1,0:T(8,128)(2,1)S(1)} collective-permute-done((bf16[40,2048]{1,0:T(8,128)(2,1)S(1)}, bf16[40,2048]{1,0:T(8,128)(2,1)S(1)}, u32[]{:S(2)}, u32[]{:S(2)}) %collective-permute-start) | collective-permute-done | bytes 163872 | tf_op jit(solution)/shard_map/ppermute | solution.py:368
  15.3 0.0 copy-start.7
  15.3 0.0 copy-start.8
  15.3 0.0 copy-start.9
  15.4 0.8 %history.1 = (bf16[32,2048]{1,0:T(8,128)(2,1)S(1)}, bf16[288,256]{1,0:T(8,128)(2,1)S(1)}) custom-call(s32[32,128]{1,0:T(8,128)S(1)} %get-tuple-element.16.refs_0_, f32[32,2048]{1,0:T(8,128)S(1)} %get-tuple-element.17.refs_1_, bf16[288,256]{1,0:T(8,128)(2,1)S(1)} %get-tuple-element.18.refs_2_, bf16[288,2048]{1,0:T(8,128)(2,1)S(1)} %bitcast.8, ...), custom_call_target="tpu_custom_call" | custom-call | tf_op jit(solution)/shard_map/history/pallas_call | solution.py:356
  16.2 1.6 %collective-permute-start.3 = (bf16[288,256]{1,0:T(8,128)(2,1)S(1)}, bf16[288,256]{1,0:T(8,128)(2,1)S(1)}, u32[]{:S(2)}, u32[]{:S(2)}) collective-permute-start(bf16[288,256]{1,0:T(8,128)(2,1)S(1)} %get-tuple-element.25.refs_10_), channel_id=1, source_target_pairs={{0,2},{1,3},{2,0},{3,1},{4,6},{5,7},{6,4},{7,5},{8,10},{9,11},{10,... | collective-permute-start | bytes 442376 | tf_op jit(solution)/shard_map/ppermute | solution.py:368
  17.7 1.3 %collective-permute-start.6 = (bf16[40,2048]{1,0:T(8,128)(2,1)S(1)}, bf16[40,2048]{1,0:T(8,128)(2,1)S(1)}, u32[]{:S(2)}, u32[]{:S(2)}) collective-permute-start(bf16[40,2048]{1,0:T(8,128)(2,1)S(1)} %collective-permute-done.1.refs_7_.refs_16_), channel_id=1, source_target_pairs={{0,4},{4,0},{8,12},{12,8},{1,5},{5,1},{9,13},{13,9},{2,6},{6,2},{1... | collective-permute-start | bytes 491528 | tf_op jit(solution)/shard_map/ppermute | solution.py:368
  19.1 0.0 collective-permute-start.5
  19.1 2.9 %collective-permute-done.3.refs_11_ = bf16[288,256]{1,0:T(8,128)(2,1)S(1)} collective-permute-done((bf16[288,256]{1,0:T(8,128)(2,1)S(1)}, bf16[288,256]{1,0:T(8,128)(2,1)S(1)}, u32[]{:S(2)}, u32[]{:S(2)}) %collective-permute-start.3) | collective-permute-done | bytes 147488 | tf_op jit(solution)/shard_map/ppermute | solution.py:368
  22.0 0.0 collective-permute-start.4
  22.0 0.5 %prepare.1 = (f32[256,2048]{1,0:T(8,128)S(1)}, f32[16,256,128]{2,1,0:T(8,128)S(1)}, f32[16,2048]{1,0:T(8,128)S(1)}) custom-call(bf16[256,2048]{1,0:T(8,128)(2,1)S(1)} %get-tuple-element.15.refs_0_.refs_3_, bf16[32,2048]{1,0:T(8,128)(2,1)S(1)} %get-tuple-element.21.refs_1_.refs_4_, bf16[256,2048]{1,0:T(8,128)(2,1)S(1)} %copy-done.2, ...), custom_call_target="tpu_custom_call" | custom-call | tf_op jit(solution)/shard_map/prepare/pallas_call | solution.py:356
  22.5 0.0 collective-permute-done.5.refs_13_
  22.6 1.0 %collective-permute-done.6.refs_17_ = bf16[40,2048]{1,0:T(8,128)(2,1)S(1)} collective-permute-done((bf16[40,2048]{1,0:T(8,128)(2,1)S(1)}, bf16[40,2048]{1,0:T(8,128)(2,1)S(1)}, u32[]{:S(2)}, u32[]{:S(2)}) %collective-permute-start.6) | collective-permute-done | bytes 163872 | tf_op jit(solution)/shard_map/ppermute | solution.py:368
  23.5 0.0 collective-permute-done.4.refs_12_
  23.6 11.7 %dt_scan_gate.1 = (bf16[256,2048]{1,0:T(8,128)(2,1)}, bf16[128,2048]{1,0:T(8,128)(2,1)}) custom-call(s32[32]{0:T(128)S(1)} %copy-done.7, s32[32]{0:T(128)S(1)} %copy-done.8, s32[32]{0:T(128)S(1)} %copy-done.9, bf16[256,2048]{1,0:T(8,128)(2,1)S(1)} %get-tuple-element.15.refs_0_.refs_3_, bf16[32,2048]{1,0:T(8,128)(2,1)S(1)} %get-tuple-element.21.refs_1_.refs_4_, ...), custom_call_target="tpu_custom_call" | custom-call | tf_op jit(solution)/shard_map/dt_scan_gate/pallas_call | solution.py:356
  (15 shorter events, 0.0 us)
Async XLA Ops:
  0.6 14.7 %copy-start.4 = (bf16[4,2048]{1,0:T(4,128)(2,1)S(1)}, bf16[4,2048]{1,0:T(4,128)(2,1)}, u32[]{:S(2)}) copy-start(bf16[4,2048]{1,0:T(4,128)(2,1)} %refs_4_.3) | copy-start | bytes 49156
  0.6 14.7 %copy-start = (bf16[2048,288]{0,1:T(8,128)(2,1)S(1)}, bf16[2048,288]{0,1:T(8,128)(2,1)}, u32[]{:S(2)}) copy-start(bf16[2048,288]{0,1:T(8,128)(2,1)} %param.18) | copy-start | bytes 3538948
  1.7 13.1 %collective-permute-start.1 = (bf16[40,2048]{1,0:T(8,128)(2,1)S(1)}, bf16[40,2048]{1,0:T(8,128)(2,1)S(1)}, u32[]{:S(2)}, u32[]{:S(2)}) collective-permute-start(bf16[40,2048]{1,0:T(8,128)(2,1)S(1)} %get-tuple-element.19.refs_5_.refs_14_), channel_id=1, source_target_pairs={{0,12},{4,8},{8,4},{12,0},{1,13},{5,9},{9,5},{13,1},{2,14},{6,10},... | collective-permute-start | bytes 491528 | tf_op jit(solution)/shard_map/ppermute | solution.py:368
  6.8 8.5 %collective-permute-start = (bf16[40,2048]{1,0:T(8,128)(2,1)S(1)}, bf16[40,2048]{1,0:T(8,128)(2,1)S(1)}, u32[]{:S(2)}, u32[]{:S(2)}) collective-permute-start(bf16[40,2048]{1,0:T(8,128)(2,1)S(1)} %get-tuple-element.19.refs_5_.refs_14_), channel_id=1, source_target_pairs={{0,4},{4,0},{8,12},{12,8},{1,5},{5,1},{9,13},{13,9},{2,6},{6,2},{1... | collective-permute-start | bytes 491528 | tf_op jit(solution)/shard_map/ppermute | solution.py:368
  6.8 8.0 %collective-permute-start.2 = (bf16[8,2048]{1,0:T(8,128)(2,1)S(1)}, bf16[8,2048]{1,0:T(8,128)(2,1)S(1)}, u32[]{:S(2)}, u32[]{:S(2)}) collective-permute-start(bf16[8,2048]{1,0:T(8,128)(2,1)S(1)} %get-tuple-element.20), channel_id=1, source_target_pairs={{0,8},{4,12},{8,0},{12,4},{1,9},{5,13},{9,1},{13,5},{2,10},{6,14},... | collective-permute-start | bytes 98312 | tf_op jit(solution)/shard_map/ppermute | solution.py:368
  7.4 14.6 %copy-start.2 = (bf16[256,2048]{1,0:T(8,128)(2,1)S(1)}, bf16[256,2048]{1,0:T(8,128)(2,1)}, u32[]{:S(2)}) copy-start(bf16[256,2048]{1,0:T(8,128)(2,1)} %refs_2_.4) | copy-start | bytes 3145732
  7.4 14.6 %copy-start.3 = (f32[16,2048]{1,0:T(8,128)S(1)}, f32[16,2048]{1,0:T(8,128)}, u32[]{:S(2)}) copy-start(f32[16,2048]{1,0:T(8,128)} %refs_3_.1) | copy-start | bytes 393220
  7.4 14.6 %copy-start.5 = (f32[2048]{0:T(1024)S(1)}, f32[2048]{0:T(1024)}, u32[]{:S(2)}) copy-start(f32[2048]{0:T(1024)} %param.22) | copy-start | bytes 24580
  15.3 8.2 %copy-start.1 = (bf16[256,2048]{1,0:T(8,128)(2,1)S(1)}, bf16[256,2048]{1,0:T(8,128)(2,1)}, u32[]{:S(2)}) copy-start(bf16[256,2048]{1,0:T(8,128)(2,1)} %refs_5_.3) | copy-start | bytes 3145732
  15.3 8.2 %copy-start.6 = (f32[2048]{0:T(1024)S(1)}, f32[2048]{0:T(1024)}, u32[]{:S(2)}) copy-start(f32[2048]{0:T(1024)} %param.20) | copy-start | bytes 24580
  15.3 8.2 %copy-start.7 = (s32[32]{0:T(128)S(1)}, s32[32]{0:T(128)}, u32[]{:S(2)}) copy-start(s32[32]{0:T(128)} %refs_0_.3) | copy-start | bytes 388
  15.3 8.2 %copy-start.8 = (s32[32]{0:T(128)S(1)}, s32[32]{0:T(128)}, u32[]{:S(2)}) copy-start(s32[32]{0:T(128)} %refs_1_.1) | copy-start | bytes 388
  15.3 8.2 %copy-start.9 = (s32[32]{0:T(128)S(1)}, s32[32]{0:T(128)}, u32[]{:S(2)}) copy-start(s32[32]{0:T(128)} %refs_2_.5) | copy-start | bytes 388
  16.2 5.8 %collective-permute-start.3 = (bf16[288,256]{1,0:T(8,128)(2,1)S(1)}, bf16[288,256]{1,0:T(8,128)(2,1)S(1)}, u32[]{:S(2)}, u32[]{:S(2)}) collective-permute-start(bf16[288,256]{1,0:T(8,128)(2,1)S(1)} %get-tuple-element.25.refs_10_), channel_id=1, source_target_pairs={{0,2},{1,3},{2,0},{3,1},{4,6},{5,7},{6,4},{7,5},{8,10},{9,11},{10,... | collective-permute-start | bytes 442376 | tf_op jit(solution)/shard_map/ppermute | solution.py:368
  17.7 5.8 %collective-permute-start.6 = (bf16[40,2048]{1,0:T(8,128)(2,1)S(1)}, bf16[40,2048]{1,0:T(8,128)(2,1)S(1)}, u32[]{:S(2)}, u32[]{:S(2)}) collective-permute-start(bf16[40,2048]{1,0:T(8,128)(2,1)S(1)} %collective-permute-done.1.refs_7_.refs_16_), channel_id=1, source_target_pairs={{0,4},{4,0},{8,12},{12,8},{1,5},{5,1},{9,13},{13,9},{2,6},{6,2},{1... | collective-permute-start | bytes 491528 | tf_op jit(solution)/shard_map/ppermute | solution.py:368
  19.1 3.5 %collective-permute-start.5 = (bf16[288,256]{1,0:T(8,128)(2,1)S(1)}, bf16[288,256]{1,0:T(8,128)(2,1)S(1)}, u32[]{:S(2)}, u32[]{:S(2)}) collective-permute-start(bf16[288,256]{1,0:T(8,128)(2,1)S(1)} %get-tuple-element.25.refs_10_), channel_id=1, source_target_pairs={{0,1},{1,0},{2,3},{3,2},{4,5},{5,4},{6,7},{7,6},{8,9},{9,8},{10,11... | collective-permute-start | bytes 442376 | tf_op jit(solution)/shard_map/ppermute | solution.py:368
  22.0 1.5 %collective-permute-start.4 = (bf16[288,256]{1,0:T(8,128)(2,1)S(1)}, bf16[288,256]{1,0:T(8,128)(2,1)S(1)}, u32[]{:S(2)}, u32[]{:S(2)}) collective-permute-start(bf16[288,256]{1,0:T(8,128)(2,1)S(1)} %collective-permute-done.3.refs_11_), channel_id=1, source_target_pairs={{0,1},{1,0},{2,3},{3,2},{4,5},{5,4},{6,7},{7,6},{8,9},{9,8},{10,11... | collective-permute-start | bytes 442376 | tf_op jit(solution)/shard_map/ppermute | solution.py:368

commit v22 on v21

--- a/solution.py
+++ b/solution.py
@@ -188,8 +188,8 @@
     per_dev, n_replica, _, _ = dims
     mixed_ref, head_ref, dtw_ref, dtb_ref, gate_ref, skipped_ref, rate_ref = refs_in[3:10]
     out_hbm, state_hbm = refs_out
-    b_tab, c_tab, dt_v, drive_v, start_tm, final_tm, y_v, out_v, state_v, out_sems, int_sems = scratch[:11]
-    ints = scratch[11:]
+    b_tab, c_tab, dt_v, drive_v, start_tm, final_rm, y_v, y_rm, out_v, state_v, out_sems, int_sems = scratch[:12]
+    ints = scratch[12:]
     int_copies = [pltpu.make_async_copy(refs_in[i], ints[i], int_sems.at[i]) for i in range(len(ints))]
     for copy in int_copies:
         copy.start()
@@ -274,10 +274,9 @@
             lanes = pl.ds(pl.multiple_of(tile * LANES, LANES), LANES)
             for r in range(per_dev):
                 here = slice(r * NEW, (r + 1) * NEW)
-                value = y_v[tile, pl.ds(r, NEW, stride=per_dev), :] * gate_ref[here, lanes]
-                out_v[here, lanes] = value.astype(BF16)
-                final = final_tm[tile, pl.ds(r, states, stride=per_dev), :]
-                state_v[r * states : (r + 1) * states, lanes] = final.astype(BF16)
+                out_v[here, lanes] = (y_rm[tile, here, :] * gate_ref[here, lanes]).astype(BF16)
+                here = slice(r * states, (r + 1) * states)
+                state_v[here, lanes] = final_rm[tile, here, :].astype(BF16)
 
     def scan_group(g):
         group = [g * tiles + j for j in range(tiles)]
@@ -302,7 +301,10 @@
                             sums[j] = term if sums[j] is None else sums[j] + term
                     for j, tile in enumerate(group):
                         before = skipped_ref[tile, now, :] if first == 0 else y_v[tile, now, :]
-                        y_v[tile, now, :] = before + sums[j]
+                        if first + half < states:
+                            y_v[tile, now, :] = before + sums[j]
+                        else:
+                            y_rm[tile, pl.ds(step * UNROLL + u, per_dev, stride=NEW), :] = before + sums[j]
                 return tuple(state)
 
             state = tuple(start_tm[tile, n * per_dev : (n + 1) * per_dev, :] for tile in group for n in ids)
@@ -312,7 +314,7 @@
                 state = lax.fori_loop(0, NEW // UNROLL, advance, state)
             for j, tile in enumerate(group):
                 for k, n in enumerate(ids):
-                    final_tm[tile, n * per_dev : (n + 1) * per_dev, :] = state[j * half + k]
+                    final_rm[tile, pl.ds(n, per_dev, stride=states), :] = state[j * half + k]
 
     def one_group(g, carry):
         before = jnp.maximum(g - 1, 0)
@@ -326,8 +328,8 @@
 
         return carry
 
-    final_tm[:tiles] = jnp.zeros((tiles,) + final_tm.shape[1:], F32)
-    y_v[:tiles] = jnp.zeros((tiles,) + y_v.shape[1:], F32)
+    final_rm[:tiles] = jnp.zeros((tiles,) + final_rm.shape[1:], F32)
+    y_rm[:tiles] = jnp.zeros((tiles,) + y_rm.shape[1:], F32)
     lax.fori_loop(0, n_groups, one_group, 0)
     finish(n_groups - 1)
     for copy in out_copies(n_groups - 1):
@@ -458,8 +460,9 @@
             vmem((n_tiles, rows, LANES), F32),
             vmem((n_tiles, rows, LANES), F32),
             vmem((n_tiles, per_dev * (states + 1), LANES), F32),
-            vmem((n_tiles, per_dev * (states + 1), LANES), F32),
-            vmem((n_tiles, rows + per_dev, LANES), F32),
+            vmem((n_tiles, (per_dev + 1) * states, LANES), F32),
+            vmem((n_tiles, rows, LANES), F32),
+            vmem((n_tiles, rows + NEW, LANES), F32),
             vmem((rows, channels), BF16),
             vmem((per_dev * states, channels), BF16),
             dma((2, n_tiles // 2)),

time: 35.4 us -> 36.2 us (1.023)
  Pallas kernels: 18.1 us -> 18.9 us
    pallas_call x5, Pallas kernels: 18.1 us -> 18.9 us  [call(): pl.pallas_call(split_refs(kernel, dims, len(ins), len(outs)), in_specs=[p...]
where the time goes in v22:
time: 36.2 us; the launch traced here: 36 us
  Pallas kernels  18.9 us (52%)
  starting transfers between devices  8.66 us (24%)
  waiting for transfers between devices  7.68 us (21%)
  between operations  0.76 us (2%)
    pallas_call x5, Pallas kernels, call(): pl.pallas_call(split_refs(kernel, dims, len(ins), len(outs)), in_specs=[p...  18.9 us
    ppermute x7, starting transfers between devices, swap(): return lax.ppermute(value, axis, [(i, i ^ mask) for i in range(size)])  8.66 us
    ppermute x7, waiting for transfers between devices, swap(): return lax.ppermute(value, axis, [(i, i ^ mask) for i in range(size)])  7.68 us
  transfers between devices with their start and end apart: 7, of which 4 were waited for; matrix products, arithmetic and copies ran while one was open for 0% of the time, Pallas kernels for 13%

profile of v22, /device:TPU:0, one launch (start us, length us, event | category | flops | bytes accessed | tf_op | source)
XLA Modules:
  0.0 36.0 jit_solution(15510604600792763227)
XLA Ops:
  0.6 0.0 copy-start.4
  0.6 0.0 copy-start
  0.7 1.0 %pack.1 = (bf16[40,2048]{1,0:T(8,128)(2,1)S(1)}, bf16[8,2048]{1,0:T(8,128)(2,1)S(1)}) custom-call(bf16[32,2048]{1,0:T(8,128)(2,1)} %bitcast.11, bf16[3,2,2048]{2,1,0:T(2,128)(2,1)} %bitcast.12), custom_call_target="tpu_custom_call" | custom-call | tf_op jit(solution)/shard_map/pack/pallas_call | solution.py:358
  1.7 5.1 %collective-permute-start.1 = (bf16[40,2048]{1,0:T(8,128)(2,1)S(1)}, bf16[40,2048]{1,0:T(8,128)(2,1)S(1)}, u32[]{:S(2)}, u32[]{:S(2)}) collective-permute-start(bf16[40,2048]{1,0:T(8,128)(2,1)S(1)} %get-tuple-element.19.refs_5_.refs_14_), channel_id=1, source_target_pairs={{0,12},{4,8},{8,4},{12,0},{1,13},{5,9},{9,5},{13,1},{2,14},{6,10},... | collective-permute-start | bytes 491528 | tf_op jit(solution)/shard_map/ppermute | solution.py:370
  6.8 0.0 collective-permute-start
  6.8 0.6 %collective-permute-start.2 = (bf16[8,2048]{1,0:T(8,128)(2,1)S(1)}, bf16[8,2048]{1,0:T(8,128)(2,1)S(1)}, u32[]{:S(2)}, u32[]{:S(2)}) collective-permute-start(bf16[8,2048]{1,0:T(8,128)(2,1)S(1)} %get-tuple-element.20), channel_id=1, source_target_pairs={{0,8},{4,12},{8,0},{12,4},{1,9},{5,13},{9,1},{13,5},{2,10},{6,14},... | collective-permute-start | bytes 98312 | tf_op jit(solution)/shard_map/ppermute | solution.py:370
  7.4 4.1 %conv_project.1 = (bf16[256,2048]{1,0:T(8,128)(2,1)S(1)}, f32[32,2048]{1,0:T(8,128)S(1)}, bf16[288,256]{1,0:T(8,128)(2,1)S(1)}, s32[32,128]{1,0:T(8,128)S(1)}) custom-call(bf16[256,2048]{1,0:T(8,128)(2,1)} %refs_0_.2, bf16[288,2048]{1,0:T(8,128)(2,1)} %bitcast.7, bf16[4,2048]{1,0:T(4,128)(2,1)} %refs_4_.3, f32[1,2048]{1,0:T(1,128)} %bitcast.13, s32[32]{0:T(128)} %refs_0_.3, ...), custom_call_target="tpu_custom_call" | custom-call | tf_op jit(solution)/shard_map/conv_project/pallas_call | solution.py:358
  11.6 3.2 %collective-permute-done.2.refs_8_ = bf16[8,2048]{1,0:T(8,128)(2,1)S(1)} collective-permute-done((bf16[8,2048]{1,0:T(8,128)(2,1)S(1)}, bf16[8,2048]{1,0:T(8,128)(2,1)S(1)}, u32[]{:S(2)}, u32[]{:S(2)}) %collective-permute-start.2) | collective-permute-done | bytes 32800 | tf_op jit(solution)/shard_map/ppermute | solution.py:370
  14.8 0.0 collective-permute-done.1.refs_7_.refs_16_
  14.8 0.5 %collective-permute-done.refs_6_.refs_15_ = bf16[40,2048]{1,0:T(8,128)(2,1)S(1)} collective-permute-done((bf16[40,2048]{1,0:T(8,128)(2,1)S(1)}, bf16[40,2048]{1,0:T(8,128)(2,1)S(1)}, u32[]{:S(2)}, u32[]{:S(2)}) %collective-permute-start) | collective-permute-done | bytes 163872 | tf_op jit(solution)/shard_map/ppermute | solution.py:370
  15.3 0.0 copy-start.7
  15.3 0.0 copy-start.8
  15.3 0.0 copy-start.9
  15.4 0.8 %history.1 = (bf16[32,2048]{1,0:T(8,128)(2,1)S(1)}, bf16[288,256]{1,0:T(8,128)(2,1)S(1)}) custom-call(s32[32,128]{1,0:T(8,128)S(1)} %get-tuple-element.16.refs_0_, f32[32,2048]{1,0:T(8,128)S(1)} %get-tuple-element.17.refs_1_, bf16[288,256]{1,0:T(8,128)(2,1)S(1)} %get-tuple-element.18.refs_2_, bf16[288,2048]{1,0:T(8,128)(2,1)S(1)} %bitcast.8, ...), custom_call_target="tpu_custom_call" | custom-call | tf_op jit(solution)/shard_map/history/pallas_call | solution.py:358
  16.2 1.6 %collective-permute-start.3 = (bf16[288,256]{1,0:T(8,128)(2,1)S(1)}, bf16[288,256]{1,0:T(8,128)(2,1)S(1)}, u32[]{:S(2)}, u32[]{:S(2)}) collective-permute-start(bf16[288,256]{1,0:T(8,128)(2,1)S(1)} %get-tuple-element.25.refs_10_), channel_id=1, source_target_pairs={{0,2},{1,3},{2,0},{3,1},{4,6},{5,7},{6,4},{7,5},{8,10},{9,11},{10,... | collective-permute-start | bytes 442376 | tf_op jit(solution)/shard_map/ppermute | solution.py:370
  17.7 1.3 %collective-permute-start.6 = (bf16[40,2048]{1,0:T(8,128)(2,1)S(1)}, bf16[40,2048]{1,0:T(8,128)(2,1)S(1)}, u32[]{:S(2)}, u32[]{:S(2)}) collective-permute-start(bf16[40,2048]{1,0:T(8,128)(2,1)S(1)} %collective-permute-done.1.refs_7_.refs_16_), channel_id=1, source_target_pairs={{0,4},{4,0},{8,12},{12,8},{1,5},{5,1},{9,13},{13,9},{2,6},{6,2},{1... | collective-permute-start | bytes 491528 | tf_op jit(solution)/shard_map/ppermute | solution.py:370
  19.1 0.0 collective-permute-start.5
  19.1 2.9 %collective-permute-done.3.refs_11_ = bf16[288,256]{1,0:T(8,128)(2,1)S(1)} collective-permute-done((bf16[288,256]{1,0:T(8,128)(2,1)S(1)}, bf16[288,256]{1,0:T(8,128)(2,1)S(1)}, u32[]{:S(2)}, u32[]{:S(2)}) %collective-permute-start.3) | collective-permute-done | bytes 147488 | tf_op jit(solution)/shard_map/ppermute | solution.py:370
  22.0 0.0 collective-permute-start.4
  22.0 0.5 %prepare.1 = (f32[256,2048]{1,0:T(8,128)S(1)}, f32[16,256,128]{2,1,0:T(8,128)S(1)}, f32[16,2048]{1,0:T(8,128)S(1)}) custom-call(bf16[256,2048]{1,0:T(8,128)(2,1)S(1)} %get-tuple-element.15.refs_0_.refs_3_, bf16[32,2048]{1,0:T(8,128)(2,1)S(1)} %get-tuple-element.21.refs_1_.refs_4_, bf16[256,2048]{1,0:T(8,128)(2,1)S(1)} %copy-done.2, ...), custom_call_target="tpu_custom_call" | custom-call | tf_op jit(solution)/shard_map/prepare/pallas_call | solution.py:358
  22.5 0.0 collective-permute-done.5.refs_13_
  22.6 1.0 %collective-permute-done.6.refs_17_ = bf16[40,2048]{1,0:T(8,128)(2,1)S(1)} collective-permute-done((bf16[40,2048]{1,0:T(8,128)(2,1)S(1)}, bf16[40,2048]{1,0:T(8,128)(2,1)S(1)}, u32[]{:S(2)}, u32[]{:S(2)}) %collective-permute-start.6) | collective-permute-done | bytes 163872 | tf_op jit(solution)/shard_map/ppermute | solution.py:370
  23.5 0.0 collective-permute-done.4.refs_12_
  23.6 12.5 %dt_scan_gate.1 = (bf16[256,2048]{1,0:T(8,128)(2,1)}, bf16[128,2048]{1,0:T(8,128)(2,1)}) custom-call(s32[32]{0:T(128)S(1)} %copy-done.7, s32[32]{0:T(128)S(1)} %copy-done.8, s32[32]{0:T(128)S(1)} %copy-done.9, bf16[256,2048]{1,0:T(8,128)(2,1)S(1)} %get-tuple-element.15.refs_0_.refs_3_, bf16[32,2048]{1,0:T(8,128)(2,1)S(1)} %get-tuple-element.21.refs_1_.refs_4_, ...), custom_call_target="tpu_custom_call" | custom-call | tf_op jit(solution)/shard_map/dt_scan_gate/pallas_call | solution.py:358
  (15 shorter events, 0.0 us)
Async XLA Ops:
  0.6 14.7 %copy-start.4 = (bf16[4,2048]{1,0:T(4,128)(2,1)S(1)}, bf16[4,2048]{1,0:T(4,128)(2,1)}, u32[]{:S(2)}) copy-start(bf16[4,2048]{1,0:T(4,128)(2,1)} %refs_4_.3) | copy-start | bytes 49156
  0.6 14.7 %copy-start = (bf16[2048,288]{0,1:T(8,128)(2,1)S(1)}, bf16[2048,288]{0,1:T(8,128)(2,1)}, u32[]{:S(2)}) copy-start(bf16[2048,288]{0,1:T(8,128)(2,1)} %param.18) | copy-start | bytes 3538948
  1.7 13.1 %collective-permute-start.1 = (bf16[40,2048]{1,0:T(8,128)(2,1)S(1)}, bf16[40,2048]{1,0:T(8,128)(2,1)S(1)}, u32[]{:S(2)}, u32[]{:S(2)}) collective-permute-start(bf16[40,2048]{1,0:T(8,128)(2,1)S(1)} %get-tuple-element.19.refs_5_.refs_14_), channel_id=1, source_target_pairs={{0,12},{4,8},{8,4},{12,0},{1,13},{5,9},{9,5},{13,1},{2,14},{6,10},... | collective-permute-start | bytes 491528 | tf_op jit(solution)/shard_map/ppermute | solution.py:370
  6.8 8.5 %collective-permute-start = (bf16[40,2048]{1,0:T(8,128)(2,1)S(1)}, bf16[40,2048]{1,0:T(8,128)(2,1)S(1)}, u32[]{:S(2)}, u32[]{:S(2)}) collective-permute-start(bf16[40,2048]{1,0:T(8,128)(2,1)S(1)} %get-tuple-element.19.refs_5_.refs_14_), channel_id=1, source_target_pairs={{0,4},{4,0},{8,12},{12,8},{1,5},{5,1},{9,13},{13,9},{2,6},{6,2},{1... | collective-permute-start | bytes 491528 | tf_op jit(solution)/shard_map/ppermute | solution.py:370
  6.8 8.0 %collective-permute-start.2 = (bf16[8,2048]{1,0:T(8,128)(2,1)S(1)}, bf16[8,2048]{1,0:T(8,128)(2,1)S(1)}, u32[]{:S(2)}, u32[]{:S(2)}) collective-permute-start(bf16[8,2048]{1,0:T(8,128)(2,1)S(1)} %get-tuple-element.20), channel_id=1, source_target_pairs={{0,8},{4,12},{8,0},{12,4},{1,9},{5,13},{9,1},{13,5},{2,10},{6,14},... | collective-permute-start | bytes 98312 | tf_op jit(solution)/shard_map/ppermute | solution.py:370
  7.4 14.6 %copy-start.2 = (bf16[256,2048]{1,0:T(8,128)(2,1)S(1)}, bf16[256,2048]{1,0:T(8,128)(2,1)}, u32[]{:S(2)}) copy-start(bf16[256,2048]{1,0:T(8,128)(2,1)} %refs_2_.4) | copy-start | bytes 3145732
  7.4 14.6 %copy-start.3 = (f32[16,2048]{1,0:T(8,128)S(1)}, f32[16,2048]{1,0:T(8,128)}, u32[]{:S(2)}) copy-start(f32[16,2048]{1,0:T(8,128)} %refs_3_.1) | copy-start | bytes 393220
  7.4 14.6 %copy-start.5 = (f32[2048]{0:T(1024)S(1)}, f32[2048]{0:T(1024)}, u32[]{:S(2)}) copy-start(f32[2048]{0:T(1024)} %param.22) | copy-start | bytes 24580
  15.3 8.2 %copy-start.1 = (bf16[256,2048]{1,0:T(8,128)(2,1)S(1)}, bf16[256,2048]{1,0:T(8,128)(2,1)}, u32[]{:S(2)}) copy-start(bf16[256,2048]{1,0:T(8,128)(2,1)} %refs_5_.3) | copy-start | bytes 3145732
  15.3 8.2 %copy-start.6 = (f32[2048]{0:T(1024)S(1)}, f32[2048]{0:T(1024)}, u32[]{:S(2)}) copy-start(f32[2048]{0:T(1024)} %param.20) | copy-start | bytes 24580
  15.3 8.2 %copy-start.7 = (s32[32]{0:T(128)S(1)}, s32[32]{0:T(128)}, u32[]{:S(2)}) copy-start(s32[32]{0:T(128)} %refs_0_.3) | copy-start | bytes 388
  15.3 8.2 %copy-start.8 = (s32[32]{0:T(128)S(1)}, s32[32]{0:T(128)}, u32[]{:S(2)}) copy-start(s32[32]{0:T(128)} %refs_1_.1) | copy-start | bytes 388
  15.3 8.2 %copy-start.9 = (s32[32]{0:T(128)S(1)}, s32[32]{0:T(128)}, u32[]{:S(2)}) copy-start(s32[32]{0:T(128)} %refs_2_.5) | copy-start | bytes 388
  16.2 5.8 %collective-permute-start.3 = (bf16[288,256]{1,0:T(8,128)(2,1)S(1)}, bf16[288,256]{1,0:T(8,128)(2,1)S(1)}, u32[]{:S(2)}, u32[]{:S(2)}) collective-permute-start(bf16[288,256]{1,0:T(8,128)(2,1)S(1)} %get-tuple-element.25.refs_10_), channel_id=1, source_target_pairs={{0,2},{1,3},{2,0},{3,1},{4,6},{5,7},{6,4},{7,5},{8,10},{9,11},{10,... | collective-permute-start | bytes 442376 | tf_op jit(solution)/shard_map/ppermute | solution.py:370
  17.7 5.8 %collective-permute-start.6 = (bf16[40,2048]{1,0:T(8,128)(2,1)S(1)}, bf16[40,2048]{1,0:T(8,128)(2,1)S(1)}, u32[]{:S(2)}, u32[]{:S(2)}) collective-permute-start(bf16[40,2048]{1,0:T(8,128)(2,1)S(1)} %collective-permute-done.1.refs_7_.refs_16_), channel_id=1, source_target_pairs={{0,4},{4,0},{8,12},{12,8},{1,5},{5,1},{9,13},{13,9},{2,6},{6,2},{1... | collective-permute-start | bytes 491528 | tf_op jit(solution)/shard_map/ppermute | solution.py:370
  19.1 3.5 %collective-permute-start.5 = (bf16[288,256]{1,0:T(8,128)(2,1)S(1)}, bf16[288,256]{1,0:T(8,128)(2,1)S(1)}, u32[]{:S(2)}, u32[]{:S(2)}) collective-permute-start(bf16[288,256]{1,0:T(8,128)(2,1)S(1)} %get-tuple-element.25.refs_10_), channel_id=1, source_target_pairs={{0,1},{1,0},{2,3},{3,2},{4,5},{5,4},{6,7},{7,6},{8,9},{9,8},{10,11... | collective-permute-start | bytes 442376 | tf_op jit(solution)/shard_map/ppermute | solution.py:370
  22.0 1.5 %collective-permute-start.4 = (bf16[288,256]{1,0:T(8,128)(2,1)S(1)}, bf16[288,256]{1,0:T(8,128)(2,1)S(1)}, u32[]{:S(2)}, u32[]{:S(2)}) collective-permute-start(bf16[288,256]{1,0:T(8,128)(2,1)S(1)} %collective-permute-done.3.refs_11_), channel_id=1, source_target_pairs={{0,1},{1,0},{2,3},{3,2},{4,5},{5,4},{6,7},{7,6},{8,9},{9,8},{10,11... | collective-permute-start | bytes 442376 | tf_op jit(solution)/shard_map/ppermute | solution.py:370

commit v23 on v21

--- a/solution.py
+++ b/solution.py
@@ -188,7 +188,7 @@
     per_dev, n_replica, _, _ = dims
     mixed_ref, head_ref, dtw_ref, dtb_ref, gate_ref, skipped_ref, rate_ref = refs_in[3:10]
     out_hbm, state_hbm = refs_out
-    b_tab, c_tab, dt_v, drive_v, start_tm, final_tm, y_v, out_v, state_v, out_sems, int_sems = scratch[:11]
+    b_tab, c_tab, dt_v, drive_v, start_rm, final_tm, y_v, out_v, state_v, out_sems, int_sems = scratch[:11]
     ints = scratch[11:]
     int_copies = [pltpu.make_async_copy(refs_in[i], ints[i], int_sems.at[i]) for i in range(len(ints))]
     for copy in int_copies:
@@ -254,7 +254,7 @@
                     value = jnp.where(places[r] == p, pieces[p][spot, lanes], value)
             value = value.astype(F32)
             value = jnp.where(lengths[r] > 0, value, jnp.zeros_like(value))
-            start_tm[tile, pl.ds(r, states, stride=per_dev), :] = value
+            start_rm[tile, r * states : (r + 1) * states, :] = value
 
     tiles = 2
     half = states // 4
@@ -305,7 +305,7 @@
                         y_v[tile, now, :] = before + sums[j]
                 return tuple(state)
 
-            state = tuple(start_tm[tile, n * per_dev : (n + 1) * per_dev, :] for tile in group for n in ids)
+            state = tuple(start_rm[tile, pl.ds(n, per_dev, stride=states), :] for tile in group for n in ids)
             if NEW == UNROLL:
                 state = advance(0, state)
             else:
@@ -457,7 +457,7 @@
             vmem((states, rows, LANES), F32),
             vmem((n_tiles, rows, LANES), F32),
             vmem((n_tiles, rows, LANES), F32),
-            vmem((n_tiles, per_dev * (states + 1), LANES), F32),
+            vmem((n_tiles, (per_dev + 1) * states, LANES), F32),
             vmem((n_tiles, per_dev * (states + 1), LANES), F32),
             vmem((n_tiles, rows + per_dev, LANES), F32),
             vmem((rows, channels), BF16),

time: 35.4 us -> 35.4 us (level)
  no operation moved by 1% of the time
where the time goes in v23:
time: 35.4 us; the launch traced here: 35.3 us
  Pallas kernels  18.1 us (51%)
  starting transfers between devices  8.66 us (24%)
  waiting for transfers between devices  7.68 us (22%)
  between operations  0.76 us (2%)
    pallas_call x5, Pallas kernels, call(): pl.pallas_call(split_refs(kernel, dims, len(ins), len(outs)), in_specs=[p...  18.1 us
    ppermute x7, starting transfers between devices, swap(): return lax.ppermute(value, axis, [(i, i ^ mask) for i in range(size)])  8.66 us
    ppermute x7, waiting for transfers between devices, swap(): return lax.ppermute(value, axis, [(i, i ^ mask) for i in range(size)])  7.68 us
  transfers between devices with their start and end apart: 7, of which 4 were waited for; matrix products, arithmetic and copies ran while one was open for 0% of the time, Pallas kernels for 13%

profile of v23, /device:TPU:0, one launch (start us, length us, event | category | flops | bytes accessed | tf_op | source)
XLA Modules:
  0.0 35.3 jit_solution(2311615366911684835)
XLA Ops:
  0.6 0.0 copy-start.4
  0.6 0.0 copy-start
  0.7 1.0 %pack.1 = (bf16[40,2048]{1,0:T(8,128)(2,1)S(1)}, bf16[8,2048]{1,0:T(8,128)(2,1)S(1)}) custom-call(bf16[32,2048]{1,0:T(8,128)(2,1)} %bitcast.11, bf16[3,2,2048]{2,1,0:T(2,128)(2,1)} %bitcast.12), custom_call_target="tpu_custom_call" | custom-call | tf_op jit(solution)/shard_map/pack/pallas_call | solution.py:356
  1.7 5.1 %collective-permute-start.1 = (bf16[40,2048]{1,0:T(8,128)(2,1)S(1)}, bf16[40,2048]{1,0:T(8,128)(2,1)S(1)}, u32[]{:S(2)}, u32[]{:S(2)}) collective-permute-start(bf16[40,2048]{1,0:T(8,128)(2,1)S(1)} %get-tuple-element.19.refs_5_.refs_14_), channel_id=1, source_target_pairs={{0,12},{4,8},{8,4},{12,0},{1,13},{5,9},{9,5},{13,1},{2,14},{6,10},... | collective-permute-start | bytes 491528 | tf_op jit(solution)/shard_map/ppermute | solution.py:368
  6.8 0.0 collective-permute-start
  6.8 0.6 %collective-permute-start.2 = (bf16[8,2048]{1,0:T(8,128)(2,1)S(1)}, bf16[8,2048]{1,0:T(8,128)(2,1)S(1)}, u32[]{:S(2)}, u32[]{:S(2)}) collective-permute-start(bf16[8,2048]{1,0:T(8,128)(2,1)S(1)} %get-tuple-element.20), channel_id=1, source_target_pairs={{0,8},{4,12},{8,0},{12,4},{1,9},{5,13},{9,1},{13,5},{2,10},{6,14},... | collective-permute-start | bytes 98312 | tf_op jit(solution)/shard_map/ppermute | solution.py:368
  7.4 4.1 %conv_project.1 = (bf16[256,2048]{1,0:T(8,128)(2,1)S(1)}, f32[32,2048]{1,0:T(8,128)S(1)}, bf16[288,256]{1,0:T(8,128)(2,1)S(1)}, s32[32,128]{1,0:T(8,128)S(1)}) custom-call(bf16[256,2048]{1,0:T(8,128)(2,1)} %refs_0_.2, bf16[288,2048]{1,0:T(8,128)(2,1)} %bitcast.7, bf16[4,2048]{1,0:T(4,128)(2,1)} %refs_4_.3, f32[1,2048]{1,0:T(1,128)} %bitcast.13, s32[32]{0:T(128)} %refs_0_.3, ...), custom_call_target="tpu_custom_call" | custom-call | tf_op jit(solution)/shard_map/conv_project/pallas_call | solution.py:356
  11.6 3.2 %collective-permute-done.2.refs_8_ = bf16[8,2048]{1,0:T(8,128)(2,1)S(1)} collective-permute-done((bf16[8,2048]{1,0:T(8,128)(2,1)S(1)}, bf16[8,2048]{1,0:T(8,128)(2,1)S(1)}, u32[]{:S(2)}, u32[]{:S(2)}) %collective-permute-start.2) | collective-permute-done | bytes 32800 | tf_op jit(solution)/shard_map/ppermute | solution.py:368
  14.8 0.0 collective-permute-done.1.refs_7_.refs_16_
  14.8 0.5 %collective-permute-done.refs_6_.refs_15_ = bf16[40,2048]{1,0:T(8,128)(2,1)S(1)} collective-permute-done((bf16[40,2048]{1,0:T(8,128)(2,1)S(1)}, bf16[40,2048]{1,0:T(8,128)(2,1)S(1)}, u32[]{:S(2)}, u32[]{:S(2)}) %collective-permute-start) | collective-permute-done | bytes 163872 | tf_op jit(solution)/shard_map/ppermute | solution.py:368
  15.3 0.0 copy-start.7
  15.3 0.0 copy-start.8
  15.3 0.0 copy-start.9
  15.4 0.8 %history.1 = (bf16[32,2048]{1,0:T(8,128)(2,1)S(1)}, bf16[288,256]{1,0:T(8,128)(2,1)S(1)}) custom-call(s32[32,128]{1,0:T(8,128)S(1)} %get-tuple-element.16.refs_0_, f32[32,2048]{1,0:T(8,128)S(1)} %get-tuple-element.17.refs_1_, bf16[288,256]{1,0:T(8,128)(2,1)S(1)} %get-tuple-element.18.refs_2_, bf16[288,2048]{1,0:T(8,128)(2,1)S(1)} %bitcast.8, ...), custom_call_target="tpu_custom_call" | custom-call | tf_op jit(solution)/shard_map/history/pallas_call | solution.py:356
  16.2 1.6 %collective-permute-start.3 = (bf16[288,256]{1,0:T(8,128)(2,1)S(1)}, bf16[288,256]{1,0:T(8,128)(2,1)S(1)}, u32[]{:S(2)}, u32[]{:S(2)}) collective-permute-start(bf16[288,256]{1,0:T(8,128)(2,1)S(1)} %get-tuple-element.25.refs_10_), channel_id=1, source_target_pairs={{0,2},{1,3},{2,0},{3,1},{4,6},{5,7},{6,4},{7,5},{8,10},{9,11},{10,... | collective-permute-start | bytes 442376 | tf_op jit(solution)/shard_map/ppermute | solution.py:368
  17.7 1.3 %collective-permute-start.6 = (bf16[40,2048]{1,0:T(8,128)(2,1)S(1)}, bf16[40,2048]{1,0:T(8,128)(2,1)S(1)}, u32[]{:S(2)}, u32[]{:S(2)}) collective-permute-start(bf16[40,2048]{1,0:T(8,128)(2,1)S(1)} %collective-permute-done.1.refs_7_.refs_16_), channel_id=1, source_target_pairs={{0,4},{4,0},{8,12},{12,8},{1,5},{5,1},{9,13},{13,9},{2,6},{6,2},{1... | collective-permute-start | bytes 491528 | tf_op jit(solution)/shard_map/ppermute | solution.py:368
  19.1 0.0 collective-permute-start.5
  19.1 2.9 %collective-permute-done.3.refs_11_ = bf16[288,256]{1,0:T(8,128)(2,1)S(1)} collective-permute-done((bf16[288,256]{1,0:T(8,128)(2,1)S(1)}, bf16[288,256]{1,0:T(8,128)(2,1)S(1)}, u32[]{:S(2)}, u32[]{:S(2)}) %collective-permute-start.3) | collective-permute-done | bytes 147488 | tf_op jit(solution)/shard_map/ppermute | solution.py:368
  22.0 0.0 collective-permute-start.4
  22.0 0.5 %prepare.1 = (f32[256,2048]{1,0:T(8,128)S(1)}, f32[16,256,128]{2,1,0:T(8,128)S(1)}, f32[16,2048]{1,0:T(8,128)S(1)}) custom-call(bf16[256,2048]{1,0:T(8,128)(2,1)S(1)} %get-tuple-element.15.refs_0_.refs_3_, bf16[32,2048]{1,0:T(8,128)(2,1)S(1)} %get-tuple-element.21.refs_1_.refs_4_, bf16[256,2048]{1,0:T(8,128)(2,1)S(1)} %copy-done.2, ...), custom_call_target="tpu_custom_call" | custom-call | tf_op jit(solution)/shard_map/prepare/pallas_call | solution.py:356
  22.5 0.0 collective-permute-done.5.refs_13_
  22.6 1.0 %collective-permute-done.6.refs_17_ = bf16[40,2048]{1,0:T(8,128)(2,1)S(1)} collective-permute-done((bf16[40,2048]{1,0:T(8,128)(2,1)S(1)}, bf16[40,2048]{1,0:T(8,128)(2,1)S(1)}, u32[]{:S(2)}, u32[]{:S(2)}) %collective-permute-start.6) | collective-permute-done | bytes 163872 | tf_op jit(solution)/shard_map/ppermute | solution.py:368
  23.5 0.0 collective-permute-done.4.refs_12_
  23.6 11.7 %dt_scan_gate.1 = (bf16[256,2048]{1,0:T(8,128)(2,1)}, bf16[128,2048]{1,0:T(8,128)(2,1)}) custom-call(s32[32]{0:T(128)S(1)} %copy-done.7, s32[32]{0:T(128)S(1)} %copy-done.8, s32[32]{0:T(128)S(1)} %copy-done.9, bf16[256,2048]{1,0:T(8,128)(2,1)S(1)} %get-tuple-element.15.refs_0_.refs_3_, bf16[32,2048]{1,0:T(8,128)(2,1)S(1)} %get-tuple-element.21.refs_1_.refs_4_, ...), custom_call_target="tpu_custom_call" | custom-call | tf_op jit(solution)/shard_map/dt_scan_gate/pallas_call | solution.py:356
  (15 shorter events, 0.0 us)
Async XLA Ops:
  0.6 14.7 %copy-start.4 = (bf16[4,2048]{1,0:T(4,128)(2,1)S(1)}, bf16[4,2048]{1,0:T(4,128)(2,1)}, u32[]{:S(2)}) copy-start(bf16[4,2048]{1,0:T(4,128)(2,1)} %refs_4_.3) | copy-start | bytes 49156
  0.6 14.7 %copy-start = (bf16[2048,288]{0,1:T(8,128)(2,1)S(1)}, bf16[2048,288]{0,1:T(8,128)(2,1)}, u32[]{:S(2)}) copy-start(bf16[2048,288]{0,1:T(8,128)(2,1)} %param.18) | copy-start | bytes 3538948
  1.7 13.1 %collective-permute-start.1 = (bf16[40,2048]{1,0:T(8,128)(2,1)S(1)}, bf16[40,2048]{1,0:T(8,128)(2,1)S(1)}, u32[]{:S(2)}, u32[]{:S(2)}) collective-permute-start(bf16[40,2048]{1,0:T(8,128)(2,1)S(1)} %get-tuple-element.19.refs_5_.refs_14_), channel_id=1, source_target_pairs={{0,12},{4,8},{8,4},{12,0},{1,13},{5,9},{9,5},{13,1},{2,14},{6,10},... | collective-permute-start | bytes 491528 | tf_op jit(solution)/shard_map/ppermute | solution.py:368
  6.8 8.5 %collective-permute-start = (bf16[40,2048]{1,0:T(8,128)(2,1)S(1)}, bf16[40,2048]{1,0:T(8,128)(2,1)S(1)}, u32[]{:S(2)}, u32[]{:S(2)}) collective-permute-start(bf16[40,2048]{1,0:T(8,128)(2,1)S(1)} %get-tuple-element.19.refs_5_.refs_14_), channel_id=1, source_target_pairs={{0,4},{4,0},{8,12},{12,8},{1,5},{5,1},{9,13},{13,9},{2,6},{6,2},{1... | collective-permute-start | bytes 491528 | tf_op jit(solution)/shard_map/ppermute | solution.py:368
  6.8 8.0 %collective-permute-start.2 = (bf16[8,2048]{1,0:T(8,128)(2,1)S(1)}, bf16[8,2048]{1,0:T(8,128)(2,1)S(1)}, u32[]{:S(2)}, u32[]{:S(2)}) collective-permute-start(bf16[8,2048]{1,0:T(8,128)(2,1)S(1)} %get-tuple-element.20), channel_id=1, source_target_pairs={{0,8},{4,12},{8,0},{12,4},{1,9},{5,13},{9,1},{13,5},{2,10},{6,14},... | collective-permute-start | bytes 98312 | tf_op jit(solution)/shard_map/ppermute | solution.py:368
  7.4 14.6 %copy-start.2 = (bf16[256,2048]{1,0:T(8,128)(2,1)S(1)}, bf16[256,2048]{1,0:T(8,128)(2,1)}, u32[]{:S(2)}) copy-start(bf16[256,2048]{1,0:T(8,128)(2,1)} %refs_2_.4) | copy-start | bytes 3145732
  7.4 14.6 %copy-start.3 = (f32[16,2048]{1,0:T(8,128)S(1)}, f32[16,2048]{1,0:T(8,128)}, u32[]{:S(2)}) copy-start(f32[16,2048]{1,0:T(8,128)} %refs_3_.1) | copy-start | bytes 393220
  7.4 14.6 %copy-start.5 = (f32[2048]{0:T(1024)S(1)}, f32[2048]{0:T(1024)}, u32[]{:S(2)}) copy-start(f32[2048]{0:T(1024)} %param.22) | copy-start | bytes 24580
  15.3 8.2 %copy-start.1 = (bf16[256,2048]{1,0:T(8,128)(2,1)S(1)}, bf16[256,2048]{1,0:T(8,128)(2,1)}, u32[]{:S(2)}) copy-start(bf16[256,2048]{1,0:T(8,128)(2,1)} %refs_5_.3) | copy-start | bytes 3145732
  15.3 8.2 %copy-start.6 = (f32[2048]{0:T(1024)S(1)}, f32[2048]{0:T(1024)}, u32[]{:S(2)}) copy-start(f32[2048]{0:T(1024)} %param.20) | copy-start | bytes 24580
  15.3 8.2 %copy-start.7 = (s32[32]{0:T(128)S(1)}, s32[32]{0:T(128)}, u32[]{:S(2)}) copy-start(s32[32]{0:T(128)} %refs_0_.3) | copy-start | bytes 388
  15.3 8.2 %copy-start.8 = (s32[32]{0:T(128)S(1)}, s32[32]{0:T(128)}, u32[]{:S(2)}) copy-start(s32[32]{0:T(128)} %refs_1_.1) | copy-start | bytes 388
  15.3 8.2 %copy-start.9 = (s32[32]{0:T(128)S(1)}, s32[32]{0:T(128)}, u32[]{:S(2)}) copy-start(s32[32]{0:T(128)} %refs_2_.5) | copy-start | bytes 388
  16.2 5.8 %collective-permute-start.3 = (bf16[288,256]{1,0:T(8,128)(2,1)S(1)}, bf16[288,256]{1,0:T(8,128)(2,1)S(1)}, u32[]{:S(2)}, u32[]{:S(2)}) collective-permute-start(bf16[288,256]{1,0:T(8,128)(2,1)S(1)} %get-tuple-element.25.refs_10_), channel_id=1, source_target_pairs={{0,2},{1,3},{2,0},{3,1},{4,6},{5,7},{6,4},{7,5},{8,10},{9,11},{10,... | collective-permute-start | bytes 442376 | tf_op jit(solution)/shard_map/ppermute | solution.py:368
  17.7 5.8 %collective-permute-start.6 = (bf16[40,2048]{1,0:T(8,128)(2,1)S(1)}, bf16[40,2048]{1,0:T(8,128)(2,1)S(1)}, u32[]{:S(2)}, u32[]{:S(2)}) collective-permute-start(bf16[40,2048]{1,0:T(8,128)(2,1)S(1)} %collective-permute-done.1.refs_7_.refs_16_), channel_id=1, source_target_pairs={{0,4},{4,0},{8,12},{12,8},{1,5},{5,1},{9,13},{13,9},{2,6},{6,2},{1... | collective-permute-start | bytes 491528 | tf_op jit(solution)/shard_map/ppermute | solution.py:368
  19.1 3.5 %collective-permute-start.5 = (bf16[288,256]{1,0:T(8,128)(2,1)S(1)}, bf16[288,256]{1,0:T(8,128)(2,1)S(1)}, u32[]{:S(2)}, u32[]{:S(2)}) collective-permute-start(bf16[288,256]{1,0:T(8,128)(2,1)S(1)} %get-tuple-element.25.refs_10_), channel_id=1, source_target_pairs={{0,1},{1,0},{2,3},{3,2},{4,5},{5,4},{6,7},{7,6},{8,9},{9,8},{10,11... | collective-permute-start | bytes 442376 | tf_op jit(solution)/shard_map/ppermute | solution.py:368
  22.0 1.5 %collective-permute-start.4 = (bf16[288,256]{1,0:T(8,128)(2,1)S(1)}, bf16[288,256]{1,0:T(8,128)(2,1)S(1)}, u32[]{:S(2)}, u32[]{:S(2)}) collective-permute-start(bf16[288,256]{1,0:T(8,128)(2,1)S(1)} %collective-permute-done.3.refs_11_), channel_id=1, source_target_pairs={{0,1},{1,0},{2,3},{3,2},{4,5},{5,4},{6,7},{7,6},{8,9},{9,8},{10,11... | collective-permute-start | bytes 442376 | tf_op jit(solution)/shard_map/ppermute | solution.py:368

commit v24 on v20

--- a/solution.py
+++ b/solution.py
@@ -10,7 +10,7 @@
 NEW = 32
 LANES = 128
 MIB = 1024 * 1024
-UNROLL = 32
+UNROLL = 16
 LOG2E = 1.4426950408889634
 F32, BF16 = jnp.float32, jnp.bfloat16
 NT = (((1,), (1,)), ((), ()))

time: 35.4 us -> 35.6 us (level)
  no operation moved by 1% of the time
where the time goes in v24:
time: 35.6 us; the launch traced here: 35.4 us
  Pallas kernels  18.7 us (53%)
  starting transfers between devices  8.67 us (24%)
  waiting for transfers between devices  5.32 us (15%)
  local copies, waits for them, and re-layouts  2 us (6%)
  between operations  0.74 us (2%)
    pallas_call x5, Pallas kernels, call(): pl.pallas_call(split_refs(kernel, dims, len(ins), len(outs)), in_specs=[p...  18.7 us
    ppermute x7, starting transfers between devices, swap(): return lax.ppermute(value, axis, [(i, i ^ mask) for i in range(size)])  8.67 us
    ppermute x7, waiting for transfers between devices, swap(): return lax.ppermute(value, axis, [(i, i ^ mask) for i in range(size)])  5.32 us
    unnamed x22, local copies, waits for them, and re-layouts  2 us
  transfers between devices with their start and end apart: 7, of which 4 were waited for; matrix products, arithmetic and copies ran while one was open for 0% of the time, Pallas kernels for 14%

profile of v24, /device:TPU:0, one launch (start us, length us, event | category | flops | bytes accessed | tf_op | source)
XLA Modules:
  0.0 35.4 jit_solution(3739720692558918822)
XLA Ops:
  0.6 0.0 copy-start.4
  0.6 0.0 copy-start
  0.7 1.0 %pack.1 = (bf16[40,2048]{1,0:T(8,128)(2,1)S(1)}, bf16[8,2048]{1,0:T(8,128)(2,1)S(1)}) custom-call(bf16[32,2048]{1,0:T(8,128)(2,1)} %bitcast.11, bf16[3,2,2048]{2,1,0:T(2,128)(2,1)} %bitcast.12), custom_call_target="tpu_custom_call" | custom-call | tf_op jit(solution)/shard_map/pack/pallas_call | solution.py:353
  1.7 5.1 %collective-permute-start.1 = (bf16[40,2048]{1,0:T(8,128)(2,1)S(1)}, bf16[40,2048]{1,0:T(8,128)(2,1)S(1)}, u32[]{:S(2)}, u32[]{:S(2)}) collective-permute-start(bf16[40,2048]{1,0:T(8,128)(2,1)S(1)} %get-tuple-element.19.refs_5_.refs_14_), channel_id=1, source_target_pairs={{0,12},{4,8},{8,4},{12,0},{1,13},{5,9},{9,5},{13,1},{2,14},{6,10},... | collective-permute-start | bytes 491528 | tf_op jit(solution)/shard_map/ppermute | solution.py:365
  6.8 0.0 collective-permute-start
  6.8 0.6 %collective-permute-start.2 = (bf16[8,2048]{1,0:T(8,128)(2,1)S(1)}, bf16[8,2048]{1,0:T(8,128)(2,1)S(1)}, u32[]{:S(2)}, u32[]{:S(2)}) collective-permute-start(bf16[8,2048]{1,0:T(8,128)(2,1)S(1)} %get-tuple-element.20), channel_id=1, source_target_pairs={{0,8},{4,12},{8,0},{12,4},{1,9},{5,13},{9,1},{13,5},{2,10},{6,14},... | collective-permute-start | bytes 98312 | tf_op jit(solution)/shard_map/ppermute | solution.py:365
  7.4 0.7 %copy-done.7 = s32[32]{0:T(128)S(1)} copy-done((s32[32]{0:T(128)S(1)}, s32[32]{0:T(128)}, u32[]{:S(2)}) %copy-start.7) | copy-done | bytes 152
  8.1 0.7 %copy-done.8 = s32[32]{0:T(128)S(1)} copy-done((s32[32]{0:T(128)S(1)}, s32[32]{0:T(128)}, u32[]{:S(2)}) %copy-start.8) | copy-done | bytes 152
  8.8 0.7 %copy-done.9 = s32[32]{0:T(128)S(1)} copy-done((s32[32]{0:T(128)S(1)}, s32[32]{0:T(128)}, u32[]{:S(2)}) %copy-start.9) | copy-done | bytes 152
  9.4 4.5 %conv_project.1 = (bf16[256,2048]{1,0:T(8,128)(2,1)S(1)}, f32[32,2048]{1,0:T(8,128)S(1)}, bf16[288,256]{1,0:T(8,128)(2,1)S(1)}, s32[32,128]{1,0:T(8,128)S(1)}) custom-call(bf16[256,2048]{1,0:T(8,128)(2,1)} %refs_0_.2, bf16[288,2048]{1,0:T(8,128)(2,1)} %bitcast.7, bf16[4,2048]{1,0:T(4,128)(2,1)} %refs_4_.3, f32[1,2048]{1,0:T(1,128)} %bitcast.13, ...), custom_call_target="tpu_custom_call" | custom-call | tf_op jit(solution)/shard_map/conv_project/pallas_call | solution.py:353
  13.9 0.9 %collective-permute-done.2.refs_8_ = bf16[8,2048]{1,0:T(8,128)(2,1)S(1)} collective-permute-done((bf16[8,2048]{1,0:T(8,128)(2,1)S(1)}, bf16[8,2048]{1,0:T(8,128)(2,1)S(1)}, u32[]{:S(2)}, u32[]{:S(2)}) %collective-permute-start.2) | collective-permute-done | bytes 32800 | tf_op jit(solution)/shard_map/ppermute | solution.py:365
  14.8 0.0 collective-permute-done.1.refs_7_.refs_16_
  14.8 0.5 %collective-permute-done.refs_6_.refs_15_ = bf16[40,2048]{1,0:T(8,128)(2,1)S(1)} collective-permute-done((bf16[40,2048]{1,0:T(8,128)(2,1)S(1)}, bf16[40,2048]{1,0:T(8,128)(2,1)S(1)}, u32[]{:S(2)}, u32[]{:S(2)}) %collective-permute-start) | collective-permute-done | bytes 163872 | tf_op jit(solution)/shard_map/ppermute | solution.py:365
  15.3 0.0 copy-start.10
  15.3 0.8 %history.1 = (bf16[32,2048]{1,0:T(8,128)(2,1)S(1)}, bf16[288,256]{1,0:T(8,128)(2,1)S(1)}) custom-call(s32[32,128]{1,0:T(8,128)S(1)} %get-tuple-element.16.refs_0_, f32[32,2048]{1,0:T(8,128)S(1)} %get-tuple-element.17.refs_1_, bf16[288,256]{1,0:T(8,128)(2,1)S(1)} %get-tuple-element.18.refs_2_, bf16[288,2048]{1,0:T(8,128)(2,1)S(1)} %bitcast.8, ...), custom_call_target="tpu_custom_call" | custom-call | tf_op jit(solution)/shard_map/history/pallas_call | solution.py:353
  16.1 1.6 %collective-permute-start.3 = (bf16[288,256]{1,0:T(8,128)(2,1)S(1)}, bf16[288,256]{1,0:T(8,128)(2,1)S(1)}, u32[]{:S(2)}, u32[]{:S(2)}) collective-permute-start(bf16[288,256]{1,0:T(8,128)(2,1)S(1)} %get-tuple-element.25.refs_10_), channel_id=1, source_target_pairs={{0,2},{1,3},{2,0},{3,1},{4,6},{5,7},{6,4},{7,5},{8,10},{9,11},{10,... | collective-permute-start | bytes 442376 | tf_op jit(solution)/shard_map/ppermute | solution.py:365
  17.7 1.3 %collective-permute-start.6 = (bf16[40,2048]{1,0:T(8,128)(2,1)S(1)}, bf16[40,2048]{1,0:T(8,128)(2,1)S(1)}, u32[]{:S(2)}, u32[]{:S(2)}) collective-permute-start(bf16[40,2048]{1,0:T(8,128)(2,1)S(1)} %collective-permute-done.1.refs_7_.refs_16_), channel_id=1, source_target_pairs={{0,4},{4,0},{8,12},{12,8},{1,5},{5,1},{9,13},{13,9},{2,6},{6,2},{1... | collective-permute-start | bytes 491528 | tf_op jit(solution)/shard_map/ppermute | solution.py:365
  19.1 0.0 collective-permute-start.5
  19.1 2.9 %collective-permute-done.3.refs_11_ = bf16[288,256]{1,0:T(8,128)(2,1)S(1)} collective-permute-done((bf16[288,256]{1,0:T(8,128)(2,1)S(1)}, bf16[288,256]{1,0:T(8,128)(2,1)S(1)}, u32[]{:S(2)}, u32[]{:S(2)}) %collective-permute-start.3) | collective-permute-done | bytes 147488 | tf_op jit(solution)/shard_map/ppermute | solution.py:365
  22.0 0.0 collective-permute-start.4
  22.0 0.5 %prepare.1 = (f32[256,2048]{1,0:T(8,128)S(1)}, f32[16,256,128]{2,1,0:T(8,128)S(1)}, f32[16,2048]{1,0:T(8,128)S(1)}) custom-call(bf16[256,2048]{1,0:T(8,128)(2,1)S(1)} %get-tuple-element.15.refs_0_.refs_3_, bf16[32,2048]{1,0:T(8,128)(2,1)S(1)} %get-tuple-element.21.refs_1_.refs_4_, bf16[256,2048]{1,0:T(8,128)(2,1)S(1)} %copy-done.2, ...), custom_call_target="tpu_custom_call" | custom-call | tf_op jit(solution)/shard_map/prepare/pallas_call | solution.py:353
  22.5 0.0 collective-permute-done.5.refs_13_
  22.5 1.0 %collective-permute-done.6.refs_17_ = bf16[40,2048]{1,0:T(8,128)(2,1)S(1)} collective-permute-done((bf16[40,2048]{1,0:T(8,128)(2,1)S(1)}, bf16[40,2048]{1,0:T(8,128)(2,1)S(1)}, u32[]{:S(2)}, u32[]{:S(2)}) %collective-permute-start.6) | collective-permute-done | bytes 163872 | tf_op jit(solution)/shard_map/ppermute | solution.py:365
  23.5 11.9 %dt_scan_gate.1 = (bf16[256,2048]{1,0:T(8,128)(2,1)}, bf16[128,2048]{1,0:T(8,128)(2,1)}) custom-call(s32[32]{0:T(128)S(1)} %copy-done.7, s32[32]{0:T(128)S(1)} %copy-done.8, s32[32]{0:T(128)S(1)} %copy-done.10, bf16[256,2048]{1,0:T(8,128)(2,1)S(1)} %get-tuple-element.15.refs_0_.refs_3_, bf16[32,2048]{1,0:T(8,128)(2,1)S(1)} %get-tuple-element.21.refs_1_.refs_4_, ...), custom_call_target="tpu_custom_call" | custom-call | tf_op jit(solution)/shard_map/dt_scan_gate/pallas_call | solution.py:353
  (17 shorter events, 0.0 us)
Async XLA Ops:
  0.6 14.7 %copy-start.4 = (bf16[4,2048]{1,0:T(4,128)(2,1)S(1)}, bf16[4,2048]{1,0:T(4,128)(2,1)}, u32[]{:S(2)}) copy-start(bf16[4,2048]{1,0:T(4,128)(2,1)} %refs_4_.3) | copy-start | bytes 49156
  0.6 14.7 %copy-start = (bf16[2048,288]{0,1:T(8,128)(2,1)S(1)}, bf16[2048,288]{0,1:T(8,128)(2,1)}, u32[]{:S(2)}) copy-start(bf16[2048,288]{0,1:T(8,128)(2,1)} %param.18) | copy-start | bytes 3538948
  1.7 13.1 %collective-permute-start.1 = (bf16[40,2048]{1,0:T(8,128)(2,1)S(1)}, bf16[40,2048]{1,0:T(8,128)(2,1)S(1)}, u32[]{:S(2)}, u32[]{:S(2)}) collective-permute-start(bf16[40,2048]{1,0:T(8,128)(2,1)S(1)} %get-tuple-element.19.refs_5_.refs_14_), channel_id=1, source_target_pairs={{0,12},{4,8},{8,4},{12,0},{1,13},{5,9},{9,5},{13,1},{2,14},{6,10},... | collective-permute-start | bytes 491528 | tf_op jit(solution)/shard_map/ppermute | solution.py:365
  6.8 8.5 %collective-permute-start = (bf16[40,2048]{1,0:T(8,128)(2,1)S(1)}, bf16[40,2048]{1,0:T(8,128)(2,1)S(1)}, u32[]{:S(2)}, u32[]{:S(2)}) collective-permute-start(bf16[40,2048]{1,0:T(8,128)(2,1)S(1)} %get-tuple-element.19.refs_5_.refs_14_), channel_id=1, source_target_pairs={{0,4},{4,0},{8,12},{12,8},{1,5},{5,1},{9,13},{13,9},{2,6},{6,2},{1... | collective-permute-start | bytes 491528 | tf_op jit(solution)/shard_map/ppermute | solution.py:365
  6.8 8.0 %collective-permute-start.2 = (bf16[8,2048]{1,0:T(8,128)(2,1)S(1)}, bf16[8,2048]{1,0:T(8,128)(2,1)S(1)}, u32[]{:S(2)}, u32[]{:S(2)}) collective-permute-start(bf16[8,2048]{1,0:T(8,128)(2,1)S(1)} %get-tuple-element.20), channel_id=1, source_target_pairs={{0,8},{4,12},{8,0},{12,4},{1,9},{5,13},{9,1},{13,5},{2,10},{6,14},... | collective-permute-start | bytes 98312 | tf_op jit(solution)/shard_map/ppermute | solution.py:365
  7.4 0.7 %copy-start.7 = (s32[32]{0:T(128)S(1)}, s32[32]{0:T(128)}, u32[]{:S(2)}) copy-start(s32[32]{0:T(128)} %refs_0_.3) | copy-start | bytes 388
  8.1 0.7 %copy-start.8 = (s32[32]{0:T(128)S(1)}, s32[32]{0:T(128)}, u32[]{:S(2)}) copy-start(s32[32]{0:T(128)} %refs_1_.1) | copy-start | bytes 388
  8.7 0.7 %copy-start.9 = (s32[32]{0:T(128)S(1)}, s32[32]{0:T(128)}, u32[]{:S(2)}) copy-start(s32[32]{0:T(128)} %refs_2_.5) | copy-start | bytes 388
  9.4 12.6 %copy-start.2 = (bf16[256,2048]{1,0:T(8,128)(2,1)S(1)}, bf16[256,2048]{1,0:T(8,128)(2,1)}, u32[]{:S(2)}) copy-start(bf16[256,2048]{1,0:T(8,128)(2,1)} %refs_2_.4) | copy-start | bytes 3145732
  9.4 12.6 %copy-start.3 = (f32[16,2048]{1,0:T(8,128)S(1)}, f32[16,2048]{1,0:T(8,128)}, u32[]{:S(2)}) copy-start(f32[16,2048]{1,0:T(8,128)} %refs_3_.1) | copy-start | bytes 393220
  9.4 12.6 %copy-start.5 = (f32[2048]{0:T(1024)S(1)}, f32[2048]{0:T(1024)}, u32[]{:S(2)}) copy-start(f32[2048]{0:T(1024)} %param.22) | copy-start | bytes 24580
  15.3 8.2 %copy-start.1 = (bf16[256,2048]{1,0:T(8,128)(2,1)S(1)}, bf16[256,2048]{1,0:T(8,128)(2,1)}, u32[]{:S(2)}) copy-start(bf16[256,2048]{1,0:T(8,128)(2,1)} %refs_5_.3) | copy-start | bytes 3145732
  15.3 8.2 %copy-start.6 = (f32[2048]{0:T(1024)S(1)}, f32[2048]{0:T(1024)}, u32[]{:S(2)}) copy-start(f32[2048]{0:T(1024)} %param.20) | copy-start | bytes 24580
  15.3 8.2 %copy-start.10 = (s32[32]{0:T(128)S(1)}, s32[32]{0:T(128)}, u32[]{:S(2)}) copy-start(s32[32]{0:T(128)} %refs_2_.5) | copy-start | bytes 388
  16.1 5.8 %collective-permute-start.3 = (bf16[288,256]{1,0:T(8,128)(2,1)S(1)}, bf16[288,256]{1,0:T(8,128)(2,1)S(1)}, u32[]{:S(2)}, u32[]{:S(2)}) collective-permute-start(bf16[288,256]{1,0:T(8,128)(2,1)S(1)} %get-tuple-element.25.refs_10_), channel_id=1, source_target_pairs={{0,2},{1,3},{2,0},{3,1},{4,6},{5,7},{6,4},{7,5},{8,10},{9,11},{10,... | collective-permute-start | bytes 442376 | tf_op jit(solution)/shard_map/ppermute | solution.py:365
  17.7 5.8 %collective-permute-start.6 = (bf16[40,2048]{1,0:T(8,128)(2,1)S(1)}, bf16[40,2048]{1,0:T(8,128)(2,1)S(1)}, u32[]{:S(2)}, u32[]{:S(2)}) collective-permute-start(bf16[40,2048]{1,0:T(8,128)(2,1)S(1)} %collective-permute-done.1.refs_7_.refs_16_), channel_id=1, source_target_pairs={{0,4},{4,0},{8,12},{12,8},{1,5},{5,1},{9,13},{13,9},{2,6},{6,2},{1... | collective-permute-start | bytes 491528 | tf_op jit(solution)/shard_map/ppermute | solution.py:365
  19.1 3.5 %collective-permute-start.5 = (bf16[288,256]{1,0:T(8,128)(2,1)S(1)}, bf16[288,256]{1,0:T(8,128)(2,1)S(1)}, u32[]{:S(2)}, u32[]{:S(2)}) collective-permute-start(bf16[288,256]{1,0:T(8,128)(2,1)S(1)} %get-tuple-element.25.refs_10_), channel_id=1, source_target_pairs={{0,1},{1,0},{2,3},{3,2},{4,5},{5,4},{6,7},{7,6},{8,9},{9,8},{10,11... | collective-permute-start | bytes 442376 | tf_op jit(solution)/shard_map/ppermute | solution.py:365
  22.0 1.5 %collective-permute-start.4 = (bf16[288,256]{1,0:T(8,128)(2,1)S(1)}, bf16[288,256]{1,0:T(8,128)(2,1)S(1)}, u32[]{:S(2)}, u32[]{:S(2)}) collective-permute-start(bf16[288,256]{1,0:T(8,128)(2,1)S(1)} %collective-permute-done.3.refs_11_), channel_id=1, source_target_pairs={{0,1},{1,0},{2,3},{3,2},{4,5},{5,4},{6,7},{7,6},{8,9},{9,8},{10,11... | collective-permute-start | bytes 442376 | tf_op jit(solution)/shard_map/ppermute | solution.py:365
